TPU v7x, 32 devices: a whole 2x2x4 slice. The times are simulated.
32 devices in a mesh: section: 4 (over x, core), fsdp: 4 (over z), dp: 2 (over y).
Axes of the slice: x: 2, y: 2, z: 4, core: 2. Of those that a mesh axis runs over, the one named last changes fastest.
Arguments:
- section_inputs: bfloat16 [4, 2, 512, 4096], P('section', 'dp', 'fsdp'), may hold values from -6 to 6
- queries: bfloat16 [4, 2, 512, 4096], P('section', 'dp', 'fsdp'), may hold values from -110 to 110
- keys: bfloat16 [4, 2, 512, 1024], P('section', 'dp', 'fsdp'), may hold values from -4.5 to 4.5
- w_value: bfloat16 [4, 4096, 1024], P('section', 'fsdp'), may hold values from -0.09375 to 0.09375
- gain: bfloat16 [4, 4096], P('section', 'fsdp'), may hold values from 0.5 to 1.5
- section_grads_in: bfloat16 [4, 2, 512, 4096], P('section', 'dp', 'fsdp'), may hold values from -6 to 6
Outputs:
- passed_grads: bfloat16 [4, 2, 512, 4096], P('section', 'dp', 'fsdp')
- w_value_grad: bfloat16 [4, 4096, 1024], P('section', ('fsdp', 'dp'))
- gain_grad: float32 [4, 4096], P('section', ('fsdp', 'dp'))
All inputs are finite; a program needn't handle non-finite values.
Results may differ from a plain program's by a relative error of at most 0.029.
Values may be sent and summed in bfloat16 or wider, within the bound.
No kernel may reach another device: no remote copies, remote signals or barrier semaphores. Data moves between devices by JAX's collectives and lax.ppermute only.
A program may use at most 64 MiB of HBM per device.

v0:
```python
import jax
import jax.numpy as jnp
from jax import lax
from jax.sharding import PartitionSpec as P

KVH = 8
DH = 128
MEM = 128
GROUP = 4


NEG_FILL = -1e30
EPSILON = 1e-05


def from_behind(block, axis, distance):
    devices = range(lax.axis_size(axis))
    route = [((i - distance) % len(devices), i) for i in devices]
    return lax.ppermute(block, axis, route)


def per_device(section_inputs, queries, keys, w_value, gain, section_grads_in):
    tok_rows = section_inputs.shape[2]
    kv_width = keys.shape[3]
    kv_heads = KVH
    group_size = GROUP
    head_dim = DH
    score_scale = head_dim ** (-0.5)
    my_slot = lax.axis_index("fsdp")
    inputs = section_inputs[0, 0].astype(jnp.float32)
    inv_rms = lax.rsqrt(jnp.mean(inputs * inputs, axis=1, keepdims=True) + EPSILON)
    normed = inputs * inv_rms
    all_keys = lax.all_gather(keys[0, 0], "fsdp", axis=0, tiled=True)
    full_weight, gain_full = (
        lax.all_gather(w_value[0], "fsdp", axis=0, tiled=True),
        lax.all_gather(gain[0], "fsdp", axis=0, tiled=True),
    )
    total_rows = all_keys.shape[0]
    query_pos = my_slot * tok_rows + jnp.arange(tok_rows, dtype=jnp.int32)
    key_pos = jnp.arange(total_rows, dtype=jnp.int32)
    visible = (key_pos[None, :] <= query_pos[:, None]) | (key_pos[None, :] < MEM)
    query_groups = (
        queries[0, 0].reshape(tok_rows, kv_heads, group_size, head_dim).transpose(1, 2, 0, 3)
    )
    key_groups = all_keys.reshape(total_rows, kv_heads, head_dim).transpose(1, 0, 2)
    cotangent = section_grads_in[0, 0]
    grad_groups = cotangent.reshape(tok_rows, kv_heads, group_size, head_dim).transpose(1, 0, 2, 3)

    def group_values(operands):
        query_group, key_group, grad_group = operands
        scores = (
            jnp.einsum("htd,kd->htk", query_group, key_group, preferred_element_type=jnp.float32)
            * score_scale
        )
        scores = jnp.where(visible[None], scores, NEG_FILL)
        row_top = jnp.max(scores, axis=2, keepdims=True)
        weights_exp = jnp.exp(scores - row_top)
        attn_probs = (weights_exp / jnp.sum(weights_exp, axis=2, keepdims=True)).astype(
            jnp.bfloat16
        )
        return jnp.einsum("htk,thd->kd", attn_probs, grad_group, preferred_element_type=jnp.float32)

    partial_values = lax.map(group_values, (query_groups, key_groups, grad_groups))
    partial_values = partial_values.transpose(1, 0, 2).reshape(total_rows, kv_width)
    value_grad = lax.psum_scatter(
        partial_values.astype(jnp.bfloat16), "fsdp", scatter_dimension=0, tiled=True
    )
    gain_float = gain_full.astype(jnp.float32)
    normed_b = (normed * gain_float).astype(jnp.bfloat16)
    normed_grad = lax.dot_general(
        value_grad, full_weight, (((1,), (1,)), ((), ())), preferred_element_type=jnp.float32
    )
    scaled = normed_grad * gain_float
    inner_mean = jnp.mean(scaled * normed, axis=1, keepdims=True)
    input_grad = (cotangent.astype(jnp.float32) + inv_rms * (scaled - normed * inner_mean)).astype(
        jnp.bfloat16
    )
    passed = from_behind(input_grad, "section", -1)
    gain_part = jnp.sum(normed_grad * normed, axis=0)
    fsdp_count = lax.axis_size("fsdp")
    columns, gain_columns = (
        lax.all_to_all(normed_b, "fsdp", split_axis=1, concat_axis=0, tiled=True),
        lax.all_to_all(
            gain_part.astype(jnp.bfloat16)[None], "fsdp", split_axis=1, concat_axis=0, tiled=True
        ),
    )
    every_value = lax.all_gather(value_grad, "fsdp", axis=0, tiled=True)
    col_width = columns.shape[1]
    block_terms = jnp.einsum(
        "ftd,ftk->fdk",
        columns.reshape(fsdp_count, tok_rows, col_width),
        every_value.reshape(fsdp_count, tok_rows, kv_width),
        preferred_element_type=jnp.float32,
    )
    rounded_terms = lax.optimization_barrier(block_terms.astype(jnp.bfloat16))
    weight_local = jnp.sum(rounded_terms.astype(jnp.float32), axis=0)
    gain_local = jnp.sum(gain_columns.astype(jnp.float32), axis=0)
    weight_shard, gain_shard = (
        lax.psum_scatter(
            weight_local.astype(jnp.bfloat16), "dp", scatter_dimension=0, tiled=True
        ).astype(jnp.float32),
        lax.psum_scatter(
            gain_local.astype(jnp.bfloat16), "dp", scatter_dimension=0, tiled=True
        ).astype(jnp.float32),
    )
    return (passed[None, None], weight_shard.astype(jnp.bfloat16)[None], gain_shard[None])


def solution(mesh):
    return jax.shard_map(
        per_device,
        mesh=mesh,
        in_specs=(
            P("section", "dp", "fsdp", None),
            P("section", "dp", "fsdp", None),
            P("section", "dp", "fsdp", None),
            P("section", "fsdp", None),
            P("section", "fsdp"),
            P("section", "dp", "fsdp", None),
        ),
        out_specs=(
            P("section", "dp", "fsdp", None),
            P("section", ("fsdp", "dp"), None),
            P("section", ("fsdp", "dp")),
        ),
        check_vma=False,
    )
```

profile of v0, /device:TPU:9, one launch (start us, length us, event | category | flops | bytes accessed | tf_op | source)
XLA Modules:
  0.0 337.7 jit_solution(6674334814127252696)
XLA Ops:
  7.2 1.9 copy.33
  9.2 1.6 copy.32
  10.8 0.7 copy.34
  11.5 26.5 %all-gather.9.cloned.1.call-done = bf16[1,1,512,1024]{2,3,1,0:T(8,128)(2,1)} async-done(((bf16[1,1,128,1024]{2,3,1,0:T(8,128)(2,1)}), bf16[1,1,512,1024]{2,3,1,0:T(8,128)(2,1)}) %all-gather.9.cloned.1.call-update) | async-done | bytes 1048592 | tf_op jit(solution)/shard_map/all_gather | solution.py:33
  38.0 34.2 %while.11 = (s32[]{:T(128)}, bf16[8,512,128]{1,2,0:T(8,128)(2,1)}, bf16[8,4,128,128]{2,3,1,0:T(8,128)(2,1)S(1)}, bf16[8,512,128]{1,2,0:T(8,128)(2,1)}, bf16[8,12...) while((s32[]{:T(128)}, bf16[8,512,128]{1,2,0:T(8,128)(2,1)}, ...), condition=%wide.region_4.5_spmd.clone, body=%wide.region_1.4_spmd.clone.sunk | while | flops 203818496 | bytes 1122389 | solution.py:63
  38.2 1.5 fusion.71
  39.6 2.7 fusion.72
  42.4 1.5 fusion.71
  43.9 2.7 fusion.72
  46.7 1.5 fusion.71
  48.2 2.7 fusion.72
  51.0 1.5 fusion.71
  52.5 2.7 fusion.72
  55.3 1.5 fusion.71
  56.7 2.7 fusion.72
  59.6 1.5 fusion.71
  61.0 2.7 fusion.72
  63.8 1.5 fusion.71
  65.3 2.7 fusion.72
  68.1 1.5 fusion.71
  69.6 2.7 fusion.72
  72.3 2.3 copy.44
  74.6 27.1 %reduce-scatter.7.cloned.1.call-done = bf16[128,1024]{1,0:T(8,128)(2,1)} async-done(((bf16[512,1024]{1,0:T(8,128)(2,1)}), bf16[128,1024]{1,0:T(8,128)(2,1)}) %reduce-scatter.7.cloned.1.call-update) | async-done | bytes 262160
  101.7 1.8 copy.45
  103.5 0.5 all-gather.11.cloned.1.call-update
  104.1 10.1 %all-gather.2 = bf16[1,4096]{1,0:T(2,128)(2,1)S(1)} all-gather(bf16[1,1024]{1,0:T(2,128)(2,1)S(1)} %copy-done.4), channel_id=4, replica_groups=mesh['section'=4,'fsdp'=4,'dp'=2] {'fsdp'}, dimensions={1}, use_global_device_ids=true | all-gather | bytes 10240 | tf_op jit(solution)/shard_map/all_gather | solution.py:36
  114.2 0.5 copy.43
  115.0 1.5 multiply_convert_fusion
  116.5 5.9 %all-to-all-start = ((bf16[128,4,1024]{0,2,1:T(8,128)(2,1)}), bf16[128,4,1024]{0,2,1:T(8,128)(2,1)S(1)}, u32[]{:S(2)}, u32[]{:S(2)}) async-start(bf16[128,4,1024]{0,2,1:T(8,128)(2,1)} %multiply_convert_fusion), calls=%async_computation | async-start | bytes 2097152 | tf_op jit(solution)/shard_map/all_to_all | solution.py:82
  122.4 25.2 %all-gather.7.cloned.1.call-done = bf16[512,1024]{0,1:T(8,128)(2,1)} async-done(((bf16[128,1024]{0,1:T(8,128)(2,1)}), bf16[512,1024]{0,1:T(8,128)(2,1)}) %all-gather.7.cloned.1.call-update) | async-done | bytes 1048592 | tf_op jit(solution)/shard_map/all_gather | solution.py:87
  147.6 1.5 copy.40
  149.1 2.1 all-to-all-done
  151.1 6.3 %convolution_convert_fusion = bf16[4,1024,1024]{2,1,0:T(8,128)(2,1)} fusion(bf16[4,128,1024]{2,1,0:T(8,128)(2,1)S(1)} %bitcast.99, bf16[128,4,1024]{0,2,1:T(8,128)(2,1)S(1)} %all-to-all-done), kind=kOutput, calls=%fused_computation.29 | convolution fusion | flops 1077936128 | bytes 10485760 | tf_op jit(solution)/shard_map/ftd,ftk->fdk/dot_general | solution.py:89
  157.4 8.2 %reduce_sum.62 = bf16[1024,1024]{1,0:T(8,128)(2,1)} reduce(bf16[4,1024,1024]{2,1,0:T(8,128)(2,1)} %convolution_convert_fusion, bf16[]{:T(256)} %constant.43.clone.1), dimensions={0}, to_apply=%region_7.8 | reduce | flops 3145728 | bytes 10485762 | tf_op jit(solution)/shard_map/reduce_sum | solution.py:96
  165.7 128.8 %all-gather.11.cloned.1.call-done = bf16[1,4096,1024]{2,1,0:T(8,128)(2,1)} async-done(((bf16[1,1024,1024]{2,1,0:T(8,128)(2,1)}), bf16[1,4096,1024]{2,1,0:T(8,128)(2,1)}) %all-gather.11.cloned.1.call-update) | async-done | bytes 8388624 | tf_op jit(solution)/shard_map/all_gather | solution.py:35
  294.4 6.6 %multiply_reduce_fusion = (bf16[4096]{0:T(1024)(128)(2,1)S(1)}, f32[128]{0:T(128)S(1)}, f32[128,4096]{1,0:T(8,128)S(1)}) fusion(bf16[1,1,128,4096]{3,2,1,0:T(8,128)(2,1)S(1)} %copy-done, f32[128]{0:T(128)S(1)} %add_rsqrt_fusion, f32[4096]{0:T(1024)S(1)} %bitcast.104, bf16[128,1024]{1,0:T(8,128)(2,1)S(1)} %copy-done.3, ...), kind=kOutput, calls=%fused_computation.35 | convolution fusion | flops 1077407616 | bytes 11822080 | tf_op jit(solution)/shard_map/dot_general | solution.py:70
  301.1 0.7 fusion.47
  301.8 0.6 collective-permute-start
  302.3 0.5 broadcast.60
  302.8 0.7 reduce.8
  303.5 0.6 reshape.101
  304.1 6.5 %all-to-all-start.1 = ((bf16[4,2,512]{2,1,0:T(2,128)(2,1)}), bf16[4,2,512]{2,1,0:T(2,128)(2,1)S(1)}, u32[]{:S(2)}, u32[]{:S(2)}) async-start(bf16[4,2,512]{2,1,0:T(2,128)(2,1)} %reshape.101), calls=%async_computation.2 | async-start | bytes 16384 | tf_op jit(solution)/shard_map/all_to_all | solution.py:83
  310.6 0.6 dynamic-slice
  311.8 2.1 all-to-all-done.1
  314.0 4.3 %all-reduce = bf16[1024]{0:T(1024)(128)(2,1)S(1)} all-reduce(bf16[1024]{0:T(1024)(128)(2,1)S(1)} %bitcast_reduce_fusion), channel_id=7, replica_groups=mesh['section'=4,'fsdp'=4,'dp'=2] {'dp'}, use_global_device_ids=true, to_apply=%region_11.12.clone | all-reduce | flops 1024 | bytes 4096
  318.2 0.7 dynamic-slice_convert_fusion
  318.9 11.3 %reduce-scatter.5.cloned.1.call-done = bf16[512,1024]{1,0:T(8,128)(2,1)} async-done(((bf16[1024,1024]{1,0:T(8,128)(2,1)}), bf16[512,1024]{1,0:T(8,128)(2,1)}) %reduce-scatter.5.cloned.1.call-update) | async-done | bytes 1048592 | tf_op jit(solution)/shard_map/reduce_scatter | solution.py:99
  330.2 1.0 copy.64
  (42 shorter events, 1.6 us)
Async XLA Ops:
  7.2 3.6 %copy-start.1 = (bf16[1,1,128,4096]{3,2,1,0:T(8,128)(2,1)S(1)}, bf16[1,1,128,4096]{3,2,1,0:T(8,128)(2,1)}, u32[]{:S(2)}) copy-start(bf16[1,1,128,4096]{3,2,1,0:T(8,128)(2,1)} %param.13) | copy-start | bytes 3145732
  7.2 30.9 %all-gather.9.cloned.1.call-start = ((), (), s32[]{:S(2)}) async-start(), calls=%async_computation.6 | async-start | bytes 1310720 | tf_op jit(solution)/shard_map/all_gather | solution.py:33
  9.1 92.5 %reduce-scatter.7.cloned.1.call-start = ((), (), s32[]{:S(2)}) async-start(), calls=%async_computation.8 | async-start | bytes 1310720
  74.5 29.5 %copy-start.4 = (bf16[1,1024]{1,0:T(2,128)(2,1)S(1)}, bf16[1,1024]{1,0:T(2,128)(2,1)}, u32[]{:S(2)}) copy-start(bf16[1,1024]{1,0:T(2,128)(2,1)} %param.12) | copy-start | bytes 6148
  74.5 39.7 %copy-start = (bf16[1,1,128,4096]{3,2,1,0:T(8,128)(2,1)S(1)}, bf16[1,1,128,4096]{3,2,1,0:T(8,128)(2,1)}, u32[]{:S(2)}) copy-start(bf16[1,1,128,4096]{3,2,1,0:T(8,128)(2,1)} %param.8) | copy-start | bytes 3145732
  74.6 73.0 %all-gather.7.cloned.1.call-start = ((), (), s32[]{:S(2)}) async-start(), calls=%async_computation.4 | async-start | bytes 1310720 | tf_op jit(solution)/shard_map/all_gather | solution.py:87
  103.5 190.9 %all-gather.11.cloned.1.call-start = ((), (), s32[]{:S(2)}) async-start(), calls=%async_computation.7 | async-start | bytes 10485760 | tf_op jit(solution)/shard_map/all_gather | solution.py:35
  116.5 34.6 %all-to-all-start = ((bf16[128,4,1024]{0,2,1:T(8,128)(2,1)}), bf16[128,4,1024]{0,2,1:T(8,128)(2,1)S(1)}, u32[]{:S(2)}, u32[]{:S(2)}) async-start(bf16[128,4,1024]{0,2,1:T(8,128)(2,1)} %multiply_convert_fusion), calls=%async_computation | async-start | bytes 2097152 | tf_op jit(solution)/shard_map/all_to_all | solution.py:82
  122.4 207.8 %reduce-scatter.5.cloned.1.call-start = ((), (), s32[]{:S(2)}) async-start(), calls=%async_computation.5 | async-start | bytes 3145728 | tf_op jit(solution)/shard_map/reduce_scatter | solution.py:99
  165.6 128.8 %copy-start.3 = (bf16[128,1024]{1,0:T(8,128)(2,1)S(1)}, bf16[128,1024]{1,0:T(8,128)(2,1)}, u32[]{:S(2)}) copy-start(bf16[128,1024]{1,0:T(8,128)(2,1)} %reduce-scatter.7.cloned.1.call-done) | copy-start | bytes 786436
  294.4 6.6 %copy-start.2 = (bf16[1,1,128,4096]{3,2,1,0:T(8,128)(2,1)S(1)}, bf16[1,1,128,4096]{3,2,1,0:T(8,128)(2,1)}, u32[]{:S(2)}) copy-start(bf16[1,1,128,4096]{3,2,1,0:T(8,128)(2,1)} %param.13) | copy-start | bytes 3145732
  301.0 9.6 %copy-start.5 = (u32[32]{0:T(128)S(1)}, u32[32]{0:T(128)}, u32[]{:S(2)}) copy-start(u32[32]{0:T(128)} %constant.52) | copy-start | bytes 388
  301.8 17.1 %collective-permute-start = (bf16[128,4096]{1,0:T(8,128)(2,1)S(1)}, bf16[128,4096]{1,0:T(8,128)(2,1)S(1)}, u32[]{:S(2)}, u32[]{:S(2)}) collective-permute-start(bf16[128,4096]{1,0:T(8,128)(2,1)S(1)} %fusion.47), channel_id=1, source_target_pairs={{8,0},{16,8},{24,16},{0,24},{9,1},{17,9},{25,17},{1,25},{10,2},{18... | collective-permute-start | bytes 3145736 | tf_op jit(solution)/shard_map/ppermute | solution.py:19
  304.1 9.8 %all-to-all-start.1 = ((bf16[4,2,512]{2,1,0:T(2,128)(2,1)}), bf16[4,2,512]{2,1,0:T(2,128)(2,1)S(1)}, u32[]{:S(2)}, u32[]{:S(2)}) async-start(bf16[4,2,512]{2,1,0:T(2,128)(2,1)} %reshape.101), calls=%async_computation.2 | async-start | bytes 16384 | tf_op jit(solution)/shard_map/all_to_all | solution.py:83
Sparse Core Ops, SparseCore 0:
  10.1 27.8 all-gather.8
  74.7 26.9 reduce-scatter.6
  103.9 43.6 all-gather.6
  149.1 145.2 all-gather.10
  297.2 32.9 reduce-scatter.4
where the time goes:
time: 340 us; the launch traced here: 338 us
  waiting for transfers between devices  224 us (66%)
  matrix products  46.2 us (14%)
  between operations  14.6 us (4%)
  blocking collectives  14.3 us (4%)
  starting transfers between devices  13.1 us (4%)
  other arithmetic  13 us (4%)
  local copies, waits for them, and re-layouts  12.9 us (4%)
    all_gather x1, waiting for transfers between devices, per_device(): lax.all_gather(w_value[0], 'fsdp', axis=0, tiled=True)  129 us
    unnamed x6, waiting for transfers between devices  27.6 us
    all_gather x1, waiting for transfers between devices, per_device(): all_keys = lax.all_gather(keys[0, 0], 'fsdp', axis=0, tiled=True)  26.5 us
    all_gather x1, waiting for transfers between devices, per_device(): every_value = lax.all_gather(value_grad, 'fsdp', axis=0, tiled=True)  25.2 us
    dot_general x8, matrix products, group_values(): jnp.einsum('htk,thd->kd', attn_probs, grad_group, preferred_element_type=...  21.6 us
    sub x8, matrix products, group_values(): weights_exp = jnp.exp(scores - row_top)  11.6 us
    reduce_scatter x1, waiting for transfers between devices, per_device(): lax.psum_scatter(weight_local.astype(jnp.bfloat16), 'dp', scatter_dimensi...  11.3 us
    unnamed x22, local copies, waits for them, and re-layouts  10.9 us
  transfers between devices with their start and end apart: 8, of which 7 were waited for; matrix products, arithmetic and copies ran while one was open for 9% of the time, Pallas kernels for 0%

commit v1 on v0

v1 whole, which is shorter than its diff:
```python
import functools

import jax
import jax.numpy as jnp
from jax import lax
from jax.experimental import pallas as pl
from jax.experimental.pallas import tpu as pltpu
from jax.sharding import PartitionSpec as P

DH = 128
MEM = 128
NEG_FILL = -1e30
EPSILON = 1e-05
LOG2E = 1.4426950408889634
VMEM_BYTES = 40 * 1024 * 1024

WHOLE = pl.BlockSpec(memory_space=pltpu.VMEM)
SCALAR = pl.BlockSpec(memory_space=pltpu.SMEM)
PARAMS = pltpu.CompilerParams(vmem_limit_bytes=VMEM_BYTES)


def shifted(block, axis, distance, wrap):
    count = lax.axis_size(axis)
    route = [
        (i, (i + distance) % count) for i in range(count) if wrap or 0 <= i + distance < count
    ]
    return lax.ppermute(block, axis, route)


def to_column_owner(block, distance):
    sections, count = lax.axis_size("section"), lax.axis_size("fsdp")
    route = [
        (s * count + f, ((s - 1) % sections) * count + (f - distance) % count)
        for s in range(sections)
        for f in range(count)
    ]
    return lax.ppermute(block, ("section", "fsdp"), route)


def attention_kernel(count, group, slot_ref, query_ref, grad_ref, *refs):
    key_refs, out_refs = refs[:count], refs[count:]
    rows = query_ref.shape[0]
    slot = slot_ref[0]
    heads = [slice(h * DH, (h + 1) * DH) for h in range(group)]
    query = jnp.concatenate([query_ref[:, h] for h in heads], axis=0)
    grad = jnp.concatenate([grad_ref[:, h] for h in heads], axis=0)
    keys = jnp.concatenate([ref[...] for ref in key_refs], axis=0)
    scores = lax.dot_general(
        keys, query, (((1,), (1,)), ((), ())), preferred_element_type=jnp.float32
    )
    key_at = lax.broadcasted_iota(jnp.int32, (rows, rows), 0)
    query_at = lax.broadcasted_iota(jnp.int32, (rows, rows), 1)
    visible = (key_at <= query_at) | (slot * rows + key_at < MEM)
    visible = jnp.concatenate([visible] * group, axis=1)
    parts = [jnp.where(visible, scores[:rows], NEG_FILL)]
    parts += [scores[d * rows : (d + 1) * rows] for d in range(1, count)]
    hidden = [jnp.where(slot >= d, 0.0, NEG_FILL) for d in range(count)]
    tops = [jnp.max(part, axis=0, keepdims=True) + hide for part, hide in zip(parts, hidden)]
    top = functools.reduce(jnp.maximum, tops)
    scale = DH ** (-0.5) * LOG2E
    weights = [
        jnp.exp2((part - (top - hide)) * scale) for part, hide in zip(parts, hidden)
    ]
    total = functools.reduce(
        jnp.add, [jnp.sum(weight, axis=0, keepdims=True) for weight in weights]
    )
    inverse = 1.0 / total
    probs = jnp.concatenate([(w * inverse).astype(jnp.bfloat16) for w in weights], axis=0)
    values = jnp.dot(probs, grad, preferred_element_type=jnp.float32)
    for d in range(count):
        out_refs[d][...] = values[d * rows : (d + 1) * rows].astype(jnp.bfloat16)


def attention(slot, queries, grads, key_blocks):
    rows, width = queries.shape
    kv_width = key_blocks[0].shape[1]
    group = width // kv_width
    count = len(key_blocks)
    wide = pl.BlockSpec((rows, group * DH), lambda g: (0, g))
    narrow = pl.BlockSpec((rows, DH), lambda g: (0, g))
    return pl.pallas_call(
        functools.partial(attention_kernel, count, group),
        grid=(kv_width // DH,),
        in_specs=[SCALAR, wide, wide] + [narrow] * count,
        out_specs=[narrow] * count,
        out_shape=[jax.ShapeDtypeStruct((rows, kv_width), jnp.bfloat16)] * count,
        compiler_params=PARAMS,
    )(slot, queries, grads, *key_blocks)


def normalise_kernel(count, slot_ref, x_ref, *out_refs):
    slot = slot_ref[0]
    x = x_ref[...].astype(jnp.float32)
    inv_rms = lax.rsqrt(jnp.mean(x * x, axis=1, keepdims=True) + EPSILON)
    width = x.shape[1] // count
    for d in range(count):
        start = pl.multiple_of(lax.rem(slot + d, count) * width, width)
        block = x_ref[:, pl.ds(start, width)].astype(jnp.float32)
        out_refs[d][...] = (block * inv_rms).astype(jnp.bfloat16)


def normalised_blocks(slot, x, count):
    rows, width = x.shape
    return pl.pallas_call(
        functools.partial(normalise_kernel, count),
        in_specs=[SCALAR, WHOLE],
        out_specs=[WHOLE] * count,
        out_shape=[jax.ShapeDtypeStruct((rows, width // count), jnp.bfloat16)] * count,
        compiler_params=PARAMS,
    )(slot, x)


def feature_kernel(count, weight_ref, gain_ref, *refs):
    value_refs, xhat_refs = refs[:count], refs[count : 2 * count]
    scaled_refs, gain_grad_ref = refs[2 * count : 3 * count], refs[3 * count]
    rows = value_refs[0].shape[0]
    values = jnp.concatenate([ref[...] for ref in value_refs], axis=0)
    normed_grad = lax.dot_general(
        values, weight_ref[...], (((1,), (1,)), ((), ())), preferred_element_type=jnp.float32
    )
    gain = gain_ref[...].astype(jnp.float32)
    gain_sum = jnp.zeros_like(gain)
    for d in range(count):
        part = normed_grad[d * rows : (d + 1) * rows]
        scaled_refs[d][...] = (part * gain).astype(jnp.bfloat16)
        gain_sum += jnp.sum(part * xhat_refs[d][...].astype(jnp.float32), axis=0, keepdims=True)
    gain_grad_ref[...] = gain_sum


def feature_grads(weight, gain, values, xhats):
    count = len(values)
    rows, kv_width = values[0].shape
    width = weight.shape[0]
    step = min(width, 256)
    whole = pl.BlockSpec((rows, kv_width), lambda c: (0, 0))
    column = pl.BlockSpec((rows, step), lambda c: (0, c))
    line = pl.BlockSpec((1, step), lambda c: (0, c))
    out = pl.pallas_call(
        functools.partial(feature_kernel, count),
        grid=(width // step,),
        in_specs=[pl.BlockSpec((step, kv_width), lambda c: (c, 0)), line]
        + [whole] * count
        + [column] * count,
        out_specs=[column] * count + [line],
        out_shape=[jax.ShapeDtypeStruct((rows, width), jnp.bfloat16)] * count
        + [jax.ShapeDtypeStruct((1, width), jnp.float32)],
        compiler_params=PARAMS,
    )(weight, gain, *values, *xhats)
    return out[:count], out[count]


def weight_kernel(count, half_ref, gain_ref, *refs):
    value_refs, xhat_refs, out_ref = refs[:count], refs[count : 2 * count], refs[2 * count]
    gain = gain_ref[...].astype(jnp.float32)
    normed = jnp.concatenate(
        [(ref[...].astype(jnp.float32) * gain).astype(jnp.bfloat16) for ref in xhat_refs], axis=0
    )
    values = jnp.concatenate([ref[...] for ref in value_refs], axis=0)
    out_ref[...] = lax.dot_general(
        normed, values, (((0,), (0,)), ((), ())), preferred_element_type=jnp.float32
    ).astype(out_ref.dtype)


def weight_grad(half, halves, gain, values, xhats, dtype):
    count = len(values)
    rows, kv_width = values[0].shape
    width = gain.shape[1] // halves
    step = min(width, 256)
    steps = width // step
    whole = pl.BlockSpec((rows, kv_width), lambda c, half_ref: (0, 0))
    column = pl.BlockSpec((rows, step), lambda c, half_ref: (0, half_ref[0] * steps + c))
    line = pl.BlockSpec((1, step), lambda c, half_ref: (0, half_ref[0] * steps + c))
    return pl.pallas_call(
        functools.partial(weight_kernel, count),
        grid_spec=pltpu.PrefetchScalarGridSpec(
            num_scalar_prefetch=1,
            grid=(steps,),
            in_specs=[line] + [whole] * count + [column] * count,
            out_specs=pl.BlockSpec((step, kv_width), lambda c, half_ref: (c, 0)),
        ),
        out_shape=jax.ShapeDtypeStruct((width, kv_width), dtype),
        compiler_params=PARAMS,
    )(half, gain, *values, *xhats)


def input_kernel(count, slot_ref, x_ref, grad_ref, *refs):
    scaled_refs, out_ref = refs[:count], refs[count]
    slot = slot_ref[0]
    x = x_ref[...].astype(jnp.float32)
    inv_rms = lax.rsqrt(jnp.mean(x * x, axis=1, keepdims=True) + EPSILON)
    width = x.shape[1] // count
    starts = [pl.multiple_of(lax.rem(slot + d, count) * width, width) for d in range(count)]
    inner = jnp.zeros_like(inv_rms)
    for d in range(count):
        xhat = x_ref[:, pl.ds(starts[d], width)].astype(jnp.float32) * inv_rms
        inner += jnp.sum(scaled_refs[d][...].astype(jnp.float32) * xhat, axis=1, keepdims=True)
    inner = inner / x.shape[1]
    for d in range(count):
        columns = pl.ds(starts[d], width)
        xhat = x_ref[:, columns].astype(jnp.float32) * inv_rms
        scaled = scaled_refs[d][...].astype(jnp.float32)
        grad = grad_ref[:, columns].astype(jnp.float32)
        out_ref[:, columns] = (grad + inv_rms * (scaled - xhat * inner)).astype(jnp.bfloat16)


def input_grad(slot, x, grads, scaled):
    count = len(scaled)
    return pl.pallas_call(
        functools.partial(input_kernel, count),
        in_specs=[SCALAR] + [WHOLE] * (2 + count),
        out_specs=WHOLE,
        out_shape=jax.ShapeDtypeStruct(x.shape, jnp.bfloat16),
        compiler_params=PARAMS,
    )(slot, x, grads, *scaled)


def per_device(section_inputs, queries, keys, w_value, gain, section_grads_in):
    count = lax.axis_size("fsdp")
    docs = lax.axis_size("dp")
    slot = lax.axis_index("fsdp").astype(jnp.int32)[None]
    half = lax.axis_index("dp").astype(jnp.int32)[None]
    x, cotangent, own_keys = section_inputs[0, 0], section_grads_in[0, 0], keys[0, 0]
    assert MEM <= x.shape[0] and docs == 2

    key_blocks = [own_keys] + [shifted(own_keys, "fsdp", d, False) for d in range(1, count)]
    xhat_out = normalised_blocks(slot, x, count)
    xhats = [xhat_out[0]] + [shifted(xhat_out[d], "fsdp", d, True) for d in range(1, count)]
    next_x = shifted(x, "section", -1, True)
    next_grad = shifted(cotangent, "section", -1, True)

    terms = attention(slot, queries[0, 0], cotangent, key_blocks)
    arrived = [terms[0]] + [shifted(terms[d], "fsdp", -d, False) for d in range(1, count)]
    value = sum(t.astype(jnp.float32) for t in arrived).astype(jnp.bfloat16)
    values = [value] + [shifted(value, "fsdp", d, True) for d in range(1, count)]

    scaled, gain_sum = feature_grads(w_value[0], gain, values, xhats)
    returned = [to_column_owner(scaled[d], d) for d in range(count)]

    sent_weight = weight_grad(1 - half, docs, gain, values, xhats, jnp.bfloat16)
    got_weight = shifted(sent_weight, "dp", 1, True)
    gain_halves = gain_sum.reshape(docs, -1)
    got_gain = shifted(
        lax.dynamic_index_in_dim(gain_halves, 1 - half[0], 0, keepdims=True), "dp", 1, True
    )
    own_weight = weight_grad(half, docs, gain, values, xhats, jnp.float32)
    weight_out = (own_weight + got_weight.astype(jnp.float32)).astype(jnp.bfloat16)
    gain_out = lax.dynamic_index_in_dim(gain_halves, half[0], 0, keepdims=True) + got_gain

    passed = input_grad(slot, next_x, next_grad, returned)
    return passed[None, None], weight_out[None], gain_out


def solution(mesh):
    return jax.shard_map(
        per_device,
        mesh=mesh,
        in_specs=(
            P("section", "dp", "fsdp", None),
            P("section", "dp", "fsdp", None),
            P("section", "dp", "fsdp", None),
            P("section", "fsdp", None),
            P("section", "fsdp"),
            P("section", "dp", "fsdp", None),
        ),
        out_specs=(
            P("section", "dp", "fsdp", None),
            P("section", ("fsdp", "dp"), None),
            P("section", ("fsdp", "dp")),
        ),
        check_vma=False,
    )
```

time: 340 us -> 164 us (0.48)
  waiting for transfers between devices: 224 us -> 62.6 us
  starting transfers between devices: 13.1 us -> 68.3 us
  matrix products: 46.2 us -> 0 us
  Pallas kernels: 0 us -> 16.5 us
  blocking collectives: 14.3 us -> 0 us
  between operations: 14.6 us -> 0.79 us
  other arithmetic: 13 us -> 3.98 us
  local copies, waits for them, and re-layouts: 12.9 us -> 9.08 us
    all_gather x3 -> x0, waiting for transfers between devices: 180 us -> none  [the longest x1 129 us: per_device(): lax.all_gather(w_value[0], 'fsdp', axis=0, tiled=True)]
    ppermute x1 -> x20, starting transfers between devices: 0.56 us -> 68.3 us  [the longest x16 51.1 us: shifted(): return lax.ppermute(block, axis, route)]
    ppermute x1 -> x20, waiting for transfers between devices: 0.01 us -> 62.6 us  [the longest x16 45.3 us: shifted(): return lax.ppermute(block, axis, route)]
    dot_general x10 -> x0, matrix products: 34.5 us -> none  [the longest x8 21.6 us: group_values(): jnp.einsum('htk,thd->kd', attn_probs, grad_group, preferred_element_type=...]
    unnamed x6 -> x0, waiting for transfers between devices: 27.6 us -> none
    pallas_call x0 -> x6, Pallas kernels: none -> 16.5 us  [the longest x1 7.22 us: attention(): pl.pallas_call(functools.partial(attention_kernel, count, group), grid=(k...]
    all_to_all x2 -> x0, starting transfers between devices: 12.3 us -> none  [the longest x1 6.46 us: per_device(): lax.all_to_all(gain_part.astype(jnp.bfloat16)[None], 'fsdp', split_axis=1...]
    sub x8 -> x0, matrix products: 11.6 us -> none  [group_values(): weights_exp = jnp.exp(scores - row_top)]
  transfers between devices with their start and end apart: 8 -> 20, of which waited for: 7 -> 9; matrix products, arithmetic and copies ran while one was open for 9% -> 1% of each run, Pallas kernels for 0% -> 6%
where the time goes in v1:
time: 164 us; the launch traced here: 161 us
  starting transfers between devices  68.3 us (42%)
  waiting for transfers between devices  62.6 us (38%)
  Pallas kernels  16.5 us (10%)
  local copies, waits for them, and re-layouts  9.08 us (6%)
  other arithmetic  3.98 us (2%)
    ppermute x16, starting transfers between devices, shifted(): return lax.ppermute(block, axis, route)  51.1 us
    ppermute x16, waiting for transfers between devices, shifted(): return lax.ppermute(block, axis, route)  45.3 us
    ppermute x4, waiting for transfers between devices, to_column_owner(): return lax.ppermute(block, ('section', 'fsdp'), route)  17.3 us
    ppermute x4, starting transfers between devices, to_column_owner(): return lax.ppermute(block, ('section', 'fsdp'), route)  17.2 us
    unnamed x24, local copies, waits for them, and re-layouts  8.54 us
    pallas_call x1, Pallas kernels, attention(): pl.pallas_call(functools.partial(attention_kernel, count, group), grid=(k...  7.22 us
    pallas_call x1, Pallas kernels, input_grad(): pl.pallas_call(functools.partial(input_kernel, count), in_specs=[SCALAR]...  3.52 us
  transfers between devices with their start and end apart: 20, of which 9 were waited for; matrix products, arithmetic and copies ran while one was open for 1% of the time, Pallas kernels for 6%

profile of v1, /device:TPU:9, one launch (start us, length us, event | category | flops | bytes accessed | tf_op | source)
XLA Modules:
  0.0 161.3 jit_solution(7363879548947082478)
XLA Ops:
  0.6 3.2 %collective-permute-start.2 = (bf16[128,1024]{1,0:T(8,128)(2,1)}, bf16[128,1024]{1,0:T(8,128)(2,1)S(1)}, u32[]{:S(2)}, u32[]{:S(2)}) collective-permute-start(bf16[128,1024]{1,0:T(8,128)(2,1)} %bitcast.16), channel_id=1, source_target_pairs={{0,2},{2,4},{4,6},{1,3},{3,5},{5,7},{8,10},{10,12},{12,14},{9,11},... | collective-permute-start | bytes 786440 | tf_op jit(solution)/shard_map/ppermute | solution.py:27
  3.8 2.3 %collective-permute-start.3 = (bf16[128,1024]{1,0:T(8,128)(2,1)}, bf16[128,1024]{1,0:T(8,128)(2,1)S(1)}, u32[]{:S(2)}, u32[]{:S(2)}) collective-permute-start(bf16[128,1024]{1,0:T(8,128)(2,1)} %bitcast.17), channel_id=1, source_target_pairs={{0,4},{2,6},{1,5},{3,7},{8,12},{10,14},{9,13},{11,15},{16,20},{18,... | collective-permute-start | bytes 786440 | tf_op jit(solution)/shard_map/ppermute | solution.py:27
  6.2 0.7 collective-permute-start.4
  6.9 3.1 %collective-permute-done.2.refs_1_ = bf16[128,1024]{1,0:T(8,128)(2,1)S(1)} collective-permute-done((bf16[128,1024]{1,0:T(8,128)(2,1)}, bf16[128,1024]{1,0:T(8,128)(2,1)S(1)}, u32[]{:S(2)}, u32[]{:S(2)}) %collective-permute-start.2) | collective-permute-done | bytes 262176 | tf_op jit(solution)/shard_map/ppermute | solution.py:27
  9.9 16.1 %collective-permute-done.3.refs_2_ = bf16[128,1024]{1,0:T(8,128)(2,1)S(1)} collective-permute-done((bf16[128,1024]{1,0:T(8,128)(2,1)}, bf16[128,1024]{1,0:T(8,128)(2,1)S(1)}, u32[]{:S(2)}, u32[]{:S(2)}) %collective-permute-start.3) | collective-permute-done | bytes 262176 | tf_op jit(solution)/shard_map/ppermute | solution.py:27
  26.0 0.0 collective-permute-done.4.refs_3_
  26.0 1.2 copy-done.1
  27.2 1.2 copy-done.3
  28.4 0.9 copy-done.6
  29.4 7.2 %shard_map.85 = (bf16[128,1024]{1,0:T(8,128)(2,1)S(1)}, bf16[128,1024]{1,0:T(8,128)(2,1)S(1)}, bf16[128,1024]{1,0:T(8,128)(2,1)S(1)}, bf16[128,1024]{1,0:T(8,128)(2,1)S(1)}) custom-call(s32[1]{0:T(128)} %bitcast.slot_ref, bf16[128,4096]{1,0:T(8,128)(2,1)S(1)} %bitcast.11, bf16[128,4096]{1,0:T(8,128)(2,1)S(1)} %bitcast.15, bf16[128,1024]{1,0:T(8,128)(2,1)S(1)} %bitcast.19, ...), custom_call_target="tpu_custom_call" | custom-call | tf_op jit(solution)/shard_map/pallas_call | solution.py:81
  36.6 1.9 %collective-permute-start.5 = (bf16[128,1024]{1,0:T(8,128)(2,1)S(1)}, bf16[128,1024]{1,0:T(8,128)(2,1)S(1)}, u32[]{:S(2)}, u32[]{:S(2)}) collective-permute-start(bf16[128,1024]{1,0:T(8,128)(2,1)S(1)} %get-tuple-element.17), channel_id=1, source_target_pairs={{2,0},{4,2},{6,4},{3,1},{5,3},{7,5},{10,8},{12,10},{14,12},{11,9},... | collective-permute-start | bytes 786440 | tf_op jit(solution)/shard_map/ppermute | solution.py:27
  38.5 1.3 collective-permute-start.6
  39.8 0.7 collective-permute-start.7
  40.5 0.5 shard_map.86
  41.0 1.5 collective-permute-start.11
  42.5 2.2 %collective-permute-start.12 = (bf16[128,1024]{1,0:T(8,128)(2,1)S(1)}, bf16[128,1024]{1,0:T(8,128)(2,1)S(1)}, u32[]{:S(2)}, u32[]{:S(2)}) collective-permute-start(bf16[128,1024]{1,0:T(8,128)(2,1)S(1)} %get-tuple-element.22), channel_id=1, source_target_pairs={{0,4},{2,6},{4,0},{6,2},{1,5},{3,7},{5,1},{7,3},{8,12},{10,14},{12... | collective-permute-start | bytes 786440 | tf_op jit(solution)/shard_map/ppermute | solution.py:27
  44.8 1.4 collective-permute-start.13
  46.2 5.5 %collective-permute-done.6 = bf16[128,1024]{1,0:T(8,128)(2,1)S(1)} collective-permute-done((bf16[128,1024]{1,0:T(8,128)(2,1)S(1)}, bf16[128,1024]{1,0:T(8,128)(2,1)S(1)}, u32[]{:S(2)}, u32[]{:S(2)}) %collective-permute-start.6) | collective-permute-done | bytes 262176 | tf_op jit(solution)/shard_map/ppermute | solution.py:27
  51.6 0.2 add_convert_fusion.1.refs_0_
  51.8 22.5 %collective-permute-start.10 = (bf16[128,1024]{1,0:T(8,128)(2,1)S(1)}, bf16[128,1024]{1,0:T(8,128)(2,1)S(1)}, u32[]{:S(2)}, u32[]{:S(2)}) collective-permute-start(bf16[128,1024]{1,0:T(8,128)(2,1)S(1)} %add_convert_fusion.1.refs_0_), channel_id=1, source_target_pairs={{0,6},{2,0},{4,2},{6,4},{1,7},{3,1},{5,3},{7,5},{8,14},{10,8},{12,... | collective-permute-start | bytes 786440 | tf_op jit(solution)/shard_map/ppermute | solution.py:27
  74.2 0.0 collective-permute-start.8
  74.3 2.1 %collective-permute-start.9 = (bf16[128,1024]{1,0:T(8,128)(2,1)S(1)}, bf16[128,1024]{1,0:T(8,128)(2,1)S(1)}, u32[]{:S(2)}, u32[]{:S(2)}) collective-permute-start(bf16[128,1024]{1,0:T(8,128)(2,1)S(1)} %add_convert_fusion.1.refs_0_), channel_id=1, source_target_pairs={{0,4},{2,6},{4,0},{6,2},{1,5},{3,7},{5,1},{7,3},{8,12},{10,14},{12... | collective-permute-start | bytes 786440 | tf_op jit(solution)/shard_map/ppermute | solution.py:27
  76.4 5.2 %collective-permute-start = (bf16[128,4096]{1,0:T(8,128)(2,1)}, bf16[128,4096]{1,0:T(8,128)(2,1)S(1)}, u32[]{:S(2)}, u32[]{:S(2)}) collective-permute-start(bf16[128,4096]{1,0:T(8,128)(2,1)} %bitcast.12), channel_id=1, source_target_pairs={{0,24},{8,0},{16,8},{24,16},{1,25},{9,1},{17,9},{25,17},{2,26},{10... | collective-permute-start | bytes 3145736 | tf_op jit(solution)/shard_map/ppermute | solution.py:27
  81.6 13.7 %collective-permute-done.13.refs_7_ = bf16[128,1024]{1,0:T(8,128)(2,1)S(1)} collective-permute-done((bf16[128,1024]{1,0:T(8,128)(2,1)S(1)}, bf16[128,1024]{1,0:T(8,128)(2,1)S(1)}, u32[]{:S(2)}, u32[]{:S(2)}) %collective-permute-start.13) | collective-permute-done | bytes 262176 | tf_op jit(solution)/shard_map/ppermute | solution.py:27
  95.3 4.5 %collective-permute-start.1 = (bf16[128,4096]{1,0:T(8,128)(2,1)}, bf16[128,4096]{1,0:T(8,128)(2,1)}, u32[]{:S(2)}, u32[]{:S(2)}) collective-permute-start(bf16[128,4096]{1,0:T(8,128)(2,1)} %bitcast.14), channel_id=1, source_target_pairs={{0,24},{8,0},{16,8},{24,16},{1,25},{9,1},{17,9},{25,17},{2,26},{10... | collective-permute-start | bytes 3145736 | tf_op jit(solution)/shard_map/ppermute | solution.py:27
  99.9 1.1 collective-permute-done.10.refs_3_
  101.0 1.9 %shard_map.90 = bf16[512,1024]{1,0:T(8,128)(2,1)} custom-call(s32[1]{0:T(128)S(6)} %sub.6.half_ref, bf16[1,1024]{1,0:T(2,128)(2,1)S(1)} %copy-done.7, bf16[128,1024]{1,0:T(8,128)(2,1)S(1)} %add_convert_fusion.1.refs_0_, bf16[128,1024]{1,0:T(8,128)(2,1)S(1)} %collective-permute-done.8.refs_1_, bf16[128,1024]{1,0:T(8,128)(2,1)S(1)} %collective-permute-done.9.refs_2_, ...), custom_call_target="tpu_custom_call" | custom-call | tf_op jit(solution)/shard_map/pallas_call | solution.py:173
  102.9 1.2 collective-permute-start.18
  104.2 1.6 copy-done
  105.7 2.3 %shard_map.87 = (bf16[128,1024]{1,0:T(8,128)(2,1)S(1)}, bf16[128,1024]{1,0:T(8,128)(2,1)S(1)}, bf16[128,1024]{1,0:T(8,128)(2,1)S(1)}, bf16[128,1024]{1,0:T(8,128)(2,1)S(1)}, f32[1,1024]{1,0:T(1,128)S(1)}) custom-call(bf16[1024,1024]{1,0:T(8,128)(2,1)S(1)} %bitcast.10, bf16[1,1024]{1,0:T(2,128)(2,1)S(1)} %copy-done.7, ...), custom_call_target="tpu_custom_call" | custom-call | tf_op jit(solution)/shard_map/pallas_call | solution.py:138
  108.0 0.7 copy-done.8
  108.8 0.7 copy-done.9
  109.5 0.7 copy-done.10
  110.2 0.7 copy-done.11
  110.9 0.5 broadcast.3
  111.4 0.6 reduce.3
  112.1 0.3 collective-permute-start.19
  112.4 5.1 %collective-permute-start.14 = (bf16[128,1024]{1,0:T(8,128)(2,1)}, bf16[128,1024]{1,0:T(8,128)(2,1)S(1)}, u32[]{:S(2)}, u32[]{:S(2)}) collective-permute-start(bf16[128,1024]{1,0:T(8,128)(2,1)} %copy-done.11), channel_id=1, source_target_pairs={{0,24},{2,26},{4,28},{6,30},{8,0},{10,2},{12,4},{14,6},{16,8},{18,... | collective-permute-start | bytes 786440 | tf_op jit(solution)/shard_map/ppermute | solution.py:37
  117.5 5.9 %collective-permute-done.19 = f32[1,512]{1,0:T(1,128)S(1)} collective-permute-done((f32[1,512]{1,0:T(1,128)S(1)}, f32[1,512]{1,0:T(1,128)S(1)}, u32[]{:S(2)}, u32[]{:S(2)}) %collective-permute-start.19) | collective-permute-done | bytes 2080 | tf_op jit(solution)/shard_map/ppermute | solution.py:27
  123.4 12.1 %collective-permute-start.15 = (bf16[128,1024]{1,0:T(8,128)(2,1)}, bf16[128,1024]{1,0:T(8,128)(2,1)S(1)}, u32[]{:S(2)}, u32[]{:S(2)}) collective-permute-start(bf16[128,1024]{1,0:T(8,128)(2,1)} %copy-done.10), channel_id=1, source_target_pairs={{0,30},{2,24},{4,26},{6,28},{8,6},{10,0},{12,2},{14,4},{16,14},{18... | collective-permute-start | bytes 786440 | tf_op jit(solution)/shard_map/ppermute | solution.py:37
  135.5 6.7 %collective-permute-done.15.refs_1_ = bf16[128,1024]{1,0:T(8,128)(2,1)S(1)} collective-permute-done((bf16[128,1024]{1,0:T(8,128)(2,1)}, bf16[128,1024]{1,0:T(8,128)(2,1)S(1)}, u32[]{:S(2)}, u32[]{:S(2)}) %collective-permute-start.15) | collective-permute-done | bytes 262176 | tf_op jit(solution)/shard_map/ppermute | solution.py:37
  142.2 0.7 copy-done.4
  142.9 1.1 shard_map.89
  144.0 0.6 dynamic-slice_add_fusion
  144.6 5.0 %collective-permute-done.16.refs_2_ = bf16[128,1024]{1,0:T(8,128)(2,1)} collective-permute-done((bf16[128,1024]{1,0:T(8,128)(2,1)}, bf16[128,1024]{1,0:T(8,128)(2,1)}, u32[]{:S(2)}, u32[]{:S(2)}) %collective-permute-start.16) | collective-permute-done | bytes 262176 | tf_op jit(solution)/shard_map/ppermute | solution.py:37
  149.6 5.6 %collective-permute-done.17.refs_3_ = bf16[128,1024]{1,0:T(8,128)(2,1)} collective-permute-done((bf16[128,1024]{1,0:T(8,128)(2,1)}, bf16[128,1024]{1,0:T(8,128)(2,1)}, u32[]{:S(2)}, u32[]{:S(2)}) %collective-permute-start.17) | collective-permute-done | bytes 262176 | tf_op jit(solution)/shard_map/ppermute | solution.py:37
  155.2 3.5 %shard_map.88 = bf16[128,4096]{1,0:T(8,128)(2,1)} custom-call(s32[1]{0:T(128)} %bitcast.slot_ref, bf16[128,4096]{1,0:T(8,128)(2,1)S(1)} %collective-permute-done.x_ref, bf16[128,4096]{1,0:T(8,128)(2,1)} %collective-permute-done.1.grad_ref, bf16[128,1024]{1,0:T(8,128)(2,1)S(1)} %collective-permute-done.14.refs_0_, bf16[128,1024]{1,0:T(8,128)(2,1)S(1)} %copy-done.5, ...), custom_call_target="tpu_custom_call" | custom-call | tf_op jit(solution)/shard_map/pallas_call | solution.py:208
  158.7 2.6 %fusion = bf16[1,512,1024]{2,1,0:T(8,128)(2,1)} fusion(f32[512,1024]{1,0:T(8,128)S(1)} %shard_map.89, bf16[512,1024]{1,0:T(8,128)(2,1)} %collective-permute-done.18), kind=kLoop, calls=%fused_computation.1 | loop fusion | flops 1572864 | bytes 4194304 | tf_op jit(solution)/shard_map/broadcast_in_dim | solution.py:250
  (29 shorter events, 0.1 us)
Async XLA Ops:
  0.6 9.3 %collective-permute-start.2 = (bf16[128,1024]{1,0:T(8,128)(2,1)}, bf16[128,1024]{1,0:T(8,128)(2,1)S(1)}, u32[]{:S(2)}, u32[]{:S(2)}) collective-permute-start(bf16[128,1024]{1,0:T(8,128)(2,1)} %bitcast.16), channel_id=1, source_target_pairs={{0,2},{2,4},{4,6},{1,3},{3,5},{5,7},{8,10},{10,12},{12,14},{9,11},... | collective-permute-start | bytes 786440 | tf_op jit(solution)/shard_map/ppermute | solution.py:27
  3.8 22.1 %collective-permute-start.3 = (bf16[128,1024]{1,0:T(8,128)(2,1)}, bf16[128,1024]{1,0:T(8,128)(2,1)S(1)}, u32[]{:S(2)}, u32[]{:S(2)}) collective-permute-start(bf16[128,1024]{1,0:T(8,128)(2,1)} %bitcast.17), channel_id=1, source_target_pairs={{0,4},{2,6},{1,5},{3,7},{8,12},{10,14},{9,13},{11,15},{16,20},{18,... | collective-permute-start | bytes 786440 | tf_op jit(solution)/shard_map/ppermute | solution.py:27
  6.2 19.8 %collective-permute-start.4 = (bf16[128,1024]{1,0:T(8,128)(2,1)}, bf16[128,1024]{1,0:T(8,128)(2,1)S(1)}, u32[]{:S(2)}, u32[]{:S(2)}) collective-permute-start(bf16[128,1024]{1,0:T(8,128)(2,1)} %bitcast.18), channel_id=1, source_target_pairs={{0,6},{1,7},{8,14},{9,15},{16,22},{17,23},{24,30},{25,31}} | collective-permute-start | bytes 786440 | tf_op jit(solution)/shard_map/ppermute | solution.py:27
  26.0 1.2 copy-start.1
  27.2 1.2 copy-start.3
  28.4 0.9 copy-start.6
  29.4 11.1 %copy-start.2 = (bf16[1,1,128,4096]{3,2,1,0:T(8,128)(2,1)S(1)}, bf16[1,1,128,4096]{3,2,1,0:T(8,128)(2,1)}, u32[]{:S(2)}) copy-start(bf16[1,1,128,4096]{3,2,1,0:T(8,128)(2,1)} %param.6) | copy-start | bytes 3145732
  29.4 71.6 %copy-start.7 = (bf16[1,1024]{1,0:T(2,128)(2,1)S(1)}, bf16[1,1024]{1,0:T(2,128)(2,1)}, u32[]{:S(2)}) copy-start(bf16[1,1024]{1,0:T(2,128)(2,1)} %gain_ref.5) | copy-start | bytes 6148
  36.6 8.2 %collective-permute-start.5 = (bf16[128,1024]{1,0:T(8,128)(2,1)S(1)}, bf16[128,1024]{1,0:T(8,128)(2,1)S(1)}, u32[]{:S(2)}, u32[]{:S(2)}) collective-permute-start(bf16[128,1024]{1,0:T(8,128)(2,1)S(1)} %get-tuple-element.17), channel_id=1, source_target_pairs={{2,0},{4,2},{6,4},{3,1},{5,3},{7,5},{10,8},{12,10},{14,12},{11,9},... | collective-permute-start | bytes 786440 | tf_op jit(solution)/shard_map/ppermute | solution.py:27
  38.5 13.1 %collective-permute-start.6 = (bf16[128,1024]{1,0:T(8,128)(2,1)S(1)}, bf16[128,1024]{1,0:T(8,128)(2,1)S(1)}, u32[]{:S(2)}, u32[]{:S(2)}) collective-permute-start(bf16[128,1024]{1,0:T(8,128)(2,1)S(1)} %get-tuple-element.18), channel_id=1, source_target_pairs={{4,0},{6,2},{5,1},{7,3},{12,8},{14,10},{13,9},{15,11},{20,16},{22,... | collective-permute-start | bytes 786440 | tf_op jit(solution)/shard_map/ppermute | solution.py:27
  39.8 11.8 %collective-permute-start.7 = (bf16[128,1024]{1,0:T(8,128)(2,1)S(1)}, bf16[128,1024]{1,0:T(8,128)(2,1)S(1)}, u32[]{:S(2)}, u32[]{:S(2)}) collective-permute-start(bf16[128,1024]{1,0:T(8,128)(2,1)S(1)} %get-tuple-element.19), channel_id=1, source_target_pairs={{6,0},{7,1},{14,8},{15,9},{22,16},{23,17},{30,24},{31,25}} | collective-permute-start | bytes 786440 | tf_op jit(solution)/shard_map/ppermute | solution.py:27
  41.0 33.2 %collective-permute-start.11 = (bf16[128,1024]{1,0:T(8,128)(2,1)S(1)}, bf16[128,1024]{1,0:T(8,128)(2,1)S(1)}, u32[]{:S(2)}, u32[]{:S(2)}) collective-permute-start(bf16[128,1024]{1,0:T(8,128)(2,1)S(1)} %get-tuple-element.21), channel_id=1, source_target_pairs={{0,2},{2,4},{4,6},{6,0},{1,3},{3,5},{5,7},{7,1},{8,10},{10,12},{12... | collective-permute-start | bytes 786440 | tf_op jit(solution)/shard_map/ppermute | solution.py:27
  42.5 33.9 %collective-permute-start.12 = (bf16[128,1024]{1,0:T(8,128)(2,1)S(1)}, bf16[128,1024]{1,0:T(8,128)(2,1)S(1)}, u32[]{:S(2)}, u32[]{:S(2)}) collective-permute-start(bf16[128,1024]{1,0:T(8,128)(2,1)S(1)} %get-tuple-element.22), channel_id=1, source_target_pairs={{0,4},{2,6},{4,0},{6,2},{1,5},{3,7},{5,1},{7,3},{8,12},{10,14},{12... | collective-permute-start | bytes 786440 | tf_op jit(solution)/shard_map/ppermute | solution.py:27
  44.8 50.6 %collective-permute-start.13 = (bf16[128,1024]{1,0:T(8,128)(2,1)S(1)}, bf16[128,1024]{1,0:T(8,128)(2,1)S(1)}, u32[]{:S(2)}, u32[]{:S(2)}) collective-permute-start(bf16[128,1024]{1,0:T(8,128)(2,1)S(1)} %get-tuple-element.23), channel_id=1, source_target_pairs={{0,6},{2,0},{4,2},{6,4},{1,7},{3,1},{5,3},{7,5},{8,14},{10,8},{12,... | collective-permute-start | bytes 786440 | tf_op jit(solution)/shard_map/ppermute | solution.py:27
  51.8 49.2 %collective-permute-start.10 = (bf16[128,1024]{1,0:T(8,128)(2,1)S(1)}, bf16[128,1024]{1,0:T(8,128)(2,1)S(1)}, u32[]{:S(2)}, u32[]{:S(2)}) collective-permute-start(bf16[128,1024]{1,0:T(8,128)(2,1)S(1)} %add_convert_fusion.1.refs_0_), channel_id=1, source_target_pairs={{0,6},{2,0},{4,2},{6,4},{1,7},{3,1},{5,3},{7,5},{8,14},{10,8},{12,... | collective-permute-start | bytes 786440 | tf_op jit(solution)/shard_map/ppermute | solution.py:27
  74.2 26.7 %collective-permute-start.8 = (bf16[128,1024]{1,0:T(8,128)(2,1)S(1)}, bf16[128,1024]{1,0:T(8,128)(2,1)S(1)}, u32[]{:S(2)}, u32[]{:S(2)}) collective-permute-start(bf16[128,1024]{1,0:T(8,128)(2,1)S(1)} %add_convert_fusion.1.refs_0_), channel_id=1, source_target_pairs={{0,2},{2,4},{4,6},{6,0},{1,3},{3,5},{5,7},{7,1},{8,10},{10,12},{12... | collective-permute-start | bytes 786440 | tf_op jit(solution)/shard_map/ppermute | solution.py:27
  74.3 26.7 %collective-permute-start.9 = (bf16[128,1024]{1,0:T(8,128)(2,1)S(1)}, bf16[128,1024]{1,0:T(8,128)(2,1)S(1)}, u32[]{:S(2)}, u32[]{:S(2)}) collective-permute-start(bf16[128,1024]{1,0:T(8,128)(2,1)S(1)} %add_convert_fusion.1.refs_0_), channel_id=1, source_target_pairs={{0,4},{2,6},{4,0},{6,2},{1,5},{3,7},{5,1},{7,3},{8,12},{10,14},{12... | collective-permute-start | bytes 786440 | tf_op jit(solution)/shard_map/ppermute | solution.py:27
  76.4 78.8 %collective-permute-start = (bf16[128,4096]{1,0:T(8,128)(2,1)}, bf16[128,4096]{1,0:T(8,128)(2,1)S(1)}, u32[]{:S(2)}, u32[]{:S(2)}) collective-permute-start(bf16[128,4096]{1,0:T(8,128)(2,1)} %bitcast.12), channel_id=1, source_target_pairs={{0,24},{8,0},{16,8},{24,16},{1,25},{9,1},{17,9},{25,17},{2,26},{10... | collective-permute-start | bytes 3145736 | tf_op jit(solution)/shard_map/ppermute | solution.py:27
  95.3 59.9 %collective-permute-start.1 = (bf16[128,4096]{1,0:T(8,128)(2,1)}, bf16[128,4096]{1,0:T(8,128)(2,1)}, u32[]{:S(2)}, u32[]{:S(2)}) collective-permute-start(bf16[128,4096]{1,0:T(8,128)(2,1)} %bitcast.14), channel_id=1, source_target_pairs={{0,24},{8,0},{16,8},{24,16},{1,25},{9,1},{17,9},{25,17},{2,26},{10... | collective-permute-start | bytes 3145736 | tf_op jit(solution)/shard_map/ppermute | solution.py:27
  102.9 55.8 %collective-permute-start.18 = (bf16[512,1024]{1,0:T(8,128)(2,1)}, bf16[512,1024]{1,0:T(8,128)(2,1)}, u32[]{:S(2)}, u32[]{:S(2)}) collective-permute-start(bf16[512,1024]{1,0:T(8,128)(2,1)} %shard_map.90), channel_id=1, source_target_pairs={{0,1},{1,0},{2,3},{3,2},{4,5},{5,4},{6,7},{7,6},{8,9},{9,8},{10,11... | collective-permute-start | bytes 3145736 | tf_op jit(solution)/shard_map/ppermute | solution.py:27
  104.2 1.6 copy-start
  108.0 0.7 copy-start.8
  108.8 0.7 copy-start.9
  109.5 0.7 copy-start.10
  110.2 0.7 copy-start.11
  112.1 11.3 %collective-permute-start.19 = (f32[1,512]{1,0:T(1,128)S(1)}, f32[1,512]{1,0:T(1,128)S(1)}, u32[]{:S(2)}, u32[]{:S(2)}) collective-permute-start(f32[1,512]{1,0:T(1,128)S(1)} %constant_dynamic-slice_fusion), channel_id=1, source_target_pairs={{0,1},{1,0},{2,3},{3,2},{4,5},{5,4},{6,7},{7,6},{8,9},{9,8},{10,11... | collective-permute-start | bytes 6152 | tf_op jit(solution)/shard_map/ppermute | solution.py:27
  112.4 23.1 %collective-permute-start.14 = (bf16[128,1024]{1,0:T(8,128)(2,1)}, bf16[128,1024]{1,0:T(8,128)(2,1)S(1)}, u32[]{:S(2)}, u32[]{:S(2)}) collective-permute-start(bf16[128,1024]{1,0:T(8,128)(2,1)} %copy-done.11), channel_id=1, source_target_pairs={{0,24},{2,26},{4,28},{6,30},{8,0},{10,2},{12,4},{14,6},{16,8},{18,... | collective-permute-start | bytes 786440 | tf_op jit(solution)/shard_map/ppermute | solution.py:37
  123.4 18.8 %collective-permute-start.15 = (bf16[128,1024]{1,0:T(8,128)(2,1)}, bf16[128,1024]{1,0:T(8,128)(2,1)S(1)}, u32[]{:S(2)}, u32[]{:S(2)}) collective-permute-start(bf16[128,1024]{1,0:T(8,128)(2,1)} %copy-done.10), channel_id=1, source_target_pairs={{0,30},{2,24},{4,26},{6,28},{8,6},{10,0},{12,2},{14,4},{16,14},{18... | collective-permute-start | bytes 786440 | tf_op jit(solution)/shard_map/ppermute | solution.py:37
  135.5 14.1 %collective-permute-start.16 = (bf16[128,1024]{1,0:T(8,128)(2,1)}, bf16[128,1024]{1,0:T(8,128)(2,1)}, u32[]{:S(2)}, u32[]{:S(2)}) collective-permute-start(bf16[128,1024]{1,0:T(8,128)(2,1)} %copy-done.9), channel_id=1, source_target_pairs={{0,28},{2,30},{4,24},{6,26},{8,4},{10,6},{12,0},{14,2},{16,12},{18... | collective-permute-start | bytes 786440 | tf_op jit(solution)/shard_map/ppermute | solution.py:37
  142.2 0.7 copy-start.4
  142.9 12.3 %collective-permute-start.17 = (bf16[128,1024]{1,0:T(8,128)(2,1)}, bf16[128,1024]{1,0:T(8,128)(2,1)}, u32[]{:S(2)}, u32[]{:S(2)}) collective-permute-start(bf16[128,1024]{1,0:T(8,128)(2,1)} %copy-done.8), channel_id=1, source_target_pairs={{0,26},{2,28},{4,30},{6,24},{8,2},{10,4},{12,6},{14,0},{16,10},{18... | collective-permute-start | bytes 786440 | tf_op jit(solution)/shard_map/ppermute | solution.py:37
  142.9 12.4 %copy-start.5 = (bf16[128,1024]{1,0:T(8,128)(2,1)S(1)}, bf16[128,1024]{1,0:T(8,128)(2,1)}, u32[]{:S(2)}) copy-start(bf16[128,1024]{1,0:T(8,128)(2,1)} %copy-done.4) | copy-start | bytes 786436

commit v2 on v1

v2 whole, which is shorter than its diff:
```python
import functools

import jax
import jax.numpy as jnp
from jax import lax
from jax.experimental import pallas as pl
from jax.experimental.pallas import tpu as pltpu
from jax.sharding import PartitionSpec as P

DH = 128
MEM = 128
NEG_FILL = -1e30
EPSILON = 1e-05
LOG2E = 1.4426950408889634
TILE = 16
MIB = 1024 * 1024

SCALAR = pl.BlockSpec(memory_space=pltpu.SMEM)
PARAMS = pltpu.CompilerParams(vmem_limit_bytes=16 * MIB)


def section_route(distance):
    count = lax.axis_size("section")
    return [(s, (s + distance) % count) for s in range(count)]


def along_line(block, distance, wrap=False, odd=None):
    sections, count = lax.axis_size("section"), lax.axis_size("fsdp")
    route = [
        (s * count + f, s * count + (f + distance) % count)
        for s in range(sections)
        for f in range(count)
        if (odd is None or s % 2 == odd) and (wrap or 0 <= f + distance < count)
    ]
    return lax.ppermute(block, ("section", "fsdp"), route)


def to_tokens_below(block, distance):
    sections, count = lax.axis_size("section"), lax.axis_size("fsdp")
    route = [
        (s * count + f, ((s - 1) % sections) * count + (f - distance) % count)
        for s in range(sections)
        for f in range(count)
    ]
    return lax.ppermute(block, ("section", "fsdp"), route)


def after(arrays, others):
    kept, _ = lax.optimization_barrier((arrays, others))
    return kept


def fixed(shape):
    return pl.BlockSpec(shape, lambda *_: (0, 0))


def in_hbm(*arrays):
    return [pltpu.with_memory_space_constraint(array, pltpu.HBM) for array in arrays]


def attention_kernel(count, group, slot_ref, query_ref, grad_ref, *refs):
    key_refs, out_refs = refs[:count], refs[count:]
    rows = query_ref.shape[0]
    slot = slot_ref[0]
    heads = [slice(h * DH, (h + 1) * DH) for h in range(group)]
    query = jnp.concatenate([query_ref[:, h] for h in heads], axis=0)
    grad = jnp.concatenate([grad_ref[:, h] for h in heads], axis=0)
    keys = jnp.concatenate([ref[...] for ref in key_refs], axis=0)
    scores = lax.dot_general(
        keys, query, (((1,), (1,)), ((), ())), preferred_element_type=jnp.float32
    )
    key_at = lax.broadcasted_iota(jnp.int32, (rows, rows), 0)
    query_at = lax.broadcasted_iota(jnp.int32, (rows, rows), 1)
    visible = (key_at <= query_at) | (slot * rows + key_at < MEM)
    visible = jnp.concatenate([visible] * group, axis=1)
    parts = [jnp.where(visible, scores[:rows], NEG_FILL)]
    parts += [scores[d * rows : (d + 1) * rows] for d in range(1, count)]
    hidden = [jnp.where(slot >= d, 0.0, NEG_FILL) for d in range(count)]
    tops = [jnp.max(part, axis=0, keepdims=True) + hide for part, hide in zip(parts, hidden)]
    top = functools.reduce(jnp.maximum, tops)
    scale = DH ** (-0.5) * LOG2E
    weights = [jnp.exp2((part - (top - hide)) * scale) for part, hide in zip(parts, hidden)]
    total = functools.reduce(
        jnp.add, [jnp.sum(weight, axis=0, keepdims=True) for weight in weights]
    )
    inverse = 1.0 / total
    probs = jnp.concatenate([(w * inverse).astype(jnp.bfloat16) for w in weights], axis=0)
    values = jnp.dot(probs, grad, preferred_element_type=jnp.float32)
    for d in range(count):
        out_refs[d][...] = values[d * rows : (d + 1) * rows].astype(jnp.bfloat16)


def attention(slot, queries, grads, key_blocks):
    rows, kv_width = key_blocks[0].shape
    group = queries.shape[1] // kv_width
    count = len(key_blocks)
    wide = pl.BlockSpec((rows, group * DH), lambda g: (0, g))
    narrow = pl.BlockSpec((rows, DH), lambda g: (0, g))
    return pl.pallas_call(
        functools.partial(attention_kernel, count, group),
        grid=(kv_width // DH,),
        in_specs=[SCALAR, wide, wide] + [narrow] * count,
        out_specs=[narrow] * count,
        out_shape=[jax.ShapeDtypeStruct((rows, kv_width), jnp.bfloat16)] * count,
        compiler_params=pltpu.CompilerParams(vmem_limit_bytes=(8 + 3 * count) * MIB),
    )(slot, *in_hbm(queries, grads, *key_blocks))


def prepare_kernel(count, slot_ref, x_ref, grad_ref, pair_ref, *xhat_refs):
    pair_ref[0] = x_ref[...]
    pair_ref[1] = grad_ref[...]
    x = x_ref[...].astype(jnp.float32)
    inv_rms = lax.rsqrt(jnp.mean(x * x, axis=1, keepdims=True) + EPSILON)
    width = x.shape[1] // count
    for d in range(count):
        start = pl.multiple_of(lax.rem(slot_ref[0] + d, count) * width, width)
        block = x_ref[:, pl.ds(start, width)].astype(jnp.float32)
        xhat_refs[d][...] = (block * inv_rms).astype(jnp.bfloat16)


def prepare(slot, x, grads, count):
    rows, width = x.shape
    step = min(rows, 2 * TILE)
    wide = pl.BlockSpec((step, width), lambda r: (r, 0))
    out = pl.pallas_call(
        functools.partial(prepare_kernel, count),
        grid=(rows // step,),
        in_specs=[SCALAR, wide, wide],
        out_specs=[pl.BlockSpec((2, step, width), lambda r: (0, r, 0))]
        + [pl.BlockSpec((step, width // count), lambda r: (r, 0))] * count,
        out_shape=[jax.ShapeDtypeStruct((2, rows, width), jnp.bfloat16)]
        + [jax.ShapeDtypeStruct((rows, width // count), jnp.bfloat16)] * count,
        compiler_params=PARAMS,
    )(slot, *in_hbm(x, grads))
    return out[0], out[1:]


def normed_kernel(count, slot_ref, half_ref, gain_ref, own_ref, *refs):
    above, below, out_ref = refs[: count - 1], refs[count - 1 : -1], refs[-1]
    rows = own_ref.shape[0]
    gain = gain_ref[...].astype(jnp.float32)
    for d in range(count):
        xhat = own_ref[...]
        if d > 0:
            xhat = jnp.where(slot_ref[0] >= d, above[d - 1][...], below[d - 1][...])
        normed = (xhat.astype(jnp.float32) * gain).astype(jnp.bfloat16)
        out_ref[:, d * rows : (d + 1) * rows] = normed.T


def normed_columns(slot, half, halves, gain, own, above, below):
    count = len(above) + 1
    rows, width = own.shape
    width = width // halves
    step = min(width, 256)
    steps = width // step

    def place(c, slot_ref, half_ref):
        return (0, half_ref[0] * steps + c)

    return pl.pallas_call(
        functools.partial(normed_kernel, count),
        grid_spec=pltpu.PrefetchScalarGridSpec(
            num_scalar_prefetch=2,
            grid=(steps,),
            in_specs=[pl.BlockSpec((1, step), place)]
            + [pl.BlockSpec((rows, step), place)] * (2 * count - 1),
            out_specs=pl.BlockSpec((step, count * rows), lambda c, *_: (c, 0)),
        ),
        out_shape=jax.ShapeDtypeStruct((width, count * rows), jnp.bfloat16),
        compiler_params=PARAMS,
    )(slot, half, *in_hbm(gain, own, *above, *below))


def feature_kernel(count, weight_ref, gain_ref, *refs):
    value_refs, scaled_refs, all_ref = refs[:count], refs[count:-1], refs[-1]
    rows = value_refs[0].shape[0]
    values = jnp.concatenate([ref[...] for ref in value_refs], axis=0)

    @pl.when(pl.program_id(0) == 0)
    def _():
        all_ref[...] = values

    normed_grad = lax.dot_general(
        values, weight_ref[...], (((1,), (1,)), ((), ())), preferred_element_type=jnp.float32
    )
    gain = gain_ref[...].astype(jnp.float32)
    for d in range(count):
        scaled_refs[d][...] = (normed_grad[d * rows : (d + 1) * rows] * gain).astype(jnp.bfloat16)


def feature_grads(weight, gain, values):
    count = len(values)
    rows, kv_width = values[0].shape
    width = weight.shape[0]
    step = min(width, 256)
    column = pl.BlockSpec((rows, step), lambda c: (0, c))
    out = pl.pallas_call(
        functools.partial(feature_kernel, count),
        grid=(width // step,),
        in_specs=[
            pl.BlockSpec((step, kv_width), lambda c: (c, 0)),
            pl.BlockSpec((1, step), lambda c: (0, c)),
        ]
        + [fixed((rows, kv_width))] * count,
        out_specs=[column] * count + [fixed((count * rows, kv_width))],
        out_shape=[jax.ShapeDtypeStruct((rows, width), jnp.bfloat16)] * count
        + [jax.ShapeDtypeStruct((count * rows, kv_width), jnp.bfloat16)],
        compiler_params=PARAMS,
    )(*in_hbm(weight, gain, *values))
    return out[:count], out[count]


def weight_kernel(docs, half_ref, weight_ref, gain_ref, *refs):
    normed_refs, value_refs, (out_ref, line_ref) = refs[:docs], refs[docs:-2], refs[-2:]
    normed = jnp.concatenate([ref[...] for ref in normed_refs], axis=1)
    values = jnp.concatenate([ref[...] for ref in value_refs], axis=0)
    grad = jnp.dot(normed, values, preferred_element_type=jnp.float32)
    kv_width = grad.shape[1]
    out_ref[...] = grad.astype(jnp.bfloat16)
    terms = grad * weight_ref[...].astype(jnp.float32)
    lanes = sum(terms[:, i : i + DH] for i in range(0, kv_width, DH))
    line_ref[...] = jnp.sum(lanes.T, axis=0, keepdims=True) / gain_ref[...].astype(jnp.float32)


def weight_grad(half, weight, gain, normed, values):
    docs = len(normed)
    blocks = [block for doc in values for block in doc]
    rows, kv_width = values[0][0].shape
    width, tokens = normed[0].shape
    step = min(width, 256)
    steps = width // step
    return pl.pallas_call(
        functools.partial(weight_kernel, docs),
        grid_spec=pltpu.PrefetchScalarGridSpec(
            num_scalar_prefetch=1,
            grid=(steps,),
            in_specs=[
                pl.BlockSpec((step, kv_width), lambda c, half_ref: (half_ref[0] * steps + c, 0)),
                pl.BlockSpec((1, step), lambda c, half_ref: (0, half_ref[0] * steps + c)),
            ]
            + [pl.BlockSpec((step, tokens), lambda c, *_: (c, 0))] * docs
            + [fixed((rows, kv_width))] * len(blocks),
            out_specs=[
                pl.BlockSpec((step, kv_width), lambda c, *_: (c, 0)),
                pl.BlockSpec((1, step), lambda c, *_: (0, c)),
            ],
        ),
        out_shape=[
            jax.ShapeDtypeStruct((width, kv_width), jnp.bfloat16),
            jax.ShapeDtypeStruct((1, width), jnp.float32),
        ],
        compiler_params=PARAMS,
    )(half, *in_hbm(weight, gain, *normed, *blocks))


def input_kernel(count, slot_ref, pair_ref, *refs):
    scaled_refs, out_ref = refs[:count], refs[count]
    slot = slot_ref[0]
    x_ref, grad_ref = pair_ref.at[0], pair_ref.at[1]
    x = x_ref[...].astype(jnp.float32)
    inv_rms = lax.rsqrt(jnp.mean(x * x, axis=1, keepdims=True) + EPSILON)
    width = x.shape[1] // count
    starts = [pl.multiple_of(lax.rem(slot + d, count) * width, width) for d in range(count)]
    inner = jnp.zeros_like(inv_rms)
    for d in range(count):
        block = x_ref[:, pl.ds(starts[d], width)].astype(jnp.float32)
        inner += jnp.sum(scaled_refs[d][...].astype(jnp.float32) * block, axis=1, keepdims=True)
    inner = inner * inv_rms * inv_rms / x.shape[1]
    for d in range(count):
        columns = pl.ds(starts[d], width)
        block = x_ref[:, columns].astype(jnp.float32)
        scaled = scaled_refs[d][...].astype(jnp.float32)
        grad = grad_ref[:, columns].astype(jnp.float32)
        out_ref[:, columns] = (grad + inv_rms * (scaled - block * inner)).astype(jnp.bfloat16)


def input_grad(slot, pair, scaled):
    count = len(scaled)
    _, rows, width = pair.shape
    step = min(rows, 2 * TILE)
    return pl.pallas_call(
        functools.partial(input_kernel, count),
        grid=(rows // step,),
        in_specs=[SCALAR, pl.BlockSpec((2, step, width), lambda r: (0, r, 0))]
        + [pl.BlockSpec((step, width // count), lambda r: (r, 0))] * count,
        out_specs=pl.BlockSpec((step, width), lambda r: (r, 0)),
        out_shape=jax.ShapeDtypeStruct((rows, width), jnp.bfloat16),
        compiler_params=PARAMS,
    )(slot, *in_hbm(pair, *scaled))


def per_device(section_inputs, queries, keys, w_value, gain, section_grads_in):
    count = lax.axis_size("fsdp")
    docs = lax.axis_size("dp")
    slot = lax.axis_index("fsdp").astype(jnp.int32)[None]
    half = lax.axis_index("dp").astype(jnp.int32)[None]
    x, cotangent, own_keys = section_inputs[0, 0], section_grads_in[0, 0], keys[0, 0]
    weight = w_value[0]
    assert MEM <= x.shape[0] and docs == 2
    distances = range(1, count)

    swap = [(0, 1), (1, 0)]

    pair, xhat = prepare(slot, x, cotangent, count)
    keys_in = [along_line(own_keys, d) for d in distances]
    below = [along_line(xhat[d], d - count) for d in distances[1:]]
    below, keys_in, xhat, slot = after((below, keys_in, xhat, slot), ())
    far_below, far_above = along_line(xhat[1], 1 - count), along_line(xhat[-1], count - 1)
    terms = attention(slot, queries[0, 0], cotangent, [own_keys] + keys_in)

    below = [far_below] + below
    terms, below, far_above, xhat = after((terms, below, far_above, xhat), ())
    arrived = [along_line(terms[d], -d) for d in distances]
    above = [along_line(xhat[d], d) for d in distances[:-1]] + [far_above]
    arrived, above = after((arrived, above), ())
    value = sum(t.astype(jnp.float32) for t in [terms[0]] + arrived).astype(jnp.bfloat16)

    value, pair = after((value, pair), ())
    values = [value] + [along_line(value, d, wrap=True) for d in distances]
    next_pair = lax.ppermute(pair, "section", section_route(-1))
    columns = (docs, gain, after(xhat[0], values[1]), above, below)
    sent = normed_columns(slot, 1 - half, *columns)
    normed = [normed_columns(slot, half, *columns), lax.ppermute(sent, "dp", swap)]
    values, normed, next_pair = after((values, normed, next_pair), ())

    scaled, all_values = feature_grads(weight, gain, values)
    other_values = lax.ppermute(all_values, "dp", swap)
    returned = [to_tokens_below(scaled[d], d) for d in range(count)]

    weight_out, gain_out = weight_grad(half, weight, gain, normed, [[all_values], [other_values]])
    slot = after(slot, weight_out)
    passed = input_grad(slot, next_pair, returned)
    return passed[None, None], weight_out[None], gain_out


def solution(mesh):
    return jax.shard_map(
        per_device,
        mesh=mesh,
        in_specs=(
            P("section", "dp", "fsdp", None),
            P("section", "dp", "fsdp", None),
            P("section", "dp", "fsdp", None),
            P("section", "fsdp", None),
            P("section", "fsdp"),
            P("section", "dp", "fsdp", None),
        ),
        out_specs=(
            P("section", "dp", "fsdp", None),
            P("section", ("fsdp", "dp"), None),
            P("section", ("fsdp", "dp")),
        ),
        check_vma=False,
    )
```

time: 164 us -> 146 us (0.89)
  starting transfers between devices: 68.3 us -> 40.9 us
  Pallas kernels: 16.5 us -> 27 us
  waiting for transfers between devices: 62.6 us -> 69.3 us
  local copies, waits for them, and re-layouts: 9.08 us -> 4.73 us
  other arithmetic: 3.98 us -> 0.87 us
    ppermute x20 -> x22, starting transfers between devices: 68.3 us -> 40.9 us  [the longest x15 29.8 us: along_line(): return lax.ppermute(block, ('section', 'fsdp'), route)]
    pallas_call x4 -> x5, Pallas kernels: 7.05 us -> 14.4 us  [the longest x1 4.26 us: input_grad(): pl.pallas_call(functools.partial(input_kernel, count), grid=(rows // step...]
    ppermute x20 -> x22, waiting for transfers between devices: 62.6 us -> 69.3 us  [the longest x15 52.5 us: along_line(): return lax.ppermute(block, ('section', 'fsdp'), route)]
    unnamed x24 -> x40, local copies, waits for them, and re-layouts: 8.54 us -> 4.73 us
    broadcast_in_dim x1 -> x0, other arithmetic: 2.58 us -> none  [per_device(): return (passed[None, None], weight_out[None], gain_out)]
    pallas_call x1, Pallas kernels: 2.28 us -> 4.3 us  [feature_grads(): pl.pallas_call(functools.partial(feature_kernel, count), grid=(width // s...]
  transfers between devices with their start and end apart: 20 -> 22, of which waited for: 9 -> 10; matrix products, arithmetic and copies ran while one was open for 1% -> 0% of each run, Pallas kernels for 6% -> 13%
where the time goes in v2:
time: 146 us; the launch traced here: 144 us
  waiting for transfers between devices  69.3 us (47%)
  starting transfers between devices  40.9 us (28%)
  Pallas kernels  27 us (18%)
  local copies, waits for them, and re-layouts  4.73 us (3%)
    ppermute x15, waiting for transfers between devices, along_line(): return lax.ppermute(block, ('section', 'fsdp'), route)  52.5 us
    ppermute x15, starting transfers between devices, along_line(): return lax.ppermute(block, ('section', 'fsdp'), route)  29.8 us
    ppermute x1, waiting for transfers between devices, per_device(): other_values = lax.ppermute(all_values, 'dp', swap)  16.8 us
    pallas_call x1, Pallas kernels, attention(): pl.pallas_call(functools.partial(attention_kernel, count, group), grid=(k...  8.32 us
    ppermute x4, starting transfers between devices, to_tokens_below(): return lax.ppermute(block, ('section', 'fsdp'), route)  7.23 us
    unnamed x40, local copies, waits for them, and re-layouts  4.73 us
    pallas_call x1, Pallas kernels, feature_grads(): pl.pallas_call(functools.partial(feature_kernel, count), grid=(width // s...  4.3 us
    pallas_call x1, Pallas kernels, input_grad(): pl.pallas_call(functools.partial(input_kernel, count), grid=(rows // step...  4.26 us
  transfers between devices with their start and end apart: 22, of which 10 were waited for; matrix products, arithmetic and copies ran while one was open for 0% of the time, Pallas kernels for 13%

profile of v2, /device:TPU:9, one launch (start us, length us, event | category | flops | bytes accessed | tf_op | source)
XLA Modules:
  0.0 143.7 jit_solution(6672040661305468848)
XLA Ops:
  0.6 0.7 collective-permute-start.4
  1.3 4.8 %collective-permute-start.3 = (bf16[128,1024]{1,0:T(8,128)(2,1)}, bf16[128,1024]{1,0:T(8,128)(2,1)S(1)}, u32[]{:S(2)}, u32[]{:S(2)}) collective-permute-start(bf16[128,1024]{1,0:T(8,128)(2,1)} %bitcast.17), channel_id=1, source_target_pairs={{0,4},{2,6},{8,12},{10,14},{16,20},{18,22},{24,28},{26,30},{1,5},{... | collective-permute-start | bytes 786440 | tf_op jit(solution)/shard_map/ppermute | solution.py:35
  6.2 1.9 %collective-permute-start.2 = (bf16[128,1024]{1,0:T(8,128)(2,1)}, bf16[128,1024]{1,0:T(8,128)(2,1)S(1)}, u32[]{:S(2)}, u32[]{:S(2)}) collective-permute-start(bf16[128,1024]{1,0:T(8,128)(2,1)} %bitcast.18), channel_id=1, source_target_pairs={{0,2},{2,4},{4,6},{8,10},{10,12},{12,14},{16,18},{18,20},{20,22},{... | collective-permute-start | bytes 786440 | tf_op jit(solution)/shard_map/ppermute | solution.py:35
  8.1 2.8 %shard_map.85 = (bf16[2,128,4096]{2,1,0:T(8,128)(2,1)S(1)}, bf16[128,1024]{1,0:T(8,128)(2,1)S(1)}, bf16[128,1024]{1,0:T(8,128)(2,1)S(1)}, bf16[128,1024]{1,0:T(8,128)(2,1)S(1)}, bf16[128,1024]{1,0:T(8,128)(2,1)S(1)}) custom-call(s32[1]{0:T(128)} %bitcast.slot_ref, bf16[128,4096]{1,0:T(8,128)(2,1)} %bitcast.14, bf16[128,4096]{1,0:T(8,128)(2,1)} %bitcast.11), custom_call_target="tpu_custom_call" | custom-call | tf_op jit(solution)/shard_map/pallas_call | solution.py:125
  10.9 0.7 copy-done.1
  11.6 1.3 collective-permute-start
  12.9 3.4 %collective-permute-start.1 = (bf16[128,1024]{1,0:T(8,128)(2,1)S(1)}, bf16[128,1024]{1,0:T(8,128)(2,1)S(1)}, u32[]{:S(2)}, u32[]{:S(2)}) collective-permute-start(bf16[128,1024]{1,0:T(8,128)(2,1)S(1)} %get-tuple-element.72), channel_id=1, source_target_pairs={{2,0},{4,2},{6,4},{10,8},{12,10},{14,12},{18,16},{20,18},{22,20},{... | collective-permute-start | bytes 786440 | tf_op jit(solution)/shard_map/ppermute | solution.py:35
  16.3 7.1 %collective-permute-done.3.refs_2_ = bf16[128,1024]{1,0:T(8,128)(2,1)S(1)} collective-permute-done((bf16[128,1024]{1,0:T(8,128)(2,1)}, bf16[128,1024]{1,0:T(8,128)(2,1)S(1)}, u32[]{:S(2)}, u32[]{:S(2)}) %collective-permute-start.3) | collective-permute-done | bytes 262176 | tf_op jit(solution)/shard_map/ppermute | solution.py:35
  23.4 5.6 %collective-permute-done.2.refs_1_ = bf16[128,1024]{1,0:T(8,128)(2,1)S(1)} collective-permute-done((bf16[128,1024]{1,0:T(8,128)(2,1)}, bf16[128,1024]{1,0:T(8,128)(2,1)S(1)}, u32[]{:S(2)}, u32[]{:S(2)}) %collective-permute-start.2) | collective-permute-done | bytes 262176 | tf_op jit(solution)/shard_map/ppermute | solution.py:35
  29.0 4.9 %collective-permute-done.1.refs_5_ = bf16[128,1024]{1,0:T(8,128)(2,1)S(1)} collective-permute-done((bf16[128,1024]{1,0:T(8,128)(2,1)S(1)}, bf16[128,1024]{1,0:T(8,128)(2,1)S(1)}, u32[]{:S(2)}, u32[]{:S(2)}) %collective-permute-start.1) | collective-permute-done | bytes 262176 | tf_op jit(solution)/shard_map/ppermute | solution.py:35
  33.9 0.7 collective-permute-start.5
  34.6 0.7 collective-permute-start.6
  35.3 8.3 %shard_map.86 = (bf16[128,1024]{1,0:T(8,128)(2,1)S(1)}, bf16[128,1024]{1,0:T(8,128)(2,1)S(1)}, bf16[128,1024]{1,0:T(8,128)(2,1)S(1)}, bf16[128,1024]{1,0:T(8,128)(2,1)S(1)}) custom-call(s32[1]{0:T(128)} %bitcast.slot_ref, bf16[128,4096]{1,0:T(8,128)(2,1)} %bitcast.15, bf16[128,4096]{1,0:T(8,128)(2,1)} %bitcast.12, bf16[128,1024]{1,0:T(8,128)(2,1)} %bitcast.19, ...), custom_call_target="tpu_custom_call" | custom-call | tf_op jit(solution)/shard_map/pallas_call | solution.py:99
  43.6 3.2 %collective-permute-start.7 = (bf16[128,1024]{1,0:T(8,128)(2,1)S(1)}, bf16[128,1024]{1,0:T(8,128)(2,1)S(1)}, u32[]{:S(2)}, u32[]{:S(2)}) collective-permute-start(bf16[128,1024]{1,0:T(8,128)(2,1)S(1)} %get-tuple-element.76), channel_id=1, source_target_pairs={{2,0},{4,2},{6,4},{10,8},{12,10},{14,12},{18,16},{20,18},{22,20},{... | collective-permute-start | bytes 786440 | tf_op jit(solution)/shard_map/ppermute | solution.py:35
  46.9 1.3 collective-permute-start.8
  48.2 0.7 collective-permute-start.9
  48.9 3.1 %collective-permute-start.10 = (bf16[128,1024]{1,0:T(8,128)(2,1)S(1)}, bf16[128,1024]{1,0:T(8,128)(2,1)S(1)}, u32[]{:S(2)}, u32[]{:S(2)}) collective-permute-start(bf16[128,1024]{1,0:T(8,128)(2,1)S(1)} %get-tuple-element.79), channel_id=1, source_target_pairs={{0,2},{2,4},{4,6},{8,10},{10,12},{12,14},{16,18},{18,20},{20,22},{... | collective-permute-start | bytes 786440 | tf_op jit(solution)/shard_map/ppermute | solution.py:35
  52.0 4.4 %collective-permute-start.11 = (bf16[128,1024]{1,0:T(8,128)(2,1)S(1)}, bf16[128,1024]{1,0:T(8,128)(2,1)}, u32[]{:S(2)}, u32[]{:S(2)}) collective-permute-start(bf16[128,1024]{1,0:T(8,128)(2,1)S(1)} %get-tuple-element.80), channel_id=1, source_target_pairs={{0,4},{2,6},{8,12},{10,14},{16,20},{18,22},{24,28},{26,30},{1,5},{... | collective-permute-start | bytes 786440 | tf_op jit(solution)/shard_map/ppermute | solution.py:35
  56.4 0.1 collective-permute-done.8
  56.5 0.1 collective-permute-done.10.refs_0_
  56.7 10.8 %collective-permute-done.11.refs_1_ = bf16[128,1024]{1,0:T(8,128)(2,1)} collective-permute-done((bf16[128,1024]{1,0:T(8,128)(2,1)S(1)}, bf16[128,1024]{1,0:T(8,128)(2,1)}, u32[]{:S(2)}, u32[]{:S(2)}) %collective-permute-start.11) | collective-permute-done | bytes 262176 | tf_op jit(solution)/shard_map/ppermute | solution.py:35
  67.5 0.9 add_convert_fusion.refs_0_
  68.4 2.2 %collective-permute-start.16 = (bf16[2,128,4096]{2,1,0:T(8,128)(2,1)S(1)}, bf16[2,128,4096]{2,1,0:T(8,128)(2,1)}, u32[]{:S(2)}, u32[]{:S(2)}) collective-permute-start(bf16[2,128,4096]{2,1,0:T(8,128)(2,1)S(1)} %get-tuple-element.95), channel_id=1, source_target_pairs={{0,24},{8,0},{16,8},{24,16},{1,25},{9,1},{17,9},{25,17},{2,26},{10... | collective-permute-start | bytes 6291464 | tf_op jit(solution)/shard_map/ppermute | solution.py:320
  70.6 0.7 collective-permute-start.12
  71.3 8.6 %collective-permute-done.12.refs_1_ = bf16[128,1024]{1,0:T(8,128)(2,1)S(1)} collective-permute-done((bf16[128,1024]{1,0:T(8,128)(2,1)}, bf16[128,1024]{1,0:T(8,128)(2,1)S(1)}, u32[]{:S(2)}, u32[]{:S(2)}) %collective-permute-start.12) | collective-permute-done | bytes 262176 | tf_op jit(solution)/shard_map/ppermute | solution.py:35
  79.9 0.0 copy-start.10
  79.9 1.6 %shard_map.88 = bf16[512,512]{1,0:T(8,128)(2,1)S(1)} custom-call(s32[1]{0:T(128)} %bitcast.slot_ref, s32[1]{0:T(128)S(6)} %sub.3.half_ref, bf16[1,1024]{1,0:T(2,128)(2,1)} %gain_ref.7, bf16[128,1024]{1,0:T(8,128)(2,1)} %copy-done.1, bf16[128,1024]{1,0:T(8,128)(2,1)} %copy-done.7, bf16[128,1024]{1,0:T(8,128)(2,1)} %collective-permute-done.11.refs_1_, ...), custom_call_target="tpu_custom_call" | custom-call | tf_op jit(solution)/shard_map/pallas_call | solution.py:160
  81.5 1.3 collective-permute-start.15
  82.8 2.9 %collective-permute-start.14 = (bf16[128,1024]{1,0:T(8,128)(2,1)}, bf16[128,1024]{1,0:T(8,128)(2,1)S(1)}, u32[]{:S(2)}, u32[]{:S(2)}) collective-permute-start(bf16[128,1024]{1,0:T(8,128)(2,1)} %add_convert_fusion.refs_0_), channel_id=1, source_target_pairs={{0,6},{2,0},{4,2},{6,4},{8,14},{10,8},{12,10},{14,12},{16,22},{18,... | collective-permute-start | bytes 786440 | tf_op jit(solution)/shard_map/ppermute | solution.py:35
  85.7 1.5 %shard_map.87.refs_0_ = bf16[512,512]{1,0:T(8,128)(2,1)S(1)} custom-call(s32[1]{0:T(128)} %bitcast.slot_ref, s32[1]{0:T(128)} %bitcast.4.half_ref, bf16[1,1024]{1,0:T(2,128)(2,1)} %gain_ref.7, bf16[128,1024]{1,0:T(8,128)(2,1)} %copy-done.1, bf16[128,1024]{1,0:T(8,128)(2,1)} %copy-done.7, bf16[128,1024]{1,0:T(8,128)(2,1)} %collective-permute-done.11.refs_1_, ...), custom_call_target="tpu_custom_call" | custom-call | tf_op jit(solution)/shard_map/pallas_call | solution.py:160
  87.3 0.8 copy-done
  88.0 2.7 %collective-permute-done.14.refs_3_ = bf16[128,1024]{1,0:T(8,128)(2,1)S(1)} collective-permute-done((bf16[128,1024]{1,0:T(8,128)(2,1)}, bf16[128,1024]{1,0:T(8,128)(2,1)S(1)}, u32[]{:S(2)}, u32[]{:S(2)}) %collective-permute-start.14) | collective-permute-done | bytes 262176 | tf_op jit(solution)/shard_map/ppermute | solution.py:35
  90.8 12.5 %collective-permute-done.13.refs_2_ = bf16[128,1024]{1,0:T(8,128)(2,1)S(1)} collective-permute-done((bf16[128,1024]{1,0:T(8,128)(2,1)}, bf16[128,1024]{1,0:T(8,128)(2,1)S(1)}, u32[]{:S(2)}, u32[]{:S(2)}) %collective-permute-start.13) | collective-permute-done | bytes 262176 | tf_op jit(solution)/shard_map/ppermute | solution.py:35
  103.3 0.7 copy-done.16
  104.0 4.3 %shard_map.89 = (bf16[128,1024]{1,0:T(8,128)(2,1)S(1)}, bf16[128,1024]{1,0:T(8,128)(2,1)S(1)}, bf16[128,1024]{1,0:T(8,128)(2,1)S(1)}, bf16[128,1024]{1,0:T(8,128)(2,1)S(1)}, bf16[512,1024]{1,0:T(8,128)(2,1)S(1)}) custom-call(bf16[1024,1024]{1,0:T(8,128)(2,1)} %bitcast.9, bf16[1,1024]{1,0:T(2,128)(2,1)} %gain_ref.7, ...), custom_call_target="tpu_custom_call" | custom-call | tf_op jit(solution)/shard_map/pallas_call | solution.py:197
  108.3 0.3 collective-permute-start.17
  108.6 0.8 collective-permute-start.18
  109.4 0.3 collective-permute-start.19
  109.6 3.5 %collective-permute-start.20 = (bf16[128,1024]{1,0:T(8,128)(2,1)S(1)}, bf16[128,1024]{1,0:T(8,128)(2,1)S(1)}, u32[]{:S(2)}, u32[]{:S(2)}) collective-permute-start(bf16[128,1024]{1,0:T(8,128)(2,1)S(1)} %get-tuple-element.108), channel_id=1, source_target_pairs={{0,28},{2,30},{4,24},{6,26},{8,4},{10,6},{12,0},{14,2},{16,12},{18... | collective-permute-start | bytes 786440 | tf_op jit(solution)/shard_map/ppermute | solution.py:45
  113.1 2.7 %collective-permute-start.21 = (bf16[128,1024]{1,0:T(8,128)(2,1)S(1)}, bf16[128,1024]{1,0:T(8,128)(2,1)S(1)}, u32[]{:S(2)}, u32[]{:S(2)}) collective-permute-start(bf16[128,1024]{1,0:T(8,128)(2,1)S(1)} %get-tuple-element.109), channel_id=1, source_target_pairs={{0,26},{2,28},{4,30},{6,24},{8,2},{10,4},{12,6},{14,0},{16,10},{18... | collective-permute-start | bytes 786440 | tf_op jit(solution)/shard_map/ppermute | solution.py:45
  115.8 16.8 %collective-permute-done.17.refs_3_ = bf16[512,1024]{1,0:T(8,128)(2,1)S(1)} collective-permute-done((bf16[512,1024]{1,0:T(8,128)(2,1)S(1)}, bf16[512,1024]{1,0:T(8,128)(2,1)S(1)}, u32[]{:S(2)}, u32[]{:S(2)}) %collective-permute-start.17) | collective-permute-done | bytes 1048608 | tf_op jit(solution)/shard_map/ppermute | solution.py:327
  132.6 1.0 copy-done.8
  133.6 4.3 %shard_map.90 = (bf16[512,1024]{1,0:T(8,128)(2,1)}, f32[1,512]{1,0:T(1,128)}) custom-call(s32[1]{0:T(128)} %bitcast.4.half_ref, bf16[1024,1024]{1,0:T(8,128)(2,1)} %bitcast.10, bf16[1,1024]{1,0:T(2,128)(2,1)} %gain_ref.7, bf16[512,512]{1,0:T(8,128)(2,1)} %copy-done, bf16[512,512]{1,0:T(8,128)(2,1)} %copy-done.9, bf16[512,1024]{1,0:T(8,128)(2,1)} %copy-done.2, ...), custom_call_target="tpu_custom_call" | custom-call | tf_op jit(solution)/shard_map/pallas_call | solution.py:232
  137.9 0.6 copy-done.11
  138.6 0.1 copy-done.12
  138.7 0.1 copy-done.13
  138.7 0.7 copy-done.15
  139.4 4.3 %shard_map.91 = bf16[128,4096]{1,0:T(8,128)(2,1)} custom-call(s32[1]{0:T(128)} %bitcast.slot_ref, bf16[2,128,4096]{2,1,0:T(8,128)(2,1)} %collective-permute-done.16.pair_ref, bf16[128,1024]{1,0:T(8,128)(2,1)} %copy-done.11, bf16[128,1024]{1,0:T(8,128)(2,1)} %copy-done.12, bf16[128,1024]{1,0:T(8,128)(2,1)} %copy-done.13, bf16[128,1024]{1,0:T(8,128)(2,1)} %copy-done.15), custom_call_target="tpu_custom_call" | custom-call | tf_op jit(solution)/shard_map/pallas_call | solution.py:281
  (44 shorter events, 0.1 us)
Async XLA Ops:
  0.6 15.6 %collective-permute-start.4 = (bf16[128,1024]{1,0:T(8,128)(2,1)}, bf16[128,1024]{1,0:T(8,128)(2,1)S(1)}, u32[]{:S(2)}, u32[]{:S(2)}) collective-permute-start(bf16[128,1024]{1,0:T(8,128)(2,1)} %bitcast.16), channel_id=1, source_target_pairs={{0,6},{8,14},{16,22},{24,30},{1,7},{9,15},{17,23},{25,31}} | collective-permute-start | bytes 786440 | tf_op jit(solution)/shard_map/ppermute | solution.py:35
  1.3 22.0 %collective-permute-start.3 = (bf16[128,1024]{1,0:T(8,128)(2,1)}, bf16[128,1024]{1,0:T(8,128)(2,1)S(1)}, u32[]{:S(2)}, u32[]{:S(2)}) collective-permute-start(bf16[128,1024]{1,0:T(8,128)(2,1)} %bitcast.17), channel_id=1, source_target_pairs={{0,4},{2,6},{8,12},{10,14},{16,20},{18,22},{24,28},{26,30},{1,5},{... | collective-permute-start | bytes 786440 | tf_op jit(solution)/shard_map/ppermute | solution.py:35
  6.2 22.8 %collective-permute-start.2 = (bf16[128,1024]{1,0:T(8,128)(2,1)}, bf16[128,1024]{1,0:T(8,128)(2,1)S(1)}, u32[]{:S(2)}, u32[]{:S(2)}) collective-permute-start(bf16[128,1024]{1,0:T(8,128)(2,1)} %bitcast.18), channel_id=1, source_target_pairs={{0,2},{2,4},{4,6},{8,10},{10,12},{12,14},{16,18},{18,20},{20,22},{... | collective-permute-start | bytes 786440 | tf_op jit(solution)/shard_map/ppermute | solution.py:35
  10.9 0.7 copy-start.1
  11.6 17.4 %collective-permute-start = (bf16[128,1024]{1,0:T(8,128)(2,1)S(1)}, bf16[128,1024]{1,0:T(8,128)(2,1)S(1)}, u32[]{:S(2)}, u32[]{:S(2)}) collective-permute-start(bf16[128,1024]{1,0:T(8,128)(2,1)S(1)} %get-tuple-element.80), channel_id=1, source_target_pairs={{4,0},{6,2},{12,8},{14,10},{20,16},{22,18},{28,24},{30,26},{5,1},{... | collective-permute-start | bytes 786440 | tf_op jit(solution)/shard_map/ppermute | solution.py:35
  12.9 21.0 %collective-permute-start.1 = (bf16[128,1024]{1,0:T(8,128)(2,1)S(1)}, bf16[128,1024]{1,0:T(8,128)(2,1)S(1)}, u32[]{:S(2)}, u32[]{:S(2)}) collective-permute-start(bf16[128,1024]{1,0:T(8,128)(2,1)S(1)} %get-tuple-element.72), channel_id=1, source_target_pairs={{2,0},{4,2},{6,4},{10,8},{12,10},{14,12},{18,16},{20,18},{22,20},{... | collective-permute-start | bytes 786440 | tf_op jit(solution)/shard_map/ppermute | solution.py:35
  16.3 19.0 %copy-start.17 = (bf16[128,1024]{1,0:T(8,128)(2,1)}, bf16[128,1024]{1,0:T(8,128)(2,1)S(1)}, u32[]{:S(2)}) copy-start(bf16[128,1024]{1,0:T(8,128)(2,1)S(1)} %collective-permute-done.4.refs_3_) | copy-start | bytes 786436
  23.4 10.5 %copy-start.18 = (bf16[128,1024]{1,0:T(8,128)(2,1)}, bf16[128,1024]{1,0:T(8,128)(2,1)S(1)}, u32[]{:S(2)}) copy-start(bf16[128,1024]{1,0:T(8,128)(2,1)S(1)} %collective-permute-done.3.refs_2_) | copy-start | bytes 786436
  29.0 4.9 %copy-start.19 = (bf16[128,1024]{1,0:T(8,128)(2,1)}, bf16[128,1024]{1,0:T(8,128)(2,1)S(1)}, u32[]{:S(2)}) copy-start(bf16[128,1024]{1,0:T(8,128)(2,1)S(1)} %collective-permute-done.2.refs_1_) | copy-start | bytes 786436
  29.0 39.4 %copy-start.3 = (bf16[128,1024]{1,0:T(8,128)(2,1)}, bf16[128,1024]{1,0:T(8,128)(2,1)S(1)}, u32[]{:S(2)}) copy-start(bf16[128,1024]{1,0:T(8,128)(2,1)S(1)} %collective-permute-done.refs_4_) | copy-start | bytes 786436
  33.9 34.5 %copy-start.4 = (bf16[128,1024]{1,0:T(8,128)(2,1)}, bf16[128,1024]{1,0:T(8,128)(2,1)S(1)}, u32[]{:S(2)}) copy-start(bf16[128,1024]{1,0:T(8,128)(2,1)S(1)} %collective-permute-done.1.refs_5_) | copy-start | bytes 786436
  33.9 9.7 %collective-permute-start.5 = (bf16[128,1024]{1,0:T(8,128)(2,1)S(1)}, bf16[128,1024]{1,0:T(8,128)(2,1)S(1)}, u32[]{:S(2)}, u32[]{:S(2)}) collective-permute-start(bf16[128,1024]{1,0:T(8,128)(2,1)S(1)} %get-tuple-element.79), channel_id=1, source_target_pairs={{6,0},{14,8},{22,16},{30,24},{7,1},{15,9},{23,17},{31,25}} | collective-permute-start | bytes 786440 | tf_op jit(solution)/shard_map/ppermute | solution.py:35
  34.6 9.0 %collective-permute-start.6 = (bf16[128,1024]{1,0:T(8,128)(2,1)S(1)}, bf16[128,1024]{1,0:T(8,128)(2,1)S(1)}, u32[]{:S(2)}, u32[]{:S(2)}) collective-permute-start(bf16[128,1024]{1,0:T(8,128)(2,1)S(1)} %get-tuple-element.72), channel_id=1, source_target_pairs={{0,6},{8,14},{16,22},{24,30},{1,7},{9,15},{17,23},{25,31}} | collective-permute-start | bytes 786440 | tf_op jit(solution)/shard_map/ppermute | solution.py:35
  43.6 36.3 %copy-start.5 = (bf16[128,1024]{1,0:T(8,128)(2,1)}, bf16[128,1024]{1,0:T(8,128)(2,1)S(1)}, u32[]{:S(2)}) copy-start(bf16[128,1024]{1,0:T(8,128)(2,1)S(1)} %collective-permute-done.5.refs_3_) | copy-start | bytes 786436
  43.6 36.3 %copy-start.6 = (bf16[128,1024]{1,0:T(8,128)(2,1)}, bf16[128,1024]{1,0:T(8,128)(2,1)S(1)}, u32[]{:S(2)}) copy-start(bf16[128,1024]{1,0:T(8,128)(2,1)S(1)} %collective-permute-done.6.refs_2_) | copy-start | bytes 786436
  43.6 12.8 %collective-permute-start.7 = (bf16[128,1024]{1,0:T(8,128)(2,1)S(1)}, bf16[128,1024]{1,0:T(8,128)(2,1)S(1)}, u32[]{:S(2)}, u32[]{:S(2)}) collective-permute-start(bf16[128,1024]{1,0:T(8,128)(2,1)S(1)} %get-tuple-element.76), channel_id=1, source_target_pairs={{2,0},{4,2},{6,4},{10,8},{12,10},{14,12},{18,16},{20,18},{22,20},{... | collective-permute-start | bytes 786440 | tf_op jit(solution)/shard_map/ppermute | solution.py:35
  46.9 9.7 %collective-permute-start.8 = (bf16[128,1024]{1,0:T(8,128)(2,1)S(1)}, bf16[128,1024]{1,0:T(8,128)(2,1)S(1)}, u32[]{:S(2)}, u32[]{:S(2)}) collective-permute-start(bf16[128,1024]{1,0:T(8,128)(2,1)S(1)} %get-tuple-element.77), channel_id=1, source_target_pairs={{4,0},{6,2},{12,8},{14,10},{20,16},{22,18},{28,24},{30,26},{5,1},{... | collective-permute-start | bytes 786440 | tf_op jit(solution)/shard_map/ppermute | solution.py:35
  48.2 8.4 %collective-permute-start.9 = (bf16[128,1024]{1,0:T(8,128)(2,1)S(1)}, bf16[128,1024]{1,0:T(8,128)(2,1)S(1)}, u32[]{:S(2)}, u32[]{:S(2)}) collective-permute-start(bf16[128,1024]{1,0:T(8,128)(2,1)S(1)} %get-tuple-element.78), channel_id=1, source_target_pairs={{6,0},{14,8},{22,16},{30,24},{7,1},{15,9},{23,17},{31,25}} | collective-permute-start | bytes 786440 | tf_op jit(solution)/shard_map/ppermute | solution.py:35
  48.9 7.8 %collective-permute-start.10 = (bf16[128,1024]{1,0:T(8,128)(2,1)S(1)}, bf16[128,1024]{1,0:T(8,128)(2,1)S(1)}, u32[]{:S(2)}, u32[]{:S(2)}) collective-permute-start(bf16[128,1024]{1,0:T(8,128)(2,1)S(1)} %get-tuple-element.79), channel_id=1, source_target_pairs={{0,2},{2,4},{4,6},{8,10},{10,12},{12,14},{16,18},{18,20},{20,22},{... | collective-permute-start | bytes 786440 | tf_op jit(solution)/shard_map/ppermute | solution.py:35
  52.0 15.5 %collective-permute-start.11 = (bf16[128,1024]{1,0:T(8,128)(2,1)S(1)}, bf16[128,1024]{1,0:T(8,128)(2,1)}, u32[]{:S(2)}, u32[]{:S(2)}) collective-permute-start(bf16[128,1024]{1,0:T(8,128)(2,1)S(1)} %get-tuple-element.80), channel_id=1, source_target_pairs={{0,4},{2,6},{8,12},{10,14},{16,20},{18,22},{24,28},{26,30},{1,5},{... | collective-permute-start | bytes 786440 | tf_op jit(solution)/shard_map/ppermute | solution.py:35
  56.6 23.2 %copy-start.7 = (bf16[128,1024]{1,0:T(8,128)(2,1)}, bf16[128,1024]{1,0:T(8,128)(2,1)S(1)}, u32[]{:S(2)}) copy-start(bf16[128,1024]{1,0:T(8,128)(2,1)S(1)} %collective-permute-done.10.refs_0_) | copy-start | bytes 786436
  68.4 34.9 %collective-permute-start.16 = (bf16[2,128,4096]{2,1,0:T(8,128)(2,1)S(1)}, bf16[2,128,4096]{2,1,0:T(8,128)(2,1)}, u32[]{:S(2)}, u32[]{:S(2)}) collective-permute-start(bf16[2,128,4096]{2,1,0:T(8,128)(2,1)S(1)} %get-tuple-element.95), channel_id=1, source_target_pairs={{0,24},{8,0},{16,8},{24,16},{1,25},{9,1},{17,9},{25,17},{2,26},{10... | collective-permute-start | bytes 6291464 | tf_op jit(solution)/shard_map/ppermute | solution.py:320
  70.6 9.3 %collective-permute-start.12 = (bf16[128,1024]{1,0:T(8,128)(2,1)}, bf16[128,1024]{1,0:T(8,128)(2,1)S(1)}, u32[]{:S(2)}, u32[]{:S(2)}) collective-permute-start(bf16[128,1024]{1,0:T(8,128)(2,1)} %add_convert_fusion.refs_0_), channel_id=1, source_target_pairs={{0,2},{2,4},{4,6},{6,0},{8,10},{10,12},{12,14},{14,8},{16,18},{18,... | collective-permute-start | bytes 786440 | tf_op jit(solution)/shard_map/ppermute | solution.py:35
  79.9 7.4 %copy-start.10 = (bf16[128,1024]{1,0:T(8,128)(2,1)}, bf16[128,1024]{1,0:T(8,128)(2,1)S(1)}, u32[]{:S(2)}) copy-start(bf16[128,1024]{1,0:T(8,128)(2,1)S(1)} %collective-permute-done.12.refs_1_) | copy-start | bytes 786436
  81.5 21.8 %collective-permute-start.15 = (bf16[512,512]{1,0:T(8,128)(2,1)S(1)}, bf16[512,512]{1,0:T(8,128)(2,1)S(1)}, u32[]{:S(2)}, u32[]{:S(2)}) collective-permute-start(bf16[512,512]{1,0:T(8,128)(2,1)S(1)} %shard_map.88), channel_id=1, source_target_pairs={{0,1},{1,0},{2,3},{3,2},{4,5},{5,4},{6,7},{7,6},{8,9},{9,8},{10,11... | collective-permute-start | bytes 1572872 | tf_op jit(solution)/shard_map/ppermute | solution.py:323
  82.8 8.0 %collective-permute-start.14 = (bf16[128,1024]{1,0:T(8,128)(2,1)}, bf16[128,1024]{1,0:T(8,128)(2,1)S(1)}, u32[]{:S(2)}, u32[]{:S(2)}) collective-permute-start(bf16[128,1024]{1,0:T(8,128)(2,1)} %add_convert_fusion.refs_0_), channel_id=1, source_target_pairs={{0,6},{2,0},{4,2},{6,4},{8,14},{10,8},{12,10},{14,12},{16,22},{18,... | collective-permute-start | bytes 786440 | tf_op jit(solution)/shard_map/ppermute | solution.py:35
  85.7 17.5 %collective-permute-start.13 = (bf16[128,1024]{1,0:T(8,128)(2,1)}, bf16[128,1024]{1,0:T(8,128)(2,1)S(1)}, u32[]{:S(2)}, u32[]{:S(2)}) collective-permute-start(bf16[128,1024]{1,0:T(8,128)(2,1)} %add_convert_fusion.refs_0_), channel_id=1, source_target_pairs={{0,4},{2,6},{4,0},{6,2},{8,12},{10,14},{12,8},{14,10},{16,20},{18,... | collective-permute-start | bytes 786440 | tf_op jit(solution)/shard_map/ppermute | solution.py:35
  87.3 0.8 copy-start
  90.8 12.5 %copy-start.14 = (bf16[128,1024]{1,0:T(8,128)(2,1)}, bf16[128,1024]{1,0:T(8,128)(2,1)S(1)}, u32[]{:S(2)}) copy-start(bf16[128,1024]{1,0:T(8,128)(2,1)S(1)} %collective-permute-done.14.refs_3_) | copy-start | bytes 786436
  103.3 0.7 copy-start.16
  103.3 29.3 %copy-start.9 = (bf16[512,512]{1,0:T(8,128)(2,1)}, bf16[512,512]{1,0:T(8,128)(2,1)S(1)}, u32[]{:S(2)}) copy-start(bf16[512,512]{1,0:T(8,128)(2,1)S(1)} %collective-permute-done.15.refs_1_) | copy-start | bytes 1572868
  108.3 24.3 %copy-start.2 = (bf16[512,1024]{1,0:T(8,128)(2,1)}, bf16[512,1024]{1,0:T(8,128)(2,1)S(1)}, u32[]{:S(2)}) copy-start(bf16[512,1024]{1,0:T(8,128)(2,1)S(1)} %get-tuple-element.102.refs_2_) | copy-start | bytes 3145732
  108.3 24.3 %collective-permute-start.17 = (bf16[512,1024]{1,0:T(8,128)(2,1)S(1)}, bf16[512,1024]{1,0:T(8,128)(2,1)S(1)}, u32[]{:S(2)}, u32[]{:S(2)}) collective-permute-start(bf16[512,1024]{1,0:T(8,128)(2,1)S(1)} %get-tuple-element.102.refs_2_), channel_id=1, source_target_pairs={{0,1},{1,0},{2,3},{3,2},{4,5},{5,4},{6,7},{7,6},{8,9},{9,8},{10,11... | collective-permute-start | bytes 3145736 | tf_op jit(solution)/shard_map/ppermute | solution.py:327
  108.6 29.3 %collective-permute-start.18 = (bf16[128,1024]{1,0:T(8,128)(2,1)S(1)}, bf16[128,1024]{1,0:T(8,128)(2,1)S(1)}, u32[]{:S(2)}, u32[]{:S(2)}) collective-permute-start(bf16[128,1024]{1,0:T(8,128)(2,1)S(1)} %get-tuple-element.106), channel_id=1, source_target_pairs={{0,24},{2,26},{4,28},{6,30},{8,0},{10,2},{12,4},{14,6},{16,8},{18,... | collective-permute-start | bytes 786440 | tf_op jit(solution)/shard_map/ppermute | solution.py:45
  109.4 28.5 %collective-permute-start.19 = (bf16[128,1024]{1,0:T(8,128)(2,1)S(1)}, bf16[128,1024]{1,0:T(8,128)(2,1)S(1)}, u32[]{:S(2)}, u32[]{:S(2)}) collective-permute-start(bf16[128,1024]{1,0:T(8,128)(2,1)S(1)} %get-tuple-element.107), channel_id=1, source_target_pairs={{0,30},{2,24},{4,26},{6,28},{8,6},{10,0},{12,2},{14,4},{16,14},{18... | collective-permute-start | bytes 786440 | tf_op jit(solution)/shard_map/ppermute | solution.py:45
  109.6 28.3 %collective-permute-start.20 = (bf16[128,1024]{1,0:T(8,128)(2,1)S(1)}, bf16[128,1024]{1,0:T(8,128)(2,1)S(1)}, u32[]{:S(2)}, u32[]{:S(2)}) collective-permute-start(bf16[128,1024]{1,0:T(8,128)(2,1)S(1)} %get-tuple-element.108), channel_id=1, source_target_pairs={{0,28},{2,30},{4,24},{6,26},{8,4},{10,6},{12,0},{14,2},{16,12},{18... | collective-permute-start | bytes 786440 | tf_op jit(solution)/shard_map/ppermute | solution.py:45
  113.1 24.8 %collective-permute-start.21 = (bf16[128,1024]{1,0:T(8,128)(2,1)S(1)}, bf16[128,1024]{1,0:T(8,128)(2,1)S(1)}, u32[]{:S(2)}, u32[]{:S(2)}) collective-permute-start(bf16[128,1024]{1,0:T(8,128)(2,1)S(1)} %get-tuple-element.109), channel_id=1, source_target_pairs={{0,26},{2,28},{4,30},{6,24},{8,2},{10,4},{12,6},{14,0},{16,10},{18... | collective-permute-start | bytes 786440 | tf_op jit(solution)/shard_map/ppermute | solution.py:45
  132.6 1.0 copy-start.8
  137.9 0.7 copy-start.11
  137.9 0.8 copy-start.12
  137.9 0.8 copy-start.13
  138.7 0.7 copy-start.15

commit v3 on v2

v3 whole, which is shorter than its diff:
```python
import functools

import jax
import jax.numpy as jnp
from jax import lax
from jax.experimental import pallas as pl
from jax.experimental.pallas import tpu as pltpu
from jax.sharding import PartitionSpec as P

DH = 128
MEM = 128
NEG_FILL = -1e30
EPSILON = 1e-05
LOG2E = 1.4426950408889634
TILE = 16
MIB = 1024 * 1024

SCALAR = pl.BlockSpec(memory_space=pltpu.SMEM)
PARAMS = pltpu.CompilerParams(vmem_limit_bytes=16 * MIB)


def section_route(distance):
    count = lax.axis_size("section")
    return [(s, (s + distance) % count) for s in range(count)]


def to_partner(block, mask, below=False):
    sections, count = lax.axis_size("section"), lax.axis_size("fsdp")
    route = [
        (s * count + f, (s - below) % sections * count + (f ^ mask))
        for s in range(sections)
        for f in range(count)
    ]
    return lax.ppermute(block, ("section", "fsdp"), route)


def after(arrays, others):
    kept, _ = lax.optimization_barrier((arrays, others))
    return kept


def fixed(shape):
    return pl.BlockSpec(shape, lambda *_: (0, 0))


def in_hbm(*arrays):
    return [pltpu.with_memory_space_constraint(array, pltpu.HBM) for array in arrays]


def attention_kernel(count, group, heads, x_steps, slot_ref, query_ref, grad_ref, *refs):
    key_refs, x_refs, out_refs = refs[:count], refs[count : -count], refs[-count:]
    rows = query_ref.shape[0]
    slot = slot_ref[0]
    key_at = lax.broadcasted_iota(jnp.int32, (rows, rows), 0)
    query_at = lax.broadcasted_iota(jnp.int32, (rows, rows), 1)
    visible = (key_at <= query_at) | (slot * rows + key_at < MEM)
    visible = jnp.concatenate([visible] * group, axis=1)
    hidden = [0.0] + [jnp.where(slot ^ m < slot, 0.0, NEG_FILL) for m in range(1, count)]
    scale = DH ** (-0.5) * LOG2E
    for head in range(heads):
        own = slice(head * DH, (head + 1) * DH)
        members = [slice(h * DH, (h + 1) * DH) for h in range(head * group, (head + 1) * group)]
        query = jnp.concatenate([query_ref[:, h] for h in members], axis=0)
        grad = jnp.concatenate([grad_ref[:, h] for h in members], axis=0)
        keys = jnp.concatenate([ref[:, own] for ref in key_refs], axis=0)
        scores = lax.dot_general(
            keys, query, (((1,), (1,)), ((), ())), preferred_element_type=jnp.float32
        )
        parts = [scores[m * rows : (m + 1) * rows] for m in range(count)]
        parts[0] = jnp.where(visible, parts[0], NEG_FILL)
        tops = [jnp.max(part, axis=0, keepdims=True) + hide for part, hide in zip(parts, hidden)]
        top = functools.reduce(jnp.maximum, tops)
        weights = [jnp.exp2((part - (top - hide)) * scale) for part, hide in zip(parts, hidden)]
        sums = [jnp.sum(weight, axis=0, keepdims=True) for weight in weights]
        inverse = 1.0 / functools.reduce(jnp.add, sums)
        probs = jnp.concatenate([(w * inverse).astype(jnp.bfloat16) for w in weights], axis=0)
        values = jnp.dot(probs, grad, preferred_element_type=jnp.float32)
        for m in range(count):
            out_refs[m][:, own] = values[m * rows : (m + 1) * rows].astype(jnp.bfloat16)
    for m in range(1, count):

        @pl.when((slot ^ m > slot) & (pl.program_id(0) < x_steps))
        def _():
            out_refs[m][...] = x_refs[m - 1][...]


def attention(slot, queries, grads, key_blocks, x):
    rows, kv_width = key_blocks[0].shape
    group = queries.shape[1] // kv_width
    count = len(key_blocks)
    x_width = x.shape[1] // count
    heads = min(4, kv_width // DH) if count <= 4 else 1
    width = heads * DH
    x_steps = x_width // width
    assert x_width <= kv_width and x_width % width == 0
    wide = pl.BlockSpec((rows, group * width), lambda g, _: (0, g))
    narrow = pl.BlockSpec((rows, width), lambda g, _: (0, g))
    columns = [
        pl.BlockSpec(
            (rows, width),
            lambda g, ref, m=m: (0, (ref[0] ^ m) * x_steps + jnp.minimum(g, x_steps - 1)),
        )
        for m in range(1, count)
    ]
    return pl.pallas_call(
        functools.partial(attention_kernel, count, group, heads, x_steps),
        grid_spec=pltpu.PrefetchScalarGridSpec(
            num_scalar_prefetch=1,
            grid=(kv_width // width,),
            in_specs=[wide, wide] + [narrow] * count + columns,
            out_specs=[narrow] * count,
        ),
        out_shape=[jax.ShapeDtypeStruct((rows, kv_width), jnp.bfloat16)] * count,
        compiler_params=pltpu.CompilerParams(vmem_limit_bytes=(24 + 2 * count) * MIB),
    )(slot, *in_hbm(queries, grads, *key_blocks, *[x] * (count - 1)))


def rms_kernel(x_ref, out_ref):
    x = x_ref[...].astype(jnp.float32)
    inv_rms = lax.rsqrt(jnp.mean(x * x, axis=1, keepdims=True) + EPSILON)
    out_ref[...] = jnp.broadcast_to(inv_rms, out_ref.shape)


def inverse_rms(x):
    rows, width = x.shape
    step = min(rows, 2 * TILE)
    return pl.pallas_call(
        rms_kernel,
        grid=(rows // step,),
        in_specs=[pl.BlockSpec((step, width), lambda r: (r, 0))],
        out_specs=pl.BlockSpec((step, DH), lambda r: (r, 0)),
        out_shape=jax.ShapeDtypeStruct((rows, DH), jnp.float32),
        compiler_params=PARAMS,
    )(*in_hbm(x))


def value_kernel(count, slot_ref, rms_ref, own_ref, *refs):
    slot = slot_ref[0]
    total = own_ref[...].astype(jnp.float32)
    for m in range(1, count):
        total += jnp.where(slot ^ m > slot, refs[m - 1][...].astype(jnp.float32), 0.0)
    refs[-1][...] = (total * rms_ref[:, :1]).astype(jnp.bfloat16)


def value_grad(slot, inv_rms, own_term, received):
    rows, width = own_term.shape
    step = min(rows, 4 * TILE)
    line = pl.BlockSpec((step, width), lambda r: (r, 0))
    return pl.pallas_call(
        functools.partial(value_kernel, len(received) + 1),
        grid=(rows // step,),
        in_specs=[SCALAR, pl.BlockSpec((step, DH), lambda r: (r, 0))]
        + [line] * (len(received) + 1),
        out_specs=line,
        out_shape=jax.ShapeDtypeStruct((rows, width), jnp.bfloat16),
        compiler_params=PARAMS,
    )(slot, *in_hbm(inv_rms, own_term, *received))


def column_kernel(count, slot_ref, half_ref, gain_ref, own_ref, *refs):
    first, second, out_ref = refs[: count - 1], refs[count - 1 : -1], refs[-1]
    slot = slot_ref[0]
    rows = own_ref.shape[0]
    gain = gain_ref[...].astype(jnp.float32)
    for m in range(count):
        x = own_ref[...]
        if m > 0:
            x = jnp.where(slot ^ m > slot, first[m - 1][...], second[m - 1][...])
        out_ref[:, m * rows : (m + 1) * rows] = (x.astype(jnp.float32) * gain).astype(jnp.bfloat16).T


def gained_columns(slot, half, halves, gain, x, first, second):
    count = len(first) + 1
    rows, width = x.shape
    width = width // count // halves
    step = min(width, 256)
    steps = width // step

    def place(c, slot_ref, half_ref):
        return (0, half_ref[0] * steps + c)

    def own_place(c, slot_ref, half_ref):
        return (0, (slot_ref[0] * halves + half_ref[0]) * steps + c)

    return pl.pallas_call(
        functools.partial(column_kernel, count),
        grid_spec=pltpu.PrefetchScalarGridSpec(
            num_scalar_prefetch=2,
            grid=(steps,),
            in_specs=[pl.BlockSpec((1, step), place), pl.BlockSpec((rows, step), own_place)]
            + [pl.BlockSpec((rows, step), place)] * (2 * count - 2),
            out_specs=pl.BlockSpec((step, count * rows), lambda c, *_: (c, 0)),
        ),
        out_shape=jax.ShapeDtypeStruct((width, count * rows), jnp.bfloat16),
        compiler_params=PARAMS,
    )(slot, half, *in_hbm(gain, x, *first, *second))


def feature_kernel(count, weight_ref, gain_ref, *refs):
    value_refs, scaled_refs, all_ref = refs[:count], refs[count:-1], refs[-1]
    rows = value_refs[0].shape[0]
    values = jnp.concatenate([ref[...] for ref in value_refs], axis=0)

    @pl.when(pl.program_id(0) == 0)
    def _():
        all_ref[...] = values

    normed_grad = lax.dot_general(
        values, weight_ref[...], (((1,), (1,)), ((), ())), preferred_element_type=jnp.float32
    )
    gain = gain_ref[...].astype(jnp.float32)
    for d in range(count):
        scaled_refs[d][...] = (normed_grad[d * rows : (d + 1) * rows] * gain).astype(jnp.bfloat16)


def feature_grads(weight, gain, values):
    count = len(values)
    rows, kv_width = values[0].shape
    width = weight.shape[0]
    step = min(width, 1024)
    column = pl.BlockSpec((rows, step), lambda c: (0, c))
    out = pl.pallas_call(
        functools.partial(feature_kernel, count),
        grid=(width // step,),
        in_specs=[
            pl.BlockSpec((step, kv_width), lambda c: (c, 0)),
            pl.BlockSpec((1, step), lambda c: (0, c)),
        ]
        + [fixed((rows, kv_width))] * count,
        out_specs=[column] * count + [fixed((count * rows, kv_width))],
        out_shape=[jax.ShapeDtypeStruct((rows, width), jnp.bfloat16)] * count
        + [jax.ShapeDtypeStruct((count * rows, kv_width), jnp.bfloat16)],
        compiler_params=PARAMS,
    )(*in_hbm(weight, gain, *values))
    return out[:count], out[count]


def weight_kernel(docs, half_ref, weight_ref, gain_ref, *refs):
    normed_refs, value_refs, (out_ref, line_ref) = refs[:docs], refs[docs:-2], refs[-2:]
    normed = jnp.concatenate([ref[...] for ref in normed_refs], axis=1)
    values = jnp.concatenate([ref[...] for ref in value_refs], axis=0)
    grad = jnp.dot(normed, values, preferred_element_type=jnp.float32)
    kv_width = grad.shape[1]
    out_ref[...] = grad.astype(jnp.bfloat16)
    terms = grad * weight_ref[...].astype(jnp.float32)
    lanes = sum(terms[:, i : i + DH] for i in range(0, kv_width, DH))
    line_ref[...] = jnp.sum(lanes.T, axis=0, keepdims=True) / gain_ref[...].astype(jnp.float32)


def weight_grad(half, weight, gain, normed, values):
    docs = len(normed)
    blocks = [block for doc in values for block in doc]
    rows, kv_width = values[0][0].shape
    width, tokens = normed[0].shape
    step = min(width, 256)
    steps = width // step
    return pl.pallas_call(
        functools.partial(weight_kernel, docs),
        grid_spec=pltpu.PrefetchScalarGridSpec(
            num_scalar_prefetch=1,
            grid=(steps,),
            in_specs=[
                pl.BlockSpec((step, kv_width), lambda c, half_ref: (half_ref[0] * steps + c, 0)),
                pl.BlockSpec((1, step), lambda c, half_ref: (0, half_ref[0] * steps + c)),
            ]
            + [pl.BlockSpec((step, tokens), lambda c, *_: (c, 0))] * docs
            + [fixed((rows, kv_width))] * len(blocks),
            out_specs=[
                pl.BlockSpec((step, kv_width), lambda c, *_: (c, 0)),
                pl.BlockSpec((1, step), lambda c, *_: (0, c)),
            ],
        ),
        out_shape=[
            jax.ShapeDtypeStruct((width, kv_width), jnp.bfloat16),
            jax.ShapeDtypeStruct((1, width), jnp.float32),
        ],
        compiler_params=PARAMS,
    )(half, *in_hbm(weight, gain, *normed, *blocks))


def input_kernel(count, slot_ref, x_ref, grad_ref, *refs):
    scaled_refs, out_ref = refs[:count], refs[count]
    slot = slot_ref[0]
    x = x_ref[...].astype(jnp.float32)
    square = 1.0 / (jnp.mean(x * x, axis=1, keepdims=True) + EPSILON)
    width = x.shape[1] // count
    starts = [pl.multiple_of((slot ^ m) * width, width) for m in range(count)]
    inner = jnp.zeros_like(square)
    for m in range(count):
        block = x_ref[:, pl.ds(starts[m], width)].astype(jnp.float32)
        inner += jnp.sum(scaled_refs[m][...].astype(jnp.float32) * block, axis=1, keepdims=True)
    inner = inner * square / x.shape[1]
    for m in range(count):
        columns = pl.ds(starts[m], width)
        block = x_ref[:, columns].astype(jnp.float32)
        grad = grad_ref[:, columns].astype(jnp.float32)
        scaled = scaled_refs[m][...].astype(jnp.float32)
        out_ref[:, columns] = (grad + (scaled - block * inner)).astype(jnp.bfloat16)


def input_grad(slot, x, grads, scaled):
    count = len(scaled)
    rows, width = x.shape
    step = min(rows, 4 * TILE)
    wide = pl.BlockSpec((step, width), lambda r: (r, 0))
    return pl.pallas_call(
        functools.partial(input_kernel, count),
        grid=(rows // step,),
        in_specs=[SCALAR, wide, wide]
        + [pl.BlockSpec((step, width // count), lambda r: (r, 0))] * count,
        out_specs=wide,
        out_shape=jax.ShapeDtypeStruct((rows, width), jnp.bfloat16),
        compiler_params=PARAMS,
    )(slot, *in_hbm(x, grads, *scaled))


def per_device(section_inputs, queries, keys, w_value, gain, section_grads_in):
    count = lax.axis_size("fsdp")
    docs = lax.axis_size("dp")
    slot = lax.axis_index("fsdp").astype(jnp.int32)[None]
    half = lax.axis_index("dp").astype(jnp.int32)[None]
    x, cotangent, own_keys = section_inputs[0, 0], section_grads_in[0, 0], keys[0, 0]
    weight = w_value[0]
    assert MEM <= x.shape[0] and docs == 2 and count & (count - 1) == 0
    masks = range(1, count)

    swap = [(0, 1), (1, 0)]

    x_width = x.shape[1] // count
    first = []
    for m in masks:
        columns = lax.dynamic_slice_in_dim(x, (slot[0] ^ m) * x_width, x_width, axis=1)
        columns = jnp.pad(columns, ((0, 0), (0, own_keys.shape[1] - x_width)))
        first.append(to_partner(jnp.where(slot[0] ^ m > slot[0], own_keys, columns), m))
    next_x = lax.ppermute(x, "section", section_route(-1))
    inv_rms = inverse_rms(x)
    first, next_x, inv_rms, slot = after((first, next_x, inv_rms, slot), ())
    terms = attention(slot, queries[0, 0], cotangent, [own_keys] + first, x)

    second = [to_partner(terms[m], m) for m in masks]
    next_grad = lax.ppermute(after(cotangent, terms), "section", section_route(-1))
    second, next_grad = after((second, next_grad), ())
    value = value_grad(slot, inv_rms, terms[0], second)
    sent = gained_columns(slot, 1 - half, docs, gain, x, first, second)

    value, sent = after((value, sent), ())
    values = [value] + [to_partner(value, m) for m in masks]
    normed = [
        gained_columns(slot, half, docs, gain, x, first, second),
        lax.ppermute(sent, "dp", swap),
    ]
    values, normed = after((values, normed), ())

    scaled, all_values = feature_grads(weight, gain, values)
    other_values = lax.ppermute(all_values, "dp", swap)
    returned = [to_partner(scaled[m], m, below=True) for m in range(count)]

    weight_out, gain_out = weight_grad(half, weight, gain, normed, [[all_values], [other_values]])
    slot = after(slot, weight_out)
    passed = input_grad(slot, next_x, next_grad, returned)
    return passed[None, None], weight_out[None], gain_out


def solution(mesh):
    return jax.shard_map(
        per_device,
        mesh=mesh,
        in_specs=(
            P("section", "dp", "fsdp", None),
            P("section", "dp", "fsdp", None),
            P("section", "dp", "fsdp", None),
            P("section", "fsdp", None),
            P("section", "fsdp"),
            P("section", "dp", "fsdp", None),
        ),
        out_specs=(
            P("section", "dp", "fsdp", None),
            P("section", ("fsdp", "dp"), None),
            P("section", ("fsdp", "dp")),
        ),
        check_vma=False,
    )
```

time: 146 us -> 130 us (0.89)
  the two profiles are of different devices: /device:TPU:9 before, /device:TPU:0 now
where the time goes in v3:
time: 130 us; the launch traced here: 129 us
  waiting for transfers between devices  71.1 us (55%)
  starting transfers between devices  25.7 us (20%)
  Pallas kernels  23.1 us (18%)
  local copies, waits for them, and re-layouts  7.32 us (6%)
  other arithmetic  1.42 us (1%)
    ppermute x13, waiting for transfers between devices, to_partner(): return lax.ppermute(block, ('section', 'fsdp'), route)  51.7 us
    ppermute x13, starting transfers between devices, to_partner(): return lax.ppermute(block, ('section', 'fsdp'), route)  20.3 us
    ppermute x1, waiting for transfers between devices, per_device(): other_values = lax.ppermute(all_values, 'dp', swap)  19.5 us
    unnamed x44, local copies, waits for them, and re-layouts  7.32 us
    pallas_call x1, Pallas kernels, attention(): pl.pallas_call(functools.partial(attention_kernel, count, group, heads, x...  5.43 us
    pallas_call x1, Pallas kernels, weight_grad(): pl.pallas_call(functools.partial(weight_kernel, docs), grid_spec=pltpu.Pr...  4.25 us
    pallas_call x1, Pallas kernels, input_grad(): pl.pallas_call(functools.partial(input_kernel, count), grid=(rows // step...  3.38 us
    pallas_call x1, Pallas kernels, feature_grads(): pl.pallas_call(functools.partial(feature_kernel, count), grid=(width // s...  3.13 us
  transfers between devices with their start and end apart: 17, of which 7 were waited for; matrix products, arithmetic and copies ran while one was open for 1% of the time, Pallas kernels for 6%

profile of v3, /device:TPU:0, one launch (start us, length us, event | category | flops | bytes accessed | tf_op | source)
XLA Modules:
  0.0 129.5 jit_solution(16140735829391385397)
XLA Ops:
  0.6 2.4 %collective-permute-start.3 = (bf16[128,4096]{1,0:T(8,128)(2,1)}, bf16[128,4096]{1,0:T(8,128)(2,1)S(1)}, u32[]{:S(2)}, u32[]{:S(2)}) collective-permute-start(bf16[128,4096]{1,0:T(8,128)(2,1)} %bitcast.18), channel_id=1, source_target_pairs={{0,24},{8,0},{16,8},{24,16},{1,25},{9,1},{17,9},{25,17},{2,26},{10... | collective-permute-start | bytes 3145736 | tf_op jit(solution)/shard_map/ppermute | solution.py:335
  3.1 1.4 %bitcast_select_fusion = (bf16[128,1024]{1,0:T(8,128)(2,1)S(1)}, bf16[128,1024]{1,0:T(8,128)(2,1)S(1)}, bf16[128,1024]{1,0:T(8,128)(2,1)S(1)}) fusion(bf16[1,1,128,4096]{3,2,1,0:T(8,128)(2,1)} %param.6, s32[]{:T(128)S(6)} %select_n.36, pred[]{:T(512)S(6)} %gt.11, bf16[1,1,128,1024]{3,2,1,0:T(8,128)(2,1)} %param.8, s32[]{:T(128)S(6)} %select_n.33, pred[]{:T(512)S(6)} %gt.10, ...), kind=kLoop, calls=%fused_computation | loop fusion | flops 393216 | bytes 1835023 | tf_op jit(solution)/shard_map/jit(_where)/select_n | solution.py:334
  4.5 3.7 %collective-permute-start.2 = (bf16[128,1024]{1,0:T(8,128)(2,1)S(1)}, bf16[128,1024]{1,0:T(8,128)(2,1)S(1)}, u32[]{:S(2)}, u32[]{:S(2)}) collective-permute-start(bf16[128,1024]{1,0:T(8,128)(2,1)S(1)} %get-tuple-element.65), channel_id=1, source_target_pairs={{0,6},{2,4},{4,2},{6,0},{8,14},{10,12},{12,10},{14,8},{16,22},{18,... | collective-permute-start | bytes 786440 | tf_op jit(solution)/shard_map/ppermute | solution.py:34
  8.2 0.0 collective-permute-start.1
  8.2 0.8 collective-permute-start
  8.9 2.4 %shard_map.85.rms_ref = f32[128,128]{1,0:T(8,128)S(1)} custom-call(bf16[128,4096]{1,0:T(8,128)(2,1)} %bitcast.19), custom_call_target="tpu_custom_call" | custom-call | tf_op jit(solution)/shard_map/pallas_call | solution.py:127
  11.3 0.6 copy-done.4
  11.9 3.7 %collective-permute-done.2.refs_3_.refs_2_ = bf16[128,1024]{1,0:T(8,128)(2,1)S(1)} collective-permute-done((bf16[128,1024]{1,0:T(8,128)(2,1)S(1)}, bf16[128,1024]{1,0:T(8,128)(2,1)S(1)}, u32[]{:S(2)}, u32[]{:S(2)}) %collective-permute-start.2) | collective-permute-done | bytes 262176 | tf_op jit(solution)/shard_map/ppermute | solution.py:34
  15.7 14.5 %collective-permute-done.1.refs_2_.refs_1_ = bf16[128,1024]{1,0:T(8,128)(2,1)S(1)} collective-permute-done((bf16[128,1024]{1,0:T(8,128)(2,1)S(1)}, bf16[128,1024]{1,0:T(8,128)(2,1)S(1)}, u32[]{:S(2)}, u32[]{:S(2)}) %collective-permute-start.1) | collective-permute-done | bytes 262176 | tf_op jit(solution)/shard_map/ppermute | solution.py:34
  30.2 0.0 collective-permute-done.refs_1_.refs_0_
  30.2 1.0 copy-done.12
  31.2 0.0 copy-done.6
  31.3 0.1 copy-done.7
  31.3 5.4 %shard_map.86 = (bf16[128,1024]{1,0:T(8,128)(2,1)S(1)}, bf16[128,1024]{1,0:T(8,128)(2,1)S(1)}, bf16[128,1024]{1,0:T(8,128)(2,1)S(1)}, bf16[128,1024]{1,0:T(8,128)(2,1)S(1)}) custom-call(s32[1]{0:T(128)} %bitcast.5.slot_ref, bf16[128,4096]{1,0:T(8,128)(2,1)} %bitcast.27, bf16[128,4096]{1,0:T(8,128)(2,1)} %bitcast.28, bf16[128,1024]{1,0:T(8,128)(2,1)} %bitcast.31, ...), custom_call_target="tpu_custom_call" | custom-call | tf_op jit(solution)/shard_map/pallas_call | solution.py:105
  36.8 0.7 copy-done.3
  37.5 0.8 collective-permute-start.7
  38.3 0.0 collective-permute-start.4
  38.3 3.0 %collective-permute-start.5 = (bf16[128,1024]{1,0:T(8,128)(2,1)S(1)}, bf16[128,1024]{1,0:T(8,128)(2,1)S(1)}, u32[]{:S(2)}, u32[]{:S(2)}) collective-permute-start(bf16[128,1024]{1,0:T(8,128)(2,1)S(1)} %get-tuple-element.41), channel_id=1, source_target_pairs={{0,4},{2,6},{4,0},{6,2},{8,12},{10,14},{12,8},{14,10},{16,20},{18,... | collective-permute-start | bytes 786440 | tf_op jit(solution)/shard_map/ppermute | solution.py:34
  41.3 1.4 %collective-permute-start.6 = (bf16[128,1024]{1,0:T(8,128)(2,1)S(1)}, bf16[128,1024]{1,0:T(8,128)(2,1)S(1)}, u32[]{:S(2)}, u32[]{:S(2)}) collective-permute-start(bf16[128,1024]{1,0:T(8,128)(2,1)S(1)} %get-tuple-element.42), channel_id=1, source_target_pairs={{0,6},{2,4},{4,2},{6,0},{8,14},{10,12},{12,10},{14,8},{16,22},{18,... | collective-permute-start | bytes 786440 | tf_op jit(solution)/shard_map/ppermute | solution.py:34
  42.7 8.5 %collective-permute-done.4.refs_0_.refs_3_ = bf16[128,1024]{1,0:T(8,128)(2,1)S(1)} collective-permute-done((bf16[128,1024]{1,0:T(8,128)(2,1)S(1)}, bf16[128,1024]{1,0:T(8,128)(2,1)S(1)}, u32[]{:S(2)}, u32[]{:S(2)}) %collective-permute-start.4) | collective-permute-done | bytes 262176 | tf_op jit(solution)/shard_map/ppermute | solution.py:34
  51.1 8.6 %collective-permute-done.5.refs_1_.refs_4_ = bf16[128,1024]{1,0:T(8,128)(2,1)S(1)} collective-permute-done((bf16[128,1024]{1,0:T(8,128)(2,1)S(1)}, bf16[128,1024]{1,0:T(8,128)(2,1)S(1)}, u32[]{:S(2)}, u32[]{:S(2)}) %collective-permute-start.5) | collective-permute-done | bytes 262176 | tf_op jit(solution)/shard_map/ppermute | solution.py:34
  59.7 0.7 copy-done.9
  60.4 0.1 copy-done.10
  60.5 1.4 %shard_map.87.refs_0_ = bf16[128,1024]{1,0:T(8,128)(2,1)S(1)} custom-call(s32[1]{0:T(128)} %bitcast.5.slot_ref, f32[128,128]{1,0:T(8,128)} %copy-done.4, bf16[128,1024]{1,0:T(8,128)(2,1)} %copy-done.3, bf16[128,1024]{1,0:T(8,128)(2,1)} %copy-done.8, bf16[128,1024]{1,0:T(8,128)(2,1)} %copy-done.9, bf16[128,1024]{1,0:T(8,128)(2,1)} %copy-done.10), custom_call_target="tpu_custom_call" | custom-call | tf_op jit(solution)/shard_map/pallas_call | solution.py:149
  62.0 1.6 %shard_map.88 = bf16[512,512]{1,0:T(8,128)(2,1)S(1)} custom-call(s32[1]{0:T(128)} %bitcast.5.slot_ref, s32[1]{0:T(128)S(6)} %sub.3.half_ref, bf16[1,1024]{1,0:T(2,128)(2,1)} %gain_ref.7, bf16[128,4096]{1,0:T(8,128)(2,1)} %bitcast.23, bf16[128,1024]{1,0:T(8,128)(2,1)} %copy-done.7, bf16[128,1024]{1,0:T(8,128)(2,1)} %copy-done.6, bf16[128,1024]{1,0:T(8,128)(2,1)} %copy-done.5, ...), custom_call_target="tpu_custom_call" | custom-call | tf_op jit(solution)/shard_map/pallas_call | solution.py:185
  63.6 1.6 %collective-permute-start.11 = (bf16[512,512]{1,0:T(8,128)(2,1)S(1)}, bf16[512,512]{1,0:T(8,128)(2,1)S(1)}, u32[]{:S(2)}, u32[]{:S(2)}) collective-permute-start(bf16[512,512]{1,0:T(8,128)(2,1)S(1)} %shard_map.88), channel_id=1, source_target_pairs={{0,1},{1,0},{2,3},{3,2},{4,5},{5,4},{6,7},{7,6},{8,9},{9,8},{10,11... | collective-permute-start | bytes 1572872 | tf_op jit(solution)/shard_map/ppermute | solution.py:350
  65.1 2.4 %collective-permute-start.10 = (bf16[128,1024]{1,0:T(8,128)(2,1)S(1)}, bf16[128,1024]{1,0:T(8,128)(2,1)S(1)}, u32[]{:S(2)}, u32[]{:S(2)}) collective-permute-start(bf16[128,1024]{1,0:T(8,128)(2,1)S(1)} %shard_map.87.refs_0_), channel_id=1, source_target_pairs={{0,6},{2,4},{4,2},{6,0},{8,14},{10,12},{12,10},{14,8},{16,22},{18,... | collective-permute-start | bytes 786440 | tf_op jit(solution)/shard_map/ppermute | solution.py:34
  67.5 4.0 %collective-permute-start.9 = (bf16[128,1024]{1,0:T(8,128)(2,1)S(1)}, bf16[128,1024]{1,0:T(8,128)(2,1)S(1)}, u32[]{:S(2)}, u32[]{:S(2)}) collective-permute-start(bf16[128,1024]{1,0:T(8,128)(2,1)S(1)} %shard_map.87.refs_0_), channel_id=1, source_target_pairs={{0,4},{2,6},{4,0},{6,2},{8,12},{10,14},{12,8},{14,10},{16,20},{18,... | collective-permute-start | bytes 786440 | tf_op jit(solution)/shard_map/ppermute | solution.py:34
  71.5 1.5 %shard_map.89.refs_0_ = bf16[512,512]{1,0:T(8,128)(2,1)S(1)} custom-call(s32[1]{0:T(128)} %bitcast.5.slot_ref, s32[1]{0:T(128)} %bitcast.6.half_ref, bf16[1,1024]{1,0:T(2,128)(2,1)} %gain_ref.7, bf16[128,4096]{1,0:T(8,128)(2,1)} %bitcast.24, bf16[128,1024]{1,0:T(8,128)(2,1)} %copy-done.7, bf16[128,1024]{1,0:T(8,128)(2,1)} %copy-done.6, ...), custom_call_target="tpu_custom_call" | custom-call | tf_op jit(solution)/shard_map/pallas_call | solution.py:185
  73.0 0.8 copy-done
  73.8 0.1 collective-permute-done.10.refs_3_
  73.9 16.2 %collective-permute-done.9.refs_2_ = bf16[128,1024]{1,0:T(8,128)(2,1)S(1)} collective-permute-done((bf16[128,1024]{1,0:T(8,128)(2,1)S(1)}, bf16[128,1024]{1,0:T(8,128)(2,1)S(1)}, u32[]{:S(2)}, u32[]{:S(2)}) %collective-permute-start.9) | collective-permute-done | bytes 262176 | tf_op jit(solution)/shard_map/ppermute | solution.py:34
  90.2 0.7 copy-done.20
  90.9 0.1 copy-done.21
  90.9 3.1 %shard_map.90 = (bf16[128,1024]{1,0:T(8,128)(2,1)S(1)}, bf16[128,1024]{1,0:T(8,128)(2,1)S(1)}, bf16[128,1024]{1,0:T(8,128)(2,1)S(1)}, bf16[128,1024]{1,0:T(8,128)(2,1)S(1)}, bf16[512,1024]{1,0:T(8,128)(2,1)S(1)}) custom-call(bf16[1024,1024]{1,0:T(8,128)(2,1)} %bitcast.25, bf16[1,1024]{1,0:T(2,128)(2,1)} %gain_ref.7, bf16[128,1024]{1,0:T(8,128)(2,1)} %copy-done.1, ...), custom_call_target="tpu_custom_call" | custom-call | tf_op jit(solution)/shard_map/pallas_call | solution.py:222
  94.1 0.0 copy-start.2
  94.1 0.6 collective-permute-start.12
  94.7 0.8 collective-permute-start.13
  95.4 2.8 %collective-permute-start.15 = (bf16[128,1024]{1,0:T(8,128)(2,1)S(1)}, bf16[128,1024]{1,0:T(8,128)(2,1)S(1)}, u32[]{:S(2)}, u32[]{:S(2)}) collective-permute-start(bf16[128,1024]{1,0:T(8,128)(2,1)S(1)} %get-tuple-element.62), channel_id=1, source_target_pairs={{0,28},{2,30},{4,24},{6,26},{8,4},{10,6},{12,0},{14,2},{16,12},{18... | collective-permute-start | bytes 786440 | tf_op jit(solution)/shard_map/ppermute | solution.py:34
  98.2 1.5 %collective-permute-start.16 = (bf16[128,1024]{1,0:T(8,128)(2,1)S(1)}, bf16[128,1024]{1,0:T(8,128)(2,1)S(1)}, u32[]{:S(2)}, u32[]{:S(2)}) collective-permute-start(bf16[128,1024]{1,0:T(8,128)(2,1)S(1)} %get-tuple-element.63), channel_id=1, source_target_pairs={{0,30},{2,28},{4,26},{6,24},{8,6},{10,4},{12,2},{14,0},{16,14},{18... | collective-permute-start | bytes 786440 | tf_op jit(solution)/shard_map/ppermute | solution.py:34
  99.8 19.5 %collective-permute-done.12.refs_3_ = bf16[512,1024]{1,0:T(8,128)(2,1)S(1)} collective-permute-done((bf16[512,1024]{1,0:T(8,128)(2,1)S(1)}, bf16[512,1024]{1,0:T(8,128)(2,1)S(1)}, u32[]{:S(2)}, u32[]{:S(2)}) %collective-permute-start.12) | collective-permute-done | bytes 1048608 | tf_op jit(solution)/shard_map/ppermute | solution.py:355
  119.2 1.0 copy-done.13
  120.2 4.3 %shard_map.91 = (bf16[512,1024]{1,0:T(8,128)(2,1)}, f32[1,512]{1,0:T(1,128)}) custom-call(s32[1]{0:T(128)} %bitcast.6.half_ref, bf16[1024,1024]{1,0:T(8,128)(2,1)} %bitcast.26, bf16[1,1024]{1,0:T(2,128)(2,1)} %gain_ref.7, bf16[512,512]{1,0:T(8,128)(2,1)} %copy-done, bf16[512,512]{1,0:T(8,128)(2,1)} %copy-done.14, bf16[512,1024]{1,0:T(8,128)(2,1)} %copy-done.2, ...), custom_call_target="tpu_custom_call" | custom-call | tf_op jit(solution)/shard_map/pallas_call | solution.py:257
  124.6 0.6 copy-done.15
  125.2 0.1 copy-done.16
  125.3 0.1 copy-done.17
  125.4 0.7 copy-done.19
  126.1 3.4 %shard_map.92 = bf16[128,4096]{1,0:T(8,128)(2,1)} custom-call(s32[1]{0:T(128)} %bitcast.5.slot_ref, bf16[128,4096]{1,0:T(8,128)(2,1)} %copy-done.12, bf16[128,4096]{1,0:T(8,128)(2,1)} %collective-permute-done.7.grad_ref, bf16[128,1024]{1,0:T(8,128)(2,1)} %copy-done.15, bf16[128,1024]{1,0:T(8,128)(2,1)} %copy-done.16, bf16[128,1024]{1,0:T(8,128)(2,1)} %copy-done.17, ...), custom_call_target="tpu_custom_call" | custom-call | tf_op jit(solution)/shard_map/pallas_call | solution.py:306
  (39 shorter events, 0.1 us)
Async XLA Ops:
  0.6 29.6 %collective-permute-start.3 = (bf16[128,4096]{1,0:T(8,128)(2,1)}, bf16[128,4096]{1,0:T(8,128)(2,1)S(1)}, u32[]{:S(2)}, u32[]{:S(2)}) collective-permute-start(bf16[128,4096]{1,0:T(8,128)(2,1)} %bitcast.18), channel_id=1, source_target_pairs={{0,24},{8,0},{16,8},{24,16},{1,25},{9,1},{17,9},{25,17},{2,26},{10... | collective-permute-start | bytes 3145736 | tf_op jit(solution)/shard_map/ppermute | solution.py:335
  4.5 11.2 %collective-permute-start.2 = (bf16[128,1024]{1,0:T(8,128)(2,1)S(1)}, bf16[128,1024]{1,0:T(8,128)(2,1)S(1)}, u32[]{:S(2)}, u32[]{:S(2)}) collective-permute-start(bf16[128,1024]{1,0:T(8,128)(2,1)S(1)} %get-tuple-element.65), channel_id=1, source_target_pairs={{0,6},{2,4},{4,2},{6,0},{8,14},{10,12},{12,10},{14,8},{16,22},{18,... | collective-permute-start | bytes 786440 | tf_op jit(solution)/shard_map/ppermute | solution.py:34
  8.2 22.1 %collective-permute-start.1 = (bf16[128,1024]{1,0:T(8,128)(2,1)S(1)}, bf16[128,1024]{1,0:T(8,128)(2,1)S(1)}, u32[]{:S(2)}, u32[]{:S(2)}) collective-permute-start(bf16[128,1024]{1,0:T(8,128)(2,1)S(1)} %get-tuple-element.66), channel_id=1, source_target_pairs={{0,4},{2,6},{4,0},{6,2},{8,12},{10,14},{12,8},{14,10},{16,20},{18,... | collective-permute-start | bytes 786440 | tf_op jit(solution)/shard_map/ppermute | solution.py:34
  8.2 22.1 %collective-permute-start = (bf16[128,1024]{1,0:T(8,128)(2,1)S(1)}, bf16[128,1024]{1,0:T(8,128)(2,1)S(1)}, u32[]{:S(2)}, u32[]{:S(2)}) collective-permute-start(bf16[128,1024]{1,0:T(8,128)(2,1)S(1)} %get-tuple-element.67), channel_id=1, source_target_pairs={{0,2},{2,0},{4,6},{6,4},{8,10},{10,8},{12,14},{14,12},{16,18},{18,... | collective-permute-start | bytes 786440 | tf_op jit(solution)/shard_map/ppermute | solution.py:34
  11.3 0.6 copy-start.4
  15.7 15.6 %copy-start.5 = (bf16[128,1024]{1,0:T(8,128)(2,1)}, bf16[128,1024]{1,0:T(8,128)(2,1)S(1)}, u32[]{:S(2)}) copy-start(bf16[128,1024]{1,0:T(8,128)(2,1)S(1)} %collective-permute-done.2.refs_3_.refs_2_) | copy-start | bytes 786436
  30.2 1.0 copy-start.6
  30.2 1.1 copy-start.7
  30.2 1.0 copy-start.12
  31.3 6.2 %copy-start.11 = (bf16[1,1,128,4096]{3,2,1,0:T(8,128)(2,1)S(1)}, bf16[1,1,128,4096]{3,2,1,0:T(8,128)(2,1)}, u32[]{:S(2)}) copy-start(bf16[1,1,128,4096]{3,2,1,0:T(8,128)(2,1)} %param.11) | copy-start | bytes 3145732
  36.8 0.7 copy-start.3
  37.5 22.2 %collective-permute-start.7 = (bf16[128,4096]{1,0:T(8,128)(2,1)S(1)}, bf16[128,4096]{1,0:T(8,128)(2,1)}, u32[]{:S(2)}, u32[]{:S(2)}) collective-permute-start(bf16[128,4096]{1,0:T(8,128)(2,1)S(1)} %bitcast.29), channel_id=1, source_target_pairs={{0,24},{8,0},{16,8},{24,16},{1,25},{9,1},{17,9},{25,17},{2,26},{10... | collective-permute-start | bytes 3145736 | tf_op jit(solution)/shard_map/ppermute | solution.py:341
  38.3 12.9 %collective-permute-start.4 = (bf16[128,1024]{1,0:T(8,128)(2,1)S(1)}, bf16[128,1024]{1,0:T(8,128)(2,1)S(1)}, u32[]{:S(2)}, u32[]{:S(2)}) collective-permute-start(bf16[128,1024]{1,0:T(8,128)(2,1)S(1)} %get-tuple-element.40), channel_id=1, source_target_pairs={{0,2},{2,0},{4,6},{6,4},{8,10},{10,8},{12,14},{14,12},{16,18},{18,... | collective-permute-start | bytes 786440 | tf_op jit(solution)/shard_map/ppermute | solution.py:34
  38.3 21.4 %collective-permute-start.5 = (bf16[128,1024]{1,0:T(8,128)(2,1)S(1)}, bf16[128,1024]{1,0:T(8,128)(2,1)S(1)}, u32[]{:S(2)}, u32[]{:S(2)}) collective-permute-start(bf16[128,1024]{1,0:T(8,128)(2,1)S(1)} %get-tuple-element.41), channel_id=1, source_target_pairs={{0,4},{2,6},{4,0},{6,2},{8,12},{10,14},{12,8},{14,10},{16,20},{18,... | collective-permute-start | bytes 786440 | tf_op jit(solution)/shard_map/ppermute | solution.py:34
  41.3 18.4 %collective-permute-start.6 = (bf16[128,1024]{1,0:T(8,128)(2,1)S(1)}, bf16[128,1024]{1,0:T(8,128)(2,1)S(1)}, u32[]{:S(2)}, u32[]{:S(2)}) collective-permute-start(bf16[128,1024]{1,0:T(8,128)(2,1)S(1)} %get-tuple-element.42), channel_id=1, source_target_pairs={{0,6},{2,4},{4,2},{6,0},{8,14},{10,12},{12,10},{14,8},{16,22},{18,... | collective-permute-start | bytes 786440 | tf_op jit(solution)/shard_map/ppermute | solution.py:34
  51.1 8.6 %copy-start.8 = (bf16[128,1024]{1,0:T(8,128)(2,1)}, bf16[128,1024]{1,0:T(8,128)(2,1)S(1)}, u32[]{:S(2)}) copy-start(bf16[128,1024]{1,0:T(8,128)(2,1)S(1)} %collective-permute-done.4.refs_0_.refs_3_) | copy-start | bytes 786436
  59.7 0.7 copy-start.9
  59.7 0.8 copy-start.10
  62.0 11.1 %copy-start.1 = (bf16[128,1024]{1,0:T(8,128)(2,1)}, bf16[128,1024]{1,0:T(8,128)(2,1)S(1)}, u32[]{:S(2)}) copy-start(bf16[128,1024]{1,0:T(8,128)(2,1)S(1)} %shard_map.87.refs_0_) | copy-start | bytes 786436
  63.6 26.6 %collective-permute-start.11 = (bf16[512,512]{1,0:T(8,128)(2,1)S(1)}, bf16[512,512]{1,0:T(8,128)(2,1)S(1)}, u32[]{:S(2)}, u32[]{:S(2)}) collective-permute-start(bf16[512,512]{1,0:T(8,128)(2,1)S(1)} %shard_map.88), channel_id=1, source_target_pairs={{0,1},{1,0},{2,3},{3,2},{4,5},{5,4},{6,7},{7,6},{8,9},{9,8},{10,11... | collective-permute-start | bytes 1572872 | tf_op jit(solution)/shard_map/ppermute | solution.py:350
  65.1 8.8 %collective-permute-start.10 = (bf16[128,1024]{1,0:T(8,128)(2,1)S(1)}, bf16[128,1024]{1,0:T(8,128)(2,1)S(1)}, u32[]{:S(2)}, u32[]{:S(2)}) collective-permute-start(bf16[128,1024]{1,0:T(8,128)(2,1)S(1)} %shard_map.87.refs_0_), channel_id=1, source_target_pairs={{0,6},{2,4},{4,2},{6,0},{8,14},{10,12},{12,10},{14,8},{16,22},{18,... | collective-permute-start | bytes 786440 | tf_op jit(solution)/shard_map/ppermute | solution.py:34
  67.5 22.7 %collective-permute-start.9 = (bf16[128,1024]{1,0:T(8,128)(2,1)S(1)}, bf16[128,1024]{1,0:T(8,128)(2,1)S(1)}, u32[]{:S(2)}, u32[]{:S(2)}) collective-permute-start(bf16[128,1024]{1,0:T(8,128)(2,1)S(1)} %shard_map.87.refs_0_), channel_id=1, source_target_pairs={{0,4},{2,6},{4,0},{6,2},{8,12},{10,14},{12,8},{14,10},{16,20},{18,... | collective-permute-start | bytes 786440 | tf_op jit(solution)/shard_map/ppermute | solution.py:34
  71.5 18.7 %collective-permute-start.8 = (bf16[128,1024]{1,0:T(8,128)(2,1)S(1)}, bf16[128,1024]{1,0:T(8,128)(2,1)S(1)}, u32[]{:S(2)}, u32[]{:S(2)}) collective-permute-start(bf16[128,1024]{1,0:T(8,128)(2,1)S(1)} %shard_map.87.refs_0_), channel_id=1, source_target_pairs={{0,2},{2,0},{4,6},{6,4},{8,10},{10,8},{12,14},{14,12},{16,18},{18,... | collective-permute-start | bytes 786440 | tf_op jit(solution)/shard_map/ppermute | solution.py:34
  73.0 0.8 copy-start
  73.9 16.3 %copy-start.18 = (bf16[128,1024]{1,0:T(8,128)(2,1)}, bf16[128,1024]{1,0:T(8,128)(2,1)S(1)}, u32[]{:S(2)}) copy-start(bf16[128,1024]{1,0:T(8,128)(2,1)S(1)} %collective-permute-done.10.refs_3_) | copy-start | bytes 786436
  90.2 0.7 copy-start.20
  90.2 0.8 copy-start.21
  90.2 29.1 %copy-start.14 = (bf16[512,512]{1,0:T(8,128)(2,1)}, bf16[512,512]{1,0:T(8,128)(2,1)S(1)}, u32[]{:S(2)}) copy-start(bf16[512,512]{1,0:T(8,128)(2,1)S(1)} %collective-permute-done.11.refs_1_) | copy-start | bytes 1572868
  94.1 25.2 %copy-start.2 = (bf16[512,1024]{1,0:T(8,128)(2,1)}, bf16[512,1024]{1,0:T(8,128)(2,1)S(1)}, u32[]{:S(2)}) copy-start(bf16[512,1024]{1,0:T(8,128)(2,1)S(1)} %get-tuple-element.55.refs_2_) | copy-start | bytes 3145732
  94.1 25.1 %collective-permute-start.12 = (bf16[512,1024]{1,0:T(8,128)(2,1)S(1)}, bf16[512,1024]{1,0:T(8,128)(2,1)S(1)}, u32[]{:S(2)}, u32[]{:S(2)}) collective-permute-start(bf16[512,1024]{1,0:T(8,128)(2,1)S(1)} %get-tuple-element.55.refs_2_), channel_id=1, source_target_pairs={{0,1},{1,0},{2,3},{3,2},{4,5},{5,4},{6,7},{7,6},{8,9},{9,8},{10,11... | collective-permute-start | bytes 3145736 | tf_op jit(solution)/shard_map/ppermute | solution.py:355
  94.7 29.8 %collective-permute-start.13 = (bf16[128,1024]{1,0:T(8,128)(2,1)S(1)}, bf16[128,1024]{1,0:T(8,128)(2,1)S(1)}, u32[]{:S(2)}, u32[]{:S(2)}) collective-permute-start(bf16[128,1024]{1,0:T(8,128)(2,1)S(1)} %get-tuple-element.60), channel_id=1, source_target_pairs={{0,24},{2,26},{4,28},{6,30},{8,0},{10,2},{12,4},{14,6},{16,8},{18,... | collective-permute-start | bytes 786440 | tf_op jit(solution)/shard_map/ppermute | solution.py:34
  95.4 29.1 %collective-permute-start.14 = (bf16[128,1024]{1,0:T(8,128)(2,1)S(1)}, bf16[128,1024]{1,0:T(8,128)(2,1)S(1)}, u32[]{:S(2)}, u32[]{:S(2)}) collective-permute-start(bf16[128,1024]{1,0:T(8,128)(2,1)S(1)} %get-tuple-element.61), channel_id=1, source_target_pairs={{0,26},{2,24},{4,30},{6,28},{8,2},{10,0},{12,6},{14,4},{16,10},{18... | collective-permute-start | bytes 786440 | tf_op jit(solution)/shard_map/ppermute | solution.py:34
  95.4 29.1 %collective-permute-start.15 = (bf16[128,1024]{1,0:T(8,128)(2,1)S(1)}, bf16[128,1024]{1,0:T(8,128)(2,1)S(1)}, u32[]{:S(2)}, u32[]{:S(2)}) collective-permute-start(bf16[128,1024]{1,0:T(8,128)(2,1)S(1)} %get-tuple-element.62), channel_id=1, source_target_pairs={{0,28},{2,30},{4,24},{6,26},{8,4},{10,6},{12,0},{14,2},{16,12},{18... | collective-permute-start | bytes 786440 | tf_op jit(solution)/shard_map/ppermute | solution.py:34
  98.2 26.3 %collective-permute-start.16 = (bf16[128,1024]{1,0:T(8,128)(2,1)S(1)}, bf16[128,1024]{1,0:T(8,128)(2,1)S(1)}, u32[]{:S(2)}, u32[]{:S(2)}) collective-permute-start(bf16[128,1024]{1,0:T(8,128)(2,1)S(1)} %get-tuple-element.63), channel_id=1, source_target_pairs={{0,30},{2,28},{4,26},{6,24},{8,6},{10,4},{12,2},{14,0},{16,14},{18... | collective-permute-start | bytes 786440 | tf_op jit(solution)/shard_map/ppermute | solution.py:34
  119.2 1.0 copy-start.13
  124.5 0.7 copy-start.15
  124.5 0.8 copy-start.16
  124.5 0.9 copy-start.17
  125.4 0.7 copy-start.19

commit v4 on v3

--- a/solution.py
+++ b/solution.py
@@ -112,7 +112,7 @@
         ),
         out_shape=[jax.ShapeDtypeStruct((rows, kv_width), jnp.bfloat16)] * count,
         compiler_params=pltpu.CompilerParams(vmem_limit_bytes=(24 + 2 * count) * MIB),
-    )(slot, *in_hbm(queries, grads, *key_blocks, *[x] * (count - 1)))
+    )(slot, *in_hbm(queries, grads, key_blocks[0]), *key_blocks[1:], *in_hbm(*[x] * (count - 1)))
 
 
 def rms_kernel(x_ref, out_ref):
@@ -154,7 +154,7 @@
         out_specs=line,
         out_shape=jax.ShapeDtypeStruct((rows, width), jnp.bfloat16),
         compiler_params=PARAMS,
-    )(slot, *in_hbm(inv_rms, own_term, *received))
+    )(slot, inv_rms, own_term, *received)
 
 
 def column_kernel(count, slot_ref, half_ref, gain_ref, own_ref, *refs):
@@ -193,7 +193,7 @@
         ),
         out_shape=jax.ShapeDtypeStruct((width, count * rows), jnp.bfloat16),
         compiler_params=PARAMS,
-    )(slot, half, *in_hbm(gain, x, *first, *second))
+    )(slot, half, *in_hbm(gain, x), *first, *second)
 
 
 def feature_kernel(count, weight_ref, gain_ref, *refs):
@@ -231,7 +231,7 @@
         out_shape=[jax.ShapeDtypeStruct((rows, width), jnp.bfloat16)] * count
         + [jax.ShapeDtypeStruct((count * rows, kv_width), jnp.bfloat16)],
         compiler_params=PARAMS,
-    )(*in_hbm(weight, gain, *values))
+    )(*in_hbm(weight, gain), *values)
     return out[:count], out[count]
 
 
@@ -275,7 +275,7 @@
             jax.ShapeDtypeStruct((1, width), jnp.float32),
         ],
         compiler_params=PARAMS,
-    )(half, *in_hbm(weight, gain, *normed, *blocks))
+    )(half, *in_hbm(weight, gain), *normed, *blocks)
 
 
 def input_kernel(count, slot_ref, x_ref, grad_ref, *refs):
@@ -311,7 +311,7 @@
         out_specs=wide,
         out_shape=jax.ShapeDtypeStruct((rows, width), jnp.bfloat16),
         compiler_params=PARAMS,
-    )(slot, *in_hbm(x, grads, *scaled))
+    )(slot, x, grads, *scaled)
 
 
 def per_device(section_inputs, queries, keys, w_value, gain, section_grads_in):
@@ -337,7 +337,7 @@
     first, next_x, inv_rms, slot = after((first, next_x, inv_rms, slot), ())
     terms = attention(slot, queries[0, 0], cotangent, [own_keys] + first, x)
 
-    second = [to_partner(terms[m], m) for m in masks]
+    second = [to_partner(terms[m], m) for m in reversed(masks)][::-1]
     next_grad = lax.ppermute(after(cotangent, terms), "section", section_route(-1))
     second, next_grad = after((second, next_grad), ())
     value = value_grad(slot, inv_rms, terms[0], second)
@@ -353,7 +353,7 @@
 
     scaled, all_values = feature_grads(weight, gain, values)
     other_values = lax.ppermute(all_values, "dp", swap)
-    returned = [to_partner(scaled[m], m, below=True) for m in range(count)]
+    returned = [to_partner(scaled[m], m, below=True) for m in reversed(range(count))][::-1]
 
     weight_out, gain_out = weight_grad(half, weight, gain, normed, [[all_values], [other_values]])
     slot = after(slot, weight_out)

time: 130 us -> 120 us (0.923)
  the two profiles are of different devices: /device:TPU:0 before, /device:TPU:9 now
where the time goes in v4:
time: 120 us; the launch traced here: 118 us
  waiting for transfers between devices  73.1 us (61%)
  starting transfers between devices  22.5 us (19%)
  Pallas kernels  20.2 us (17%)
  other arithmetic  1.42 us (1%)
    ppermute x13, waiting for transfers between devices, to_partner(): return lax.ppermute(block, ('section', 'fsdp'), route)  56.3 us
    ppermute x13, starting transfers between devices, to_partner(): return lax.ppermute(block, ('section', 'fsdp'), route)  18.5 us
    ppermute x1, waiting for transfers between devices, per_device(): other_values = lax.ppermute(all_values, 'dp', swap)  16.8 us
    pallas_call x1, Pallas kernels, attention(): pl.pallas_call(functools.partial(attention_kernel, count, group, heads, x...  5.81 us
    pallas_call x1, Pallas kernels, weight_grad(): pl.pallas_call(functools.partial(weight_kernel, docs), grid_spec=pltpu.Pr...  3.41 us
    pallas_call x1, Pallas kernels, input_grad(): pl.pallas_call(functools.partial(input_kernel, count), grid=(rows // step...  3.08 us
    pallas_call x1, Pallas kernels, feature_grads(): pl.pallas_call(functools.partial(feature_kernel, count), grid=(width // s...  2.89 us
    pallas_call x2, Pallas kernels, gained_columns(): pl.pallas_call(functools.partial(column_kernel, count), grid_spec=pltpu.P...  2.44 us
  transfers between devices with their start and end apart: 17, of which 9 were waited for; matrix products, arithmetic and copies ran while one was open for 1% of the time, Pallas kernels for 6%

profile of v4, /device:TPU:9, one launch (start us, length us, event | category | flops | bytes accessed | tf_op | source)
XLA Modules:
  0.0 117.9 jit_solution(14994310723418163885)
XLA Ops:
  0.6 0.7 collective-permute-start.3
  1.4 1.4 %bitcast_select_fusion = (bf16[128,1024]{1,0:T(8,128)(2,1)S(1)}, bf16[128,1024]{1,0:T(8,128)(2,1)S(1)}, bf16[128,1024]{1,0:T(8,128)(2,1)S(1)}) fusion(bf16[1,1,128,4096]{3,2,1,0:T(8,128)(2,1)} %param.6, s32[]{:T(128)S(6)} %select_n.36, pred[]{:T(512)S(6)} %gt.11, bf16[1,1,128,1024]{3,2,1,0:T(8,128)(2,1)} %param.8, s32[]{:T(128)S(6)} %select_n.33, pred[]{:T(512)S(6)} %gt.10, ...), kind=kLoop, calls=%fused_computation | loop fusion | flops 393216 | bytes 1835023 | tf_op jit(solution)/shard_map/jit(_where)/select_n | solution.py:334
  2.8 1.4 %collective-permute-start.2 = (bf16[128,1024]{1,0:T(8,128)(2,1)S(1)}, bf16[128,1024]{1,0:T(8,128)(2,1)S(1)}, u32[]{:S(2)}, u32[]{:S(2)}) collective-permute-start(bf16[128,1024]{1,0:T(8,128)(2,1)S(1)} %get-tuple-element.65), channel_id=1, source_target_pairs={{0,6},{2,4},{4,2},{6,0},{8,14},{10,12},{12,10},{14,8},{16,22},{18,... | collective-permute-start | bytes 786440 | tf_op jit(solution)/shard_map/ppermute | solution.py:34
  4.1 1.1 collective-permute-start.1
  5.2 1.1 collective-permute-start
  6.3 2.4 %shard_map.85.rms_ref = f32[128,128]{1,0:T(8,128)S(1)} custom-call(bf16[128,4096]{1,0:T(8,128)(2,1)} %bitcast.19), custom_call_target="tpu_custom_call" | custom-call | tf_op jit(solution)/shard_map/pallas_call | solution.py:127
  8.7 12.7 %collective-permute-done.2.refs_3_.refs_2_ = bf16[128,1024]{1,0:T(8,128)(2,1)S(1)} collective-permute-done((bf16[128,1024]{1,0:T(8,128)(2,1)S(1)}, bf16[128,1024]{1,0:T(8,128)(2,1)S(1)}, u32[]{:S(2)}, u32[]{:S(2)}) %collective-permute-start.2) | collective-permute-done | bytes 262176 | tf_op jit(solution)/shard_map/ppermute | solution.py:34
  21.4 4.3 %collective-permute-done.1.refs_2_.refs_1_ = bf16[128,1024]{1,0:T(8,128)(2,1)S(1)} collective-permute-done((bf16[128,1024]{1,0:T(8,128)(2,1)S(1)}, bf16[128,1024]{1,0:T(8,128)(2,1)S(1)}, u32[]{:S(2)}, u32[]{:S(2)}) %collective-permute-start.1) | collective-permute-done | bytes 262176 | tf_op jit(solution)/shard_map/ppermute | solution.py:34
  25.7 0.0 collective-permute-done.refs_1_.refs_0_
  25.7 0.0 collective-permute-done.3.x_ref
  25.7 5.8 %shard_map.86 = (bf16[128,1024]{1,0:T(8,128)(2,1)S(1)}, bf16[128,1024]{1,0:T(8,128)(2,1)}, bf16[128,1024]{1,0:T(8,128)(2,1)S(1)}, bf16[128,1024]{1,0:T(8,128)(2,1)S(1)}) custom-call(s32[1]{0:T(128)} %bitcast.5.slot_ref, bf16[128,4096]{1,0:T(8,128)(2,1)} %bitcast.27, bf16[128,4096]{1,0:T(8,128)(2,1)} %bitcast.9.grad_ref, bf16[128,1024]{1,0:T(8,128)(2,1)} %bitcast.29, ...), custom_call_target="tpu_custom_call" | custom-call | tf_op jit(solution)/shard_map/pallas_call | solution.py:105
  31.5 1.8 %collective-permute-start.7 = (bf16[128,4096]{1,0:T(8,128)(2,1)}, bf16[128,4096]{1,0:T(8,128)(2,1)}, u32[]{:S(2)}, u32[]{:S(2)}) collective-permute-start(bf16[128,4096]{1,0:T(8,128)(2,1)} %bitcast.9.grad_ref), channel_id=1, source_target_pairs={{0,24},{8,0},{16,8},{24,16},{1,25},{9,1},{17,9},{25,17},{2,26},{10... | collective-permute-start | bytes 3145736 | tf_op jit(solution)/shard_map/ppermute | solution.py:341
  33.3 2.1 %collective-permute-start.4 = (bf16[128,1024]{1,0:T(8,128)(2,1)}, bf16[128,1024]{1,0:T(8,128)(2,1)S(1)}, u32[]{:S(2)}, u32[]{:S(2)}) collective-permute-start(bf16[128,1024]{1,0:T(8,128)(2,1)} %get-tuple-element.40), channel_id=1, source_target_pairs={{0,2},{2,0},{4,6},{6,4},{8,10},{10,8},{12,14},{14,12},{16,18},{18,... | collective-permute-start | bytes 786440 | tf_op jit(solution)/shard_map/ppermute | solution.py:34
  35.4 1.0 collective-permute-start.5
  36.4 0.3 collective-permute-start.6
  36.7 9.3 %collective-permute-done.4.refs_0_.refs_3_ = bf16[128,1024]{1,0:T(8,128)(2,1)S(1)} collective-permute-done((bf16[128,1024]{1,0:T(8,128)(2,1)}, bf16[128,1024]{1,0:T(8,128)(2,1)S(1)}, u32[]{:S(2)}, u32[]{:S(2)}) %collective-permute-start.4) | collective-permute-done | bytes 262176 | tf_op jit(solution)/shard_map/ppermute | solution.py:34
  46.0 2.2 %collective-permute-done.5.refs_1_.refs_4_ = bf16[128,1024]{1,0:T(8,128)(2,1)S(1)} collective-permute-done((bf16[128,1024]{1,0:T(8,128)(2,1)S(1)}, bf16[128,1024]{1,0:T(8,128)(2,1)S(1)}, u32[]{:S(2)}, u32[]{:S(2)}) %collective-permute-start.5) | collective-permute-done | bytes 262176 | tf_op jit(solution)/shard_map/ppermute | solution.py:34
  48.2 11.0 %collective-permute-done.6.refs_2_.refs_5_ = bf16[128,1024]{1,0:T(8,128)(2,1)S(1)} collective-permute-done((bf16[128,1024]{1,0:T(8,128)(2,1)S(1)}, bf16[128,1024]{1,0:T(8,128)(2,1)S(1)}, u32[]{:S(2)}, u32[]{:S(2)}) %collective-permute-start.6) | collective-permute-done | bytes 262176 | tf_op jit(solution)/shard_map/ppermute | solution.py:34
  59.2 0.0 collective-permute-done.7.grad_ref
  59.2 0.2 shard_map.87.refs_0_
  59.5 1.2 %shard_map.88 = bf16[512,512]{1,0:T(8,128)(2,1)S(1)} custom-call(s32[1]{0:T(128)} %bitcast.5.slot_ref, s32[1]{0:T(128)S(6)} %sub.3.half_ref, bf16[1,1024]{1,0:T(2,128)(2,1)} %gain_ref.7, bf16[128,4096]{1,0:T(8,128)(2,1)} %bitcast.23, bf16[128,1024]{1,0:T(8,128)(2,1)S(1)} %collective-permute-done.refs_1_.refs_0_, ...), custom_call_target="tpu_custom_call" | custom-call | tf_op jit(solution)/shard_map/pallas_call | solution.py:185
  60.7 1.3 %collective-permute-start.11 = (bf16[512,512]{1,0:T(8,128)(2,1)S(1)}, bf16[512,512]{1,0:T(8,128)(2,1)S(1)}, u32[]{:S(2)}, u32[]{:S(2)}) collective-permute-start(bf16[512,512]{1,0:T(8,128)(2,1)S(1)} %shard_map.88), channel_id=1, source_target_pairs={{0,1},{1,0},{2,3},{3,2},{4,5},{5,4},{6,7},{7,6},{8,9},{9,8},{10,11... | collective-permute-start | bytes 1572872 | tf_op jit(solution)/shard_map/ppermute | solution.py:350
  62.0 4.0 %collective-permute-start.10 = (bf16[128,1024]{1,0:T(8,128)(2,1)S(1)}, bf16[128,1024]{1,0:T(8,128)(2,1)S(1)}, u32[]{:S(2)}, u32[]{:S(2)}) collective-permute-start(bf16[128,1024]{1,0:T(8,128)(2,1)S(1)} %shard_map.87.refs_0_), channel_id=1, source_target_pairs={{0,6},{2,4},{4,2},{6,0},{8,14},{10,12},{12,10},{14,8},{16,22},{18,... | collective-permute-start | bytes 786440 | tf_op jit(solution)/shard_map/ppermute | solution.py:34
  66.0 0.0 collective-permute-start.9
  66.0 1.2 %collective-permute-start.8 = (bf16[128,1024]{1,0:T(8,128)(2,1)S(1)}, bf16[128,1024]{1,0:T(8,128)(2,1)S(1)}, u32[]{:S(2)}, u32[]{:S(2)}) collective-permute-start(bf16[128,1024]{1,0:T(8,128)(2,1)S(1)} %shard_map.87.refs_0_), channel_id=1, source_target_pairs={{0,2},{2,0},{4,6},{6,4},{8,10},{10,8},{12,14},{14,12},{16,18},{18,... | collective-permute-start | bytes 786440 | tf_op jit(solution)/shard_map/ppermute | solution.py:34
  67.2 1.2 %shard_map.89.refs_0_ = bf16[512,512]{1,0:T(8,128)(2,1)S(1)} custom-call(s32[1]{0:T(128)} %bitcast.5.slot_ref, s32[1]{0:T(128)} %bitcast.6.half_ref, bf16[1,1024]{1,0:T(2,128)(2,1)} %gain_ref.7, bf16[128,4096]{1,0:T(8,128)(2,1)} %bitcast.24, bf16[128,1024]{1,0:T(8,128)(2,1)S(1)} %collective-permute-done.refs_1_.refs_0_, ...), custom_call_target="tpu_custom_call" | custom-call | tf_op jit(solution)/shard_map/pallas_call | solution.py:185
  68.4 8.1 %collective-permute-done.10.refs_3_ = bf16[128,1024]{1,0:T(8,128)(2,1)S(1)} collective-permute-done((bf16[128,1024]{1,0:T(8,128)(2,1)S(1)}, bf16[128,1024]{1,0:T(8,128)(2,1)S(1)}, u32[]{:S(2)}, u32[]{:S(2)}) %collective-permute-start.10) | collective-permute-done | bytes 262176 | tf_op jit(solution)/shard_map/ppermute | solution.py:34
  76.6 5.8 %collective-permute-done.9.refs_2_ = bf16[128,1024]{1,0:T(8,128)(2,1)S(1)} collective-permute-done((bf16[128,1024]{1,0:T(8,128)(2,1)S(1)}, bf16[128,1024]{1,0:T(8,128)(2,1)S(1)}, u32[]{:S(2)}, u32[]{:S(2)}) %collective-permute-start.9) | collective-permute-done | bytes 262176 | tf_op jit(solution)/shard_map/ppermute | solution.py:34
  82.3 0.0 collective-permute-done.8.refs_1_
  82.3 0.0 collective-permute-done.11.refs_1_
  82.3 2.9 %shard_map.90 = (bf16[128,1024]{1,0:T(8,128)(2,1)S(1)}, bf16[128,1024]{1,0:T(8,128)(2,1)S(1)}, bf16[128,1024]{1,0:T(8,128)(2,1)S(1)}, bf16[128,1024]{1,0:T(8,128)(2,1)S(1)}, bf16[512,1024]{1,0:T(8,128)(2,1)S(1)}) custom-call(bf16[1024,1024]{1,0:T(8,128)(2,1)} %bitcast.25, bf16[1,1024]{1,0:T(2,128)(2,1)} %gain_ref.7, ...), custom_call_target="tpu_custom_call" | custom-call | tf_op jit(solution)/shard_map/pallas_call | solution.py:222
  85.2 0.1 collective-permute-start.12
  85.3 1.8 %collective-permute-start.13 = (bf16[128,1024]{1,0:T(8,128)(2,1)S(1)}, bf16[128,1024]{1,0:T(8,128)(2,1)S(1)}, u32[]{:S(2)}, u32[]{:S(2)}) collective-permute-start(bf16[128,1024]{1,0:T(8,128)(2,1)S(1)} %get-tuple-element.60), channel_id=1, source_target_pairs={{0,24},{2,26},{4,28},{6,30},{8,0},{10,2},{12,4},{14,6},{16,8},{18,... | collective-permute-start | bytes 786440 | tf_op jit(solution)/shard_map/ppermute | solution.py:34
  87.1 2.9 %collective-permute-start.14 = (bf16[128,1024]{1,0:T(8,128)(2,1)S(1)}, bf16[128,1024]{1,0:T(8,128)(2,1)S(1)}, u32[]{:S(2)}, u32[]{:S(2)}) collective-permute-start(bf16[128,1024]{1,0:T(8,128)(2,1)S(1)} %get-tuple-element.61), channel_id=1, source_target_pairs={{0,26},{2,24},{4,30},{6,28},{8,2},{10,0},{12,6},{14,4},{16,10},{18... | collective-permute-start | bytes 786440 | tf_op jit(solution)/shard_map/ppermute | solution.py:34
  90.1 0.7 collective-permute-start.15
  90.7 1.0 collective-permute-start.16
  91.7 16.8 %collective-permute-done.12.refs_3_ = bf16[512,1024]{1,0:T(8,128)(2,1)S(1)} collective-permute-done((bf16[512,1024]{1,0:T(8,128)(2,1)S(1)}, bf16[512,1024]{1,0:T(8,128)(2,1)S(1)}, u32[]{:S(2)}, u32[]{:S(2)}) %collective-permute-start.12) | collective-permute-done | bytes 1048608 | tf_op jit(solution)/shard_map/ppermute | solution.py:355
  108.5 3.4 %shard_map.91 = (bf16[512,1024]{1,0:T(8,128)(2,1)}, f32[1,512]{1,0:T(1,128)}) custom-call(s32[1]{0:T(128)} %bitcast.6.half_ref, bf16[1024,1024]{1,0:T(8,128)(2,1)} %bitcast.26, bf16[1,1024]{1,0:T(2,128)(2,1)} %gain_ref.7, bf16[512,512]{1,0:T(8,128)(2,1)S(1)} %shard_map.89.refs_0_, bf16[512,512]{1,0:T(8,128)(2,1)S(1)} %collective-permute-done.11.refs_1_, ...), custom_call_target="tpu_custom_call" | custom-call | tf_op jit(solution)/shard_map/pallas_call | solution.py:257
  111.9 0.0 collective-permute-done.13.refs_0_
  111.9 0.0 collective-permute-done.14.refs_1_
  111.9 0.0 collective-permute-done.15.refs_2_
  111.9 2.9 %collective-permute-done.16.refs_3_ = bf16[128,1024]{1,0:T(8,128)(2,1)S(1)} collective-permute-done((bf16[128,1024]{1,0:T(8,128)(2,1)S(1)}, bf16[128,1024]{1,0:T(8,128)(2,1)S(1)}, u32[]{:S(2)}, u32[]{:S(2)}) %collective-permute-start.16) | collective-permute-done | bytes 262176 | tf_op jit(solution)/shard_map/ppermute | solution.py:34
  114.8 3.1 %shard_map.92 = bf16[128,4096]{1,0:T(8,128)(2,1)} custom-call(s32[1]{0:T(128)} %bitcast.5.slot_ref, bf16[128,4096]{1,0:T(8,128)(2,1)S(1)} %collective-permute-done.3.x_ref, bf16[128,4096]{1,0:T(8,128)(2,1)} %collective-permute-done.7.grad_ref, bf16[128,1024]{1,0:T(8,128)(2,1)S(1)} %collective-permute-done.13.refs_0_, ...), custom_call_target="tpu_custom_call" | custom-call | tf_op jit(solution)/shard_map/pallas_call | solution.py:306
Async XLA Ops:
  0.6 25.1 %collective-permute-start.3 = (bf16[128,4096]{1,0:T(8,128)(2,1)}, bf16[128,4096]{1,0:T(8,128)(2,1)S(1)}, u32[]{:S(2)}, u32[]{:S(2)}) collective-permute-start(bf16[128,4096]{1,0:T(8,128)(2,1)} %bitcast.18), channel_id=1, source_target_pairs={{0,24},{8,0},{16,8},{24,16},{1,25},{9,1},{17,9},{25,17},{2,26},{10... | collective-permute-start | bytes 3145736 | tf_op jit(solution)/shard_map/ppermute | solution.py:335
  2.8 18.6 %collective-permute-start.2 = (bf16[128,1024]{1,0:T(8,128)(2,1)S(1)}, bf16[128,1024]{1,0:T(8,128)(2,1)S(1)}, u32[]{:S(2)}, u32[]{:S(2)}) collective-permute-start(bf16[128,1024]{1,0:T(8,128)(2,1)S(1)} %get-tuple-element.65), channel_id=1, source_target_pairs={{0,6},{2,4},{4,2},{6,0},{8,14},{10,12},{12,10},{14,8},{16,22},{18,... | collective-permute-start | bytes 786440 | tf_op jit(solution)/shard_map/ppermute | solution.py:34
  4.1 21.5 %collective-permute-start.1 = (bf16[128,1024]{1,0:T(8,128)(2,1)S(1)}, bf16[128,1024]{1,0:T(8,128)(2,1)S(1)}, u32[]{:S(2)}, u32[]{:S(2)}) collective-permute-start(bf16[128,1024]{1,0:T(8,128)(2,1)S(1)} %get-tuple-element.66), channel_id=1, source_target_pairs={{0,4},{2,6},{4,0},{6,2},{8,12},{10,14},{12,8},{14,10},{16,20},{18,... | collective-permute-start | bytes 786440 | tf_op jit(solution)/shard_map/ppermute | solution.py:34
  5.2 20.4 %collective-permute-start = (bf16[128,1024]{1,0:T(8,128)(2,1)S(1)}, bf16[128,1024]{1,0:T(8,128)(2,1)S(1)}, u32[]{:S(2)}, u32[]{:S(2)}) collective-permute-start(bf16[128,1024]{1,0:T(8,128)(2,1)S(1)} %get-tuple-element.67), channel_id=1, source_target_pairs={{0,2},{2,0},{4,6},{6,4},{8,10},{10,8},{12,14},{14,12},{16,18},{18,... | collective-permute-start | bytes 786440 | tf_op jit(solution)/shard_map/ppermute | solution.py:34
  31.5 27.7 %collective-permute-start.7 = (bf16[128,4096]{1,0:T(8,128)(2,1)}, bf16[128,4096]{1,0:T(8,128)(2,1)}, u32[]{:S(2)}, u32[]{:S(2)}) collective-permute-start(bf16[128,4096]{1,0:T(8,128)(2,1)} %bitcast.9.grad_ref), channel_id=1, source_target_pairs={{0,24},{8,0},{16,8},{24,16},{1,25},{9,1},{17,9},{25,17},{2,26},{10... | collective-permute-start | bytes 3145736 | tf_op jit(solution)/shard_map/ppermute | solution.py:341
  33.3 12.6 %collective-permute-start.4 = (bf16[128,1024]{1,0:T(8,128)(2,1)}, bf16[128,1024]{1,0:T(8,128)(2,1)S(1)}, u32[]{:S(2)}, u32[]{:S(2)}) collective-permute-start(bf16[128,1024]{1,0:T(8,128)(2,1)} %get-tuple-element.40), channel_id=1, source_target_pairs={{0,2},{2,0},{4,6},{6,4},{8,10},{10,8},{12,14},{14,12},{16,18},{18,... | collective-permute-start | bytes 786440 | tf_op jit(solution)/shard_map/ppermute | solution.py:34
  35.4 12.8 %collective-permute-start.5 = (bf16[128,1024]{1,0:T(8,128)(2,1)S(1)}, bf16[128,1024]{1,0:T(8,128)(2,1)S(1)}, u32[]{:S(2)}, u32[]{:S(2)}) collective-permute-start(bf16[128,1024]{1,0:T(8,128)(2,1)S(1)} %get-tuple-element.41), channel_id=1, source_target_pairs={{0,4},{2,6},{4,0},{6,2},{8,12},{10,14},{12,8},{14,10},{16,20},{18,... | collective-permute-start | bytes 786440 | tf_op jit(solution)/shard_map/ppermute | solution.py:34
  36.4 22.8 %collective-permute-start.6 = (bf16[128,1024]{1,0:T(8,128)(2,1)S(1)}, bf16[128,1024]{1,0:T(8,128)(2,1)S(1)}, u32[]{:S(2)}, u32[]{:S(2)}) collective-permute-start(bf16[128,1024]{1,0:T(8,128)(2,1)S(1)} %get-tuple-element.42), channel_id=1, source_target_pairs={{0,6},{2,4},{4,2},{6,0},{8,14},{10,12},{12,10},{14,8},{16,22},{18,... | collective-permute-start | bytes 786440 | tf_op jit(solution)/shard_map/ppermute | solution.py:34
  60.7 21.6 %collective-permute-start.11 = (bf16[512,512]{1,0:T(8,128)(2,1)S(1)}, bf16[512,512]{1,0:T(8,128)(2,1)S(1)}, u32[]{:S(2)}, u32[]{:S(2)}) collective-permute-start(bf16[512,512]{1,0:T(8,128)(2,1)S(1)} %shard_map.88), channel_id=1, source_target_pairs={{0,1},{1,0},{2,3},{3,2},{4,5},{5,4},{6,7},{7,6},{8,9},{9,8},{10,11... | collective-permute-start | bytes 1572872 | tf_op jit(solution)/shard_map/ppermute | solution.py:350
  62.0 14.5 %collective-permute-start.10 = (bf16[128,1024]{1,0:T(8,128)(2,1)S(1)}, bf16[128,1024]{1,0:T(8,128)(2,1)S(1)}, u32[]{:S(2)}, u32[]{:S(2)}) collective-permute-start(bf16[128,1024]{1,0:T(8,128)(2,1)S(1)} %shard_map.87.refs_0_), channel_id=1, source_target_pairs={{0,6},{2,4},{4,2},{6,0},{8,14},{10,12},{12,10},{14,8},{16,22},{18,... | collective-permute-start | bytes 786440 | tf_op jit(solution)/shard_map/ppermute | solution.py:34
  66.0 16.3 %collective-permute-start.9 = (bf16[128,1024]{1,0:T(8,128)(2,1)S(1)}, bf16[128,1024]{1,0:T(8,128)(2,1)S(1)}, u32[]{:S(2)}, u32[]{:S(2)}) collective-permute-start(bf16[128,1024]{1,0:T(8,128)(2,1)S(1)} %shard_map.87.refs_0_), channel_id=1, source_target_pairs={{0,4},{2,6},{4,0},{6,2},{8,12},{10,14},{12,8},{14,10},{16,20},{18,... | collective-permute-start | bytes 786440 | tf_op jit(solution)/shard_map/ppermute | solution.py:34
  66.0 16.3 %collective-permute-start.8 = (bf16[128,1024]{1,0:T(8,128)(2,1)S(1)}, bf16[128,1024]{1,0:T(8,128)(2,1)S(1)}, u32[]{:S(2)}, u32[]{:S(2)}) collective-permute-start(bf16[128,1024]{1,0:T(8,128)(2,1)S(1)} %shard_map.87.refs_0_), channel_id=1, source_target_pairs={{0,2},{2,0},{4,6},{6,4},{8,10},{10,8},{12,14},{14,12},{16,18},{18,... | collective-permute-start | bytes 786440 | tf_op jit(solution)/shard_map/ppermute | solution.py:34
  85.2 23.3 %collective-permute-start.12 = (bf16[512,1024]{1,0:T(8,128)(2,1)S(1)}, bf16[512,1024]{1,0:T(8,128)(2,1)S(1)}, u32[]{:S(2)}, u32[]{:S(2)}) collective-permute-start(bf16[512,1024]{1,0:T(8,128)(2,1)S(1)} %get-tuple-element.55.refs_2_), channel_id=1, source_target_pairs={{0,1},{1,0},{2,3},{3,2},{4,5},{5,4},{6,7},{7,6},{8,9},{9,8},{10,11... | collective-permute-start | bytes 3145736 | tf_op jit(solution)/shard_map/ppermute | solution.py:355
  85.3 26.6 %collective-permute-start.13 = (bf16[128,1024]{1,0:T(8,128)(2,1)S(1)}, bf16[128,1024]{1,0:T(8,128)(2,1)S(1)}, u32[]{:S(2)}, u32[]{:S(2)}) collective-permute-start(bf16[128,1024]{1,0:T(8,128)(2,1)S(1)} %get-tuple-element.60), channel_id=1, source_target_pairs={{0,24},{2,26},{4,28},{6,30},{8,0},{10,2},{12,4},{14,6},{16,8},{18,... | collective-permute-start | bytes 786440 | tf_op jit(solution)/shard_map/ppermute | solution.py:34
  87.1 24.8 %collective-permute-start.14 = (bf16[128,1024]{1,0:T(8,128)(2,1)S(1)}, bf16[128,1024]{1,0:T(8,128)(2,1)S(1)}, u32[]{:S(2)}, u32[]{:S(2)}) collective-permute-start(bf16[128,1024]{1,0:T(8,128)(2,1)S(1)} %get-tuple-element.61), channel_id=1, source_target_pairs={{0,26},{2,24},{4,30},{6,28},{8,2},{10,0},{12,6},{14,4},{16,10},{18... | collective-permute-start | bytes 786440 | tf_op jit(solution)/shard_map/ppermute | solution.py:34
  90.1 21.9 %collective-permute-start.15 = (bf16[128,1024]{1,0:T(8,128)(2,1)S(1)}, bf16[128,1024]{1,0:T(8,128)(2,1)S(1)}, u32[]{:S(2)}, u32[]{:S(2)}) collective-permute-start(bf16[128,1024]{1,0:T(8,128)(2,1)S(1)} %get-tuple-element.62), channel_id=1, source_target_pairs={{0,28},{2,30},{4,24},{6,26},{8,4},{10,6},{12,0},{14,2},{16,12},{18... | collective-permute-start | bytes 786440 | tf_op jit(solution)/shard_map/ppermute | solution.py:34
  90.7 24.1 %collective-permute-start.16 = (bf16[128,1024]{1,0:T(8,128)(2,1)S(1)}, bf16[128,1024]{1,0:T(8,128)(2,1)S(1)}, u32[]{:S(2)}, u32[]{:S(2)}) collective-permute-start(bf16[128,1024]{1,0:T(8,128)(2,1)S(1)} %get-tuple-element.63), channel_id=1, source_target_pairs={{0,30},{2,28},{4,26},{6,24},{8,6},{10,4},{12,2},{14,0},{16,14},{18... | collective-permute-start | bytes 786440 | tf_op jit(solution)/shard_map/ppermute | solution.py:34

commit v5 on v4

--- a/solution.py
+++ b/solution.py
@@ -48,7 +48,8 @@
 
 
 def attention_kernel(count, group, heads, x_steps, slot_ref, query_ref, grad_ref, *refs):
-    key_refs, x_refs, out_refs = refs[:count], refs[count : -count], refs[-count:]
+    key_refs, x_refs = refs[:count], refs[count : 2 * count - 1]
+    out_refs, kept_refs = refs[2 * count - 1 : 3 * count - 1], refs[3 * count - 1 :]
     rows = query_ref.shape[0]
     slot = slot_ref[0]
     key_at = lax.broadcasted_iota(jnp.int32, (rows, rows), 0)
@@ -78,6 +79,7 @@
         for m in range(count):
             out_refs[m][:, own] = values[m * rows : (m + 1) * rows].astype(jnp.bfloat16)
     for m in range(1, count):
+        kept_refs[m - 1][...] = key_refs[m][...]
 
         @pl.when((slot ^ m > slot) & (pl.program_id(0) < x_steps))
         def _():
@@ -102,17 +104,19 @@
         )
         for m in range(1, count)
     ]
-    return pl.pallas_call(
+    out = pl.pallas_call(
         functools.partial(attention_kernel, count, group, heads, x_steps),
         grid_spec=pltpu.PrefetchScalarGridSpec(
             num_scalar_prefetch=1,
             grid=(kv_width // width,),
             in_specs=[wide, wide] + [narrow] * count + columns,
-            out_specs=[narrow] * count,
+            out_specs=[narrow] * (2 * count - 1),
         ),
-        out_shape=[jax.ShapeDtypeStruct((rows, kv_width), jnp.bfloat16)] * count,
+        out_shape=[jax.ShapeDtypeStruct((rows, kv_width), jnp.bfloat16)] * count
+        + [pltpu.HBM((rows, kv_width), jnp.bfloat16)] * (count - 1),
         compiler_params=pltpu.CompilerParams(vmem_limit_bytes=(24 + 2 * count) * MIB),
     )(slot, *in_hbm(queries, grads, key_blocks[0]), *key_blocks[1:], *in_hbm(*[x] * (count - 1)))
+    return out[:count], out[count:]
 
 
 def rms_kernel(x_ref, out_ref):
@@ -139,25 +143,48 @@
     total = own_ref[...].astype(jnp.float32)
     for m in range(1, count):
         total += jnp.where(slot ^ m > slot, refs[m - 1][...].astype(jnp.float32), 0.0)
-    refs[-1][...] = (total * rms_ref[:, :1]).astype(jnp.bfloat16)
+        refs[count - 1 + m][...] = refs[m - 1][...]
+    refs[count - 1][...] = (total * rms_ref[:, :1]).astype(jnp.bfloat16)
 
 
 def value_grad(slot, inv_rms, own_term, received):
     rows, width = own_term.shape
     step = min(rows, 4 * TILE)
+    count = len(received) + 1
     line = pl.BlockSpec((step, width), lambda r: (r, 0))
-    return pl.pallas_call(
-        functools.partial(value_kernel, len(received) + 1),
+    out = pl.pallas_call(
+        functools.partial(value_kernel, count),
         grid=(rows // step,),
-        in_specs=[SCALAR, pl.BlockSpec((step, DH), lambda r: (r, 0))]
-        + [line] * (len(received) + 1),
-        out_specs=line,
-        out_shape=jax.ShapeDtypeStruct((rows, width), jnp.bfloat16),
+        in_specs=[SCALAR, pl.BlockSpec((step, DH), lambda r: (r, 0))] + [line] * count,
+        out_specs=[line] * count,
+        out_shape=[jax.ShapeDtypeStruct((rows, width), jnp.bfloat16)]
+        + [pltpu.HBM((rows, width), jnp.bfloat16)] * (count - 1),
         compiler_params=PARAMS,
     )(slot, inv_rms, own_term, *received)
-
-
-def column_kernel(count, slot_ref, half_ref, gain_ref, own_ref, *refs):
+    return out[0], out[1:]
+
+
+def hold_kernel(*refs):
+    count = len(refs) // 2
+    for in_ref, out_ref in zip(refs[:count], refs[count:]):
+        out_ref[...] = in_ref[...]
+
+
+def held(*arrays):
+    rows, width = arrays[0].shape
+    step = min(rows, 2 * TILE)
+    wide = [pl.BlockSpec((step, width), lambda r: (r, 0))] * len(arrays)
+    return pl.pallas_call(
+        hold_kernel,
+        grid=(rows // step,),
+        in_specs=wide,
+        out_specs=wide,
+        out_shape=[pltpu.HBM(array.shape, array.dtype) for array in arrays],
+        compiler_params=PARAMS,
+    )(*arrays)
+
+
+def column_kernel(count, slot_ref, gain_ref, own_ref, *refs):
     first, second, out_ref = refs[: count - 1], refs[count - 1 : -1], refs[-1]
     slot = slot_ref[0]
     rows = own_ref.shape[0]
@@ -169,48 +196,40 @@
         out_ref[:, m * rows : (m + 1) * rows] = (x.astype(jnp.float32) * gain).astype(jnp.bfloat16).T
 
 
-def gained_columns(slot, half, halves, gain, x, first, second):
+def gained_columns(slot, gain, x, first, second):
     count = len(first) + 1
     rows, width = x.shape
-    width = width // count // halves
+    width = width // count
     step = min(width, 256)
     steps = width // step
-
-    def place(c, slot_ref, half_ref):
-        return (0, half_ref[0] * steps + c)
-
-    def own_place(c, slot_ref, half_ref):
-        return (0, (slot_ref[0] * halves + half_ref[0]) * steps + c)
-
+    column = pl.BlockSpec((rows, step), lambda c, _: (0, c))
     return pl.pallas_call(
         functools.partial(column_kernel, count),
         grid_spec=pltpu.PrefetchScalarGridSpec(
-            num_scalar_prefetch=2,
+            num_scalar_prefetch=1,
             grid=(steps,),
-            in_specs=[pl.BlockSpec((1, step), place), pl.BlockSpec((rows, step), own_place)]
-            + [pl.BlockSpec((rows, step), place)] * (2 * count - 2),
-            out_specs=pl.BlockSpec((step, count * rows), lambda c, *_: (c, 0)),
+            in_specs=[
+                pl.BlockSpec((1, step), lambda c, _: (0, c)),
+                pl.BlockSpec((rows, step), lambda c, slot_ref: (0, slot_ref[0] * steps + c)),
+            ]
+            + [column] * (2 * count - 2),
+            out_specs=pl.BlockSpec((step, count * rows), lambda c, _: (c, 0)),
         ),
         out_shape=jax.ShapeDtypeStruct((width, count * rows), jnp.bfloat16),
         compiler_params=PARAMS,
-    )(slot, half, *in_hbm(gain, x), *first, *second)
+    )(slot, *in_hbm(gain, x), *first, *second)
 
 
 def feature_kernel(count, weight_ref, gain_ref, *refs):
-    value_refs, scaled_refs, all_ref = refs[:count], refs[count:-1], refs[-1]
+    value_refs, scaled_refs = refs[:count], refs[count:]
     rows = value_refs[0].shape[0]
     values = jnp.concatenate([ref[...] for ref in value_refs], axis=0)
-
-    @pl.when(pl.program_id(0) == 0)
-    def _():
-        all_ref[...] = values
-
     normed_grad = lax.dot_general(
         values, weight_ref[...], (((1,), (1,)), ((), ())), preferred_element_type=jnp.float32
     )
     gain = gain_ref[...].astype(jnp.float32)
-    for d in range(count):
-        scaled_refs[d][...] = (normed_grad[d * rows : (d + 1) * rows] * gain).astype(jnp.bfloat16)
+    for m in range(count):
+        scaled_refs[m][...] = (normed_grad[m * rows : (m + 1) * rows] * gain).astype(jnp.bfloat16)
 
 
 def feature_grads(weight, gain, values):
@@ -219,7 +238,7 @@
     width = weight.shape[0]
     step = min(width, 1024)
     column = pl.BlockSpec((rows, step), lambda c: (0, c))
-    out = pl.pallas_call(
+    return pl.pallas_call(
         functools.partial(feature_kernel, count),
         grid=(width // step,),
         in_specs=[
@@ -227,59 +246,88 @@
             pl.BlockSpec((1, step), lambda c: (0, c)),
         ]
         + [fixed((rows, kv_width))] * count,
-        out_specs=[column] * count + [fixed((count * rows, kv_width))],
-        out_shape=[jax.ShapeDtypeStruct((rows, width), jnp.bfloat16)] * count
-        + [jax.ShapeDtypeStruct((count * rows, kv_width), jnp.bfloat16)],
-        compiler_params=PARAMS,
-    )(*in_hbm(weight, gain), *values)
-    return out[:count], out[count]
-
-
-def weight_kernel(docs, half_ref, weight_ref, gain_ref, *refs):
-    normed_refs, value_refs, (out_ref, line_ref) = refs[:docs], refs[docs:-2], refs[-2:]
-    normed = jnp.concatenate([ref[...] for ref in normed_refs], axis=1)
+        out_specs=[column] * count,
+        out_shape=[jax.ShapeDtypeStruct((rows, width), jnp.bfloat16)] * count,
+        compiler_params=PARAMS,
+    )(weight, *in_hbm(gain), *values)
+
+
+def weight_product(weight_ref, gain_ref, columns_ref, value_refs):
     values = jnp.concatenate([ref[...] for ref in value_refs], axis=0)
-    grad = jnp.dot(normed, values, preferred_element_type=jnp.float32)
-    kv_width = grad.shape[1]
-    out_ref[...] = grad.astype(jnp.bfloat16)
+    grad = jnp.dot(columns_ref[...], values, preferred_element_type=jnp.float32)
     terms = grad * weight_ref[...].astype(jnp.float32)
-    lanes = sum(terms[:, i : i + DH] for i in range(0, kv_width, DH))
-    line_ref[...] = jnp.sum(lanes.T, axis=0, keepdims=True) / gain_ref[...].astype(jnp.float32)
-
-
-def weight_grad(half, weight, gain, normed, values):
-    docs = len(normed)
-    blocks = [block for doc in values for block in doc]
-    rows, kv_width = values[0][0].shape
-    width, tokens = normed[0].shape
-    step = min(width, 256)
-    steps = width // step
-    return pl.pallas_call(
-        functools.partial(weight_kernel, docs),
+    lanes = sum(terms[:, i : i + DH] for i in range(0, grad.shape[1], DH))
+    line = jnp.sum(lanes.T, axis=0, keepdims=True) / gain_ref[...].astype(jnp.float32)
+    return grad, line
+
+
+def sent_kernel(half_ref, weight_ref, gain_ref, columns_ref, *refs):
+    out_ref = refs[-1]
+    grad, line = weight_product(weight_ref, gain_ref, columns_ref, refs[:-1])
+    width, kv_width = grad.shape
+    out_ref[:width, :] = grad.astype(jnp.bfloat16)
+    out_ref[width:, :] = jnp.zeros((TILE, kv_width), jnp.bfloat16)
+    out_ref[width:, :width] = jnp.broadcast_to(line, (TILE, width)).astype(jnp.bfloat16)
+
+
+def kept_kernel(half_ref, weight_ref, gain_ref, columns_ref, got_ref, *refs):
+    out_ref, line_ref = refs[-2:]
+    grad, line = weight_product(weight_ref, gain_ref, columns_ref, refs[:-2])
+    width = grad.shape[0]
+    out_ref[...] = (grad + got_ref[:width, :].astype(jnp.float32)).astype(jnp.bfloat16)
+    line_ref[...] = line + got_ref[width:, :width].astype(jnp.float32)[:1]
+
+
+def weight_grad(half, halves, weight, gain, columns, values, got=None):
+    rows, kv_width = values[0].shape
+    width, tokens = columns.shape
+    width = width // halves
+    message = (width + TILE, kv_width)
+    if got is None:
+        kernel, extra = sent_kernel, []
+        out_specs, out_shape = fixed(message), jax.ShapeDtypeStruct(message, jnp.bfloat16)
+    else:
+        kernel, extra = kept_kernel, [got]
+        out_specs = [fixed((width, kv_width)), fixed((1, width))]
+        out_shape = [
+            jax.ShapeDtypeStruct((width, kv_width), jnp.bfloat16),
+            jax.ShapeDtypeStruct((1, width), jnp.float32),
+        ]
+    return pl.pallas_call(
+        kernel,
         grid_spec=pltpu.PrefetchScalarGridSpec(
             num_scalar_prefetch=1,
-            grid=(steps,),
+            grid=(1,),
             in_specs=[
-                pl.BlockSpec((step, kv_width), lambda c, half_ref: (half_ref[0] * steps + c, 0)),
-                pl.BlockSpec((1, step), lambda c, half_ref: (0, half_ref[0] * steps + c)),
+                pl.BlockSpec((width, kv_width), lambda c, half_ref: (half_ref[0], 0)),
+                pl.BlockSpec((1, width), lambda c, half_ref: (0, half_ref[0])),
+                pl.BlockSpec((width, tokens), lambda c, half_ref: (half_ref[0], 0)),
             ]
-            + [pl.BlockSpec((step, tokens), lambda c, *_: (c, 0))] * docs
-            + [fixed((rows, kv_width))] * len(blocks),
-            out_specs=[
-                pl.BlockSpec((step, kv_width), lambda c, *_: (c, 0)),
-                pl.BlockSpec((1, step), lambda c, *_: (0, c)),
-            ],
+            + [fixed(message)] * len(extra)
+            + [fixed((rows, kv_width))] * len(values),
+            out_specs=out_specs,
         ),
-        out_shape=[
-            jax.ShapeDtypeStruct((width, kv_width), jnp.bfloat16),
-            jax.ShapeDtypeStruct((1, width), jnp.float32),
-        ],
-        compiler_params=PARAMS,
-    )(half, *in_hbm(weight, gain), *normed, *blocks)
+        out_shape=out_shape,
+        compiler_params=PARAMS,
+    )(half, weight, *in_hbm(gain), columns, *extra, *values)
+
+
+def stage_kernel(in_ref, out_ref):
+    pltpu.sync_copy(in_ref, out_ref)
+
+
+def staged(array):
+    return pl.pallas_call(
+        stage_kernel,
+        in_specs=[pl.BlockSpec(memory_space=pltpu.HBM)],
+        out_specs=pl.BlockSpec(memory_space=pltpu.VMEM),
+        out_shape=pltpu.VMEM(array.shape, array.dtype),
+        compiler_params=PARAMS,
+    )(array)
 
 
 def input_kernel(count, slot_ref, x_ref, grad_ref, *refs):
-    scaled_refs, out_ref = refs[:count], refs[count]
+    scaled_refs, out_ref = [refs[count - 1], refs[count - 2], *refs[: count - 2]], refs[count]
     slot = slot_ref[0]
     x = x_ref[...].astype(jnp.float32)
     square = 1.0 / (jnp.mean(x * x, axis=1, keepdims=True) + EPSILON)
@@ -311,7 +359,7 @@
         out_specs=wide,
         out_shape=jax.ShapeDtypeStruct((rows, width), jnp.bfloat16),
         compiler_params=PARAMS,
-    )(slot, x, grads, *scaled)
+    )(slot, x, grads, *scaled[2:], *scaled[1::-1])
 
 
 def per_device(section_inputs, queries, keys, w_value, gain, section_grads_in):
@@ -323,6 +371,7 @@
     weight = w_value[0]
     assert MEM <= x.shape[0] and docs == 2 and count & (count - 1) == 0
     masks = range(1, count)
+    turns = [*masks[1:], 1]
 
     swap = [(0, 1), (1, 0)]
 
@@ -333,29 +382,28 @@
         columns = jnp.pad(columns, ((0, 0), (0, own_keys.shape[1] - x_width)))
         first.append(to_partner(jnp.where(slot[0] ^ m > slot[0], own_keys, columns), m))
     next_x = lax.ppermute(x, "section", section_route(-1))
+    next_grad = lax.ppermute(cotangent, "section", section_route(-1))
     inv_rms = inverse_rms(x)
-    first, next_x, inv_rms, slot = after((first, next_x, inv_rms, slot), ())
-    terms = attention(slot, queries[0, 0], cotangent, [own_keys] + first, x)
+    first, inv_rms, slot = after((first, inv_rms, slot), ())
+    terms, first = attention(slot, queries[0, 0], cotangent, [own_keys] + first, x)
 
     second = [to_partner(terms[m], m) for m in reversed(masks)][::-1]
-    next_grad = lax.ppermute(after(cotangent, terms), "section", section_route(-1))
-    second, next_grad = after((second, next_grad), ())
-    value = value_grad(slot, inv_rms, terms[0], second)
-    sent = gained_columns(slot, 1 - half, docs, gain, x, first, second)
-
-    value, sent = after((value, sent), ())
+    next_x, next_grad = held(next_x, next_grad)
+    second, next_x, next_grad = after(([second[m - 1] for m in turns], next_x, next_grad), ())
+    second = [second[turns.index(m)] for m in masks]
+    value, second = value_grad(slot, inv_rms, terms[0], second)
+
     values = [value] + [to_partner(value, m) for m in masks]
-    normed = [
-        gained_columns(slot, half, docs, gain, x, first, second),
-        lax.ppermute(sent, "dp", swap),
-    ]
-    values, normed = after((values, normed), ())
-
-    scaled, all_values = feature_grads(weight, gain, values)
-    other_values = lax.ppermute(all_values, "dp", swap)
-    returned = [to_partner(scaled[m], m, below=True) for m in reversed(range(count))][::-1]
-
-    weight_out, gain_out = weight_grad(half, weight, gain, normed, [[all_values], [other_values]])
+    columns = gained_columns(slot, gain, x, first, second)
+    weight = staged(weight)
+    others, columns, weight = after(([values[m] for m in turns], columns, weight), ())
+    values = [value] + [others[turns.index(m)] for m in masks]
+
+    sent = weight_grad(1 - half, docs, weight, gain, columns, values)
+    scaled = feature_grads(weight, gain, values)
+    returned = [to_partner(scaled[m], m, below=True) for m in range(count)]
+    got = lax.ppermute(sent, "dp", swap)
+    weight_out, gain_out = weight_grad(half, docs, weight, gain, columns, values, got)
     slot = after(slot, weight_out)
     passed = input_grad(slot, next_x, next_grad, returned)
     return passed[None, None], weight_out[None], gain_out

time: 120 us -> 115 us (0.958); the launches traced: 118 us -> 115 us
  starting transfers between devices: 22.5 us -> 18.2 us
  waiting for transfers between devices: 73.1 us -> 69.9 us
  Pallas kernels: 20.2 us -> 23.3 us
    pallas_call x2 -> x5, Pallas kernels: 3.64 us -> 8.69 us  [the longest x2 3.98 us: weight_grad(): pl.pallas_call(kernel, grid_spec=pltpu.PrefetchScalarGridSpec(num_scalar_...]
    ppermute x13, starting transfers between devices: 18.5 us -> 15.2 us  [to_partner(): return lax.ppermute(block, ('section', 'fsdp'), route)]
    ppermute x13, waiting for transfers between devices: 56.3 us -> 54.2 us  [to_partner(): return lax.ppermute(block, ('section', 'fsdp'), route)]
    ppermute x3 -> x2, waiting for transfers between devices: 16.8 us -> 15.7 us  [the longest x1 15.7 us: per_device(): got = lax.ppermute(sent, 'dp', swap)]
    ppermute x3 -> x2, starting transfers between devices: 3.22 us -> 2.23 us  [the longest x1 1.3 us: per_device(): got = lax.ppermute(sent, 'dp', swap)]
    pallas_call x2 -> x1, Pallas kernels: 2.44 us -> 2.23 us  [gained_columns(): pl.pallas_call(functools.partial(column_kernel, count), grid_spec=pltpu.P...]
  transfers between devices with their start and end apart: 17 -> 16, of which waited for: 9 -> 9; matrix products, arithmetic and copies ran while one was open for 1% -> 1% of each run, Pallas kernels for 6% -> 16%
where the time goes in v5:
time: 115 us
  waiting for transfers between devices  69.9 us (61%)
  Pallas kernels  23.3 us (20%)
  starting transfers between devices  18.2 us (16%)
  other arithmetic  1.42 us (1%)
  local copies, waits for them, and re-layouts  1.18 us (1%)
    ppermute x13, waiting for transfers between devices, to_partner(): return lax.ppermute(block, ('section', 'fsdp'), route)  54.2 us
    ppermute x1, waiting for transfers between devices, per_device(): got = lax.ppermute(sent, 'dp', swap)  15.7 us
    ppermute x13, starting transfers between devices, to_partner(): return lax.ppermute(block, ('section', 'fsdp'), route)  15.2 us
    pallas_call x1, Pallas kernels, attention(): pl.pallas_call(functools.partial(attention_kernel, count, group, heads, x...  5.96 us
    pallas_call x2, Pallas kernels, weight_grad(): pl.pallas_call(kernel, grid_spec=pltpu.PrefetchScalarGridSpec(num_scalar_...  3.98 us
    pallas_call x1, Pallas kernels, held(): pl.pallas_call(hold_kernel, grid=(rows // step,), in_specs=wide, out_spec...  3.59 us
    pallas_call x1, Pallas kernels, inverse_rms(): pl.pallas_call(rms_kernel, grid=(rows // step,), in_specs=[pl.BlockSpec((...  2.36 us
  transfers between devices with their start and end apart: 16, of which 9 were waited for; matrix products, arithmetic and copies ran while one was open for 1% of the time, Pallas kernels for 16%

profile of v5, /device:TPU:9, one launch (start us, length us, event | category | flops | bytes accessed | tf_op | source)
XLA Modules:
  0.0 114.7 jit_solution(15919754466600998708)
XLA Ops:
  0.6 0.7 collective-permute-start.6
  1.4 0.9 collective-permute-start.7
  2.3 1.4 %bitcast_select_fusion = (bf16[128,1024]{1,0:T(8,128)(2,1)S(1)}, bf16[128,1024]{1,0:T(8,128)(2,1)S(1)}, bf16[128,1024]{1,0:T(8,128)(2,1)S(1)}) fusion(bf16[1,1,128,4096]{3,2,1,0:T(8,128)(2,1)} %param.6, s32[]{:T(128)S(6)} %select_n.36, pred[]{:T(512)S(6)} %gt.11, bf16[1,1,128,1024]{3,2,1,0:T(8,128)(2,1)} %param.8, s32[]{:T(128)S(6)} %select_n.33, pred[]{:T(512)S(6)} %gt.10, ...), kind=kLoop, calls=%fused_computation | loop fusion | flops 393216 | bytes 1835023 | tf_op jit(solution)/shard_map/jit(_where)/select_n | solution.py:383
  3.7 0.2 collective-permute-start
  4.0 2.3 %collective-permute-start.1 = (bf16[128,1024]{1,0:T(8,128)(2,1)S(1)}, bf16[128,1024]{1,0:T(8,128)(2,1)S(1)}, u32[]{:S(2)}, u32[]{:S(2)}) collective-permute-start(bf16[128,1024]{1,0:T(8,128)(2,1)S(1)} %get-tuple-element.74), channel_id=1, source_target_pairs={{0,4},{2,6},{4,0},{6,2},{8,12},{10,14},{12,8},{14,10},{16,20},{18,... | collective-permute-start | bytes 786440 | tf_op jit(solution)/shard_map/ppermute | solution.py:34
  6.3 0.2 collective-permute-start.2
  6.4 2.4 %shard_map.85.rms_ref = f32[128,128]{1,0:T(8,128)S(1)} custom-call(bf16[128,4096]{1,0:T(8,128)(2,1)} %bitcast.20), custom_call_target="tpu_custom_call" | custom-call | tf_op jit(solution)/shard_map/pallas_call | solution.py:131
  8.8 4.8 %collective-permute-done.refs_1_ = bf16[128,1024]{1,0:T(8,128)(2,1)S(1)} collective-permute-done((bf16[128,1024]{1,0:T(8,128)(2,1)S(1)}, bf16[128,1024]{1,0:T(8,128)(2,1)S(1)}, u32[]{:S(2)}, u32[]{:S(2)}) %collective-permute-start) | collective-permute-done | bytes 262176 | tf_op jit(solution)/shard_map/ppermute | solution.py:34
  13.6 4.0 %collective-permute-done.1.refs_2_ = bf16[128,1024]{1,0:T(8,128)(2,1)S(1)} collective-permute-done((bf16[128,1024]{1,0:T(8,128)(2,1)S(1)}, bf16[128,1024]{1,0:T(8,128)(2,1)S(1)}, u32[]{:S(2)}, u32[]{:S(2)}) %collective-permute-start.1) | collective-permute-done | bytes 262176 | tf_op jit(solution)/shard_map/ppermute | solution.py:34
  17.6 11.1 %collective-permute-done.2.refs_3_ = bf16[128,1024]{1,0:T(8,128)(2,1)S(1)} collective-permute-done((bf16[128,1024]{1,0:T(8,128)(2,1)S(1)}, bf16[128,1024]{1,0:T(8,128)(2,1)S(1)}, u32[]{:S(2)}, u32[]{:S(2)}) %collective-permute-start.2) | collective-permute-done | bytes 262176 | tf_op jit(solution)/shard_map/ppermute | solution.py:34
  28.8 6.0 %shard_map.86 = (bf16[128,1024]{1,0:T(8,128)(2,1)S(1)}, bf16[128,1024]{1,0:T(8,128)(2,1)S(1)}, bf16[128,1024]{1,0:T(8,128)(2,1)S(1)}, bf16[128,1024]{1,0:T(8,128...) custom-call(s32[1]{0:T(128)} %bitcast.5.slot_ref, ...), custom_call_target="tpu_custom_call" | custom-call | tf_op jit(solution)/shard_map/pallas_call | solution.py:107
  34.7 0.1 collective-permute-start.3
  34.8 1.3 %collective-permute-start.4 = (bf16[128,1024]{1,0:T(8,128)(2,1)S(1)}, bf16[128,1024]{1,0:T(8,128)(2,1)S(1)}, u32[]{:S(2)}, u32[]{:S(2)}) collective-permute-start(bf16[128,1024]{1,0:T(8,128)(2,1)S(1)} %get-tuple-element.45), channel_id=1, source_target_pairs={{0,6},{2,4},{4,2},{6,0},{8,14},{10,12},{12,10},{14,8},{16,22},{18,... | collective-permute-start | bytes 786440 | tf_op jit(solution)/shard_map/ppermute | solution.py:34
  36.1 2.2 %collective-permute-start.5 = (bf16[128,1024]{1,0:T(8,128)(2,1)S(1)}, bf16[128,1024]{1,0:T(8,128)(2,1)S(1)}, u32[]{:S(2)}, u32[]{:S(2)}) collective-permute-start(bf16[128,1024]{1,0:T(8,128)(2,1)S(1)} %get-tuple-element.46), channel_id=1, source_target_pairs={{0,2},{2,0},{4,6},{6,4},{8,10},{10,8},{12,14},{14,12},{16,18},{18,... | collective-permute-start | bytes 786440 | tf_op jit(solution)/shard_map/ppermute | solution.py:34
  38.3 0.0 collective-permute-done.6.refs_0_
  38.3 0.0 collective-permute-done.7.refs_1_
  38.3 3.6 %shard_map.87 = (bf16[128,4096]{1,0:T(8,128)(2,1)}, bf16[128,4096]{1,0:T(8,128)(2,1)}) custom-call(bf16[128,4096]{1,0:T(8,128)(2,1)S(1)} %collective-permute-done.6.refs_0_, bf16[128,4096]{1,0:T(8,128)(2,1)} %collective-permute-done.7.refs_1_), custom_call_target="tpu_custom_call" | custom-call | tf_op jit(solution)/shard_map/pallas_call | solution.py:177
  41.9 6.8 %collective-permute-done.3.refs_1_ = bf16[128,1024]{1,0:T(8,128)(2,1)S(1)} collective-permute-done((bf16[128,1024]{1,0:T(8,128)(2,1)S(1)}, bf16[128,1024]{1,0:T(8,128)(2,1)S(1)}, u32[]{:S(2)}, u32[]{:S(2)}) %collective-permute-start.3) | collective-permute-done | bytes 262176 | tf_op jit(solution)/shard_map/ppermute | solution.py:34
  48.7 9.8 %collective-permute-done.4.refs_2_ = bf16[128,1024]{1,0:T(8,128)(2,1)S(1)} collective-permute-done((bf16[128,1024]{1,0:T(8,128)(2,1)S(1)}, bf16[128,1024]{1,0:T(8,128)(2,1)S(1)}, u32[]{:S(2)}, u32[]{:S(2)}) %collective-permute-start.4) | collective-permute-done | bytes 262176 | tf_op jit(solution)/shard_map/ppermute | solution.py:34
  58.5 0.0 collective-permute-done.5.refs_0_
  58.6 1.0 shard_map.88
  59.5 0.0 collective-permute-start.8
  59.5 0.0 collective-permute-start.9
  59.5 3.5 %collective-permute-start.10 = (bf16[128,1024]{1,0:T(8,128)(2,1)S(1)}, bf16[128,1024]{1,0:T(8,128)(2,1)S(1)}, u32[]{:S(2)}, u32[]{:S(2)}) collective-permute-start(bf16[128,1024]{1,0:T(8,128)(2,1)S(1)} %get-tuple-element.52.refs_0_), channel_id=1, source_target_pairs={{0,2},{2,0},{4,6},{6,4},{8,10},{10,8},{12,14},{14,12},{16,18},{18,... | collective-permute-start | bytes 786440 | tf_op jit(solution)/shard_map/ppermute | solution.py:34
  63.1 0.1 shard_map.90.weight_ref
  63.3 0.8 copy-done.3
  64.0 0.1 copy-done.4
  64.1 0.1 copy-done.5
  64.2 0.1 copy-done.6
  64.3 0.1 copy-done.7
  64.4 0.1 copy-done.8
  64.4 2.2 %shard_map.89.columns_ref = bf16[1024,512]{1,0:T(8,128)(2,1)S(1)} custom-call(s32[1]{0:T(128)} %bitcast.5.slot_ref, bf16[1,1024]{1,0:T(2,128)(2,1)} %gain_ref.7, bf16[128,4096]{1,0:T(8,128)(2,1)} %bitcast.24, bf16[128,1024]{1,0:T(8,128)(2,1)S(1)} %copy-done.3, bf16[128,1024]{1,0:T(8,128)(2,1)S(1)} %copy-done.4, bf16[128,1024]{1,0:T(8,128)(2,1)S(1)} %copy-done.5, ...), custom_call_target="tpu_custom_call" | custom-call | tf_op jit(solution)/shard_map/pallas_call | solution.py:206
  66.7 9.8 %collective-permute-done.8.refs_2_ = bf16[128,1024]{1,0:T(8,128)(2,1)S(1)} collective-permute-done((bf16[128,1024]{1,0:T(8,128)(2,1)S(1)}, bf16[128,1024]{1,0:T(8,128)(2,1)S(1)}, u32[]{:S(2)}, u32[]{:S(2)}) %collective-permute-start.8) | collective-permute-done | bytes 262176 | tf_op jit(solution)/shard_map/ppermute | solution.py:34
  76.4 5.6 %collective-permute-done.9.refs_3_ = bf16[128,1024]{1,0:T(8,128)(2,1)S(1)} collective-permute-done((bf16[128,1024]{1,0:T(8,128)(2,1)S(1)}, bf16[128,1024]{1,0:T(8,128)(2,1)S(1)}, u32[]{:S(2)}, u32[]{:S(2)}) %collective-permute-start.9) | collective-permute-done | bytes 262176 | tf_op jit(solution)/shard_map/ppermute | solution.py:34
  82.0 0.0 collective-permute-done.10.refs_1_
  82.1 1.5 %shard_map.91 = bf16[528,1024]{1,0:T(8,128)(2,1)S(1)} custom-call(s32[1]{0:T(128)S(6)} %sub.3.half_ref, bf16[1024,1024]{1,0:T(8,128)(2,1)S(1)} %shard_map.90.weight_ref, bf16[1,1024]{1,0:T(2,128)(2,1)} %gain_ref.7, bf16[1024,512]{1,0:T(8,128)(2,1)S(1)} %shard_map.89.columns_ref, bf16[128,1024]{1,0:T(8,128)(2,1)S(1)} %get-tuple-element.52.refs_0_, ...), custom_call_target="tpu_custom_call" | custom-call | tf_op jit(solution)/shard_map/pallas_call | solution.py:296
  83.5 1.3 %collective-permute-start.11 = (bf16[528,1024]{1,0:T(8,128)(2,1)S(1)}, bf16[528,1024]{1,0:T(8,128)(2,1)S(1)}, u32[]{:S(2)}, u32[]{:S(2)}) collective-permute-start(bf16[528,1024]{1,0:T(8,128)(2,1)S(1)} %shard_map.91), channel_id=1, source_target_pairs={{0,1},{1,0},{2,3},{3,2},{4,5},{5,4},{6,7},{7,6},{8,9},{9,8},{10,11... | collective-permute-start | bytes 3244040 | tf_op jit(solution)/shard_map/ppermute | solution.py:405
  84.8 2.0 %shard_map.93 = (bf16[128,1024]{1,0:T(8,128)(2,1)S(1)}, bf16[128,1024]{1,0:T(8,128)(2,1)S(1)}, bf16[128,1024]{1,0:T(8,128)(2,1)S(1)}, bf16[128,1024]{1,0:T(8,128)(2,1)S(1)}) custom-call(bf16[1024,1024]{1,0:T(8,128)(2,1)S(1)} %shard_map.90.weight_ref, bf16[1,1024]{1,0:T(2,128)(2,1)} %gain_ref.7, bf16[128,1024]{1,0:T(8,128)(2,1)S(1)} %get-tuple-element.52.refs_0_, ...), custom_call_target="tpu_custom_call" | custom-call | tf_op jit(solution)/shard_map/pallas_call | solution.py:241
  86.8 0.1 collective-permute-start.12
  86.9 3.3 %collective-permute-start.13 = (bf16[128,1024]{1,0:T(8,128)(2,1)S(1)}, bf16[128,1024]{1,0:T(8,128)(2,1)S(1)}, u32[]{:S(2)}, u32[]{:S(2)}) collective-permute-start(bf16[128,1024]{1,0:T(8,128)(2,1)S(1)} %get-tuple-element.69), channel_id=1, source_target_pairs={{0,30},{2,28},{4,26},{6,24},{8,6},{10,4},{12,2},{14,0},{16,14},{18... | collective-permute-start | bytes 786440 | tf_op jit(solution)/shard_map/ppermute | solution.py:34
  90.2 2.0 %collective-permute-start.14 = (bf16[128,1024]{1,0:T(8,128)(2,1)S(1)}, bf16[128,1024]{1,0:T(8,128)(2,1)S(1)}, u32[]{:S(2)}, u32[]{:S(2)}) collective-permute-start(bf16[128,1024]{1,0:T(8,128)(2,1)S(1)} %get-tuple-element.70), channel_id=1, source_target_pairs={{0,26},{2,24},{4,30},{6,28},{8,2},{10,0},{12,6},{14,4},{16,10},{18... | collective-permute-start | bytes 786440 | tf_op jit(solution)/shard_map/ppermute | solution.py:34
  92.2 0.0 collective-permute-start.15
  92.2 15.7 %collective-permute-done.11.got_ref = bf16[528,1024]{1,0:T(8,128)(2,1)S(1)} collective-permute-done((bf16[528,1024]{1,0:T(8,128)(2,1)S(1)}, bf16[528,1024]{1,0:T(8,128)(2,1)S(1)}, u32[]{:S(2)}, u32[]{:S(2)}) %collective-permute-start.11) | collective-permute-done | bytes 1081376 | tf_op jit(solution)/shard_map/ppermute | solution.py:405
  107.9 2.5 %shard_map.92 = (bf16[512,1024]{1,0:T(8,128)(2,1)}, f32[1,512]{1,0:T(1,128)}) custom-call(s32[1]{0:T(128)} %bitcast.6.half_ref, bf16[1024,1024]{1,0:T(8,128)(2,1)S(1)} %shard_map.90.weight_ref, bf16[1,1024]{1,0:T(2,128)(2,1)} %gain_ref.7, bf16[1024,512]{1,0:T(8,128)(2,1)S(1)} %shard_map.89.columns_ref, ...), custom_call_target="tpu_custom_call" | custom-call | tf_op jit(solution)/shard_map/pallas_call | solution.py:296
  110.4 0.0 collective-permute-done.12.refs_0_
  110.4 2.2 %collective-permute-done.13.refs_1_ = bf16[128,1024]{1,0:T(8,128)(2,1)S(1)} collective-permute-done((bf16[128,1024]{1,0:T(8,128)(2,1)S(1)}, bf16[128,1024]{1,0:T(8,128)(2,1)S(1)}, u32[]{:S(2)}, u32[]{:S(2)}) %collective-permute-start.13) | collective-permute-done | bytes 262176 | tf_op jit(solution)/shard_map/ppermute | solution.py:34
  112.7 0.0 collective-permute-done.14.refs_2_
  112.7 2.1 %shard_map.94 = bf16[128,4096]{1,0:T(8,128)(2,1)} custom-call(s32[1]{0:T(128)} %bitcast.5.slot_ref, bf16[128,4096]{1,0:T(8,128)(2,1)S(1)} %copy-done.1, bf16[128,4096]{1,0:T(8,128)(2,1)S(1)} %copy-done.2, bf16[128,1024]{1,0:T(8,128)(2,1)S(1)} %collective-permute-done.12.refs_0_, bf16[128,1024]{1,0:T(8,128)(2,1)S(1)} %collective-permute-done.13.refs_1_, ...), custom_call_target="tpu_custom_call" | custom-call | tf_op jit(solution)/shard_map/pallas_call | solution.py:354
  (13 shorter events, 0.0 us)
Async XLA Ops:
  0.6 37.7 %collective-permute-start.6 = (bf16[128,4096]{1,0:T(8,128)(2,1)}, bf16[128,4096]{1,0:T(8,128)(2,1)S(1)}, u32[]{:S(2)}, u32[]{:S(2)}) collective-permute-start(bf16[128,4096]{1,0:T(8,128)(2,1)} %bitcast.19), channel_id=1, source_target_pairs={{0,24},{8,0},{16,8},{24,16},{1,25},{9,1},{17,9},{25,17},{2,26},{10... | collective-permute-start | bytes 3145736 | tf_op jit(solution)/shard_map/ppermute | solution.py:384
  1.4 37.0 %collective-permute-start.7 = (bf16[128,4096]{1,0:T(8,128)(2,1)}, bf16[128,4096]{1,0:T(8,128)(2,1)}, u32[]{:S(2)}, u32[]{:S(2)}) collective-permute-start(bf16[128,4096]{1,0:T(8,128)(2,1)} %bitcast.26), channel_id=1, source_target_pairs={{0,24},{8,0},{16,8},{24,16},{1,25},{9,1},{17,9},{25,17},{2,26},{10... | collective-permute-start | bytes 3145736 | tf_op jit(solution)/shard_map/ppermute | solution.py:385
  3.7 9.9 %collective-permute-start = (bf16[128,1024]{1,0:T(8,128)(2,1)S(1)}, bf16[128,1024]{1,0:T(8,128)(2,1)S(1)}, u32[]{:S(2)}, u32[]{:S(2)}) collective-permute-start(bf16[128,1024]{1,0:T(8,128)(2,1)S(1)} %get-tuple-element.75), channel_id=1, source_target_pairs={{0,2},{2,0},{4,6},{6,4},{8,10},{10,8},{12,14},{14,12},{16,18},{18,... | collective-permute-start | bytes 786440 | tf_op jit(solution)/shard_map/ppermute | solution.py:34
  4.0 13.7 %collective-permute-start.1 = (bf16[128,1024]{1,0:T(8,128)(2,1)S(1)}, bf16[128,1024]{1,0:T(8,128)(2,1)S(1)}, u32[]{:S(2)}, u32[]{:S(2)}) collective-permute-start(bf16[128,1024]{1,0:T(8,128)(2,1)S(1)} %get-tuple-element.74), channel_id=1, source_target_pairs={{0,4},{2,6},{4,0},{6,2},{8,12},{10,14},{12,8},{14,10},{16,20},{18,... | collective-permute-start | bytes 786440 | tf_op jit(solution)/shard_map/ppermute | solution.py:34
  6.3 22.5 %collective-permute-start.2 = (bf16[128,1024]{1,0:T(8,128)(2,1)S(1)}, bf16[128,1024]{1,0:T(8,128)(2,1)S(1)}, u32[]{:S(2)}, u32[]{:S(2)}) collective-permute-start(bf16[128,1024]{1,0:T(8,128)(2,1)S(1)} %get-tuple-element.73), channel_id=1, source_target_pairs={{0,6},{2,4},{4,2},{6,0},{8,14},{10,12},{12,10},{14,8},{16,22},{18,... | collective-permute-start | bytes 786440 | tf_op jit(solution)/shard_map/ppermute | solution.py:34
  34.7 28.4 %copy-start = (bf16[1,1024,1024]{2,1,0:T(8,128)(2,1)S(1)}, bf16[1,1024,1024]{2,1,0:T(8,128)(2,1)}, u32[]{:S(2)}) copy-start(bf16[1,1024,1024]{2,1,0:T(8,128)(2,1)} %param.9) | copy-start | bytes 6291460
  34.7 14.0 %collective-permute-start.3 = (bf16[128,1024]{1,0:T(8,128)(2,1)S(1)}, bf16[128,1024]{1,0:T(8,128)(2,1)S(1)}, u32[]{:S(2)}, u32[]{:S(2)}) collective-permute-start(bf16[128,1024]{1,0:T(8,128)(2,1)S(1)} %get-tuple-element.44), channel_id=1, source_target_pairs={{0,4},{2,6},{4,0},{6,2},{8,12},{10,14},{12,8},{14,10},{16,20},{18,... | collective-permute-start | bytes 786440 | tf_op jit(solution)/shard_map/ppermute | solution.py:34
  34.8 23.7 %collective-permute-start.4 = (bf16[128,1024]{1,0:T(8,128)(2,1)S(1)}, bf16[128,1024]{1,0:T(8,128)(2,1)S(1)}, u32[]{:S(2)}, u32[]{:S(2)}) collective-permute-start(bf16[128,1024]{1,0:T(8,128)(2,1)S(1)} %get-tuple-element.45), channel_id=1, source_target_pairs={{0,6},{2,4},{4,2},{6,0},{8,14},{10,12},{12,10},{14,8},{16,22},{18,... | collective-permute-start | bytes 786440 | tf_op jit(solution)/shard_map/ppermute | solution.py:34
  36.1 22.4 %collective-permute-start.5 = (bf16[128,1024]{1,0:T(8,128)(2,1)S(1)}, bf16[128,1024]{1,0:T(8,128)(2,1)S(1)}, u32[]{:S(2)}, u32[]{:S(2)}) collective-permute-start(bf16[128,1024]{1,0:T(8,128)(2,1)S(1)} %get-tuple-element.46), channel_id=1, source_target_pairs={{0,2},{2,0},{4,6},{6,4},{8,10},{10,8},{12,14},{14,12},{16,18},{18,... | collective-permute-start | bytes 786440 | tf_op jit(solution)/shard_map/ppermute | solution.py:34
  59.5 16.9 %collective-permute-start.8 = (bf16[128,1024]{1,0:T(8,128)(2,1)S(1)}, bf16[128,1024]{1,0:T(8,128)(2,1)S(1)}, u32[]{:S(2)}, u32[]{:S(2)}) collective-permute-start(bf16[128,1024]{1,0:T(8,128)(2,1)S(1)} %get-tuple-element.52.refs_0_), channel_id=1, source_target_pairs={{0,4},{2,6},{4,0},{6,2},{8,12},{10,14},{12,8},{14,10},{16,20},{18,... | collective-permute-start | bytes 786440 | tf_op jit(solution)/shard_map/ppermute | solution.py:34
  59.5 22.5 %collective-permute-start.9 = (bf16[128,1024]{1,0:T(8,128)(2,1)S(1)}, bf16[128,1024]{1,0:T(8,128)(2,1)S(1)}, u32[]{:S(2)}, u32[]{:S(2)}) collective-permute-start(bf16[128,1024]{1,0:T(8,128)(2,1)S(1)} %get-tuple-element.52.refs_0_), channel_id=1, source_target_pairs={{0,6},{2,4},{4,2},{6,0},{8,14},{10,12},{12,10},{14,8},{16,22},{18,... | collective-permute-start | bytes 786440 | tf_op jit(solution)/shard_map/ppermute | solution.py:34
  59.5 22.5 %collective-permute-start.10 = (bf16[128,1024]{1,0:T(8,128)(2,1)S(1)}, bf16[128,1024]{1,0:T(8,128)(2,1)S(1)}, u32[]{:S(2)}, u32[]{:S(2)}) collective-permute-start(bf16[128,1024]{1,0:T(8,128)(2,1)S(1)} %get-tuple-element.52.refs_0_), channel_id=1, source_target_pairs={{0,2},{2,0},{4,6},{6,4},{8,10},{10,8},{12,14},{14,12},{16,18},{18,... | collective-permute-start | bytes 786440 | tf_op jit(solution)/shard_map/ppermute | solution.py:34
  63.1 1.0 copy-start.3
  63.1 1.0 copy-start.4
  63.1 1.1 copy-start.5
  63.1 1.2 %copy-start.6 = (bf16[128,1024]{1,0:T(8,128)(2,1)S(1)}, bf16[128,1024]{1,0:T(8,128)(2,1)}, u32[]{:S(2)}) copy-start(bf16[128,1024]{1,0:T(8,128)(2,1)} %get-tuple-element.56.refs_3_) | copy-start | bytes 786436
  63.1 1.2 %copy-start.7 = (bf16[128,1024]{1,0:T(8,128)(2,1)S(1)}, bf16[128,1024]{1,0:T(8,128)(2,1)}, u32[]{:S(2)}) copy-start(bf16[128,1024]{1,0:T(8,128)(2,1)} %get-tuple-element.57.refs_4_) | copy-start | bytes 786436
  63.1 1.3 %copy-start.8 = (bf16[128,1024]{1,0:T(8,128)(2,1)S(1)}, bf16[128,1024]{1,0:T(8,128)(2,1)}, u32[]{:S(2)}) copy-start(bf16[128,1024]{1,0:T(8,128)(2,1)} %get-tuple-element.58.refs_5_) | copy-start | bytes 786436
  83.5 24.4 %collective-permute-start.11 = (bf16[528,1024]{1,0:T(8,128)(2,1)S(1)}, bf16[528,1024]{1,0:T(8,128)(2,1)S(1)}, u32[]{:S(2)}, u32[]{:S(2)}) collective-permute-start(bf16[528,1024]{1,0:T(8,128)(2,1)S(1)} %shard_map.91), channel_id=1, source_target_pairs={{0,1},{1,0},{2,3},{3,2},{4,5},{5,4},{6,7},{7,6},{8,9},{9,8},{10,11... | collective-permute-start | bytes 3244040 | tf_op jit(solution)/shard_map/ppermute | solution.py:405
  86.8 23.6 %collective-permute-start.12 = (bf16[128,1024]{1,0:T(8,128)(2,1)S(1)}, bf16[128,1024]{1,0:T(8,128)(2,1)S(1)}, u32[]{:S(2)}, u32[]{:S(2)}) collective-permute-start(bf16[128,1024]{1,0:T(8,128)(2,1)S(1)} %get-tuple-element.68), channel_id=1, source_target_pairs={{0,28},{2,30},{4,24},{6,26},{8,4},{10,6},{12,0},{14,2},{16,12},{18... | collective-permute-start | bytes 786440 | tf_op jit(solution)/shard_map/ppermute | solution.py:34
  86.9 25.8 %collective-permute-start.13 = (bf16[128,1024]{1,0:T(8,128)(2,1)S(1)}, bf16[128,1024]{1,0:T(8,128)(2,1)S(1)}, u32[]{:S(2)}, u32[]{:S(2)}) collective-permute-start(bf16[128,1024]{1,0:T(8,128)(2,1)S(1)} %get-tuple-element.69), channel_id=1, source_target_pairs={{0,30},{2,28},{4,26},{6,24},{8,6},{10,4},{12,2},{14,0},{16,14},{18... | collective-permute-start | bytes 786440 | tf_op jit(solution)/shard_map/ppermute | solution.py:34
  90.2 22.5 %collective-permute-start.14 = (bf16[128,1024]{1,0:T(8,128)(2,1)S(1)}, bf16[128,1024]{1,0:T(8,128)(2,1)S(1)}, u32[]{:S(2)}, u32[]{:S(2)}) collective-permute-start(bf16[128,1024]{1,0:T(8,128)(2,1)S(1)} %get-tuple-element.70), channel_id=1, source_target_pairs={{0,26},{2,24},{4,30},{6,28},{8,2},{10,0},{12,6},{14,4},{16,10},{18... | collective-permute-start | bytes 786440 | tf_op jit(solution)/shard_map/ppermute | solution.py:34
  92.2 20.5 %copy-start.1 = (bf16[128,4096]{1,0:T(8,128)(2,1)S(1)}, bf16[128,4096]{1,0:T(8,128)(2,1)}, u32[]{:S(2)}) copy-start(bf16[128,4096]{1,0:T(8,128)(2,1)} %get-tuple-element.66.x_ref) | copy-start | bytes 3145732
  92.2 20.5 %copy-start.2 = (bf16[128,4096]{1,0:T(8,128)(2,1)S(1)}, bf16[128,4096]{1,0:T(8,128)(2,1)}, u32[]{:S(2)}) copy-start(bf16[128,4096]{1,0:T(8,128)(2,1)} %get-tuple-element.67.grad_ref) | copy-start | bytes 3145732
  92.2 20.5 %collective-permute-start.15 = (bf16[128,1024]{1,0:T(8,128)(2,1)S(1)}, bf16[128,1024]{1,0:T(8,128)(2,1)S(1)}, u32[]{:S(2)}, u32[]{:S(2)}) collective-permute-start(bf16[128,1024]{1,0:T(8,128)(2,1)S(1)} %get-tuple-element.71), channel_id=1, source_target_pairs={{0,24},{2,26},{4,28},{6,30},{8,0},{10,2},{12,4},{14,6},{16,8},{18,... | collective-permute-start | bytes 786440 | tf_op jit(solution)/shard_map/ppermute | solution.py:34

commit v6 on v5

--- a/solution.py
+++ b/solution.py
@@ -16,6 +16,8 @@
 MIB = 1024 * 1024
 
 SCALAR = pl.BlockSpec(memory_space=pltpu.SMEM)
+IN_VMEM = pl.BlockSpec(memory_space=pltpu.VMEM)
+IN_HBM = pl.BlockSpec(memory_space=pltpu.HBM)
 PARAMS = pltpu.CompilerParams(vmem_limit_bytes=16 * MIB)
 
 
@@ -47,10 +49,21 @@
     return [pltpu.with_memory_space_constraint(array, pltpu.HBM) for array in arrays]
 
 
-def attention_kernel(count, group, heads, x_steps, slot_ref, query_ref, grad_ref, *refs):
+def started(refs, others, sems):
+    copies = [
+        pltpu.make_async_copy(ref, other, sems.at[i])
+        for i, (ref, other) in enumerate(zip(refs, others))
+    ]
+    for copy in copies:
+        copy.start()
+    return copies
+
+
+def attention_kernel(count, group, heads, slot_ref, query_ref, grad_ref, *refs):
     key_refs, x_refs = refs[:count], refs[count : 2 * count - 1]
-    out_refs, kept_refs = refs[2 * count - 1 : 3 * count - 1], refs[3 * count - 1 :]
-    rows = query_ref.shape[0]
+    out_refs, kept_refs = refs[2 * count - 1 : 3 * count - 1], refs[3 * count - 1 : -1]
+    copies = started(key_refs[1:], kept_refs, refs[-1])
+    rows, kv_width = key_refs[0].shape
     slot = slot_ref[0]
     key_at = lax.broadcasted_iota(jnp.int32, (rows, rows), 0)
     query_at = lax.broadcasted_iota(jnp.int32, (rows, rows), 1)
@@ -58,9 +71,12 @@
     visible = jnp.concatenate([visible] * group, axis=1)
     hidden = [0.0] + [jnp.where(slot ^ m < slot, 0.0, NEG_FILL) for m in range(1, count)]
     scale = DH ** (-0.5) * LOG2E
-    for head in range(heads):
-        own = slice(head * DH, (head + 1) * DH)
-        members = [slice(h * DH, (h + 1) * DH) for h in range(head * group, (head + 1) * group)]
+
+    def head_values(head):
+        own = pl.ds(pl.multiple_of(head * DH, DH), DH)
+        members = [
+            pl.ds(pl.multiple_of((head * group + h) * DH, DH), DH) for h in range(group)
+        ]
         query = jnp.concatenate([query_ref[:, h] for h in members], axis=0)
         grad = jnp.concatenate([grad_ref[:, h] for h in members], axis=0)
         keys = jnp.concatenate([ref[:, own] for ref in key_refs], axis=0)
@@ -78,87 +94,90 @@
         values = jnp.dot(probs, grad, preferred_element_type=jnp.float32)
         for m in range(count):
             out_refs[m][:, own] = values[m * rows : (m + 1) * rows].astype(jnp.bfloat16)
+
+    @pl.loop(0, kv_width // DH // heads)
+    def _(step):
+        for head in range(heads):
+            head_values(step * heads + head)
+
     for m in range(1, count):
-        kept_refs[m - 1][...] = key_refs[m][...]
-
-        @pl.when((slot ^ m > slot) & (pl.program_id(0) < x_steps))
+
+        @pl.when(slot ^ m > slot)
         def _():
-            out_refs[m][...] = x_refs[m - 1][...]
-
-
-def attention(slot, queries, grads, key_blocks, x):
+            out_refs[m][:, : x_refs[m - 1].shape[1]] = x_refs[m - 1][...]
+
+    for copy in copies:
+        copy.wait()
+
+
+def attention(slot, queries, grads, key_blocks, x_blocks):
     rows, kv_width = key_blocks[0].shape
     group = queries.shape[1] // kv_width
     count = len(key_blocks)
-    x_width = x.shape[1] // count
     heads = min(4, kv_width // DH) if count <= 4 else 1
-    width = heads * DH
-    x_steps = x_width // width
-    assert x_width <= kv_width and x_width % width == 0
-    wide = pl.BlockSpec((rows, group * width), lambda g, _: (0, g))
-    narrow = pl.BlockSpec((rows, width), lambda g, _: (0, g))
-    columns = [
-        pl.BlockSpec(
-            (rows, width),
-            lambda g, ref, m=m: (0, (ref[0] ^ m) * x_steps + jnp.minimum(g, x_steps - 1)),
-        )
-        for m in range(1, count)
-    ]
+    assert x_blocks[0].shape[1] <= kv_width
+    block = (rows, kv_width)
     out = pl.pallas_call(
-        functools.partial(attention_kernel, count, group, heads, x_steps),
-        grid_spec=pltpu.PrefetchScalarGridSpec(
-            num_scalar_prefetch=1,
-            grid=(kv_width // width,),
-            in_specs=[wide, wide] + [narrow] * count + columns,
-            out_specs=[narrow] * (2 * count - 1),
-        ),
-        out_shape=[jax.ShapeDtypeStruct((rows, kv_width), jnp.bfloat16)] * count
-        + [pltpu.HBM((rows, kv_width), jnp.bfloat16)] * (count - 1),
-        compiler_params=pltpu.CompilerParams(vmem_limit_bytes=(24 + 2 * count) * MIB),
-    )(slot, *in_hbm(queries, grads, key_blocks[0]), *key_blocks[1:], *in_hbm(*[x] * (count - 1)))
+        functools.partial(attention_kernel, count, group, heads),
+        in_specs=[SCALAR] + [IN_VMEM] * (2 * count + 1),
+        out_specs=[IN_VMEM] * count + [IN_HBM] * (count - 1),
+        out_shape=[pltpu.VMEM(block, jnp.bfloat16)] * count
+        + [pltpu.HBM(block, jnp.bfloat16)] * (count - 1),
+        scratch_shapes=[pltpu.SemaphoreType.DMA((count - 1,))],
+        compiler_params=pltpu.CompilerParams(vmem_limit_bytes=(12 + 2 * count) * MIB),
+    )(slot, queries, grads, *key_blocks, *x_blocks)
     return out[:count], out[count:]
 
 
-def rms_kernel(x_ref, out_ref):
+def prepare_kernel(count, slot_ref, x_ref, rms_ref, *out_refs):
     x = x_ref[...].astype(jnp.float32)
     inv_rms = lax.rsqrt(jnp.mean(x * x, axis=1, keepdims=True) + EPSILON)
-    out_ref[...] = jnp.broadcast_to(inv_rms, out_ref.shape)
-
-
-def inverse_rms(x):
+    rms_ref[...] = jnp.broadcast_to(inv_rms, rms_ref.shape)
+    width = x.shape[1] // count
+    for m in range(1, count):
+        start = pl.multiple_of((slot_ref[0] ^ m) * width, width)
+        out_refs[m - 1][...] = x_ref[:, pl.ds(start, width)]
+
+
+def prepared(slot, x, count):
     rows, width = x.shape
     step = min(rows, 2 * TILE)
-    return pl.pallas_call(
-        rms_kernel,
+    block = (rows, width // count)
+    out = pl.pallas_call(
+        functools.partial(prepare_kernel, count),
         grid=(rows // step,),
-        in_specs=[pl.BlockSpec((step, width), lambda r: (r, 0))],
-        out_specs=pl.BlockSpec((step, DH), lambda r: (r, 0)),
-        out_shape=jax.ShapeDtypeStruct((rows, DH), jnp.float32),
-        compiler_params=PARAMS,
-    )(*in_hbm(x))
+        in_specs=[SCALAR, pl.BlockSpec((step, width), lambda r: (r, 0))],
+        out_specs=[pl.BlockSpec((step, DH), lambda r: (r, 0))]
+        + [pl.BlockSpec((step, width // count), lambda r: (r, 0))] * (count - 1),
+        out_shape=[pltpu.VMEM((rows, DH), jnp.float32)]
+        + [pltpu.VMEM(block, jnp.bfloat16)] * (count - 1),
+        compiler_params=PARAMS,
+    )(slot, *in_hbm(x))
+    return out[0], out[1:]
 
 
 def value_kernel(count, slot_ref, rms_ref, own_ref, *refs):
+    received, out_ref, kept_refs = refs[: count - 1], refs[count - 1], refs[count:-1]
+    copies = started(received, kept_refs, refs[-1])
     slot = slot_ref[0]
     total = own_ref[...].astype(jnp.float32)
     for m in range(1, count):
-        total += jnp.where(slot ^ m > slot, refs[m - 1][...].astype(jnp.float32), 0.0)
-        refs[count - 1 + m][...] = refs[m - 1][...]
-    refs[count - 1][...] = (total * rms_ref[:, :1]).astype(jnp.bfloat16)
+        total += jnp.where(slot ^ m > slot, received[m - 1][...].astype(jnp.float32), 0.0)
+    out_ref[...] = (total * rms_ref[:, :1]).astype(jnp.bfloat16)
+    for copy in copies:
+        copy.wait()
 
 
 def value_grad(slot, inv_rms, own_term, received):
-    rows, width = own_term.shape
-    step = min(rows, 4 * TILE)
+    block = own_term.shape
     count = len(received) + 1
-    line = pl.BlockSpec((step, width), lambda r: (r, 0))
     out = pl.pallas_call(
         functools.partial(value_kernel, count),
-        grid=(rows // step,),
-        in_specs=[SCALAR, pl.BlockSpec((step, DH), lambda r: (r, 0))] + [line] * count,
-        out_specs=[line] * count,
-        out_shape=[jax.ShapeDtypeStruct((rows, width), jnp.bfloat16)]
-        + [pltpu.HBM((rows, width), jnp.bfloat16)] * (count - 1),
+        in_specs=[SCALAR] + [IN_VMEM] * (count + 1),
+        out_specs=[IN_VMEM] + [IN_HBM] * (count - 1),
+        out_shape=[pltpu.VMEM(block, jnp.bfloat16)]
+        + [pltpu.HBM(block, jnp.bfloat16)] * (count - 1),
+        scratch_shapes=[pltpu.SemaphoreType.DMA((count - 1,))],
         compiler_params=PARAMS,
     )(slot, inv_rms, own_term, *received)
     return out[0], out[1:]
@@ -215,7 +234,7 @@
             + [column] * (2 * count - 2),
             out_specs=pl.BlockSpec((step, count * rows), lambda c, _: (c, 0)),
         ),
-        out_shape=jax.ShapeDtypeStruct((width, count * rows), jnp.bfloat16),
+        out_shape=pltpu.VMEM((width, count * rows), jnp.bfloat16),
         compiler_params=PARAMS,
     )(slot, *in_hbm(gain, x), *first, *second)
 
@@ -234,37 +253,31 @@
 
 def feature_grads(weight, gain, values):
     count = len(values)
-    rows, kv_width = values[0].shape
-    width = weight.shape[0]
-    step = min(width, 1024)
-    column = pl.BlockSpec((rows, step), lambda c: (0, c))
+    block = (values[0].shape[0], weight.shape[0])
     return pl.pallas_call(
         functools.partial(feature_kernel, count),
-        grid=(width // step,),
-        in_specs=[
-            pl.BlockSpec((step, kv_width), lambda c: (c, 0)),
-            pl.BlockSpec((1, step), lambda c: (0, c)),
-        ]
-        + [fixed((rows, kv_width))] * count,
-        out_specs=[column] * count,
-        out_shape=[jax.ShapeDtypeStruct((rows, width), jnp.bfloat16)] * count,
-        compiler_params=PARAMS,
-    )(weight, *in_hbm(gain), *values)
-
-
-def weight_product(weight_ref, gain_ref, columns_ref, value_refs):
+        in_specs=[IN_VMEM] * (count + 2),
+        out_specs=[IN_VMEM] * count,
+        out_shape=[pltpu.VMEM(block, jnp.bfloat16)] * count,
+        compiler_params=PARAMS,
+    )(weight, gain, *values)
+
+
+def weight_product(half, width, weight_ref, gain_ref, columns_ref, value_refs):
     values = jnp.concatenate([ref[...] for ref in value_refs], axis=0)
-    grad = jnp.dot(columns_ref[...], values, preferred_element_type=jnp.float32)
-    terms = grad * weight_ref[...].astype(jnp.float32)
+    start = pl.multiple_of(half * width, width)
+    lines = pl.ds(start, width)
+    grad = jnp.dot(columns_ref[lines, :], values, preferred_element_type=jnp.float32)
+    terms = grad * weight_ref[lines, :].astype(jnp.float32)
     lanes = sum(terms[:, i : i + DH] for i in range(0, grad.shape[1], DH))
-    line = jnp.sum(lanes.T, axis=0, keepdims=True) / gain_ref[...].astype(jnp.float32)
+    line = jnp.sum(lanes.T, axis=0, keepdims=True) / gain_ref[:, lines].astype(jnp.float32)
     return grad, line
 
 
 def sent_kernel(half_ref, weight_ref, gain_ref, columns_ref, *refs):
     out_ref = refs[-1]
-    grad, line = weight_product(weight_ref, gain_ref, columns_ref, refs[:-1])
-    width, kv_width = grad.shape
+    width, kv_width = out_ref.shape[0] - TILE, out_ref.shape[1]
+    grad, line = weight_product(half_ref[0], width, weight_ref, gain_ref, columns_ref, refs[:-1])
     out_ref[:width, :] = grad.astype(jnp.bfloat16)
     out_ref[width:, :] = jnp.zeros((TILE, kv_width), jnp.bfloat16)
     out_ref[width:, :width] = jnp.broadcast_to(line, (TILE, width)).astype(jnp.bfloat16)
@@ -272,20 +285,19 @@
 
 def kept_kernel(half_ref, weight_ref, gain_ref, columns_ref, got_ref, *refs):
     out_ref, line_ref = refs[-2:]
-    grad, line = weight_product(weight_ref, gain_ref, columns_ref, refs[:-2])
-    width = grad.shape[0]
+    width = out_ref.shape[0]
+    grad, line = weight_product(half_ref[0], width, weight_ref, gain_ref, columns_ref, refs[:-2])
     out_ref[...] = (grad + got_ref[:width, :].astype(jnp.float32)).astype(jnp.bfloat16)
     line_ref[...] = line + got_ref[width:, :width].astype(jnp.float32)[:1]
 
 
 def weight_grad(half, halves, weight, gain, columns, values, got=None):
-    rows, kv_width = values[0].shape
-    width, tokens = columns.shape
-    width = width // halves
+    kv_width = values[0].shape[1]
+    width = columns.shape[0] // halves
     message = (width + TILE, kv_width)
     if got is None:
         kernel, extra = sent_kernel, []
-        out_specs, out_shape = fixed(message), jax.ShapeDtypeStruct(message, jnp.bfloat16)
+        out_specs, out_shape = IN_VMEM, pltpu.VMEM(message, jnp.bfloat16)
     else:
         kernel, extra = kept_kernel, [got]
         out_specs = [fixed((width, kv_width)), fixed((1, width))]
@@ -295,21 +307,12 @@
         ]
     return pl.pallas_call(
         kernel,
-        grid_spec=pltpu.PrefetchScalarGridSpec(
-            num_scalar_prefetch=1,
-            grid=(1,),
-            in_specs=[
-                pl.BlockSpec((width, kv_width), lambda c, half_ref: (half_ref[0], 0)),
-                pl.BlockSpec((1, width), lambda c, half_ref: (0, half_ref[0])),
-                pl.BlockSpec((width, tokens), lambda c, half_ref: (half_ref[0], 0)),
-            ]
-            + [fixed(message)] * len(extra)
-            + [fixed((rows, kv_width))] * len(values),
-            out_specs=out_specs,
-        ),
+        grid=(1,),
+        in_specs=[SCALAR] + [IN_VMEM] * (3 + len(extra) + len(values)),
+        out_specs=out_specs,
         out_shape=out_shape,
         compiler_params=PARAMS,
-    )(half, weight, *in_hbm(gain), columns, *extra, *values)
+    )(half, weight, gain, columns, *extra, *values)
 
 
 def stage_kernel(in_ref, out_ref):
@@ -319,8 +322,8 @@
 def staged(array):
     return pl.pallas_call(
         stage_kernel,
-        in_specs=[pl.BlockSpec(memory_space=pltpu.HBM)],
-        out_specs=pl.BlockSpec(memory_space=pltpu.VMEM),
+        in_specs=[IN_HBM],
+        out_specs=IN_VMEM,
         out_shape=pltpu.VMEM(array.shape, array.dtype),
         compiler_params=PARAMS,
     )(array)
@@ -383,9 +386,12 @@
         first.append(to_partner(jnp.where(slot[0] ^ m > slot[0], own_keys, columns), m))
     next_x = lax.ppermute(x, "section", section_route(-1))
     next_grad = lax.ppermute(cotangent, "section", section_route(-1))
-    inv_rms = inverse_rms(x)
-    first, inv_rms, slot = after((first, inv_rms, slot), ())
-    terms, first = attention(slot, queries[0, 0], cotangent, [own_keys] + first, x)
+    inv_rms, x_blocks = prepared(slot, x, count)
+    query, grad, held_keys = staged(queries[0, 0]), staged(cotangent), staged(own_keys)
+    first, inv_rms, x_blocks, query, grad, held_keys = after(
+        (first, inv_rms, x_blocks, query, grad, held_keys), ()
+    )
+    terms, first = attention(slot, query, grad, [held_keys] + first, x_blocks)
 
     second = [to_partner(terms[m], m) for m in reversed(masks)][::-1]
     next_x, next_grad = held(next_x, next_grad)
@@ -395,15 +401,17 @@
 
     values = [value] + [to_partner(value, m) for m in masks]
     columns = gained_columns(slot, gain, x, first, second)
-    weight = staged(weight)
-    others, columns, weight = after(([values[m] for m in turns], columns, weight), ())
+    weight, held_gain = staged(weight), staged(gain)
+    others, columns, weight, held_gain = after(
+        ([values[m] for m in turns], columns, weight, held_gain), ()
+    )
     values = [value] + [others[turns.index(m)] for m in masks]
 
-    sent = weight_grad(1 - half, docs, weight, gain, columns, values)
-    scaled = feature_grads(weight, gain, values)
+    sent = weight_grad(1 - half, docs, weight, held_gain, columns, values)
+    scaled = feature_grads(weight, held_gain, values)
     returned = [to_partner(scaled[m], m, below=True) for m in range(count)]
     got = lax.ppermute(sent, "dp", swap)
-    weight_out, gain_out = weight_grad(half, docs, weight, gain, columns, values, got)
+    weight_out, gain_out = weight_grad(half, docs, weight, held_gain, columns, values, got)
     slot = after(slot, weight_out)
     passed = input_grad(slot, next_x, next_grad, returned)
     return passed[None, None], weight_out[None], gain_out

time: 115 us -> 112 us (0.974)
  Pallas kernels: 23.3 us -> 19.5 us
    pallas_call x7 -> x11, Pallas kernels: 15.4 us -> 11.4 us  [the longest x1 3.89 us: attention(): pl.pallas_call(functools.partial(attention_kernel, count, group, heads),...]
  transfers between devices with their start and end apart: 16 -> 16, of which waited for: 9 -> 9; matrix products, arithmetic and copies ran while one was open for 1% -> 1% of each run, Pallas kernels for 16% -> 14%
where the time goes in v6:
time: 112 us
  waiting for transfers between devices  70.3 us (63%)
  Pallas kernels  19.5 us (17%)
  starting transfers between devices  18.1 us (16%)
  other arithmetic  1.51 us (1%)
  local copies, waits for them, and re-layouts  1.2 us (1%)
    ppermute x13, waiting for transfers between devices, to_partner(): return lax.ppermute(block, ('section', 'fsdp'), route)  53.7 us
    ppermute x1, waiting for transfers between devices, per_device(): got = lax.ppermute(sent, 'dp', swap)  16.6 us
    ppermute x13, starting transfers between devices, to_partner(): return lax.ppermute(block, ('section', 'fsdp'), route)  15.2 us
    pallas_call x1, Pallas kernels, attention(): pl.pallas_call(functools.partial(attention_kernel, count, group, heads),...  3.89 us
    pallas_call x1, Pallas kernels, held(): pl.pallas_call(hold_kernel, grid=(rows // step,), in_specs=wide, out_spec...  3.75 us
    pallas_call x2, Pallas kernels, weight_grad(): pl.pallas_call(kernel, grid=(1,), in_specs=[SCALAR] + [IN_VMEM] * (3 + le...  2.59 us
    pallas_call x1, Pallas kernels, prepared(): pl.pallas_call(functools.partial(prepare_kernel, count), grid=(rows // st...  2.42 us
  transfers between devices with their start and end apart: 16, of which 9 were waited for; matrix products, arithmetic and copies ran while one was open for 1% of the time, Pallas kernels for 14%

profile of v6, /device:TPU:9, one launch (start us, length us, event | category | flops | bytes accessed | tf_op | source)
XLA Modules:
  0.0 111.5 jit_solution(16161299298095252426)
XLA Ops:
  0.6 0.7 collective-permute-start.6
  1.4 0.9 collective-permute-start.7
  2.3 1.5 %bitcast_select_fusion = (bf16[128,1024]{1,0:T(8,128)(2,1)S(1)}, bf16[128,1024]{1,0:T(8,128)(2,1)S(1)}, bf16[128,1024]{1,0:T(8,128)(2,1)S(1)}) fusion(bf16[1,1,128,4096]{3,2,1,0:T(8,128)(2,1)} %param.6, s32[]{:T(128)S(6)} %select_n.36, pred[]{:T(512)S(6)} %gt.11, bf16[1,1,128,1024]{3,2,1,0:T(8,128)(2,1)} %param.8, s32[]{:T(128)S(6)} %select_n.33, pred[]{:T(512)S(6)} %gt.10, ...), kind=kLoop, calls=%fused_computation | loop fusion | flops 393216 | bytes 1835023 | tf_op jit(solution)/shard_map/jit(_where)/select_n | solution.py:386
  3.8 0.2 collective-permute-start
  4.1 2.3 %collective-permute-start.1 = (bf16[128,1024]{1,0:T(8,128)(2,1)S(1)}, bf16[128,1024]{1,0:T(8,128)(2,1)S(1)}, u32[]{:S(2)}, u32[]{:S(2)}) collective-permute-start(bf16[128,1024]{1,0:T(8,128)(2,1)S(1)} %get-tuple-element.94), channel_id=1, source_target_pairs={{0,4},{2,6},{4,0},{6,2},{8,12},{10,14},{12,8},{14,10},{16,20},{18,... | collective-permute-start | bytes 786440 | tf_op jit(solution)/shard_map/ppermute | solution.py:36
  6.4 0.2 collective-permute-start.2
  6.5 0.1 shard_map.87.grad_ref
  6.6 0.0 copy-start.5
  6.6 2.4 %shard_map.85 = (f32[128,128]{1,0:T(8,128)S(1)}, bf16[128,1024]{1,0:T(8,128)(2,1)S(1)}, bf16[128,1024]{1,0:T(8,128)(2,1)S(1)}, bf16[128,1024]{1,0:T(8,128)(2,1)S(1)}) custom-call(s32[1]{0:T(128)} %bitcast.slot_ref, bf16[128,4096]{1,0:T(8,128)(2,1)} %bitcast.24), custom_call_target="tpu_custom_call" | custom-call | tf_op jit(solution)/shard_map/pallas_call | solution.py:146
  9.1 0.1 shard_map.86.query_ref
  9.2 4.6 %collective-permute-done.refs_1_ = bf16[128,1024]{1,0:T(8,128)(2,1)S(1)} collective-permute-done((bf16[128,1024]{1,0:T(8,128)(2,1)S(1)}, bf16[128,1024]{1,0:T(8,128)(2,1)S(1)}, u32[]{:S(2)}, u32[]{:S(2)}) %collective-permute-start) | collective-permute-done | bytes 262176 | tf_op jit(solution)/shard_map/ppermute | solution.py:36
  13.7 4.0 %collective-permute-done.1.refs_2_ = bf16[128,1024]{1,0:T(8,128)(2,1)S(1)} collective-permute-done((bf16[128,1024]{1,0:T(8,128)(2,1)S(1)}, bf16[128,1024]{1,0:T(8,128)(2,1)S(1)}, u32[]{:S(2)}, u32[]{:S(2)}) %collective-permute-start.1) | collective-permute-done | bytes 262176 | tf_op jit(solution)/shard_map/ppermute | solution.py:36
  17.7 11.1 %collective-permute-done.2.refs_3_ = bf16[128,1024]{1,0:T(8,128)(2,1)S(1)} collective-permute-done((bf16[128,1024]{1,0:T(8,128)(2,1)S(1)}, bf16[128,1024]{1,0:T(8,128)(2,1)S(1)}, u32[]{:S(2)}, u32[]{:S(2)}) %collective-permute-start.2) | collective-permute-done | bytes 262176 | tf_op jit(solution)/shard_map/ppermute | solution.py:36
  28.9 3.9 %shard_map.89 = (bf16[128,1024]{1,0:T(8,128)(2,1)S(1)}, bf16[128,1024]{1,0:T(8,128)(2,1)S(1)}, bf16[128,1024]{1,0:T(8,128)(2,1)S(1)}, bf16[128,1024]{1,0:T(8,128...) custom-call(s32[1]{0:T(128)} %bitcast.slot_ref, ...), custom_call_target="tpu_custom_call" | custom-call | tf_op jit(solution)/shard_map/pallas_call | solution.py:120
  32.8 0.0 copy-start
  32.8 0.1 collective-permute-start.3
  32.9 1.3 %collective-permute-start.4 = (bf16[128,1024]{1,0:T(8,128)(2,1)S(1)}, bf16[128,1024]{1,0:T(8,128)(2,1)S(1)}, u32[]{:S(2)}, u32[]{:S(2)}) collective-permute-start(bf16[128,1024]{1,0:T(8,128)(2,1)S(1)} %get-tuple-element.64), channel_id=1, source_target_pairs={{0,6},{2,4},{4,2},{6,0},{8,14},{10,12},{12,10},{14,8},{16,22},{18,... | collective-permute-start | bytes 786440 | tf_op jit(solution)/shard_map/ppermute | solution.py:36
  34.2 2.2 %collective-permute-start.5 = (bf16[128,1024]{1,0:T(8,128)(2,1)S(1)}, bf16[128,1024]{1,0:T(8,128)(2,1)S(1)}, u32[]{:S(2)}, u32[]{:S(2)}) collective-permute-start(bf16[128,1024]{1,0:T(8,128)(2,1)S(1)} %get-tuple-element.65), channel_id=1, source_target_pairs={{0,2},{2,0},{4,6},{6,4},{8,10},{10,8},{12,14},{14,12},{16,18},{18,... | collective-permute-start | bytes 786440 | tf_op jit(solution)/shard_map/ppermute | solution.py:36
  36.4 0.0 collective-permute-done.6.refs_0_
  36.4 0.0 collective-permute-done.7.refs_1_
  36.4 3.8 %shard_map.90 = (bf16[128,4096]{1,0:T(8,128)(2,1)}, bf16[128,4096]{1,0:T(8,128)(2,1)}) custom-call(bf16[128,4096]{1,0:T(8,128)(2,1)} %collective-permute-done.6.refs_0_, bf16[128,4096]{1,0:T(8,128)(2,1)} %collective-permute-done.7.refs_1_), custom_call_target="tpu_custom_call" | custom-call | tf_op jit(solution)/shard_map/pallas_call | solution.py:196
  40.2 6.6 %collective-permute-done.3.refs_1_ = bf16[128,1024]{1,0:T(8,128)(2,1)S(1)} collective-permute-done((bf16[128,1024]{1,0:T(8,128)(2,1)S(1)}, bf16[128,1024]{1,0:T(8,128)(2,1)S(1)}, u32[]{:S(2)}, u32[]{:S(2)}) %collective-permute-start.3) | collective-permute-done | bytes 262176 | tf_op jit(solution)/shard_map/ppermute | solution.py:36
  46.8 9.9 %collective-permute-done.4.refs_2_ = bf16[128,1024]{1,0:T(8,128)(2,1)S(1)} collective-permute-done((bf16[128,1024]{1,0:T(8,128)(2,1)S(1)}, bf16[128,1024]{1,0:T(8,128)(2,1)S(1)}, u32[]{:S(2)}, u32[]{:S(2)}) %collective-permute-start.4) | collective-permute-done | bytes 262176 | tf_op jit(solution)/shard_map/ppermute | solution.py:36
  56.7 0.9 shard_map.91
  57.6 0.1 collective-permute-start.8
  57.7 0.1 collective-permute-start.9
  57.8 3.5 %collective-permute-start.10 = (bf16[128,1024]{1,0:T(8,128)(2,1)S(1)}, bf16[128,1024]{1,0:T(8,128)(2,1)S(1)}, u32[]{:S(2)}, u32[]{:S(2)}) collective-permute-start(bf16[128,1024]{1,0:T(8,128)(2,1)S(1)} %get-tuple-element.71.refs_0_), channel_id=1, source_target_pairs={{0,2},{2,0},{4,6},{6,4},{8,10},{10,8},{12,14},{14,12},{16,18},{18,... | collective-permute-start | bytes 786440 | tf_op jit(solution)/shard_map/ppermute | solution.py:36
  61.3 0.1 shard_map.93.weight_ref
  61.4 0.5 copy-done.12
  61.9 0.3 copy-done.6
  62.2 0.1 copy-done.7
  62.3 0.1 copy-done.8
  62.3 0.1 copy-done.9
  62.4 0.1 copy-done.10
  62.5 0.1 copy-done.11
  62.6 2.2 %shard_map.92.columns_ref = bf16[1024,512]{1,0:T(8,128)(2,1)S(1)} custom-call(s32[1]{0:T(128)} %bitcast.slot_ref, bf16[1,1024]{1,0:T(2,128)(2,1)} %in_ref.1, bf16[128,4096]{1,0:T(8,128)(2,1)} %bitcast.25, bf16[128,1024]{1,0:T(8,128)(2,1)S(1)} %copy-done.6, bf16[128,1024]{1,0:T(8,128)(2,1)S(1)} %copy-done.7, bf16[128,1024]{1,0:T(8,128)(2,1)S(1)} %copy-done.8, ...), custom_call_target="tpu_custom_call" | custom-call | tf_op jit(solution)/shard_map/pallas_call | solution.py:225
  64.8 9.8 %collective-permute-done.8.refs_2_ = bf16[128,1024]{1,0:T(8,128)(2,1)S(1)} collective-permute-done((bf16[128,1024]{1,0:T(8,128)(2,1)S(1)}, bf16[128,1024]{1,0:T(8,128)(2,1)S(1)}, u32[]{:S(2)}, u32[]{:S(2)}) %collective-permute-start.8) | collective-permute-done | bytes 262176 | tf_op jit(solution)/shard_map/ppermute | solution.py:36
  74.6 5.6 %collective-permute-done.9.refs_3_ = bf16[128,1024]{1,0:T(8,128)(2,1)S(1)} collective-permute-done((bf16[128,1024]{1,0:T(8,128)(2,1)S(1)}, bf16[128,1024]{1,0:T(8,128)(2,1)S(1)}, u32[]{:S(2)}, u32[]{:S(2)}) %collective-permute-start.9) | collective-permute-done | bytes 262176 | tf_op jit(solution)/shard_map/ppermute | solution.py:36
  80.2 0.8 shard_map.95
  81.0 1.3 %collective-permute-start.11 = (bf16[528,1024]{1,0:T(8,128)(2,1)S(1)}, bf16[528,1024]{1,0:T(8,128)(2,1)S(1)}, u32[]{:S(2)}, u32[]{:S(2)}) collective-permute-start(bf16[528,1024]{1,0:T(8,128)(2,1)S(1)} %shard_map.95), channel_id=1, source_target_pairs={{0,1},{1,0},{2,3},{3,2},{4,5},{5,4},{6,7},{7,6},{8,9},{9,8},{10,11... | collective-permute-start | bytes 3244040 | tf_op jit(solution)/shard_map/ppermute | solution.py:413
  82.3 1.3 %shard_map.97 = (bf16[128,1024]{1,0:T(8,128)(2,1)S(1)}, bf16[128,1024]{1,0:T(8,128)(2,1)S(1)}, bf16[128,1024]{1,0:T(8,128)(2,1)S(1)}, bf16[128,1024]{1,0:T(8,128)(2,1)S(1)}) custom-call(bf16[1024,1024]{1,0:T(8,128)(2,1)S(1)} %shard_map.93.weight_ref, bf16[1,1024]{1,0:T(2,128)(2,1)S(1)} %shard_map.94.gain_ref, ...), custom_call_target="tpu_custom_call" | custom-call | tf_op jit(solution)/shard_map/pallas_call | solution.py:257
  83.6 0.1 collective-permute-start.12
  83.7 3.2 %collective-permute-start.13 = (bf16[128,1024]{1,0:T(8,128)(2,1)S(1)}, bf16[128,1024]{1,0:T(8,128)(2,1)S(1)}, u32[]{:S(2)}, u32[]{:S(2)}) collective-permute-start(bf16[128,1024]{1,0:T(8,128)(2,1)S(1)} %get-tuple-element.89), channel_id=1, source_target_pairs={{0,30},{2,28},{4,26},{6,24},{8,6},{10,4},{12,2},{14,0},{16,14},{18... | collective-permute-start | bytes 786440 | tf_op jit(solution)/shard_map/ppermute | solution.py:36
  86.9 2.0 %collective-permute-start.14 = (bf16[128,1024]{1,0:T(8,128)(2,1)S(1)}, bf16[128,1024]{1,0:T(8,128)(2,1)S(1)}, u32[]{:S(2)}, u32[]{:S(2)}) collective-permute-start(bf16[128,1024]{1,0:T(8,128)(2,1)S(1)} %get-tuple-element.90), channel_id=1, source_target_pairs={{0,26},{2,24},{4,30},{6,28},{8,2},{10,0},{12,6},{14,4},{16,10},{18... | collective-permute-start | bytes 786440 | tf_op jit(solution)/shard_map/ppermute | solution.py:36
  88.9 16.6 %collective-permute-done.11.got_ref = bf16[528,1024]{1,0:T(8,128)(2,1)S(1)} collective-permute-done((bf16[528,1024]{1,0:T(8,128)(2,1)S(1)}, bf16[528,1024]{1,0:T(8,128)(2,1)S(1)}, u32[]{:S(2)}, u32[]{:S(2)}) %collective-permute-start.11) | collective-permute-done | bytes 1081376 | tf_op jit(solution)/shard_map/ppermute | solution.py:413
  105.5 1.8 %shard_map.96 = (bf16[512,1024]{1,0:T(8,128)(2,1)}, f32[1,512]{1,0:T(1,128)}) custom-call(s32[1]{0:T(128)} %bitcast.1.half_ref, bf16[1024,1024]{1,0:T(8,128)(2,1)S(1)} %shard_map.93.weight_ref, bf16[1,1024]{1,0:T(2,128)(2,1)S(1)} %shard_map.94.gain_ref, bf16[1024,512]{1,0:T(8,128)(2,1)S(1)} %shard_map.92.columns_ref, ...), custom_call_target="tpu_custom_call" | custom-call | tf_op jit(solution)/shard_map/pallas_call | solution.py:308
  107.3 2.1 %collective-permute-done.13.refs_1_ = bf16[128,1024]{1,0:T(8,128)(2,1)S(1)} collective-permute-done((bf16[128,1024]{1,0:T(8,128)(2,1)S(1)}, bf16[128,1024]{1,0:T(8,128)(2,1)S(1)}, u32[]{:S(2)}, u32[]{:S(2)}) %collective-permute-start.13) | collective-permute-done | bytes 262176 | tf_op jit(solution)/shard_map/ppermute | solution.py:36
  109.5 2.1 %shard_map.98 = bf16[128,4096]{1,0:T(8,128)(2,1)} custom-call(s32[1]{0:T(128)} %bitcast.slot_ref, bf16[128,4096]{1,0:T(8,128)(2,1)S(1)} %copy-done.1, bf16[128,4096]{1,0:T(8,128)(2,1)S(1)} %copy-done.2, bf16[128,1024]{1,0:T(8,128)(2,1)S(1)} %collective-permute-done.12.refs_0_, bf16[128,1024]{1,0:T(8,128)(2,1)S(1)} %collective-permute-done.13.refs_1_, ...), custom_call_target="tpu_custom_call" | custom-call | tf_op jit(solution)/shard_map/pallas_call | solution.py:357
  (25 shorter events, 0.1 us)
Async XLA Ops:
  0.6 5.9 %copy-start.4 = (bf16[1,1,128,4096]{3,2,1,0:T(8,128)(2,1)S(1)}, bf16[1,1,128,4096]{3,2,1,0:T(8,128)(2,1)}, u32[]{:S(2)}) copy-start(bf16[1,1,128,4096]{3,2,1,0:T(8,128)(2,1)} %param.11) | copy-start | bytes 3145732
  0.6 35.8 %collective-permute-start.6 = (bf16[128,4096]{1,0:T(8,128)(2,1)}, bf16[128,4096]{1,0:T(8,128)(2,1)}, u32[]{:S(2)}, u32[]{:S(2)}) collective-permute-start(bf16[128,4096]{1,0:T(8,128)(2,1)} %bitcast.23), channel_id=1, source_target_pairs={{0,24},{8,0},{16,8},{24,16},{1,25},{9,1},{17,9},{25,17},{2,26},{10... | collective-permute-start | bytes 3145736 | tf_op jit(solution)/shard_map/ppermute | solution.py:387
  1.4 35.0 %collective-permute-start.7 = (bf16[128,4096]{1,0:T(8,128)(2,1)}, bf16[128,4096]{1,0:T(8,128)(2,1)}, u32[]{:S(2)}, u32[]{:S(2)}) collective-permute-start(bf16[128,4096]{1,0:T(8,128)(2,1)} %bitcast.20), channel_id=1, source_target_pairs={{0,24},{8,0},{16,8},{24,16},{1,25},{9,1},{17,9},{25,17},{2,26},{10... | collective-permute-start | bytes 3145736 | tf_op jit(solution)/shard_map/ppermute | solution.py:388
  2.3 6.8 %copy-start.3 = (bf16[1,1,128,4096]{3,2,1,0:T(8,128)(2,1)S(1)}, bf16[1,1,128,4096]{3,2,1,0:T(8,128)(2,1)}, u32[]{:S(2)}) copy-start(bf16[1,1,128,4096]{3,2,1,0:T(8,128)(2,1)} %param.7) | copy-start | bytes 3145732
  3.8 9.9 %collective-permute-start = (bf16[128,1024]{1,0:T(8,128)(2,1)S(1)}, bf16[128,1024]{1,0:T(8,128)(2,1)S(1)}, u32[]{:S(2)}, u32[]{:S(2)}) collective-permute-start(bf16[128,1024]{1,0:T(8,128)(2,1)S(1)} %get-tuple-element.95), channel_id=1, source_target_pairs={{0,2},{2,0},{4,6},{6,4},{8,10},{10,8},{12,14},{14,12},{16,18},{18,... | collective-permute-start | bytes 786440 | tf_op jit(solution)/shard_map/ppermute | solution.py:36
  4.1 13.7 %collective-permute-start.1 = (bf16[128,1024]{1,0:T(8,128)(2,1)S(1)}, bf16[128,1024]{1,0:T(8,128)(2,1)S(1)}, u32[]{:S(2)}, u32[]{:S(2)}) collective-permute-start(bf16[128,1024]{1,0:T(8,128)(2,1)S(1)} %get-tuple-element.94), channel_id=1, source_target_pairs={{0,4},{2,6},{4,0},{6,2},{8,12},{10,14},{12,8},{14,10},{16,20},{18,... | collective-permute-start | bytes 786440 | tf_op jit(solution)/shard_map/ppermute | solution.py:36
  6.4 22.5 %collective-permute-start.2 = (bf16[128,1024]{1,0:T(8,128)(2,1)S(1)}, bf16[128,1024]{1,0:T(8,128)(2,1)S(1)}, u32[]{:S(2)}, u32[]{:S(2)}) collective-permute-start(bf16[128,1024]{1,0:T(8,128)(2,1)S(1)} %get-tuple-element.93), channel_id=1, source_target_pairs={{0,6},{2,4},{4,2},{6,0},{8,14},{10,12},{12,10},{14,8},{16,22},{18,... | collective-permute-start | bytes 786440 | tf_op jit(solution)/shard_map/ppermute | solution.py:36
  6.6 2.5 %copy-start.5 = (bf16[1,1,128,1024]{3,2,1,0:T(8,128)(2,1)S(1)}, bf16[1,1,128,1024]{3,2,1,0:T(8,128)(2,1)}, u32[]{:S(2)}) copy-start(bf16[1,1,128,1024]{3,2,1,0:T(8,128)(2,1)} %param.8) | copy-start | bytes 786436
  32.8 28.4 %copy-start = (bf16[1,1024,1024]{2,1,0:T(8,128)(2,1)S(1)}, bf16[1,1024,1024]{2,1,0:T(8,128)(2,1)}, u32[]{:S(2)}) copy-start(bf16[1,1024,1024]{2,1,0:T(8,128)(2,1)} %param.9) | copy-start | bytes 6291460
  32.8 14.0 %collective-permute-start.3 = (bf16[128,1024]{1,0:T(8,128)(2,1)S(1)}, bf16[128,1024]{1,0:T(8,128)(2,1)S(1)}, u32[]{:S(2)}, u32[]{:S(2)}) collective-permute-start(bf16[128,1024]{1,0:T(8,128)(2,1)S(1)} %get-tuple-element.63), channel_id=1, source_target_pairs={{0,4},{2,6},{4,0},{6,2},{8,12},{10,14},{12,8},{14,10},{16,20},{18,... | collective-permute-start | bytes 786440 | tf_op jit(solution)/shard_map/ppermute | solution.py:36
  32.9 23.8 %collective-permute-start.4 = (bf16[128,1024]{1,0:T(8,128)(2,1)S(1)}, bf16[128,1024]{1,0:T(8,128)(2,1)S(1)}, u32[]{:S(2)}, u32[]{:S(2)}) collective-permute-start(bf16[128,1024]{1,0:T(8,128)(2,1)S(1)} %get-tuple-element.64), channel_id=1, source_target_pairs={{0,6},{2,4},{4,2},{6,0},{8,14},{10,12},{12,10},{14,8},{16,22},{18,... | collective-permute-start | bytes 786440 | tf_op jit(solution)/shard_map/ppermute | solution.py:36
  34.2 22.4 %collective-permute-start.5 = (bf16[128,1024]{1,0:T(8,128)(2,1)S(1)}, bf16[128,1024]{1,0:T(8,128)(2,1)S(1)}, u32[]{:S(2)}, u32[]{:S(2)}) collective-permute-start(bf16[128,1024]{1,0:T(8,128)(2,1)S(1)} %get-tuple-element.65), channel_id=1, source_target_pairs={{0,2},{2,0},{4,6},{6,4},{8,10},{10,8},{12,14},{14,12},{16,18},{18,... | collective-permute-start | bytes 786440 | tf_op jit(solution)/shard_map/ppermute | solution.py:36
  57.6 17.0 %collective-permute-start.8 = (bf16[128,1024]{1,0:T(8,128)(2,1)S(1)}, bf16[128,1024]{1,0:T(8,128)(2,1)S(1)}, u32[]{:S(2)}, u32[]{:S(2)}) collective-permute-start(bf16[128,1024]{1,0:T(8,128)(2,1)S(1)} %get-tuple-element.71.refs_0_), channel_id=1, source_target_pairs={{0,4},{2,6},{4,0},{6,2},{8,12},{10,14},{12,8},{14,10},{16,20},{18,... | collective-permute-start | bytes 786440 | tf_op jit(solution)/shard_map/ppermute | solution.py:36
  57.7 22.6 %collective-permute-start.9 = (bf16[128,1024]{1,0:T(8,128)(2,1)S(1)}, bf16[128,1024]{1,0:T(8,128)(2,1)S(1)}, u32[]{:S(2)}, u32[]{:S(2)}) collective-permute-start(bf16[128,1024]{1,0:T(8,128)(2,1)S(1)} %get-tuple-element.71.refs_0_), channel_id=1, source_target_pairs={{0,6},{2,4},{4,2},{6,0},{8,14},{10,12},{12,10},{14,8},{16,22},{18,... | collective-permute-start | bytes 786440 | tf_op jit(solution)/shard_map/ppermute | solution.py:36
  57.8 22.5 %collective-permute-start.10 = (bf16[128,1024]{1,0:T(8,128)(2,1)S(1)}, bf16[128,1024]{1,0:T(8,128)(2,1)S(1)}, u32[]{:S(2)}, u32[]{:S(2)}) collective-permute-start(bf16[128,1024]{1,0:T(8,128)(2,1)S(1)} %get-tuple-element.71.refs_0_), channel_id=1, source_target_pairs={{0,2},{2,0},{4,6},{6,4},{8,10},{10,8},{12,14},{14,12},{16,18},{18,... | collective-permute-start | bytes 786440 | tf_op jit(solution)/shard_map/ppermute | solution.py:36
  61.2 0.7 copy-start.12
  61.2 1.0 copy-start.6
  61.2 1.0 copy-start.7
  61.2 1.1 copy-start.8
  61.2 1.2 %copy-start.9 = (bf16[128,1024]{1,0:T(8,128)(2,1)S(1)}, bf16[128,1024]{1,0:T(8,128)(2,1)}, u32[]{:S(2)}) copy-start(bf16[128,1024]{1,0:T(8,128)(2,1)} %get-tuple-element.75.refs_3_) | copy-start | bytes 786436
  61.2 1.3 %copy-start.10 = (bf16[128,1024]{1,0:T(8,128)(2,1)S(1)}, bf16[128,1024]{1,0:T(8,128)(2,1)}, u32[]{:S(2)}) copy-start(bf16[128,1024]{1,0:T(8,128)(2,1)} %get-tuple-element.76.refs_4_) | copy-start | bytes 786436
  61.3 1.3 %copy-start.11 = (bf16[128,1024]{1,0:T(8,128)(2,1)S(1)}, bf16[128,1024]{1,0:T(8,128)(2,1)}, u32[]{:S(2)}) copy-start(bf16[128,1024]{1,0:T(8,128)(2,1)} %get-tuple-element.77.refs_5_) | copy-start | bytes 786436
  81.0 24.5 %collective-permute-start.11 = (bf16[528,1024]{1,0:T(8,128)(2,1)S(1)}, bf16[528,1024]{1,0:T(8,128)(2,1)S(1)}, u32[]{:S(2)}, u32[]{:S(2)}) collective-permute-start(bf16[528,1024]{1,0:T(8,128)(2,1)S(1)} %shard_map.95), channel_id=1, source_target_pairs={{0,1},{1,0},{2,3},{3,2},{4,5},{5,4},{6,7},{7,6},{8,9},{9,8},{10,11... | collective-permute-start | bytes 3244040 | tf_op jit(solution)/shard_map/ppermute | solution.py:413
  83.6 23.7 %collective-permute-start.12 = (bf16[128,1024]{1,0:T(8,128)(2,1)S(1)}, bf16[128,1024]{1,0:T(8,128)(2,1)S(1)}, u32[]{:S(2)}, u32[]{:S(2)}) collective-permute-start(bf16[128,1024]{1,0:T(8,128)(2,1)S(1)} %get-tuple-element.88), channel_id=1, source_target_pairs={{0,28},{2,30},{4,24},{6,26},{8,4},{10,6},{12,0},{14,2},{16,12},{18... | collective-permute-start | bytes 786440 | tf_op jit(solution)/shard_map/ppermute | solution.py:36
  83.7 25.8 %collective-permute-start.13 = (bf16[128,1024]{1,0:T(8,128)(2,1)S(1)}, bf16[128,1024]{1,0:T(8,128)(2,1)S(1)}, u32[]{:S(2)}, u32[]{:S(2)}) collective-permute-start(bf16[128,1024]{1,0:T(8,128)(2,1)S(1)} %get-tuple-element.89), channel_id=1, source_target_pairs={{0,30},{2,28},{4,26},{6,24},{8,6},{10,4},{12,2},{14,0},{16,14},{18... | collective-permute-start | bytes 786440 | tf_op jit(solution)/shard_map/ppermute | solution.py:36
  86.9 22.5 %collective-permute-start.14 = (bf16[128,1024]{1,0:T(8,128)(2,1)S(1)}, bf16[128,1024]{1,0:T(8,128)(2,1)S(1)}, u32[]{:S(2)}, u32[]{:S(2)}) collective-permute-start(bf16[128,1024]{1,0:T(8,128)(2,1)S(1)} %get-tuple-element.90), channel_id=1, source_target_pairs={{0,26},{2,24},{4,30},{6,28},{8,2},{10,0},{12,6},{14,4},{16,10},{18... | collective-permute-start | bytes 786440 | tf_op jit(solution)/shard_map/ppermute | solution.py:36
  88.9 20.5 %copy-start.1 = (bf16[128,4096]{1,0:T(8,128)(2,1)S(1)}, bf16[128,4096]{1,0:T(8,128)(2,1)}, u32[]{:S(2)}) copy-start(bf16[128,4096]{1,0:T(8,128)(2,1)} %get-tuple-element.86.x_ref) | copy-start | bytes 3145732
  88.9 20.6 %copy-start.2 = (bf16[128,4096]{1,0:T(8,128)(2,1)S(1)}, bf16[128,4096]{1,0:T(8,128)(2,1)}, u32[]{:S(2)}) copy-start(bf16[128,4096]{1,0:T(8,128)(2,1)} %get-tuple-element.87.grad_ref) | copy-start | bytes 3145732
  88.9 20.5 %collective-permute-start.15 = (bf16[128,1024]{1,0:T(8,128)(2,1)S(1)}, bf16[128,1024]{1,0:T(8,128)(2,1)S(1)}, u32[]{:S(2)}, u32[]{:S(2)}) collective-permute-start(bf16[128,1024]{1,0:T(8,128)(2,1)S(1)} %get-tuple-element.91), channel_id=1, source_target_pairs={{0,24},{2,26},{4,28},{6,30},{8,0},{10,2},{12,4},{14,6},{16,8},{18,... | collective-permute-start | bytes 786440 | tf_op jit(solution)/shard_map/ppermute | solution.py:36

commit v7 on v6

--- a/solution.py
+++ b/solution.py
@@ -129,6 +129,51 @@
     return out[:count], out[count:]
 
 
+def first_kernel(count, slot_ref, keys_ref, x_ref, *refs):
+    out_refs, sems = refs[:-1], refs[-1]
+    slot = slot_ref[0]
+    width = x_ref.shape[1] // count
+    for m in range(1, count):
+        out_ref = out_refs[m - 1]
+        columns = pl.ds(pl.multiple_of((slot ^ m) * width, width), width)
+
+        @pl.when(slot ^ m > slot)
+        def _():
+            pltpu.make_async_copy(keys_ref, out_ref, sems.at[m - 1]).start()
+
+        @pl.when(slot ^ m < slot)
+        def _():
+            if width < out_ref.shape[1]:
+                out_ref[:, width:] = jnp.zeros_like(out_ref[:, width:])
+            pltpu.make_async_copy(
+                x_ref.at[:, columns], out_ref.at[:, :width], sems.at[m - 1]
+            ).start()
+
+    for m in range(1, count):
+        out_ref = out_refs[m - 1]
+
+        @pl.when(slot ^ m > slot)
+        def _():
+            pltpu.make_async_copy(keys_ref, out_ref, sems.at[m - 1]).wait()
+
+        @pl.when(slot ^ m < slot)
+        def _():
+            pltpu.make_async_copy(
+                x_ref.at[:, :width], out_ref.at[:, :width], sems.at[m - 1]
+            ).wait()
+
+
+def first_blocks(slot, keys, x, count):
+    return pl.pallas_call(
+        functools.partial(first_kernel, count),
+        in_specs=[SCALAR, IN_HBM, IN_HBM],
+        out_specs=[IN_VMEM] * (count - 1),
+        out_shape=[pltpu.VMEM(keys.shape, keys.dtype)] * (count - 1),
+        scratch_shapes=[pltpu.SemaphoreType.DMA((count - 1,))],
+        compiler_params=PARAMS,
+    )(slot, *in_hbm(keys, x))
+
+
 def prepare_kernel(count, slot_ref, x_ref, rms_ref, *out_refs):
     x = x_ref[...].astype(jnp.float32)
     inv_rms = lax.rsqrt(jnp.mean(x * x, axis=1, keepdims=True) + EPSILON)
@@ -326,43 +371,43 @@
         out_specs=IN_VMEM,
         out_shape=pltpu.VMEM(array.shape, array.dtype),
         compiler_params=PARAMS,
-    )(array)
-
-
-def input_kernel(count, slot_ref, x_ref, grad_ref, *refs):
-    scaled_refs, out_ref = [refs[count - 1], refs[count - 2], *refs[: count - 2]], refs[count]
+    )(*in_hbm(array))
+
+
+def input_kernel(count, step, order, slot_ref, x_ref, grad_ref, *refs):
+    scaled_refs, out_ref = refs[:count], refs[count]
+    scaled_refs = [scaled_refs[order.index(m)] for m in range(count)]
     slot = slot_ref[0]
-    x = x_ref[...].astype(jnp.float32)
+    lines = pl.ds(pl.multiple_of(pl.program_id(0) * step, step), step)
+    x = x_ref[lines, :].astype(jnp.float32)
     square = 1.0 / (jnp.mean(x * x, axis=1, keepdims=True) + EPSILON)
     width = x.shape[1] // count
-    starts = [pl.multiple_of((slot ^ m) * width, width) for m in range(count)]
+    places = [pl.ds(pl.multiple_of((slot ^ m) * width, width), width) for m in range(count)]
     inner = jnp.zeros_like(square)
     for m in range(count):
-        block = x_ref[:, pl.ds(starts[m], width)].astype(jnp.float32)
-        inner += jnp.sum(scaled_refs[m][...].astype(jnp.float32) * block, axis=1, keepdims=True)
+        block = x_ref[lines, places[m]].astype(jnp.float32)
+        scaled = scaled_refs[m][lines, :].astype(jnp.float32)
+        inner += jnp.sum(scaled * block, axis=1, keepdims=True)
     inner = inner * square / x.shape[1]
     for m in range(count):
-        columns = pl.ds(starts[m], width)
-        block = x_ref[:, columns].astype(jnp.float32)
-        grad = grad_ref[:, columns].astype(jnp.float32)
-        scaled = scaled_refs[m][...].astype(jnp.float32)
-        out_ref[:, columns] = (grad + (scaled - block * inner)).astype(jnp.bfloat16)
-
-
-def input_grad(slot, x, grads, scaled):
+        block = x_ref[lines, places[m]].astype(jnp.float32)
+        grad = grad_ref[lines, places[m]].astype(jnp.float32)
+        scaled = scaled_refs[m][lines, :].astype(jnp.float32)
+        out_ref[:, places[m]] = (grad + (scaled - block * inner)).astype(jnp.bfloat16)
+
+
+def input_grad(slot, x, grads, scaled, order):
     count = len(scaled)
     rows, width = x.shape
     step = min(rows, 4 * TILE)
-    wide = pl.BlockSpec((step, width), lambda r: (r, 0))
-    return pl.pallas_call(
-        functools.partial(input_kernel, count),
+    return pl.pallas_call(
+        functools.partial(input_kernel, count, step, order),
         grid=(rows // step,),
-        in_specs=[SCALAR, wide, wide]
-        + [pl.BlockSpec((step, width // count), lambda r: (r, 0))] * count,
-        out_specs=wide,
+        in_specs=[SCALAR] + [IN_VMEM] * (2 + count),
+        out_specs=pl.BlockSpec((step, width), lambda r: (r, 0)),
         out_shape=jax.ShapeDtypeStruct((rows, width), jnp.bfloat16),
         compiler_params=PARAMS,
-    )(slot, x, grads, *scaled[2:], *scaled[1::-1])
+    )(slot, x, grads, *[scaled[m] for m in order])
 
 
 def per_device(section_inputs, queries, keys, w_value, gain, section_grads_in):
@@ -374,16 +419,12 @@
     weight = w_value[0]
     assert MEM <= x.shape[0] and docs == 2 and count & (count - 1) == 0
     masks = range(1, count)
-    turns = [*masks[1:], 1]
+    middle_first, far_first = [*masks[1:2], 1, *masks[2:]], masks[::-1]
 
     swap = [(0, 1), (1, 0)]
 
-    x_width = x.shape[1] // count
-    first = []
-    for m in masks:
-        columns = lax.dynamic_slice_in_dim(x, (slot[0] ^ m) * x_width, x_width, axis=1)
-        columns = jnp.pad(columns, ((0, 0), (0, own_keys.shape[1] - x_width)))
-        first.append(to_partner(jnp.where(slot[0] ^ m > slot[0], own_keys, columns), m))
+    sent_first = first_blocks(slot, own_keys, x, count)
+    first = [to_partner(sent_first[m - 1], m) for m in masks]
     next_x = lax.ppermute(x, "section", section_route(-1))
     next_grad = lax.ppermute(cotangent, "section", section_route(-1))
     inv_rms, x_blocks = prepared(slot, x, count)
@@ -395,17 +436,17 @@
 
     second = [to_partner(terms[m], m) for m in reversed(masks)][::-1]
     next_x, next_grad = held(next_x, next_grad)
-    second, next_x, next_grad = after(([second[m - 1] for m in turns], next_x, next_grad), ())
-    second = [second[turns.index(m)] for m in masks]
+    second, next_x, next_grad = after(([second[m - 1] for m in middle_first], next_x, next_grad), ())
+    second = [second[middle_first.index(m)] for m in masks]
     value, second = value_grad(slot, inv_rms, terms[0], second)
 
     values = [value] + [to_partner(value, m) for m in masks]
     columns = gained_columns(slot, gain, x, first, second)
     weight, held_gain = staged(weight), staged(gain)
     others, columns, weight, held_gain = after(
-        ([values[m] for m in turns], columns, weight, held_gain), ()
+        ([values[m] for m in far_first], columns, weight, held_gain), ()
     )
-    values = [value] + [others[turns.index(m)] for m in masks]
+    values = [value] + [others[far_first.index(m)] for m in masks]
 
     sent = weight_grad(1 - half, docs, weight, held_gain, columns, values)
     scaled = feature_grads(weight, held_gain, values)
@@ -413,7 +454,7 @@
     got = lax.ppermute(sent, "dp", swap)
     weight_out, gain_out = weight_grad(half, docs, weight, held_gain, columns, values, got)
     slot = after(slot, weight_out)
-    passed = input_grad(slot, next_x, next_grad, returned)
+    passed = input_grad(slot, next_x, next_grad, returned, [*middle_first, 0])
     return passed[None, None], weight_out[None], gain_out
 
 

time: 112 us -> 110 us (0.982); the launches traced: 112 us -> 108 us
  waiting for transfers between devices: 70.3 us -> 58.5 us
  starting transfers between devices: 18.1 us -> 24.4 us
  Pallas kernels: 19.5 us -> 24.2 us
  other arithmetic: 1.51 us -> 0 us
  local copies, waits for them, and re-layouts: 1.2 us -> 0.03 us
    ppermute x1, waiting for transfers between devices: 16.6 us -> 0.99 us  [per_device(): got = lax.ppermute(sent, 'dp', swap)]
    ppermute x13, starting transfers between devices: 15.2 us -> 21.4 us  [to_partner(): return lax.ppermute(block, ('section', 'fsdp'), route)]
    pallas_call x5, Pallas kernels: 0.31 us -> 5.79 us  [staged(): pl.pallas_call(stage_kernel, in_specs=[IN_HBM], out_specs=IN_VMEM, out_sh...]
    ppermute x13, waiting for transfers between devices: 53.7 us -> 57.6 us  [to_partner(): return lax.ppermute(block, ('section', 'fsdp'), route)]
    pallas_call x1, Pallas kernels: 3.75 us -> 1.88 us  [held(): pl.pallas_call(hold_kernel, grid=(rows // step,), in_specs=wide, out_spec...]
    select_n x1 -> x0, other arithmetic: 1.51 us -> none  [per_device(): jnp.where(slot[0] ^ m > slot[0], own_keys, columns)]
    unnamed x26 -> x16, local copies, waits for them, and re-layouts: 1.2 us -> 0.03 us
    pallas_call x1 -> x2, Pallas kernels: 2.05 us -> 3.2 us  [the longest x1 2.06 us: input_grad(): pl.pallas_call(functools.partial(input_kernel, count, step, order), grid=...]
  transfers between devices with their start and end apart: 16 -> 16, of which waited for: 9 -> 12; matrix products, arithmetic and copies ran while one was open for 1% -> 0% of each run, Pallas kernels for 14% -> 19%
where the time goes in v7:
time: 110 us; the launch traced here: 108 us
  waiting for transfers between devices  58.5 us (53%)
  starting transfers between devices  24.4 us (22%)
  Pallas kernels  24.2 us (22%)
    ppermute x13, waiting for transfers between devices, to_partner(): return lax.ppermute(block, ('section', 'fsdp'), route)  57.6 us
    ppermute x13, starting transfers between devices, to_partner(): return lax.ppermute(block, ('section', 'fsdp'), route)  21.4 us
    pallas_call x5, Pallas kernels, staged(): pl.pallas_call(stage_kernel, in_specs=[IN_HBM], out_specs=IN_VMEM, out_sh...  5.79 us
    pallas_call x1, Pallas kernels, attention(): pl.pallas_call(functools.partial(attention_kernel, count, group, heads),...  3.9 us
    pallas_call x2, Pallas kernels, weight_grad(): pl.pallas_call(kernel, grid=(1,), in_specs=[SCALAR] + [IN_VMEM] * (3 + le...  2.59 us
    pallas_call x1, Pallas kernels, prepared(): pl.pallas_call(functools.partial(prepare_kernel, count), grid=(rows // st...  2.36 us
    pallas_call x1, Pallas kernels, gained_columns(): pl.pallas_call(functools.partial(column_kernel, count), grid_spec=pltpu.P...  2.25 us
  transfers between devices with their start and end apart: 16, of which 12 were waited for; matrix products, arithmetic and copies ran while one was open for 0% of the time, Pallas kernels for 19%

profile of v7, /device:TPU:9, one launch (start us, length us, event | category | flops | bytes accessed | tf_op | source)
XLA Modules:
  0.0 107.9 jit_solution(5155866721886451275)
XLA Ops:
  0.6 0.7 collective-permute-start.6
  1.4 0.9 collective-permute-start.7
  2.3 1.1 %shard_map.85 = (bf16[128,1024]{1,0:T(8,128)(2,1)S(1)}, bf16[128,1024]{1,0:T(8,128)(2,1)S(1)}, bf16[128,1024]{1,0:T(8,128)(2,1)S(1)}) custom-call(s32[1]{0:T(128)} %bitcast.slot_ref, bf16[128,1024]{1,0:T(8,128)(2,1)} %bitcast.15, bf16[128,4096]{1,0:T(8,128)(2,1)} %bitcast.10), custom_call_target="tpu_custom_call" | custom-call | tf_op jit(solution)/shard_map/pallas_call | solution.py:167
  3.4 0.4 collective-permute-start
  3.8 2.2 %collective-permute-start.1 = (bf16[128,1024]{1,0:T(8,128)(2,1)S(1)}, bf16[128,1024]{1,0:T(8,128)(2,1)S(1)}, u32[]{:S(2)}, u32[]{:S(2)}) collective-permute-start(bf16[128,1024]{1,0:T(8,128)(2,1)S(1)} %get-tuple-element.52), channel_id=1, source_target_pairs={{0,4},{2,6},{4,0},{6,2},{8,12},{10,14},{12,8},{14,10},{16,20},{18,... | collective-permute-start | bytes 786440 | tf_op jit(solution)/shard_map/ppermute | solution.py:36
  6.0 0.2 collective-permute-start.2
  6.1 2.4 %shard_map.86 = (f32[128,128]{1,0:T(8,128)S(1)}, bf16[128,1024]{1,0:T(8,128)(2,1)S(1)}, bf16[128,1024]{1,0:T(8,128)(2,1)S(1)}, bf16[128,1024]{1,0:T(8,128)(2,1)S(1)}) custom-call(s32[1]{0:T(128)} %bitcast.slot_ref, bf16[128,4096]{1,0:T(8,128)(2,1)} %bitcast.11), custom_call_target="tpu_custom_call" | custom-call | tf_op jit(solution)/shard_map/pallas_call | solution.py:191
  8.5 1.2 %shard_map.88.grad_ref = bf16[128,4096]{1,0:T(8,128)(2,1)S(1)} custom-call(bf16[128,4096]{1,0:T(8,128)(2,1)} %bitcast.19), custom_call_target="tpu_custom_call" | custom-call | tf_op jit(solution)/shard_map/pallas_call | solution.py:368
  9.7 0.9 shard_map.89.refs_0_
  10.7 1.2 %shard_map.87.query_ref = bf16[128,4096]{1,0:T(8,128)(2,1)S(1)} custom-call(bf16[128,4096]{1,0:T(8,128)(2,1)} %bitcast.17), custom_call_target="tpu_custom_call" | custom-call | tf_op jit(solution)/shard_map/pallas_call | solution.py:368
  11.9 1.5 %collective-permute-done.refs_1_ = bf16[128,1024]{1,0:T(8,128)(2,1)S(1)} collective-permute-done((bf16[128,1024]{1,0:T(8,128)(2,1)S(1)}, bf16[128,1024]{1,0:T(8,128)(2,1)S(1)}, u32[]{:S(2)}, u32[]{:S(2)}) %collective-permute-start) | collective-permute-done | bytes 262176 | tf_op jit(solution)/shard_map/ppermute | solution.py:36
  13.5 3.9 %collective-permute-done.1.refs_2_ = bf16[128,1024]{1,0:T(8,128)(2,1)S(1)} collective-permute-done((bf16[128,1024]{1,0:T(8,128)(2,1)S(1)}, bf16[128,1024]{1,0:T(8,128)(2,1)S(1)}, u32[]{:S(2)}, u32[]{:S(2)}) %collective-permute-start.1) | collective-permute-done | bytes 262176 | tf_op jit(solution)/shard_map/ppermute | solution.py:36
  17.3 11.1 %collective-permute-done.2.refs_3_ = bf16[128,1024]{1,0:T(8,128)(2,1)S(1)} collective-permute-done((bf16[128,1024]{1,0:T(8,128)(2,1)S(1)}, bf16[128,1024]{1,0:T(8,128)(2,1)S(1)}, u32[]{:S(2)}, u32[]{:S(2)}) %collective-permute-start.2) | collective-permute-done | bytes 262176 | tf_op jit(solution)/shard_map/ppermute | solution.py:36
  28.5 3.9 %shard_map.90 = (bf16[128,1024]{1,0:T(8,128)(2,1)S(1)}, bf16[128,1024]{1,0:T(8,128)(2,1)S(1)}, bf16[128,1024]{1,0:T(8,128)(2,1)S(1)}, bf16[128,1024]{1,0:T(8,128...) custom-call(s32[1]{0:T(128)} %bitcast.slot_ref, ...), custom_call_target="tpu_custom_call" | custom-call | tf_op jit(solution)/shard_map/pallas_call | solution.py:120
  32.4 0.1 collective-permute-start.3
  32.5 2.5 %collective-permute-start.4 = (bf16[128,1024]{1,0:T(8,128)(2,1)S(1)}, bf16[128,1024]{1,0:T(8,128)(2,1)S(1)}, u32[]{:S(2)}, u32[]{:S(2)}) collective-permute-start(bf16[128,1024]{1,0:T(8,128)(2,1)S(1)} %get-tuple-element.70), channel_id=1, source_target_pairs={{0,2},{2,0},{4,6},{6,4},{8,10},{10,8},{12,14},{14,12},{16,18},{18,... | collective-permute-start | bytes 786440 | tf_op jit(solution)/shard_map/ppermute | solution.py:36
  34.9 0.2 collective-permute-start.5
  35.1 0.0 collective-permute-done.6.refs_0_
  35.1 0.0 collective-permute-done.7.refs_1_
  35.1 1.9 %shard_map.91 = (bf16[128,4096]{1,0:T(8,128)(2,1)}, bf16[128,4096]{1,0:T(8,128)(2,1)}) custom-call(bf16[128,4096]{1,0:T(8,128)(2,1)S(1)} %collective-permute-done.6.refs_0_, bf16[128,4096]{1,0:T(8,128)(2,1)S(1)} %collective-permute-done.7.refs_1_), custom_call_target="tpu_custom_call" | custom-call | tf_op jit(solution)/shard_map/pallas_call | solution.py:241
  37.0 3.7 %collective-permute-done.3.refs_1_ = bf16[128,1024]{1,0:T(8,128)(2,1)S(1)} collective-permute-done((bf16[128,1024]{1,0:T(8,128)(2,1)S(1)}, bf16[128,1024]{1,0:T(8,128)(2,1)S(1)}, u32[]{:S(2)}, u32[]{:S(2)}) %collective-permute-start.3) | collective-permute-done | bytes 262176 | tf_op jit(solution)/shard_map/ppermute | solution.py:36
  40.7 4.5 %collective-permute-done.4.refs_0_ = bf16[128,1024]{1,0:T(8,128)(2,1)S(1)} collective-permute-done((bf16[128,1024]{1,0:T(8,128)(2,1)S(1)}, bf16[128,1024]{1,0:T(8,128)(2,1)S(1)}, u32[]{:S(2)}, u32[]{:S(2)}) %collective-permute-start.4) | collective-permute-done | bytes 262176 | tf_op jit(solution)/shard_map/ppermute | solution.py:36
  45.1 11.1 %collective-permute-done.5.refs_2_ = bf16[128,1024]{1,0:T(8,128)(2,1)S(1)} collective-permute-done((bf16[128,1024]{1,0:T(8,128)(2,1)S(1)}, bf16[128,1024]{1,0:T(8,128)(2,1)S(1)}, u32[]{:S(2)}, u32[]{:S(2)}) %collective-permute-start.5) | collective-permute-done | bytes 262176 | tf_op jit(solution)/shard_map/ppermute | solution.py:36
  56.2 0.9 shard_map.92
  57.2 0.1 collective-permute-start.8
  57.3 0.1 collective-permute-start.9
  57.3 2.6 %collective-permute-start.10 = (bf16[128,1024]{1,0:T(8,128)(2,1)S(1)}, bf16[128,1024]{1,0:T(8,128)(2,1)S(1)}, u32[]{:S(2)}, u32[]{:S(2)}) collective-permute-start(bf16[128,1024]{1,0:T(8,128)(2,1)S(1)} %get-tuple-element.77.refs_0_), channel_id=1, source_target_pairs={{0,2},{2,0},{4,6},{6,4},{8,10},{10,8},{12,14},{14,12},{16,18},{18,... | collective-permute-start | bytes 786440 | tf_op jit(solution)/shard_map/ppermute | solution.py:36
  59.9 0.0 copy-start.6
  59.9 1.7 %shard_map.94.weight_ref = bf16[1024,1024]{1,0:T(8,128)(2,1)S(1)} custom-call(bf16[1024,1024]{1,0:T(8,128)(2,1)} %bitcast.13), custom_call_target="tpu_custom_call" | custom-call | tf_op jit(solution)/shard_map/pallas_call | solution.py:368
  61.6 0.7 shard_map.95.gain_ref
  62.4 2.3 %shard_map.93.columns_ref = bf16[1024,512]{1,0:T(8,128)(2,1)S(1)} custom-call(s32[1]{0:T(128)} %bitcast.slot_ref, bf16[1,1024]{1,0:T(2,128)(2,1)} %in_ref.1, bf16[128,4096]{1,0:T(8,128)(2,1)} %bitcast.12, bf16[128,1024]{1,0:T(8,128)(2,1)S(1)} %copy-done.2, bf16[128,1024]{1,0:T(8,128)(2,1)S(1)} %copy-done.3, bf16[128,1024]{1,0:T(8,128)(2,1)S(1)} %copy-done.4, ...), custom_call_target="tpu_custom_call" | custom-call | tf_op jit(solution)/shard_map/pallas_call | solution.py:270
  64.6 3.8 %collective-permute-done.8.refs_3_ = bf16[128,1024]{1,0:T(8,128)(2,1)S(1)} collective-permute-done((bf16[128,1024]{1,0:T(8,128)(2,1)S(1)}, bf16[128,1024]{1,0:T(8,128)(2,1)S(1)}, u32[]{:S(2)}, u32[]{:S(2)}) %collective-permute-start.8) | collective-permute-done | bytes 262176 | tf_op jit(solution)/shard_map/ppermute | solution.py:36
  68.4 1.8 %collective-permute-done.9.refs_2_ = bf16[128,1024]{1,0:T(8,128)(2,1)S(1)} collective-permute-done((bf16[128,1024]{1,0:T(8,128)(2,1)S(1)}, bf16[128,1024]{1,0:T(8,128)(2,1)S(1)}, u32[]{:S(2)}, u32[]{:S(2)}) %collective-permute-start.9) | collective-permute-done | bytes 262176 | tf_op jit(solution)/shard_map/ppermute | solution.py:36
  70.2 0.0 collective-permute-done.10.refs_1_
  70.2 0.8 shard_map.96
  71.0 1.3 %collective-permute-start.11 = (bf16[528,1024]{1,0:T(8,128)(2,1)S(1)}, bf16[528,1024]{1,0:T(8,128)(2,1)S(1)}, u32[]{:S(2)}, u32[]{:S(2)}) collective-permute-start(bf16[528,1024]{1,0:T(8,128)(2,1)S(1)} %shard_map.96), channel_id=1, source_target_pairs={{0,1},{1,0},{2,3},{3,2},{4,5},{5,4},{6,7},{7,6},{8,9},{9,8},{10,11... | collective-permute-start | bytes 3244040 | tf_op jit(solution)/shard_map/ppermute | solution.py:454
  72.3 1.3 %shard_map.98 = (bf16[128,1024]{1,0:T(8,128)(2,1)S(1)}, bf16[128,1024]{1,0:T(8,128)(2,1)S(1)}, bf16[128,1024]{1,0:T(8,128)(2,1)S(1)}, bf16[128,1024]{1,0:T(8,128)(2,1)S(1)}) custom-call(bf16[1024,1024]{1,0:T(8,128)(2,1)S(1)} %shard_map.94.weight_ref, bf16[1,1024]{1,0:T(2,128)(2,1)S(1)} %shard_map.95.gain_ref, ...), custom_call_target="tpu_custom_call" | custom-call | tf_op jit(solution)/shard_map/pallas_call | solution.py:302
  73.6 11.4 %collective-permute-start.12 = (bf16[128,1024]{1,0:T(8,128)(2,1)S(1)}, bf16[128,1024]{1,0:T(8,128)(2,1)S(1)}, u32[]{:S(2)}, u32[]{:S(2)}) collective-permute-start(bf16[128,1024]{1,0:T(8,128)(2,1)S(1)} %get-tuple-element.94), channel_id=1, source_target_pairs={{0,28},{2,30},{4,24},{6,26},{8,4},{10,6},{12,0},{14,2},{16,12},{18... | collective-permute-start | bytes 786440 | tf_op jit(solution)/shard_map/ppermute | solution.py:36
  85.0 0.2 collective-permute-start.13
  85.2 0.2 collective-permute-start.14
  85.4 1.5 %collective-permute-start.15 = (bf16[128,1024]{1,0:T(8,128)(2,1)S(1)}, bf16[128,1024]{1,0:T(8,128)(2,1)S(1)}, u32[]{:S(2)}, u32[]{:S(2)}) collective-permute-start(bf16[128,1024]{1,0:T(8,128)(2,1)S(1)} %get-tuple-element.97), channel_id=1, source_target_pairs={{0,24},{2,26},{4,28},{6,30},{8,0},{10,2},{12,4},{14,6},{16,8},{18,... | collective-permute-start | bytes 786440 | tf_op jit(solution)/shard_map/ppermute | solution.py:36
  86.9 1.0 collective-permute-done.11.got_ref
  87.9 1.8 %shard_map.97 = (bf16[512,1024]{1,0:T(8,128)(2,1)}, f32[1,512]{1,0:T(1,128)}) custom-call(s32[1]{0:T(128)} %bitcast.1.half_ref, bf16[1024,1024]{1,0:T(8,128)(2,1)S(1)} %shard_map.94.weight_ref, bf16[1,1024]{1,0:T(2,128)(2,1)S(1)} %shard_map.95.gain_ref, bf16[1024,512]{1,0:T(8,128)(2,1)S(1)} %shard_map.93.columns_ref, ...), custom_call_target="tpu_custom_call" | custom-call | tf_op jit(solution)/shard_map/pallas_call | solution.py:353
  89.7 7.0 %collective-permute-done.12.refs_0_ = bf16[128,1024]{1,0:T(8,128)(2,1)S(1)} collective-permute-done((bf16[128,1024]{1,0:T(8,128)(2,1)S(1)}, bf16[128,1024]{1,0:T(8,128)(2,1)S(1)}, u32[]{:S(2)}, u32[]{:S(2)}) %collective-permute-start.12) | collective-permute-done | bytes 262176 | tf_op jit(solution)/shard_map/ppermute | solution.py:36
  96.7 1.1 collective-permute-done.13.refs_1_
  97.8 8.0 %collective-permute-done.14.refs_2_ = bf16[128,1024]{1,0:T(8,128)(2,1)S(1)} collective-permute-done((bf16[128,1024]{1,0:T(8,128)(2,1)S(1)}, bf16[128,1024]{1,0:T(8,128)(2,1)S(1)}, u32[]{:S(2)}, u32[]{:S(2)}) %collective-permute-start.14) | collective-permute-done | bytes 262176 | tf_op jit(solution)/shard_map/ppermute | solution.py:36
  105.9 0.0 collective-permute-done.15.refs_3_
  105.9 2.1 %shard_map.99 = bf16[128,4096]{1,0:T(8,128)(2,1)} custom-call(s32[1]{0:T(128)} %bitcast.slot_ref, bf16[128,4096]{1,0:T(8,128)(2,1)S(1)} %copy-done, bf16[128,4096]{1,0:T(8,128)(2,1)S(1)} %copy-done.1, bf16[128,1024]{1,0:T(8,128)(2,1)S(1)} %collective-permute-done.12.refs_0_, bf16[128,1024]{1,0:T(8,128)(2,1)S(1)} %collective-permute-done.13.refs_1_, ...), custom_call_target="tpu_custom_call" | custom-call | tf_op jit(solution)/shard_map/pallas_call | solution.py:403
  (15 shorter events, 0.0 us)
Async XLA Ops:
  0.6 34.5 %collective-permute-start.6 = (bf16[128,4096]{1,0:T(8,128)(2,1)}, bf16[128,4096]{1,0:T(8,128)(2,1)S(1)}, u32[]{:S(2)}, u32[]{:S(2)}) collective-permute-start(bf16[128,4096]{1,0:T(8,128)(2,1)} %bitcast.9), channel_id=1, source_target_pairs={{0,24},{8,0},{16,8},{24,16},{1,25},{9,1},{17,9},{25,17},{2,26},{10... | collective-permute-start | bytes 3145736 | tf_op jit(solution)/shard_map/ppermute | solution.py:428
  1.4 33.7 %collective-permute-start.7 = (bf16[128,4096]{1,0:T(8,128)(2,1)}, bf16[128,4096]{1,0:T(8,128)(2,1)S(1)}, u32[]{:S(2)}, u32[]{:S(2)}) collective-permute-start(bf16[128,4096]{1,0:T(8,128)(2,1)} %bitcast.18), channel_id=1, source_target_pairs={{0,24},{8,0},{16,8},{24,16},{1,25},{9,1},{17,9},{25,17},{2,26},{10... | collective-permute-start | bytes 3145736 | tf_op jit(solution)/shard_map/ppermute | solution.py:429
  3.4 10.0 %collective-permute-start = (bf16[128,1024]{1,0:T(8,128)(2,1)S(1)}, bf16[128,1024]{1,0:T(8,128)(2,1)S(1)}, u32[]{:S(2)}, u32[]{:S(2)}) collective-permute-start(bf16[128,1024]{1,0:T(8,128)(2,1)S(1)} %get-tuple-element.51), channel_id=1, source_target_pairs={{0,2},{2,0},{4,6},{6,4},{8,10},{10,8},{12,14},{14,12},{16,18},{18,... | collective-permute-start | bytes 786440 | tf_op jit(solution)/shard_map/ppermute | solution.py:36
  3.8 13.6 %collective-permute-start.1 = (bf16[128,1024]{1,0:T(8,128)(2,1)S(1)}, bf16[128,1024]{1,0:T(8,128)(2,1)S(1)}, u32[]{:S(2)}, u32[]{:S(2)}) collective-permute-start(bf16[128,1024]{1,0:T(8,128)(2,1)S(1)} %get-tuple-element.52), channel_id=1, source_target_pairs={{0,4},{2,6},{4,0},{6,2},{8,12},{10,14},{12,8},{14,10},{16,20},{18,... | collective-permute-start | bytes 786440 | tf_op jit(solution)/shard_map/ppermute | solution.py:36
  6.0 22.5 %collective-permute-start.2 = (bf16[128,1024]{1,0:T(8,128)(2,1)S(1)}, bf16[128,1024]{1,0:T(8,128)(2,1)S(1)}, u32[]{:S(2)}, u32[]{:S(2)}) collective-permute-start(bf16[128,1024]{1,0:T(8,128)(2,1)S(1)} %get-tuple-element.53), channel_id=1, source_target_pairs={{0,6},{2,4},{4,2},{6,0},{8,14},{10,12},{12,10},{14,8},{16,22},{18,... | collective-permute-start | bytes 786440 | tf_op jit(solution)/shard_map/ppermute | solution.py:36
  32.4 8.3 %collective-permute-start.3 = (bf16[128,1024]{1,0:T(8,128)(2,1)S(1)}, bf16[128,1024]{1,0:T(8,128)(2,1)S(1)}, u32[]{:S(2)}, u32[]{:S(2)}) collective-permute-start(bf16[128,1024]{1,0:T(8,128)(2,1)S(1)} %get-tuple-element.69), channel_id=1, source_target_pairs={{0,4},{2,6},{4,0},{6,2},{8,12},{10,14},{12,8},{14,10},{16,20},{18,... | collective-permute-start | bytes 786440 | tf_op jit(solution)/shard_map/ppermute | solution.py:36
  32.5 12.7 %collective-permute-start.4 = (bf16[128,1024]{1,0:T(8,128)(2,1)S(1)}, bf16[128,1024]{1,0:T(8,128)(2,1)S(1)}, u32[]{:S(2)}, u32[]{:S(2)}) collective-permute-start(bf16[128,1024]{1,0:T(8,128)(2,1)S(1)} %get-tuple-element.70), channel_id=1, source_target_pairs={{0,2},{2,0},{4,6},{6,4},{8,10},{10,8},{12,14},{14,12},{16,18},{18,... | collective-permute-start | bytes 786440 | tf_op jit(solution)/shard_map/ppermute | solution.py:36
  34.9 21.3 %collective-permute-start.5 = (bf16[128,1024]{1,0:T(8,128)(2,1)S(1)}, bf16[128,1024]{1,0:T(8,128)(2,1)S(1)}, u32[]{:S(2)}, u32[]{:S(2)}) collective-permute-start(bf16[128,1024]{1,0:T(8,128)(2,1)S(1)} %get-tuple-element.71), channel_id=1, source_target_pairs={{0,6},{2,4},{4,2},{6,0},{8,14},{10,12},{12,10},{14,8},{16,22},{18,... | collective-permute-start | bytes 786440 | tf_op jit(solution)/shard_map/ppermute | solution.py:36
  57.2 11.2 %collective-permute-start.8 = (bf16[128,1024]{1,0:T(8,128)(2,1)S(1)}, bf16[128,1024]{1,0:T(8,128)(2,1)S(1)}, u32[]{:S(2)}, u32[]{:S(2)}) collective-permute-start(bf16[128,1024]{1,0:T(8,128)(2,1)S(1)} %get-tuple-element.77.refs_0_), channel_id=1, source_target_pairs={{0,6},{2,4},{4,2},{6,0},{8,14},{10,12},{12,10},{14,8},{16,22},{18,... | collective-permute-start | bytes 786440 | tf_op jit(solution)/shard_map/ppermute | solution.py:36
  57.3 12.9 %collective-permute-start.9 = (bf16[128,1024]{1,0:T(8,128)(2,1)S(1)}, bf16[128,1024]{1,0:T(8,128)(2,1)S(1)}, u32[]{:S(2)}, u32[]{:S(2)}) collective-permute-start(bf16[128,1024]{1,0:T(8,128)(2,1)S(1)} %get-tuple-element.77.refs_0_), channel_id=1, source_target_pairs={{0,4},{2,6},{4,0},{6,2},{8,12},{10,14},{12,8},{14,10},{16,20},{18,... | collective-permute-start | bytes 786440 | tf_op jit(solution)/shard_map/ppermute | solution.py:36
  57.3 12.8 %collective-permute-start.10 = (bf16[128,1024]{1,0:T(8,128)(2,1)S(1)}, bf16[128,1024]{1,0:T(8,128)(2,1)S(1)}, u32[]{:S(2)}, u32[]{:S(2)}) collective-permute-start(bf16[128,1024]{1,0:T(8,128)(2,1)S(1)} %get-tuple-element.77.refs_0_), channel_id=1, source_target_pairs={{0,2},{2,0},{4,6},{6,4},{8,10},{10,8},{12,14},{14,12},{16,18},{18,... | collective-permute-start | bytes 786440 | tf_op jit(solution)/shard_map/ppermute | solution.py:36
  59.9 2.4 %copy-start.2 = (bf16[128,1024]{1,0:T(8,128)(2,1)S(1)}, bf16[128,1024]{1,0:T(8,128)(2,1)}, u32[]{:S(2)}) copy-start(bf16[128,1024]{1,0:T(8,128)(2,1)} %get-tuple-element.78.refs_0_) | copy-start | bytes 786436
  59.9 2.4 %copy-start.3 = (bf16[128,1024]{1,0:T(8,128)(2,1)S(1)}, bf16[128,1024]{1,0:T(8,128)(2,1)}, u32[]{:S(2)}) copy-start(bf16[128,1024]{1,0:T(8,128)(2,1)} %get-tuple-element.79.refs_1_) | copy-start | bytes 786436
  59.9 2.4 %copy-start.4 = (bf16[128,1024]{1,0:T(8,128)(2,1)S(1)}, bf16[128,1024]{1,0:T(8,128)(2,1)}, u32[]{:S(2)}) copy-start(bf16[128,1024]{1,0:T(8,128)(2,1)} %get-tuple-element.80.refs_2_) | copy-start | bytes 786436
  59.9 2.4 %copy-start.5 = (bf16[128,1024]{1,0:T(8,128)(2,1)S(1)}, bf16[128,1024]{1,0:T(8,128)(2,1)}, u32[]{:S(2)}) copy-start(bf16[128,1024]{1,0:T(8,128)(2,1)} %get-tuple-element.81.refs_3_) | copy-start | bytes 786436
  59.9 2.4 %copy-start.6 = (bf16[128,1024]{1,0:T(8,128)(2,1)S(1)}, bf16[128,1024]{1,0:T(8,128)(2,1)}, u32[]{:S(2)}) copy-start(bf16[128,1024]{1,0:T(8,128)(2,1)} %get-tuple-element.82.refs_4_) | copy-start | bytes 786436
  59.9 2.4 %copy-start.7 = (bf16[128,1024]{1,0:T(8,128)(2,1)S(1)}, bf16[128,1024]{1,0:T(8,128)(2,1)}, u32[]{:S(2)}) copy-start(bf16[128,1024]{1,0:T(8,128)(2,1)} %get-tuple-element.83.refs_5_) | copy-start | bytes 786436
  71.0 16.9 %collective-permute-start.11 = (bf16[528,1024]{1,0:T(8,128)(2,1)S(1)}, bf16[528,1024]{1,0:T(8,128)(2,1)S(1)}, u32[]{:S(2)}, u32[]{:S(2)}) collective-permute-start(bf16[528,1024]{1,0:T(8,128)(2,1)S(1)} %shard_map.96), channel_id=1, source_target_pairs={{0,1},{1,0},{2,3},{3,2},{4,5},{5,4},{6,7},{7,6},{8,9},{9,8},{10,11... | collective-permute-start | bytes 3244040 | tf_op jit(solution)/shard_map/ppermute | solution.py:454
  73.6 23.2 %collective-permute-start.12 = (bf16[128,1024]{1,0:T(8,128)(2,1)S(1)}, bf16[128,1024]{1,0:T(8,128)(2,1)S(1)}, u32[]{:S(2)}, u32[]{:S(2)}) collective-permute-start(bf16[128,1024]{1,0:T(8,128)(2,1)S(1)} %get-tuple-element.94), channel_id=1, source_target_pairs={{0,28},{2,30},{4,24},{6,26},{8,4},{10,6},{12,0},{14,2},{16,12},{18... | collective-permute-start | bytes 786440 | tf_op jit(solution)/shard_map/ppermute | solution.py:36
  85.0 12.8 %collective-permute-start.13 = (bf16[128,1024]{1,0:T(8,128)(2,1)S(1)}, bf16[128,1024]{1,0:T(8,128)(2,1)S(1)}, u32[]{:S(2)}, u32[]{:S(2)}) collective-permute-start(bf16[128,1024]{1,0:T(8,128)(2,1)S(1)} %get-tuple-element.95), channel_id=1, source_target_pairs={{0,26},{2,24},{4,30},{6,28},{8,2},{10,0},{12,6},{14,4},{16,10},{18... | collective-permute-start | bytes 786440 | tf_op jit(solution)/shard_map/ppermute | solution.py:36
  85.2 20.6 %collective-permute-start.14 = (bf16[128,1024]{1,0:T(8,128)(2,1)S(1)}, bf16[128,1024]{1,0:T(8,128)(2,1)S(1)}, u32[]{:S(2)}, u32[]{:S(2)}) collective-permute-start(bf16[128,1024]{1,0:T(8,128)(2,1)S(1)} %get-tuple-element.96), channel_id=1, source_target_pairs={{0,30},{2,28},{4,26},{6,24},{8,6},{10,4},{12,2},{14,0},{16,14},{18... | collective-permute-start | bytes 786440 | tf_op jit(solution)/shard_map/ppermute | solution.py:36
  85.4 20.4 %copy-start = (bf16[128,4096]{1,0:T(8,128)(2,1)S(1)}, bf16[128,4096]{1,0:T(8,128)(2,1)}, u32[]{:S(2)}) copy-start(bf16[128,4096]{1,0:T(8,128)(2,1)} %get-tuple-element.92.x_ref) | copy-start | bytes 3145732
  85.4 20.4 %copy-start.1 = (bf16[128,4096]{1,0:T(8,128)(2,1)S(1)}, bf16[128,4096]{1,0:T(8,128)(2,1)}, u32[]{:S(2)}) copy-start(bf16[128,4096]{1,0:T(8,128)(2,1)} %get-tuple-element.93.grad_ref) | copy-start | bytes 3145732
  85.4 20.4 %collective-permute-start.15 = (bf16[128,1024]{1,0:T(8,128)(2,1)S(1)}, bf16[128,1024]{1,0:T(8,128)(2,1)S(1)}, u32[]{:S(2)}, u32[]{:S(2)}) collective-permute-start(bf16[128,1024]{1,0:T(8,128)(2,1)S(1)} %get-tuple-element.97), channel_id=1, source_target_pairs={{0,24},{2,26},{4,28},{6,30},{8,0},{10,2},{12,4},{14,6},{16,8},{18,... | collective-permute-start | bytes 786440 | tf_op jit(solution)/shard_map/ppermute | solution.py:36

commit v8 on v7

--- a/solution.py
+++ b/solution.py
@@ -69,21 +69,20 @@
     query_at = lax.broadcasted_iota(jnp.int32, (rows, rows), 1)
     visible = (key_at <= query_at) | (slot * rows + key_at < MEM)
     visible = jnp.concatenate([visible] * group, axis=1)
-    hidden = [0.0] + [jnp.where(slot ^ m < slot, 0.0, NEG_FILL) for m in range(1, count)]
     scale = DH ** (-0.5) * LOG2E
 
-    def head_values(head):
+    def head_values(head, masks, hidden):
         own = pl.ds(pl.multiple_of(head * DH, DH), DH)
         members = [
             pl.ds(pl.multiple_of((head * group + h) * DH, DH), DH) for h in range(group)
         ]
         query = jnp.concatenate([query_ref[:, h] for h in members], axis=0)
         grad = jnp.concatenate([grad_ref[:, h] for h in members], axis=0)
-        keys = jnp.concatenate([ref[:, own] for ref in key_refs], axis=0)
+        keys = jnp.concatenate([key_refs[m][:, own] for m in masks], axis=0)
         scores = lax.dot_general(
             keys, query, (((1,), (1,)), ((), ())), preferred_element_type=jnp.float32
         )
-        parts = [scores[m * rows : (m + 1) * rows] for m in range(count)]
+        parts = [scores[i * rows : (i + 1) * rows] for i in range(len(masks))]
         parts[0] = jnp.where(visible, parts[0], NEG_FILL)
         tops = [jnp.max(part, axis=0, keepdims=True) + hide for part, hide in zip(parts, hidden)]
         top = functools.reduce(jnp.maximum, tops)
@@ -92,13 +91,26 @@
         inverse = 1.0 / functools.reduce(jnp.add, sums)
         probs = jnp.concatenate([(w * inverse).astype(jnp.bfloat16) for w in weights], axis=0)
         values = jnp.dot(probs, grad, preferred_element_type=jnp.float32)
-        for m in range(count):
-            out_refs[m][:, own] = values[m * rows : (m + 1) * rows].astype(jnp.bfloat16)
-
-    @pl.loop(0, kv_width // DH // heads)
-    def _(step):
-        for head in range(heads):
-            head_values(step * heads + head)
+        for i, m in enumerate(masks):
+            out_refs[m][:, own] = values[i * rows : (i + 1) * rows].astype(jnp.bfloat16)
+
+    def all_heads(masks, hidden):
+        @pl.loop(0, kv_width // DH // heads)
+        def _(step):
+            for head in range(heads):
+                head_values(step * heads + head, masks, hidden)
+
+    if count <= 4:
+        for place in range(count):
+            masks = [0] + [m for m in range(1, count) if place ^ m < place]
+
+            @pl.when(slot == place)
+            def _():
+                all_heads(masks, [0.0] * len(masks))
+
+    else:
+        hidden = [0.0] + [jnp.where(slot ^ m < slot, 0.0, NEG_FILL) for m in range(1, count)]
+        all_heads(list(range(count)), hidden)
 
     for m in range(1, count):
 
@@ -114,7 +126,7 @@
     rows, kv_width = key_blocks[0].shape
     group = queries.shape[1] // kv_width
     count = len(key_blocks)
-    heads = min(4, kv_width // DH) if count <= 4 else 1
+    heads = min(8, kv_width // DH) if count <= 4 else 1
     assert x_blocks[0].shape[1] <= kv_width
     block = (rows, kv_width)
     out = pl.pallas_call(
@@ -228,24 +240,27 @@
     return out[0], out[1:]
 
 
-def hold_kernel(*refs):
-    count = len(refs) // 2
-    for in_ref, out_ref in zip(refs[:count], refs[count:]):
-        out_ref[...] = in_ref[...]
-
-
-def held(*arrays):
-    rows, width = arrays[0].shape
+def hold_kernel(x_ref, grad_ref, x_out, grad_out, square_ref):
+    x_out[...] = x_ref[...]
+    grad_out[...] = grad_ref[...]
+    x = x_ref[...].astype(jnp.float32)
+    square = 1.0 / (jnp.mean(x * x, axis=1, keepdims=True) + EPSILON)
+    square_ref[...] = jnp.broadcast_to(square, square_ref.shape)
+
+
+def held(x, grads):
+    rows, width = x.shape
     step = min(rows, 2 * TILE)
-    wide = [pl.BlockSpec((step, width), lambda r: (r, 0))] * len(arrays)
+    wide = pl.BlockSpec((step, width), lambda r: (r, 0))
     return pl.pallas_call(
         hold_kernel,
         grid=(rows // step,),
-        in_specs=wide,
-        out_specs=wide,
-        out_shape=[pltpu.HBM(array.shape, array.dtype) for array in arrays],
-        compiler_params=PARAMS,
-    )(*arrays)
+        in_specs=[wide, wide],
+        out_specs=[wide, wide, pl.BlockSpec((step, DH), lambda r: (r, 0))],
+        out_shape=[pltpu.HBM(x.shape, x.dtype), pltpu.HBM(grads.shape, grads.dtype)]
+        + [pltpu.HBM((rows, DH), jnp.float32)],
+        compiler_params=PARAMS,
+    )(x, grads)
 
 
 def column_kernel(count, slot_ref, gain_ref, own_ref, *refs):
@@ -374,21 +389,20 @@
     )(*in_hbm(array))
 
 
-def input_kernel(count, step, order, slot_ref, x_ref, grad_ref, *refs):
+def input_kernel(count, step, order, slot_ref, x_ref, grad_ref, square_ref, *refs):
     scaled_refs, out_ref = refs[:count], refs[count]
     scaled_refs = [scaled_refs[order.index(m)] for m in range(count)]
     slot = slot_ref[0]
     lines = pl.ds(pl.multiple_of(pl.program_id(0) * step, step), step)
-    x = x_ref[lines, :].astype(jnp.float32)
-    square = 1.0 / (jnp.mean(x * x, axis=1, keepdims=True) + EPSILON)
-    width = x.shape[1] // count
+    square = square_ref[lines, :][:, :1]
+    width = x_ref.shape[1] // count
     places = [pl.ds(pl.multiple_of((slot ^ m) * width, width), width) for m in range(count)]
     inner = jnp.zeros_like(square)
     for m in range(count):
         block = x_ref[lines, places[m]].astype(jnp.float32)
         scaled = scaled_refs[m][lines, :].astype(jnp.float32)
         inner += jnp.sum(scaled * block, axis=1, keepdims=True)
-    inner = inner * square / x.shape[1]
+    inner = inner * square / x_ref.shape[1]
     for m in range(count):
         block = x_ref[lines, places[m]].astype(jnp.float32)
         grad = grad_ref[lines, places[m]].astype(jnp.float32)
@@ -396,18 +410,18 @@
         out_ref[:, places[m]] = (grad + (scaled - block * inner)).astype(jnp.bfloat16)
 
 
-def input_grad(slot, x, grads, scaled, order):
+def input_grad(slot, x, grads, square, scaled, order):
     count = len(scaled)
     rows, width = x.shape
     step = min(rows, 4 * TILE)
     return pl.pallas_call(
         functools.partial(input_kernel, count, step, order),
         grid=(rows // step,),
-        in_specs=[SCALAR] + [IN_VMEM] * (2 + count),
+        in_specs=[SCALAR] + [IN_VMEM] * (3 + count),
         out_specs=pl.BlockSpec((step, width), lambda r: (r, 0)),
         out_shape=jax.ShapeDtypeStruct((rows, width), jnp.bfloat16),
         compiler_params=PARAMS,
-    )(slot, x, grads, *[scaled[m] for m in order])
+    )(slot, x, grads, square, *[scaled[m] for m in order])
 
 
 def per_device(section_inputs, queries, keys, w_value, gain, section_grads_in):
@@ -435,8 +449,10 @@
     terms, first = attention(slot, query, grad, [held_keys] + first, x_blocks)
 
     second = [to_partner(terms[m], m) for m in reversed(masks)][::-1]
-    next_x, next_grad = held(next_x, next_grad)
-    second, next_x, next_grad = after(([second[m - 1] for m in middle_first], next_x, next_grad), ())
+    next_x, next_grad, square = held(next_x, next_grad)
+    second, next_x, next_grad, square = after(
+        ([second[m - 1] for m in middle_first], next_x, next_grad, square), ()
+    )
     second = [second[middle_first.index(m)] for m in masks]
     value, second = value_grad(slot, inv_rms, terms[0], second)
 
@@ -454,7 +470,7 @@
     got = lax.ppermute(sent, "dp", swap)
     weight_out, gain_out = weight_grad(half, docs, weight, held_gain, columns, values, got)
     slot = after(slot, weight_out)
-    passed = input_grad(slot, next_x, next_grad, returned, [*middle_first, 0])
+    passed = input_grad(slot, next_x, next_grad, square, returned, [*middle_first, 0])
     return passed[None, None], weight_out[None], gain_out
 
 

time: 110 us -> 109 us (level)
  no operation moved by 1% of the time
where the time goes in v8:
time: 109 us; the launch traced here: 107 us
  waiting for transfers between devices  58.6 us (54%)
  starting transfers between devices  24.1 us (22%)
  Pallas kernels  23.6 us (22%)
    ppermute x13, waiting for transfers between devices, to_partner(): return lax.ppermute(block, ('section', 'fsdp'), route)  56.8 us
    ppermute x13, starting transfers between devices, to_partner(): return lax.ppermute(block, ('section', 'fsdp'), route)  21.1 us
    pallas_call x5, Pallas kernels, staged(): pl.pallas_call(stage_kernel, in_specs=[IN_HBM], out_specs=IN_VMEM, out_sh...  5.79 us
    pallas_call x1, Pallas kernels, attention(): pl.pallas_call(functools.partial(attention_kernel, count, group, heads),...  3.42 us
    pallas_call x2, Pallas kernels, weight_grad(): pl.pallas_call(kernel, grid=(1,), in_specs=[SCALAR] + [IN_VMEM] * (3 + le...  2.59 us
    pallas_call x1, Pallas kernels, prepared(): pl.pallas_call(functools.partial(prepare_kernel, count), grid=(rows // st...  2.36 us
    pallas_call x1, Pallas kernels, gained_columns(): pl.pallas_call(functools.partial(column_kernel, count), grid_spec=pltpu.P...  2.25 us
  transfers between devices with their start and end apart: 16, of which 12 were waited for; matrix products, arithmetic and copies ran while one was open for 0% of the time, Pallas kernels for 19%

profile of v8, /device:TPU:9, one launch (start us, length us, event | category | flops | bytes accessed | tf_op | source)
XLA Modules:
  0.0 107.0 jit_solution(1452993947802010800)
XLA Ops:
  0.6 0.7 collective-permute-start.6
  1.4 0.9 collective-permute-start.7
  2.3 1.1 %shard_map.85 = (bf16[128,1024]{1,0:T(8,128)(2,1)S(1)}, bf16[128,1024]{1,0:T(8,128)(2,1)S(1)}, bf16[128,1024]{1,0:T(8,128)(2,1)S(1)}) custom-call(s32[1]{0:T(128)} %bitcast.slot_ref, bf16[128,1024]{1,0:T(8,128)(2,1)} %bitcast.15, bf16[128,4096]{1,0:T(8,128)(2,1)} %bitcast.10), custom_call_target="tpu_custom_call" | custom-call | tf_op jit(solution)/shard_map/pallas_call | solution.py:179
  3.4 0.3 collective-permute-start
  3.7 2.2 %collective-permute-start.1 = (bf16[128,1024]{1,0:T(8,128)(2,1)S(1)}, bf16[128,1024]{1,0:T(8,128)(2,1)S(1)}, u32[]{:S(2)}, u32[]{:S(2)}) collective-permute-start(bf16[128,1024]{1,0:T(8,128)(2,1)S(1)} %get-tuple-element.54), channel_id=1, source_target_pairs={{0,4},{2,6},{4,0},{6,2},{8,12},{10,14},{12,8},{14,10},{16,20},{18,... | collective-permute-start | bytes 786440 | tf_op jit(solution)/shard_map/ppermute | solution.py:36
  6.0 0.2 collective-permute-start.2
  6.1 2.4 %shard_map.86 = (f32[128,128]{1,0:T(8,128)S(1)}, bf16[128,1024]{1,0:T(8,128)(2,1)S(1)}, bf16[128,1024]{1,0:T(8,128)(2,1)S(1)}, bf16[128,1024]{1,0:T(8,128)(2,1)S(1)}) custom-call(s32[1]{0:T(128)} %bitcast.slot_ref, bf16[128,4096]{1,0:T(8,128)(2,1)} %bitcast.11), custom_call_target="tpu_custom_call" | custom-call | tf_op jit(solution)/shard_map/pallas_call | solution.py:203
  8.5 1.2 %shard_map.88.grad_ref = bf16[128,4096]{1,0:T(8,128)(2,1)S(1)} custom-call(bf16[128,4096]{1,0:T(8,128)(2,1)} %bitcast.19), custom_call_target="tpu_custom_call" | custom-call | tf_op jit(solution)/shard_map/pallas_call | solution.py:383
  9.7 0.9 shard_map.89.refs_0_
  10.7 1.2 %shard_map.87.query_ref = bf16[128,4096]{1,0:T(8,128)(2,1)S(1)} custom-call(bf16[128,4096]{1,0:T(8,128)(2,1)} %bitcast.17), custom_call_target="tpu_custom_call" | custom-call | tf_op jit(solution)/shard_map/pallas_call | solution.py:383
  11.9 1.5 %collective-permute-done.refs_1_ = bf16[128,1024]{1,0:T(8,128)(2,1)S(1)} collective-permute-done((bf16[128,1024]{1,0:T(8,128)(2,1)S(1)}, bf16[128,1024]{1,0:T(8,128)(2,1)S(1)}, u32[]{:S(2)}, u32[]{:S(2)}) %collective-permute-start) | collective-permute-done | bytes 262176 | tf_op jit(solution)/shard_map/ppermute | solution.py:36
  13.4 3.9 %collective-permute-done.1.refs_2_ = bf16[128,1024]{1,0:T(8,128)(2,1)S(1)} collective-permute-done((bf16[128,1024]{1,0:T(8,128)(2,1)S(1)}, bf16[128,1024]{1,0:T(8,128)(2,1)S(1)}, u32[]{:S(2)}, u32[]{:S(2)}) %collective-permute-start.1) | collective-permute-done | bytes 262176 | tf_op jit(solution)/shard_map/ppermute | solution.py:36
  17.3 11.1 %collective-permute-done.2.refs_3_ = bf16[128,1024]{1,0:T(8,128)(2,1)S(1)} collective-permute-done((bf16[128,1024]{1,0:T(8,128)(2,1)S(1)}, bf16[128,1024]{1,0:T(8,128)(2,1)S(1)}, u32[]{:S(2)}, u32[]{:S(2)}) %collective-permute-start.2) | collective-permute-done | bytes 262176 | tf_op jit(solution)/shard_map/ppermute | solution.py:36
  28.5 3.4 %shard_map.90 = (bf16[128,1024]{1,0:T(8,128)(2,1)S(1)}, bf16[128,1024]{1,0:T(8,128)(2,1)S(1)}, bf16[128,1024]{1,0:T(8,128)(2,1)S(1)}, bf16[128,1024]{1,0:T(8,128...) custom-call(s32[1]{0:T(128)} %bitcast.slot_ref, ...), custom_call_target="tpu_custom_call" | custom-call | tf_op jit(solution)/shard_map/pallas_call | solution.py:132
  31.9 0.1 collective-permute-start.3
  32.0 2.2 %collective-permute-start.4 = (bf16[128,1024]{1,0:T(8,128)(2,1)S(1)}, bf16[128,1024]{1,0:T(8,128)(2,1)S(1)}, u32[]{:S(2)}, u32[]{:S(2)}) collective-permute-start(bf16[128,1024]{1,0:T(8,128)(2,1)S(1)} %get-tuple-element.72), channel_id=1, source_target_pairs={{0,2},{2,0},{4,6},{6,4},{8,10},{10,8},{12,14},{14,12},{16,18},{18,... | collective-permute-start | bytes 786440 | tf_op jit(solution)/shard_map/ppermute | solution.py:36
  34.1 0.5 collective-permute-start.5
  34.6 0.0 collective-permute-done.6.x_ref
  34.6 0.0 collective-permute-done.7.grad_ref
  34.6 1.9 %shard_map.91 = (bf16[128,4096]{1,0:T(8,128)(2,1)}, bf16[128,4096]{1,0:T(8,128)(2,1)}, f32[128,128]{1,0:T(8,128)}) custom-call(bf16[128,4096]{1,0:T(8,128)(2,1)S(1)} %collective-permute-done.6.x_ref, bf16[128,4096]{1,0:T(8,128)(2,1)S(1)} %collective-permute-done.7.grad_ref), custom_call_target="tpu_custom_call" | custom-call | tf_op jit(solution)/shard_map/pallas_call | solution.py:255
  36.6 3.9 %collective-permute-done.3.refs_1_ = bf16[128,1024]{1,0:T(8,128)(2,1)S(1)} collective-permute-done((bf16[128,1024]{1,0:T(8,128)(2,1)S(1)}, bf16[128,1024]{1,0:T(8,128)(2,1)S(1)}, u32[]{:S(2)}, u32[]{:S(2)}) %collective-permute-start.3) | collective-permute-done | bytes 262176 | tf_op jit(solution)/shard_map/ppermute | solution.py:36
  40.5 3.9 %collective-permute-done.4.refs_0_ = bf16[128,1024]{1,0:T(8,128)(2,1)S(1)} collective-permute-done((bf16[128,1024]{1,0:T(8,128)(2,1)S(1)}, bf16[128,1024]{1,0:T(8,128)(2,1)S(1)}, u32[]{:S(2)}, u32[]{:S(2)}) %collective-permute-start.4) | collective-permute-done | bytes 262176 | tf_op jit(solution)/shard_map/ppermute | solution.py:36
  44.4 10.8 %collective-permute-done.5.refs_2_ = bf16[128,1024]{1,0:T(8,128)(2,1)S(1)} collective-permute-done((bf16[128,1024]{1,0:T(8,128)(2,1)S(1)}, bf16[128,1024]{1,0:T(8,128)(2,1)S(1)}, u32[]{:S(2)}, u32[]{:S(2)}) %collective-permute-start.5) | collective-permute-done | bytes 262176 | tf_op jit(solution)/shard_map/ppermute | solution.py:36
  55.1 0.9 shard_map.92
  56.1 0.1 collective-permute-start.8
  56.2 0.1 collective-permute-start.9
  56.3 2.6 %collective-permute-start.10 = (bf16[128,1024]{1,0:T(8,128)(2,1)S(1)}, bf16[128,1024]{1,0:T(8,128)(2,1)S(1)}, u32[]{:S(2)}, u32[]{:S(2)}) collective-permute-start(bf16[128,1024]{1,0:T(8,128)(2,1)S(1)} %get-tuple-element.80.refs_0_), channel_id=1, source_target_pairs={{0,2},{2,0},{4,6},{6,4},{8,10},{10,8},{12,14},{14,12},{16,18},{18,... | collective-permute-start | bytes 786440 | tf_op jit(solution)/shard_map/ppermute | solution.py:36
  58.8 1.7 %shard_map.94.weight_ref = bf16[1024,1024]{1,0:T(8,128)(2,1)S(1)} custom-call(bf16[1024,1024]{1,0:T(8,128)(2,1)} %bitcast.13), custom_call_target="tpu_custom_call" | custom-call | tf_op jit(solution)/shard_map/pallas_call | solution.py:383
  60.5 0.7 shard_map.95.gain_ref
  61.3 2.3 %shard_map.93.columns_ref = bf16[1024,512]{1,0:T(8,128)(2,1)S(1)} custom-call(s32[1]{0:T(128)} %bitcast.slot_ref, bf16[1,1024]{1,0:T(2,128)(2,1)} %in_ref.1, bf16[128,4096]{1,0:T(8,128)(2,1)} %bitcast.12, bf16[128,1024]{1,0:T(8,128)(2,1)S(1)} %copy-done.2, bf16[128,1024]{1,0:T(8,128)(2,1)S(1)} %copy-done.3, bf16[128,1024]{1,0:T(8,128)(2,1)S(1)} %copy-done.4, ...), custom_call_target="tpu_custom_call" | custom-call | tf_op jit(solution)/shard_map/pallas_call | solution.py:285
  63.5 4.1 %collective-permute-done.8.refs_3_ = bf16[128,1024]{1,0:T(8,128)(2,1)S(1)} collective-permute-done((bf16[128,1024]{1,0:T(8,128)(2,1)S(1)}, bf16[128,1024]{1,0:T(8,128)(2,1)S(1)}, u32[]{:S(2)}, u32[]{:S(2)}) %collective-permute-start.8) | collective-permute-done | bytes 262176 | tf_op jit(solution)/shard_map/ppermute | solution.py:36
  67.6 2.1 %collective-permute-done.9.refs_2_ = bf16[128,1024]{1,0:T(8,128)(2,1)S(1)} collective-permute-done((bf16[128,1024]{1,0:T(8,128)(2,1)S(1)}, bf16[128,1024]{1,0:T(8,128)(2,1)S(1)}, u32[]{:S(2)}, u32[]{:S(2)}) %collective-permute-start.9) | collective-permute-done | bytes 262176 | tf_op jit(solution)/shard_map/ppermute | solution.py:36
  69.7 0.0 collective-permute-done.10.refs_1_
  69.7 0.8 shard_map.96
  70.5 1.3 %collective-permute-start.11 = (bf16[528,1024]{1,0:T(8,128)(2,1)S(1)}, bf16[528,1024]{1,0:T(8,128)(2,1)S(1)}, u32[]{:S(2)}, u32[]{:S(2)}) collective-permute-start(bf16[528,1024]{1,0:T(8,128)(2,1)S(1)} %shard_map.96), channel_id=1, source_target_pairs={{0,1},{1,0},{2,3},{3,2},{4,5},{5,4},{6,7},{7,6},{8,9},{9,8},{10,11... | collective-permute-start | bytes 3244040 | tf_op jit(solution)/shard_map/ppermute | solution.py:470
  71.8 1.3 %shard_map.98 = (bf16[128,1024]{1,0:T(8,128)(2,1)S(1)}, bf16[128,1024]{1,0:T(8,128)(2,1)S(1)}, bf16[128,1024]{1,0:T(8,128)(2,1)S(1)}, bf16[128,1024]{1,0:T(8,128)(2,1)S(1)}) custom-call(bf16[1024,1024]{1,0:T(8,128)(2,1)S(1)} %shard_map.94.weight_ref, bf16[1,1024]{1,0:T(2,128)(2,1)S(1)} %shard_map.95.gain_ref, ...), custom_call_target="tpu_custom_call" | custom-call | tf_op jit(solution)/shard_map/pallas_call | solution.py:317
  73.1 11.4 %collective-permute-start.12 = (bf16[128,1024]{1,0:T(8,128)(2,1)S(1)}, bf16[128,1024]{1,0:T(8,128)(2,1)S(1)}, u32[]{:S(2)}, u32[]{:S(2)}) collective-permute-start(bf16[128,1024]{1,0:T(8,128)(2,1)S(1)} %get-tuple-element.98), channel_id=1, source_target_pairs={{0,28},{2,30},{4,24},{6,26},{8,4},{10,6},{12,0},{14,2},{16,12},{18... | collective-permute-start | bytes 786440 | tf_op jit(solution)/shard_map/ppermute | solution.py:36
  84.5 0.0 collective-permute-start.13
  84.5 0.0 collective-permute-start.14
  84.6 1.5 %collective-permute-start.15 = (bf16[128,1024]{1,0:T(8,128)(2,1)S(1)}, bf16[128,1024]{1,0:T(8,128)(2,1)S(1)}, u32[]{:S(2)}, u32[]{:S(2)}) collective-permute-start(bf16[128,1024]{1,0:T(8,128)(2,1)S(1)} %get-tuple-element.101), channel_id=1, source_target_pairs={{0,24},{2,26},{4,28},{6,30},{8,0},{10,2},{12,4},{14,6},{16,8},{18,... | collective-permute-start | bytes 786440 | tf_op jit(solution)/shard_map/ppermute | solution.py:36
  86.1 1.7 %collective-permute-done.11.got_ref = bf16[528,1024]{1,0:T(8,128)(2,1)S(1)} collective-permute-done((bf16[528,1024]{1,0:T(8,128)(2,1)S(1)}, bf16[528,1024]{1,0:T(8,128)(2,1)S(1)}, u32[]{:S(2)}, u32[]{:S(2)}) %collective-permute-start.11) | collective-permute-done | bytes 1081376 | tf_op jit(solution)/shard_map/ppermute | solution.py:470
  87.8 1.8 %shard_map.97 = (bf16[512,1024]{1,0:T(8,128)(2,1)}, f32[1,512]{1,0:T(1,128)}) custom-call(s32[1]{0:T(128)} %bitcast.1.half_ref, bf16[1024,1024]{1,0:T(8,128)(2,1)S(1)} %shard_map.94.weight_ref, bf16[1,1024]{1,0:T(2,128)(2,1)S(1)} %shard_map.95.gain_ref, bf16[1024,512]{1,0:T(8,128)(2,1)S(1)} %shard_map.93.columns_ref, ...), custom_call_target="tpu_custom_call" | custom-call | tf_op jit(solution)/shard_map/pallas_call | solution.py:368
  89.6 6.3 %collective-permute-done.12.refs_0_ = bf16[128,1024]{1,0:T(8,128)(2,1)S(1)} collective-permute-done((bf16[128,1024]{1,0:T(8,128)(2,1)S(1)}, bf16[128,1024]{1,0:T(8,128)(2,1)S(1)}, u32[]{:S(2)}, u32[]{:S(2)}) %collective-permute-start.12) | collective-permute-done | bytes 262176 | tf_op jit(solution)/shard_map/ppermute | solution.py:36
  95.9 1.1 collective-permute-done.13.refs_1_
  97.0 8.1 %collective-permute-done.14.refs_2_ = bf16[128,1024]{1,0:T(8,128)(2,1)S(1)} collective-permute-done((bf16[128,1024]{1,0:T(8,128)(2,1)S(1)}, bf16[128,1024]{1,0:T(8,128)(2,1)S(1)}, u32[]{:S(2)}, u32[]{:S(2)}) %collective-permute-start.14) | collective-permute-done | bytes 262176 | tf_op jit(solution)/shard_map/ppermute | solution.py:36
  105.1 0.0 collective-permute-done.15.refs_3_
  105.1 0.0 copy-done.1
  105.1 1.9 %shard_map.99 = bf16[128,4096]{1,0:T(8,128)(2,1)} custom-call(s32[1]{0:T(128)} %bitcast.slot_ref, bf16[128,4096]{1,0:T(8,128)(2,1)S(1)} %copy-done, bf16[128,4096]{1,0:T(8,128)(2,1)S(1)} %copy-done.1, f32[128,128]{1,0:T(8,128)S(1)} %copy-done.8, bf16[128,1024]{1,0:T(8,128)(2,1)S(1)} %collective-permute-done.12.refs_0_, ...), custom_call_target="tpu_custom_call" | custom-call | tf_op jit(solution)/shard_map/pallas_call | solution.py:417
  (17 shorter events, 0.0 us)
Async XLA Ops:
  0.6 34.0 %collective-permute-start.6 = (bf16[128,4096]{1,0:T(8,128)(2,1)}, bf16[128,4096]{1,0:T(8,128)(2,1)S(1)}, u32[]{:S(2)}, u32[]{:S(2)}) collective-permute-start(bf16[128,4096]{1,0:T(8,128)(2,1)} %bitcast.9), channel_id=1, source_target_pairs={{0,24},{8,0},{16,8},{24,16},{1,25},{9,1},{17,9},{25,17},{2,26},{10... | collective-permute-start | bytes 3145736 | tf_op jit(solution)/shard_map/ppermute | solution.py:442
  1.4 33.3 %collective-permute-start.7 = (bf16[128,4096]{1,0:T(8,128)(2,1)}, bf16[128,4096]{1,0:T(8,128)(2,1)S(1)}, u32[]{:S(2)}, u32[]{:S(2)}) collective-permute-start(bf16[128,4096]{1,0:T(8,128)(2,1)} %bitcast.18), channel_id=1, source_target_pairs={{0,24},{8,0},{16,8},{24,16},{1,25},{9,1},{17,9},{25,17},{2,26},{10... | collective-permute-start | bytes 3145736 | tf_op jit(solution)/shard_map/ppermute | solution.py:443
  3.4 10.0 %collective-permute-start = (bf16[128,1024]{1,0:T(8,128)(2,1)S(1)}, bf16[128,1024]{1,0:T(8,128)(2,1)S(1)}, u32[]{:S(2)}, u32[]{:S(2)}) collective-permute-start(bf16[128,1024]{1,0:T(8,128)(2,1)S(1)} %get-tuple-element.53), channel_id=1, source_target_pairs={{0,2},{2,0},{4,6},{6,4},{8,10},{10,8},{12,14},{14,12},{16,18},{18,... | collective-permute-start | bytes 786440 | tf_op jit(solution)/shard_map/ppermute | solution.py:36
  3.7 13.6 %collective-permute-start.1 = (bf16[128,1024]{1,0:T(8,128)(2,1)S(1)}, bf16[128,1024]{1,0:T(8,128)(2,1)S(1)}, u32[]{:S(2)}, u32[]{:S(2)}) collective-permute-start(bf16[128,1024]{1,0:T(8,128)(2,1)S(1)} %get-tuple-element.54), channel_id=1, source_target_pairs={{0,4},{2,6},{4,0},{6,2},{8,12},{10,14},{12,8},{14,10},{16,20},{18,... | collective-permute-start | bytes 786440 | tf_op jit(solution)/shard_map/ppermute | solution.py:36
  6.0 22.5 %collective-permute-start.2 = (bf16[128,1024]{1,0:T(8,128)(2,1)S(1)}, bf16[128,1024]{1,0:T(8,128)(2,1)S(1)}, u32[]{:S(2)}, u32[]{:S(2)}) collective-permute-start(bf16[128,1024]{1,0:T(8,128)(2,1)S(1)} %get-tuple-element.55), channel_id=1, source_target_pairs={{0,6},{2,4},{4,2},{6,0},{8,14},{10,12},{12,10},{14,8},{16,22},{18,... | collective-permute-start | bytes 786440 | tf_op jit(solution)/shard_map/ppermute | solution.py:36
  31.9 8.6 %collective-permute-start.3 = (bf16[128,1024]{1,0:T(8,128)(2,1)S(1)}, bf16[128,1024]{1,0:T(8,128)(2,1)S(1)}, u32[]{:S(2)}, u32[]{:S(2)}) collective-permute-start(bf16[128,1024]{1,0:T(8,128)(2,1)S(1)} %get-tuple-element.71), channel_id=1, source_target_pairs={{0,4},{2,6},{4,0},{6,2},{8,12},{10,14},{12,8},{14,10},{16,20},{18,... | collective-permute-start | bytes 786440 | tf_op jit(solution)/shard_map/ppermute | solution.py:36
  32.0 12.4 %collective-permute-start.4 = (bf16[128,1024]{1,0:T(8,128)(2,1)S(1)}, bf16[128,1024]{1,0:T(8,128)(2,1)S(1)}, u32[]{:S(2)}, u32[]{:S(2)}) collective-permute-start(bf16[128,1024]{1,0:T(8,128)(2,1)S(1)} %get-tuple-element.72), channel_id=1, source_target_pairs={{0,2},{2,0},{4,6},{6,4},{8,10},{10,8},{12,14},{14,12},{16,18},{18,... | collective-permute-start | bytes 786440 | tf_op jit(solution)/shard_map/ppermute | solution.py:36
  34.1 21.0 %collective-permute-start.5 = (bf16[128,1024]{1,0:T(8,128)(2,1)S(1)}, bf16[128,1024]{1,0:T(8,128)(2,1)S(1)}, u32[]{:S(2)}, u32[]{:S(2)}) collective-permute-start(bf16[128,1024]{1,0:T(8,128)(2,1)S(1)} %get-tuple-element.73), channel_id=1, source_target_pairs={{0,6},{2,4},{4,2},{6,0},{8,14},{10,12},{12,10},{14,8},{16,22},{18,... | collective-permute-start | bytes 786440 | tf_op jit(solution)/shard_map/ppermute | solution.py:36
  56.1 11.5 %collective-permute-start.8 = (bf16[128,1024]{1,0:T(8,128)(2,1)S(1)}, bf16[128,1024]{1,0:T(8,128)(2,1)S(1)}, u32[]{:S(2)}, u32[]{:S(2)}) collective-permute-start(bf16[128,1024]{1,0:T(8,128)(2,1)S(1)} %get-tuple-element.80.refs_0_), channel_id=1, source_target_pairs={{0,6},{2,4},{4,2},{6,0},{8,14},{10,12},{12,10},{14,8},{16,22},{18,... | collective-permute-start | bytes 786440 | tf_op jit(solution)/shard_map/ppermute | solution.py:36
  56.2 13.5 %collective-permute-start.9 = (bf16[128,1024]{1,0:T(8,128)(2,1)S(1)}, bf16[128,1024]{1,0:T(8,128)(2,1)S(1)}, u32[]{:S(2)}, u32[]{:S(2)}) collective-permute-start(bf16[128,1024]{1,0:T(8,128)(2,1)S(1)} %get-tuple-element.80.refs_0_), channel_id=1, source_target_pairs={{0,4},{2,6},{4,0},{6,2},{8,12},{10,14},{12,8},{14,10},{16,20},{18,... | collective-permute-start | bytes 786440 | tf_op jit(solution)/shard_map/ppermute | solution.py:36
  56.3 13.5 %collective-permute-start.10 = (bf16[128,1024]{1,0:T(8,128)(2,1)S(1)}, bf16[128,1024]{1,0:T(8,128)(2,1)S(1)}, u32[]{:S(2)}, u32[]{:S(2)}) collective-permute-start(bf16[128,1024]{1,0:T(8,128)(2,1)S(1)} %get-tuple-element.80.refs_0_), channel_id=1, source_target_pairs={{0,2},{2,0},{4,6},{6,4},{8,10},{10,8},{12,14},{14,12},{16,18},{18,... | collective-permute-start | bytes 786440 | tf_op jit(solution)/shard_map/ppermute | solution.py:36
  58.8 2.4 %copy-start.2 = (bf16[128,1024]{1,0:T(8,128)(2,1)S(1)}, bf16[128,1024]{1,0:T(8,128)(2,1)}, u32[]{:S(2)}) copy-start(bf16[128,1024]{1,0:T(8,128)(2,1)} %get-tuple-element.81.refs_0_) | copy-start | bytes 786436
  58.8 2.4 %copy-start.3 = (bf16[128,1024]{1,0:T(8,128)(2,1)S(1)}, bf16[128,1024]{1,0:T(8,128)(2,1)}, u32[]{:S(2)}) copy-start(bf16[128,1024]{1,0:T(8,128)(2,1)} %get-tuple-element.82.refs_1_) | copy-start | bytes 786436
  58.8 2.4 %copy-start.4 = (bf16[128,1024]{1,0:T(8,128)(2,1)S(1)}, bf16[128,1024]{1,0:T(8,128)(2,1)}, u32[]{:S(2)}) copy-start(bf16[128,1024]{1,0:T(8,128)(2,1)} %get-tuple-element.83.refs_2_) | copy-start | bytes 786436
  58.8 2.4 %copy-start.5 = (bf16[128,1024]{1,0:T(8,128)(2,1)S(1)}, bf16[128,1024]{1,0:T(8,128)(2,1)}, u32[]{:S(2)}) copy-start(bf16[128,1024]{1,0:T(8,128)(2,1)} %get-tuple-element.84.refs_3_) | copy-start | bytes 786436
  58.8 2.4 %copy-start.6 = (bf16[128,1024]{1,0:T(8,128)(2,1)S(1)}, bf16[128,1024]{1,0:T(8,128)(2,1)}, u32[]{:S(2)}) copy-start(bf16[128,1024]{1,0:T(8,128)(2,1)} %get-tuple-element.85.refs_4_) | copy-start | bytes 786436
  58.8 2.4 %copy-start.7 = (bf16[128,1024]{1,0:T(8,128)(2,1)S(1)}, bf16[128,1024]{1,0:T(8,128)(2,1)}, u32[]{:S(2)}) copy-start(bf16[128,1024]{1,0:T(8,128)(2,1)} %get-tuple-element.86.refs_5_) | copy-start | bytes 786436
  70.5 17.3 %collective-permute-start.11 = (bf16[528,1024]{1,0:T(8,128)(2,1)S(1)}, bf16[528,1024]{1,0:T(8,128)(2,1)S(1)}, u32[]{:S(2)}, u32[]{:S(2)}) collective-permute-start(bf16[528,1024]{1,0:T(8,128)(2,1)S(1)} %shard_map.96), channel_id=1, source_target_pairs={{0,1},{1,0},{2,3},{3,2},{4,5},{5,4},{6,7},{7,6},{8,9},{9,8},{10,11... | collective-permute-start | bytes 3244040 | tf_op jit(solution)/shard_map/ppermute | solution.py:470
  73.1 22.8 %collective-permute-start.12 = (bf16[128,1024]{1,0:T(8,128)(2,1)S(1)}, bf16[128,1024]{1,0:T(8,128)(2,1)S(1)}, u32[]{:S(2)}, u32[]{:S(2)}) collective-permute-start(bf16[128,1024]{1,0:T(8,128)(2,1)S(1)} %get-tuple-element.98), channel_id=1, source_target_pairs={{0,28},{2,30},{4,24},{6,26},{8,4},{10,6},{12,0},{14,2},{16,12},{18... | collective-permute-start | bytes 786440 | tf_op jit(solution)/shard_map/ppermute | solution.py:36
  84.5 12.5 %collective-permute-start.13 = (bf16[128,1024]{1,0:T(8,128)(2,1)S(1)}, bf16[128,1024]{1,0:T(8,128)(2,1)S(1)}, u32[]{:S(2)}, u32[]{:S(2)}) collective-permute-start(bf16[128,1024]{1,0:T(8,128)(2,1)S(1)} %get-tuple-element.99), channel_id=1, source_target_pairs={{0,26},{2,24},{4,30},{6,28},{8,2},{10,0},{12,6},{14,4},{16,10},{18... | collective-permute-start | bytes 786440 | tf_op jit(solution)/shard_map/ppermute | solution.py:36
  84.5 20.6 %collective-permute-start.14 = (bf16[128,1024]{1,0:T(8,128)(2,1)S(1)}, bf16[128,1024]{1,0:T(8,128)(2,1)S(1)}, u32[]{:S(2)}, u32[]{:S(2)}) collective-permute-start(bf16[128,1024]{1,0:T(8,128)(2,1)S(1)} %get-tuple-element.100), channel_id=1, source_target_pairs={{0,30},{2,28},{4,26},{6,24},{8,6},{10,4},{12,2},{14,0},{16,14},{18... | collective-permute-start | bytes 786440 | tf_op jit(solution)/shard_map/ppermute | solution.py:36
  84.5 20.6 %copy-start = (bf16[128,4096]{1,0:T(8,128)(2,1)S(1)}, bf16[128,4096]{1,0:T(8,128)(2,1)}, u32[]{:S(2)}) copy-start(bf16[128,4096]{1,0:T(8,128)(2,1)} %get-tuple-element.95.x_ref) | copy-start | bytes 3145732
  84.6 20.6 %copy-start.1 = (bf16[128,4096]{1,0:T(8,128)(2,1)S(1)}, bf16[128,4096]{1,0:T(8,128)(2,1)}, u32[]{:S(2)}) copy-start(bf16[128,4096]{1,0:T(8,128)(2,1)} %get-tuple-element.96.grad_ref) | copy-start | bytes 3145732
  84.6 20.6 %copy-start.8 = (f32[128,128]{1,0:T(8,128)S(1)}, f32[128,128]{1,0:T(8,128)}, u32[]{:S(2)}) copy-start(f32[128,128]{1,0:T(8,128)} %get-tuple-element.97.square_ref) | copy-start | bytes 196612
  84.6 20.6 %collective-permute-start.15 = (bf16[128,1024]{1,0:T(8,128)(2,1)S(1)}, bf16[128,1024]{1,0:T(8,128)(2,1)S(1)}, u32[]{:S(2)}, u32[]{:S(2)}) collective-permute-start(bf16[128,1024]{1,0:T(8,128)(2,1)S(1)} %get-tuple-element.101), channel_id=1, source_target_pairs={{0,24},{2,26},{4,28},{6,30},{8,0},{10,2},{12,4},{14,6},{16,8},{18,... | collective-permute-start | bytes 786440 | tf_op jit(solution)/shard_map/ppermute | solution.py:36

commit v9 on v8

--- a/solution.py
+++ b/solution.py
@@ -375,6 +375,28 @@
     )(half, weight, gain, columns, *extra, *values)
 
 
+def turn_kernel(count, half_ref, weight_ref, gain_ref, columns_ref, *refs):
+    value_refs, out_refs = refs[:count], refs[count:]
+    feature_kernel(count, weight_ref, gain_ref, *value_refs, *out_refs[:count])
+    sent_kernel(half_ref, weight_ref, gain_ref, columns_ref, *value_refs, out_refs[count])
+
+
+def turned(half, halves, weight, gain, columns, values):
+    count = len(values)
+    rows, kv_width = values[0].shape
+    width = weight.shape[0]
+    message = (width // halves + TILE, kv_width)
+    out = pl.pallas_call(
+        functools.partial(turn_kernel, count),
+        in_specs=[SCALAR] + [IN_VMEM] * (count + 3),
+        out_specs=[IN_VMEM] * (count + 1),
+        out_shape=[pltpu.VMEM((rows, width), jnp.bfloat16)] * count
+        + [pltpu.VMEM(message, jnp.bfloat16)],
+        compiler_params=PARAMS,
+    )(half, weight, gain, columns, *values)
+    return out[:count], out[count]
+
+
 def stage_kernel(in_ref, out_ref):
     pltpu.sync_copy(in_ref, out_ref)
 
@@ -433,7 +455,7 @@
     weight = w_value[0]
     assert MEM <= x.shape[0] and docs == 2 and count & (count - 1) == 0
     masks = range(1, count)
-    middle_first, far_first = [*masks[1:2], 1, *masks[2:]], masks[::-1]
+    middle_first, gather_order = [*masks[1:2], 1, *masks[2:]], list(masks)
 
     swap = [(0, 1), (1, 0)]
 
@@ -460,12 +482,11 @@
     columns = gained_columns(slot, gain, x, first, second)
     weight, held_gain = staged(weight), staged(gain)
     others, columns, weight, held_gain = after(
-        ([values[m] for m in far_first], columns, weight, held_gain), ()
+        ([values[m] for m in gather_order], columns, weight, held_gain), ()
     )
-    values = [value] + [others[far_first.index(m)] for m in masks]
-
-    sent = weight_grad(1 - half, docs, weight, held_gain, columns, values)
-    scaled = feature_grads(weight, held_gain, values)
+    values = [value] + [others[gather_order.index(m)] for m in masks]
+
+    scaled, sent = turned(1 - half, docs, weight, held_gain, columns, values)
     returned = [to_partner(scaled[m], m, below=True) for m in range(count)]
     got = lax.ppermute(sent, "dp", swap)
     weight_out, gain_out = weight_grad(half, docs, weight, held_gain, columns, values, got)

time: 109 us -> 108 us (level)
    ppermute x13, waiting for transfers between devices: 56.8 us -> 55.2 us  [to_partner(): return lax.ppermute(block, ('section', 'fsdp'), route)]
    ppermute x1, waiting for transfers between devices: 1.71 us -> 3.01 us  [per_device(): got = lax.ppermute(sent, 'dp', swap)]
    pallas_call x2 -> x1, Pallas kernels: 2.59 us -> 1.8 us  [weight_grad(): pl.pallas_call(kernel, grid=(1,), in_specs=[SCALAR] + [IN_VMEM] * (3 + le...]
  transfers between devices with their start and end apart: 16 -> 16, of which waited for: 12 -> 12; matrix products, arithmetic and copies ran while one was open for 0% -> 0% of each run, Pallas kernels for 19% -> 17%
where the time goes in v9:
time: 108 us; the launch traced here: 107 us
  waiting for transfers between devices  58.3 us (54%)
  starting transfers between devices  24 us (22%)
  Pallas kernels  23.4 us (22%)
    ppermute x13, waiting for transfers between devices, to_partner(): return lax.ppermute(block, ('section', 'fsdp'), route)  55.2 us
    ppermute x13, starting transfers between devices, to_partner(): return lax.ppermute(block, ('section', 'fsdp'), route)  21 us
    pallas_call x5, Pallas kernels, staged(): pl.pallas_call(stage_kernel, in_specs=[IN_HBM], out_specs=IN_VMEM, out_sh...  5.79 us
    pallas_call x1, Pallas kernels, attention(): pl.pallas_call(functools.partial(attention_kernel, count, group, heads),...  3.4 us
    ppermute x1, waiting for transfers between devices, per_device(): got = lax.ppermute(sent, 'dp', swap)  3.01 us
    pallas_call x1, Pallas kernels, prepared(): pl.pallas_call(functools.partial(prepare_kernel, count), grid=(rows // st...  2.36 us
    pallas_call x1, Pallas kernels, gained_columns(): pl.pallas_call(functools.partial(column_kernel, count), grid_spec=pltpu.P...  2.23 us
  transfers between devices with their start and end apart: 16, of which 12 were waited for; matrix products, arithmetic and copies ran while one was open for 0% of the time, Pallas kernels for 17%

profile of v9, /device:TPU:9, one launch (start us, length us, event | category | flops | bytes accessed | tf_op | source)
XLA Modules:
  0.0 106.6 jit_solution(12233289960061008658)
XLA Ops:
  0.6 0.7 collective-permute-start.6
  1.4 0.9 collective-permute-start.7
  2.3 1.1 %shard_map.85 = (bf16[128,1024]{1,0:T(8,128)(2,1)S(1)}, bf16[128,1024]{1,0:T(8,128)(2,1)S(1)}, bf16[128,1024]{1,0:T(8,128)(2,1)S(1)}) custom-call(s32[1]{0:T(128)} %bitcast.slot_ref, bf16[128,1024]{1,0:T(8,128)(2,1)} %bitcast.15, bf16[128,4096]{1,0:T(8,128)(2,1)} %bitcast.10), custom_call_target="tpu_custom_call" | custom-call | tf_op jit(solution)/shard_map/pallas_call | solution.py:179
  3.4 0.3 collective-permute-start
  3.7 2.2 %collective-permute-start.1 = (bf16[128,1024]{1,0:T(8,128)(2,1)S(1)}, bf16[128,1024]{1,0:T(8,128)(2,1)S(1)}, u32[]{:S(2)}, u32[]{:S(2)}) collective-permute-start(bf16[128,1024]{1,0:T(8,128)(2,1)S(1)} %get-tuple-element.55), channel_id=1, source_target_pairs={{0,4},{2,6},{4,0},{6,2},{8,12},{10,14},{12,8},{14,10},{16,20},{18,... | collective-permute-start | bytes 786440 | tf_op jit(solution)/shard_map/ppermute | solution.py:36
  6.0 0.2 collective-permute-start.2
  6.1 0.9 shard_map.89.refs_0_
  7.1 2.4 %shard_map.86 = (f32[128,128]{1,0:T(8,128)S(1)}, bf16[128,1024]{1,0:T(8,128)(2,1)S(1)}, bf16[128,1024]{1,0:T(8,128)(2,1)S(1)}, bf16[128,1024]{1,0:T(8,128)(2,1)S(1)}) custom-call(s32[1]{0:T(128)} %bitcast.slot_ref, bf16[128,4096]{1,0:T(8,128)(2,1)} %bitcast.11), custom_call_target="tpu_custom_call" | custom-call | tf_op jit(solution)/shard_map/pallas_call | solution.py:203
  9.5 1.2 %shard_map.88.grad_ref = bf16[128,4096]{1,0:T(8,128)(2,1)S(1)} custom-call(bf16[128,4096]{1,0:T(8,128)(2,1)} %bitcast.19), custom_call_target="tpu_custom_call" | custom-call | tf_op jit(solution)/shard_map/pallas_call | solution.py:405
  10.7 1.2 %shard_map.87.query_ref = bf16[128,4096]{1,0:T(8,128)(2,1)S(1)} custom-call(bf16[128,4096]{1,0:T(8,128)(2,1)} %bitcast.17), custom_call_target="tpu_custom_call" | custom-call | tf_op jit(solution)/shard_map/pallas_call | solution.py:405
  11.9 1.5 %collective-permute-done.refs_1_ = bf16[128,1024]{1,0:T(8,128)(2,1)S(1)} collective-permute-done((bf16[128,1024]{1,0:T(8,128)(2,1)S(1)}, bf16[128,1024]{1,0:T(8,128)(2,1)S(1)}, u32[]{:S(2)}, u32[]{:S(2)}) %collective-permute-start) | collective-permute-done | bytes 262176 | tf_op jit(solution)/shard_map/ppermute | solution.py:36
  13.4 3.9 %collective-permute-done.1.refs_2_ = bf16[128,1024]{1,0:T(8,128)(2,1)S(1)} collective-permute-done((bf16[128,1024]{1,0:T(8,128)(2,1)S(1)}, bf16[128,1024]{1,0:T(8,128)(2,1)S(1)}, u32[]{:S(2)}, u32[]{:S(2)}) %collective-permute-start.1) | collective-permute-done | bytes 262176 | tf_op jit(solution)/shard_map/ppermute | solution.py:36
  17.3 11.1 %collective-permute-done.2.refs_3_ = bf16[128,1024]{1,0:T(8,128)(2,1)S(1)} collective-permute-done((bf16[128,1024]{1,0:T(8,128)(2,1)S(1)}, bf16[128,1024]{1,0:T(8,128)(2,1)S(1)}, u32[]{:S(2)}, u32[]{:S(2)}) %collective-permute-start.2) | collective-permute-done | bytes 262176 | tf_op jit(solution)/shard_map/ppermute | solution.py:36
  28.5 3.4 %shard_map.90 = (bf16[128,1024]{1,0:T(8,128)(2,1)S(1)}, bf16[128,1024]{1,0:T(8,128)(2,1)S(1)}, bf16[128,1024]{1,0:T(8,128)(2,1)S(1)}, bf16[128,1024]{1,0:T(8,128...) custom-call(s32[1]{0:T(128)} %bitcast.slot_ref, ...), custom_call_target="tpu_custom_call" | custom-call | tf_op jit(solution)/shard_map/pallas_call | solution.py:132
  31.9 0.1 collective-permute-start.3
  32.0 2.1 %collective-permute-start.4 = (bf16[128,1024]{1,0:T(8,128)(2,1)S(1)}, bf16[128,1024]{1,0:T(8,128)(2,1)S(1)}, u32[]{:S(2)}, u32[]{:S(2)}) collective-permute-start(bf16[128,1024]{1,0:T(8,128)(2,1)S(1)} %get-tuple-element.73), channel_id=1, source_target_pairs={{0,2},{2,0},{4,6},{6,4},{8,10},{10,8},{12,14},{14,12},{16,18},{18,... | collective-permute-start | bytes 786440 | tf_op jit(solution)/shard_map/ppermute | solution.py:36
  34.1 0.5 collective-permute-start.5
  34.6 0.0 collective-permute-done.6.x_ref
  34.6 0.0 collective-permute-done.7.grad_ref
  34.6 1.9 %shard_map.91 = (bf16[128,4096]{1,0:T(8,128)(2,1)}, bf16[128,4096]{1,0:T(8,128)(2,1)}, f32[128,128]{1,0:T(8,128)}) custom-call(bf16[128,4096]{1,0:T(8,128)(2,1)S(1)} %collective-permute-done.6.x_ref, bf16[128,4096]{1,0:T(8,128)(2,1)S(1)} %collective-permute-done.7.grad_ref), custom_call_target="tpu_custom_call" | custom-call | tf_op jit(solution)/shard_map/pallas_call | solution.py:255
  36.5 4.1 %collective-permute-done.3.refs_1_ = bf16[128,1024]{1,0:T(8,128)(2,1)S(1)} collective-permute-done((bf16[128,1024]{1,0:T(8,128)(2,1)S(1)}, bf16[128,1024]{1,0:T(8,128)(2,1)S(1)}, u32[]{:S(2)}, u32[]{:S(2)}) %collective-permute-start.3) | collective-permute-done | bytes 262176 | tf_op jit(solution)/shard_map/ppermute | solution.py:36
  40.7 3.6 %collective-permute-done.4.refs_0_ = bf16[128,1024]{1,0:T(8,128)(2,1)S(1)} collective-permute-done((bf16[128,1024]{1,0:T(8,128)(2,1)S(1)}, bf16[128,1024]{1,0:T(8,128)(2,1)S(1)}, u32[]{:S(2)}, u32[]{:S(2)}) %collective-permute-start.4) | collective-permute-done | bytes 262176 | tf_op jit(solution)/shard_map/ppermute | solution.py:36
  44.3 10.7 %collective-permute-done.5.refs_2_ = bf16[128,1024]{1,0:T(8,128)(2,1)S(1)} collective-permute-done((bf16[128,1024]{1,0:T(8,128)(2,1)S(1)}, bf16[128,1024]{1,0:T(8,128)(2,1)S(1)}, u32[]{:S(2)}, u32[]{:S(2)}) %collective-permute-start.5) | collective-permute-done | bytes 262176 | tf_op jit(solution)/shard_map/ppermute | solution.py:36
  55.0 0.9 shard_map.92
  56.0 0.2 collective-permute-start.10
  56.2 0.0 collective-permute-start.9
  56.2 2.5 %collective-permute-start.8 = (bf16[128,1024]{1,0:T(8,128)(2,1)S(1)}, bf16[128,1024]{1,0:T(8,128)(2,1)S(1)}, u32[]{:S(2)}, u32[]{:S(2)}) collective-permute-start(bf16[128,1024]{1,0:T(8,128)(2,1)S(1)} %get-tuple-element.81.refs_0_), channel_id=1, source_target_pairs={{0,2},{2,0},{4,6},{6,4},{8,10},{10,8},{12,14},{14,12},{16,18},{18,... | collective-permute-start | bytes 786440 | tf_op jit(solution)/shard_map/ppermute | solution.py:36
  58.7 0.7 shard_map.95.gain_ref
  59.4 1.7 %shard_map.94.weight_ref = bf16[1024,1024]{1,0:T(8,128)(2,1)S(1)} custom-call(bf16[1024,1024]{1,0:T(8,128)(2,1)} %bitcast.13), custom_call_target="tpu_custom_call" | custom-call | tf_op jit(solution)/shard_map/pallas_call | solution.py:405
  61.1 0.1 copy-done.5
  61.2 0.1 copy-done.6
  61.2 0.1 copy-done.7
  61.3 2.2 %shard_map.93.columns_ref = bf16[1024,512]{1,0:T(8,128)(2,1)S(1)} custom-call(s32[1]{0:T(128)} %bitcast.slot_ref, bf16[1,1024]{1,0:T(2,128)(2,1)} %in_ref.1, bf16[128,4096]{1,0:T(8,128)(2,1)} %bitcast.12, bf16[128,1024]{1,0:T(8,128)(2,1)S(1)} %copy-done.2, bf16[128,1024]{1,0:T(8,128)(2,1)S(1)} %copy-done.3, bf16[128,1024]{1,0:T(8,128)(2,1)S(1)} %copy-done.4, ...), custom_call_target="tpu_custom_call" | custom-call | tf_op jit(solution)/shard_map/pallas_call | solution.py:285
  63.6 4.0 %collective-permute-done.10.refs_3_ = bf16[128,1024]{1,0:T(8,128)(2,1)S(1)} collective-permute-done((bf16[128,1024]{1,0:T(8,128)(2,1)S(1)}, bf16[128,1024]{1,0:T(8,128)(2,1)S(1)}, u32[]{:S(2)}, u32[]{:S(2)}) %collective-permute-start.10) | collective-permute-done | bytes 262176 | tf_op jit(solution)/shard_map/ppermute | solution.py:36
  67.5 2.1 %collective-permute-done.9.refs_2_ = bf16[128,1024]{1,0:T(8,128)(2,1)S(1)} collective-permute-done((bf16[128,1024]{1,0:T(8,128)(2,1)S(1)}, bf16[128,1024]{1,0:T(8,128)(2,1)S(1)}, u32[]{:S(2)}, u32[]{:S(2)}) %collective-permute-start.9) | collective-permute-done | bytes 262176 | tf_op jit(solution)/shard_map/ppermute | solution.py:36
  69.6 0.0 collective-permute-done.8.refs_1_
  69.6 1.9 %shard_map.96 = (bf16[128,1024]{1,0:T(8,128)(2,1)S(1)}, bf16[128,1024]{1,0:T(8,128)(2,1)S(1)}, bf16[128,1024]{1,0:T(8,128)(2,1)S(1)}, bf16[128,1024]{1,0:T(8,128)(2,1)S(1)}, bf16[528,1024]{1,0:T(8,128)(2,1)S(1)}) custom-call(s32[1]{0:T(128)S(6)} %sub.3.half_ref, bf16[1024,1024]{1,0:T(8,128)(2,1)S(1)} %shard_map.94.weight_ref, ...), custom_call_target="tpu_custom_call" | custom-call | tf_op jit(solution)/shard_map/pallas_call | solution.py:389
  71.6 1.3 %collective-permute-start.11 = (bf16[528,1024]{1,0:T(8,128)(2,1)S(1)}, bf16[528,1024]{1,0:T(8,128)(2,1)S(1)}, u32[]{:S(2)}, u32[]{:S(2)}) collective-permute-start(bf16[528,1024]{1,0:T(8,128)(2,1)S(1)} %get-tuple-element.94), channel_id=1, source_target_pairs={{0,1},{1,0},{2,3},{3,2},{4,5},{5,4},{6,7},{7,6},{8,9},{9,8},{10,11... | collective-permute-start | bytes 3244040 | tf_op jit(solution)/shard_map/ppermute | solution.py:491
  72.9 11.4 %collective-permute-start.12 = (bf16[128,1024]{1,0:T(8,128)(2,1)S(1)}, bf16[128,1024]{1,0:T(8,128)(2,1)S(1)}, u32[]{:S(2)}, u32[]{:S(2)}) collective-permute-start(bf16[128,1024]{1,0:T(8,128)(2,1)S(1)} %get-tuple-element.100), channel_id=1, source_target_pairs={{0,28},{2,30},{4,24},{6,26},{8,4},{10,6},{12,0},{14,2},{16,12},{18... | collective-permute-start | bytes 786440 | tf_op jit(solution)/shard_map/ppermute | solution.py:36
  84.3 0.0 collective-permute-start.13
  84.3 1.5 %collective-permute-start.15 = (bf16[128,1024]{1,0:T(8,128)(2,1)S(1)}, bf16[128,1024]{1,0:T(8,128)(2,1)S(1)}, u32[]{:S(2)}, u32[]{:S(2)}) collective-permute-start(bf16[128,1024]{1,0:T(8,128)(2,1)S(1)} %get-tuple-element.103), channel_id=1, source_target_pairs={{0,24},{2,26},{4,28},{6,30},{8,0},{10,2},{12,4},{14,6},{16,8},{18,... | collective-permute-start | bytes 786440 | tf_op jit(solution)/shard_map/ppermute | solution.py:36
  85.8 3.0 %collective-permute-done.11.got_ref = bf16[528,1024]{1,0:T(8,128)(2,1)S(1)} collective-permute-done((bf16[528,1024]{1,0:T(8,128)(2,1)S(1)}, bf16[528,1024]{1,0:T(8,128)(2,1)S(1)}, u32[]{:S(2)}, u32[]{:S(2)}) %collective-permute-start.11) | collective-permute-done | bytes 1081376 | tf_op jit(solution)/shard_map/ppermute | solution.py:491
  88.8 1.8 %shard_map.97 = (bf16[512,1024]{1,0:T(8,128)(2,1)}, f32[1,512]{1,0:T(1,128)}) custom-call(s32[1]{0:T(128)} %bitcast.1.half_ref, bf16[1024,1024]{1,0:T(8,128)(2,1)S(1)} %shard_map.94.weight_ref, bf16[1,1024]{1,0:T(2,128)(2,1)S(1)} %shard_map.95.gain_ref, bf16[1024,512]{1,0:T(8,128)(2,1)S(1)} %shard_map.93.columns_ref, ...), custom_call_target="tpu_custom_call" | custom-call | tf_op jit(solution)/shard_map/pallas_call | solution.py:368
  90.6 5.0 %collective-permute-done.12.refs_0_ = bf16[128,1024]{1,0:T(8,128)(2,1)S(1)} collective-permute-done((bf16[128,1024]{1,0:T(8,128)(2,1)S(1)}, bf16[128,1024]{1,0:T(8,128)(2,1)S(1)}, u32[]{:S(2)}, u32[]{:S(2)}) %collective-permute-start.12) | collective-permute-done | bytes 262176 | tf_op jit(solution)/shard_map/ppermute | solution.py:36
  95.6 1.1 %collective-permute-done.13.refs_1_ = bf16[128,1024]{1,0:T(8,128)(2,1)S(1)} collective-permute-done((bf16[128,1024]{1,0:T(8,128)(2,1)S(1)}, bf16[128,1024]{1,0:T(8,128)(2,1)S(1)}, u32[]{:S(2)}, u32[]{:S(2)}) %collective-permute-start.13) | collective-permute-done | bytes 262176 | tf_op jit(solution)/shard_map/ppermute | solution.py:36
  96.7 8.1 %collective-permute-done.14.refs_2_ = bf16[128,1024]{1,0:T(8,128)(2,1)S(1)} collective-permute-done((bf16[128,1024]{1,0:T(8,128)(2,1)S(1)}, bf16[128,1024]{1,0:T(8,128)(2,1)S(1)}, u32[]{:S(2)}, u32[]{:S(2)}) %collective-permute-start.14) | collective-permute-done | bytes 262176 | tf_op jit(solution)/shard_map/ppermute | solution.py:36
  104.7 0.0 collective-permute-done.15.refs_3_
  104.8 1.9 %shard_map.98 = bf16[128,4096]{1,0:T(8,128)(2,1)} custom-call(s32[1]{0:T(128)} %bitcast.slot_ref, bf16[128,4096]{1,0:T(8,128)(2,1)S(1)} %copy-done, bf16[128,4096]{1,0:T(8,128)(2,1)S(1)} %copy-done.1, f32[128,128]{1,0:T(8,128)S(1)} %copy-done.8, bf16[128,1024]{1,0:T(8,128)(2,1)S(1)} %collective-permute-done.12.refs_0_, ...), custom_call_target="tpu_custom_call" | custom-call | tf_op jit(solution)/shard_map/pallas_call | solution.py:439
  (16 shorter events, 0.0 us)
Async XLA Ops:
  0.6 34.0 %collective-permute-start.6 = (bf16[128,4096]{1,0:T(8,128)(2,1)}, bf16[128,4096]{1,0:T(8,128)(2,1)S(1)}, u32[]{:S(2)}, u32[]{:S(2)}) collective-permute-start(bf16[128,4096]{1,0:T(8,128)(2,1)} %bitcast.9), channel_id=1, source_target_pairs={{0,24},{8,0},{16,8},{24,16},{1,25},{9,1},{17,9},{25,17},{2,26},{10... | collective-permute-start | bytes 3145736 | tf_op jit(solution)/shard_map/ppermute | solution.py:464
  1.4 33.2 %collective-permute-start.7 = (bf16[128,4096]{1,0:T(8,128)(2,1)}, bf16[128,4096]{1,0:T(8,128)(2,1)S(1)}, u32[]{:S(2)}, u32[]{:S(2)}) collective-permute-start(bf16[128,4096]{1,0:T(8,128)(2,1)} %bitcast.18), channel_id=1, source_target_pairs={{0,24},{8,0},{16,8},{24,16},{1,25},{9,1},{17,9},{25,17},{2,26},{10... | collective-permute-start | bytes 3145736 | tf_op jit(solution)/shard_map/ppermute | solution.py:465
  3.4 10.0 %collective-permute-start = (bf16[128,1024]{1,0:T(8,128)(2,1)S(1)}, bf16[128,1024]{1,0:T(8,128)(2,1)S(1)}, u32[]{:S(2)}, u32[]{:S(2)}) collective-permute-start(bf16[128,1024]{1,0:T(8,128)(2,1)S(1)} %get-tuple-element.54), channel_id=1, source_target_pairs={{0,2},{2,0},{4,6},{6,4},{8,10},{10,8},{12,14},{14,12},{16,18},{18,... | collective-permute-start | bytes 786440 | tf_op jit(solution)/shard_map/ppermute | solution.py:36
  3.7 13.6 %collective-permute-start.1 = (bf16[128,1024]{1,0:T(8,128)(2,1)S(1)}, bf16[128,1024]{1,0:T(8,128)(2,1)S(1)}, u32[]{:S(2)}, u32[]{:S(2)}) collective-permute-start(bf16[128,1024]{1,0:T(8,128)(2,1)S(1)} %get-tuple-element.55), channel_id=1, source_target_pairs={{0,4},{2,6},{4,0},{6,2},{8,12},{10,14},{12,8},{14,10},{16,20},{18,... | collective-permute-start | bytes 786440 | tf_op jit(solution)/shard_map/ppermute | solution.py:36
  6.0 22.5 %collective-permute-start.2 = (bf16[128,1024]{1,0:T(8,128)(2,1)S(1)}, bf16[128,1024]{1,0:T(8,128)(2,1)S(1)}, u32[]{:S(2)}, u32[]{:S(2)}) collective-permute-start(bf16[128,1024]{1,0:T(8,128)(2,1)S(1)} %get-tuple-element.56), channel_id=1, source_target_pairs={{0,6},{2,4},{4,2},{6,0},{8,14},{10,12},{12,10},{14,8},{16,22},{18,... | collective-permute-start | bytes 786440 | tf_op jit(solution)/shard_map/ppermute | solution.py:36
  31.9 8.8 %collective-permute-start.3 = (bf16[128,1024]{1,0:T(8,128)(2,1)S(1)}, bf16[128,1024]{1,0:T(8,128)(2,1)S(1)}, u32[]{:S(2)}, u32[]{:S(2)}) collective-permute-start(bf16[128,1024]{1,0:T(8,128)(2,1)S(1)} %get-tuple-element.72), channel_id=1, source_target_pairs={{0,4},{2,6},{4,0},{6,2},{8,12},{10,14},{12,8},{14,10},{16,20},{18,... | collective-permute-start | bytes 786440 | tf_op jit(solution)/shard_map/ppermute | solution.py:36
  32.0 12.3 %collective-permute-start.4 = (bf16[128,1024]{1,0:T(8,128)(2,1)S(1)}, bf16[128,1024]{1,0:T(8,128)(2,1)S(1)}, u32[]{:S(2)}, u32[]{:S(2)}) collective-permute-start(bf16[128,1024]{1,0:T(8,128)(2,1)S(1)} %get-tuple-element.73), channel_id=1, source_target_pairs={{0,2},{2,0},{4,6},{6,4},{8,10},{10,8},{12,14},{14,12},{16,18},{18,... | collective-permute-start | bytes 786440 | tf_op jit(solution)/shard_map/ppermute | solution.py:36
  34.1 20.9 %collective-permute-start.5 = (bf16[128,1024]{1,0:T(8,128)(2,1)S(1)}, bf16[128,1024]{1,0:T(8,128)(2,1)S(1)}, u32[]{:S(2)}, u32[]{:S(2)}) collective-permute-start(bf16[128,1024]{1,0:T(8,128)(2,1)S(1)} %get-tuple-element.74), channel_id=1, source_target_pairs={{0,6},{2,4},{4,2},{6,0},{8,14},{10,12},{12,10},{14,8},{16,22},{18,... | collective-permute-start | bytes 786440 | tf_op jit(solution)/shard_map/ppermute | solution.py:36
  56.0 11.6 %collective-permute-start.10 = (bf16[128,1024]{1,0:T(8,128)(2,1)S(1)}, bf16[128,1024]{1,0:T(8,128)(2,1)S(1)}, u32[]{:S(2)}, u32[]{:S(2)}) collective-permute-start(bf16[128,1024]{1,0:T(8,128)(2,1)S(1)} %get-tuple-element.81.refs_0_), channel_id=1, source_target_pairs={{0,6},{2,4},{4,2},{6,0},{8,14},{10,12},{12,10},{14,8},{16,22},{18,... | collective-permute-start | bytes 786440 | tf_op jit(solution)/shard_map/ppermute | solution.py:36
  56.2 13.5 %collective-permute-start.9 = (bf16[128,1024]{1,0:T(8,128)(2,1)S(1)}, bf16[128,1024]{1,0:T(8,128)(2,1)S(1)}, u32[]{:S(2)}, u32[]{:S(2)}) collective-permute-start(bf16[128,1024]{1,0:T(8,128)(2,1)S(1)} %get-tuple-element.81.refs_0_), channel_id=1, source_target_pairs={{0,4},{2,6},{4,0},{6,2},{8,12},{10,14},{12,8},{14,10},{16,20},{18,... | collective-permute-start | bytes 786440 | tf_op jit(solution)/shard_map/ppermute | solution.py:36
  56.2 13.5 %collective-permute-start.8 = (bf16[128,1024]{1,0:T(8,128)(2,1)S(1)}, bf16[128,1024]{1,0:T(8,128)(2,1)S(1)}, u32[]{:S(2)}, u32[]{:S(2)}) collective-permute-start(bf16[128,1024]{1,0:T(8,128)(2,1)S(1)} %get-tuple-element.81.refs_0_), channel_id=1, source_target_pairs={{0,2},{2,0},{4,6},{6,4},{8,10},{10,8},{12,14},{14,12},{16,18},{18,... | collective-permute-start | bytes 786440 | tf_op jit(solution)/shard_map/ppermute | solution.py:36
  59.4 1.7 %copy-start.2 = (bf16[128,1024]{1,0:T(8,128)(2,1)S(1)}, bf16[128,1024]{1,0:T(8,128)(2,1)}, u32[]{:S(2)}) copy-start(bf16[128,1024]{1,0:T(8,128)(2,1)} %get-tuple-element.82.refs_0_) | copy-start | bytes 786436
  59.4 1.7 %copy-start.3 = (bf16[128,1024]{1,0:T(8,128)(2,1)S(1)}, bf16[128,1024]{1,0:T(8,128)(2,1)}, u32[]{:S(2)}) copy-start(bf16[128,1024]{1,0:T(8,128)(2,1)} %get-tuple-element.83.refs_1_) | copy-start | bytes 786436
  59.4 1.7 %copy-start.4 = (bf16[128,1024]{1,0:T(8,128)(2,1)S(1)}, bf16[128,1024]{1,0:T(8,128)(2,1)}, u32[]{:S(2)}) copy-start(bf16[128,1024]{1,0:T(8,128)(2,1)} %get-tuple-element.84.refs_2_) | copy-start | bytes 786436
  59.4 1.8 %copy-start.5 = (bf16[128,1024]{1,0:T(8,128)(2,1)S(1)}, bf16[128,1024]{1,0:T(8,128)(2,1)}, u32[]{:S(2)}) copy-start(bf16[128,1024]{1,0:T(8,128)(2,1)} %get-tuple-element.85.refs_3_) | copy-start | bytes 786436
  59.4 1.9 %copy-start.6 = (bf16[128,1024]{1,0:T(8,128)(2,1)S(1)}, bf16[128,1024]{1,0:T(8,128)(2,1)}, u32[]{:S(2)}) copy-start(bf16[128,1024]{1,0:T(8,128)(2,1)} %get-tuple-element.86.refs_4_) | copy-start | bytes 786436
  59.4 2.0 %copy-start.7 = (bf16[128,1024]{1,0:T(8,128)(2,1)S(1)}, bf16[128,1024]{1,0:T(8,128)(2,1)}, u32[]{:S(2)}) copy-start(bf16[128,1024]{1,0:T(8,128)(2,1)} %get-tuple-element.87.refs_5_) | copy-start | bytes 786436
  71.6 17.2 %collective-permute-start.11 = (bf16[528,1024]{1,0:T(8,128)(2,1)S(1)}, bf16[528,1024]{1,0:T(8,128)(2,1)S(1)}, u32[]{:S(2)}, u32[]{:S(2)}) collective-permute-start(bf16[528,1024]{1,0:T(8,128)(2,1)S(1)} %get-tuple-element.94), channel_id=1, source_target_pairs={{0,1},{1,0},{2,3},{3,2},{4,5},{5,4},{6,7},{7,6},{8,9},{9,8},{10,11... | collective-permute-start | bytes 3244040 | tf_op jit(solution)/shard_map/ppermute | solution.py:491
  72.9 22.8 %collective-permute-start.12 = (bf16[128,1024]{1,0:T(8,128)(2,1)S(1)}, bf16[128,1024]{1,0:T(8,128)(2,1)S(1)}, u32[]{:S(2)}, u32[]{:S(2)}) collective-permute-start(bf16[128,1024]{1,0:T(8,128)(2,1)S(1)} %get-tuple-element.100), channel_id=1, source_target_pairs={{0,28},{2,30},{4,24},{6,26},{8,4},{10,6},{12,0},{14,2},{16,12},{18... | collective-permute-start | bytes 786440 | tf_op jit(solution)/shard_map/ppermute | solution.py:36
  84.3 12.4 %collective-permute-start.13 = (bf16[128,1024]{1,0:T(8,128)(2,1)S(1)}, bf16[128,1024]{1,0:T(8,128)(2,1)S(1)}, u32[]{:S(2)}, u32[]{:S(2)}) collective-permute-start(bf16[128,1024]{1,0:T(8,128)(2,1)S(1)} %get-tuple-element.101), channel_id=1, source_target_pairs={{0,26},{2,24},{4,30},{6,28},{8,2},{10,0},{12,6},{14,4},{16,10},{18... | collective-permute-start | bytes 786440 | tf_op jit(solution)/shard_map/ppermute | solution.py:36
  84.3 20.4 %collective-permute-start.14 = (bf16[128,1024]{1,0:T(8,128)(2,1)S(1)}, bf16[128,1024]{1,0:T(8,128)(2,1)S(1)}, u32[]{:S(2)}, u32[]{:S(2)}) collective-permute-start(bf16[128,1024]{1,0:T(8,128)(2,1)S(1)} %get-tuple-element.102), channel_id=1, source_target_pairs={{0,30},{2,28},{4,26},{6,24},{8,6},{10,4},{12,2},{14,0},{16,14},{18... | collective-permute-start | bytes 786440 | tf_op jit(solution)/shard_map/ppermute | solution.py:36
  84.3 20.4 %copy-start = (bf16[128,4096]{1,0:T(8,128)(2,1)S(1)}, bf16[128,4096]{1,0:T(8,128)(2,1)}, u32[]{:S(2)}) copy-start(bf16[128,4096]{1,0:T(8,128)(2,1)} %get-tuple-element.97.x_ref) | copy-start | bytes 3145732
  84.3 20.4 %copy-start.1 = (bf16[128,4096]{1,0:T(8,128)(2,1)S(1)}, bf16[128,4096]{1,0:T(8,128)(2,1)}, u32[]{:S(2)}) copy-start(bf16[128,4096]{1,0:T(8,128)(2,1)} %get-tuple-element.98.grad_ref) | copy-start | bytes 3145732
  84.3 20.4 %copy-start.8 = (f32[128,128]{1,0:T(8,128)S(1)}, f32[128,128]{1,0:T(8,128)}, u32[]{:S(2)}) copy-start(f32[128,128]{1,0:T(8,128)} %get-tuple-element.99.square_ref) | copy-start | bytes 196612
  84.3 20.4 %collective-permute-start.15 = (bf16[128,1024]{1,0:T(8,128)(2,1)S(1)}, bf16[128,1024]{1,0:T(8,128)(2,1)S(1)}, u32[]{:S(2)}, u32[]{:S(2)}) collective-permute-start(bf16[128,1024]{1,0:T(8,128)(2,1)S(1)} %get-tuple-element.103), channel_id=1, source_target_pairs={{0,24},{2,26},{4,28},{6,30},{8,0},{10,2},{12,4},{14,6},{16,8},{18,... | collective-permute-start | bytes 786440 | tf_op jit(solution)/shard_map/ppermute | solution.py:36
